TPU v7x, 256 devices: a whole 4x4x8 slice. The times are simulated.
256 devices in a mesh: replica: 32 (over z, y_lo, core), mp: 8 (over x, y_hi).
Axes of the slice: x: 4, y: 4 (y_hi: 2, y_lo: 2; y = y_hi * 2 + y_lo), z: 8, core: 2. Of those that a mesh axis runs over, the one named last changes fastest.
Arguments:
- local_weights: bfloat16 [2, 32, 8, 128, 3072], P(None, 'replica', 'mp'), may hold values from -32 to 32, as said below
- global_params: float32 [2, 8, 128, 3072], P(None, 'mp', 'replica'), may hold values from -25 to 25
- momentum: float32 [2, 8, 128, 3072], P(None, 'mp', 'replica'), may hold values from -3 to 3
Outputs:
- mixed_weights: bfloat16 [2, 32, 8, 128, 3072], P(None, 'replica', 'mp')
- new_global: float32 [2, 8, 128, 3072], P(None, 'mp', 'replica')
- new_momentum: float32 [2, 8, 128, 3072], P(None, 'mp', 'replica')
Inputs may be any that keep to these rules, and one draw needn't show every extreme that they name: `local_weights`: replica groups' weights.
All inputs are finite; a program needn't handle non-finite values.
Results may differ from a plain program's by a relative error of at most 0.0042.
Values may be sent and summed in bfloat16 or wider, within the bound.
No kernel may reach another device: no remote copies, remote signals or barrier semaphores. Data moves between devices by JAX's collectives and lax.ppermute only.
A program may use at most 64 MiB of HBM per device.

v0:
```python
import math

import jax
import jax.numpy as jnp
from jax import lax
from jax.sharding import PartitionSpec as P


def clip_factor(share, max_norm):
    square_sum = lax.psum(jnp.sum(share * share), ("replica", "mp"))
    return jnp.minimum(1.0, max_norm / (jnp.sqrt(square_sum) + 1e-06))


def shards(local_weights, global_params, momentum):
    replicas = lax.axis_size("replica")
    rank = lax.axis_index("replica")
    share_rows = global_params.shape[2]
    count = share_rows * global_params.shape[3] * replicas * lax.axis_size("mp")
    max_norm = 0.5 * math.sqrt(count)
    mixed_list = []
    global_list = []
    moment_list = []
    for frag in range(global_params.shape[0]):
        own = local_weights[frag, 0, 0]
        outer = global_params[frag, 0]
        moment = momentum[frag, 0]
        total = lax.psum(own.astype(jnp.float32), "replica")
        outer_all, moment_all = (
            lax.all_gather(outer, "replica", axis=0, tiled=True),
            lax.all_gather(moment, "replica", axis=0, tiled=True),
        )
        pseudo = outer_all - total / replicas
        mine = lax.dynamic_slice_in_dim(pseudo, rank * share_rows, share_rows, 0)
        factor = clip_factor(mine, max_norm)
        clipped = factor * pseudo
        moment_all = 0.9 * moment_all + clipped
        outer_all = outer_all - 0.7 * (clipped + 0.9 * moment_all)
        mix_source = lax.optimization_barrier(outer_all.astype(jnp.bfloat16)).astype(jnp.float32)
        mixed = (0.5 * own.astype(jnp.float32) + 0.5 * mix_source).astype(jnp.bfloat16)
        outer_next = lax.dynamic_slice_in_dim(outer_all, rank * share_rows, share_rows, 0)
        moment_next = lax.dynamic_slice_in_dim(moment_all, rank * share_rows, share_rows, 0)
        mixed_list.append(mixed[None, None])
        global_list.append(outer_next[None])
        moment_list.append(moment_next[None])
    return (jnp.stack(mixed_list), jnp.stack(global_list), jnp.stack(moment_list))


def solution(mesh):
    placed = (
        P(None, "replica", "mp", None, None),
        P(None, "mp", "replica", None),
        P(None, "mp", "replica", None),
    )
    return jax.shard_map(
        shards,
        mesh=mesh,
        in_specs=placed,
        out_specs=(
            P(None, "replica", "mp", None, None),
            P(None, "mp", "replica", None),
            P(None, "mp", "replica", None),
        ),
        check_vma=False,
    )
```

profile of v0, /device:TPU:1, one launch (start us, length us, event | category | flops | bytes accessed | tf_op | source)
XLA Modules:
  0.0 530.3 jit_solution(11038040507168009723)
XLA Ops:
  7.2 0.0 all-gather.13.cloned.1.call-start
  7.2 0.8 fusion.5
  8.0 0.7 copy.16
  8.7 0.0 all-gather.13.cloned.1.call-update
  8.7 0.0 all-reduce.4.cloned.1.call-start
  8.8 3.4 bitcast_convert_fusion.1
  12.2 0.0 copy-start.2
  12.2 0.0 all-reduce.4.cloned.1.call-update
  12.2 0.0 all-gather.9.cloned.1.call-start
  12.2 0.7 copy.14
  12.9 0.0 all-gather.9.cloned.1.call-update
  12.9 0.0 all-gather.15.cloned.1.call-start
  13.0 0.1 copy-done.2
  13.1 0.7 copy.17
  13.7 0.0 all-gather.15.cloned.1.call-update
  13.7 0.0 all-gather.11.cloned.1.call-start
  13.8 0.7 copy.15
  14.5 0.0 all-gather.11.cloned.1.call-update
  14.5 63.9 %all-gather.13.cloned.1.call-done = f32[1,1,128,3072]{3,1,0,2:T(1,128)} async-done(((f32[1,1,4,3072]{3,1,0,2:T(1,128)}), f32[1,1,128,3072]{3,1,0,2:T(1,128)}) %all-gather.13.cloned.1.call-update) | async-done | bytes 1572880 | tf_op jit(solution)/shard_map/all_gather | solution.py:29
  78.4 237.5 %all-reduce.4.cloned.1.call-done = (f32[128,3072]{1,0:T(8,128)}, f32[128,3072]{1,0:T(8,128)}) async-done(((f32[128,3072]{1,0:T(8,128)}, f32[128,3072]{1,0:T(8,128)}), (f32[128,3072]{1,0:T(8,128)}, f32[128,3072]{1,0:T(8,128)})) %all-reduce.4.cloned.1.call-update) | async-done | bytes 3145744 | tf_op jit(solution)/shard_map/psum | solution.py:27
  315.9 2.3 bitcast_subtract_fusion.1
  318.2 0.6 multiply_reduce_fusion
  318.8 64.6 %all-gather.9.cloned.1.call-done = f32[1,1,128,3072]{3,1,0,2:T(1,128)} async-done(((f32[1,1,4,3072]{3,1,0,2:T(1,128)}), f32[1,1,128,3072]{3,1,0,2:T(1,128)}) %all-gather.9.cloned.1.call-update) | async-done | bytes 1572880 | tf_op jit(solution)/shard_map/all_gather | solution.py:29
  383.4 2.3 bitcast_subtract_fusion.3
  385.7 0.6 multiply_reduce_fusion.1
  386.3 76.0 %all-reduce = (f32[]{:T(128)}, f32[]{:T(128)}) all-reduce(f32[]{:T(128)} %multiply_reduce_fusion, f32[]{:T(128)} %multiply_reduce_fusion.1), channel_id=1, replica_groups=mesh['replica'=32,'mp'=8] {'replica','mp'}, use_global_device_ids=true, to_apply=%region_5.0 | all-reduce | flops 2 | bytes 16 | tf_op jit(solution)/shard_map/psum | solution.py:10
  463.7 0.0 all-gather.15.cloned.1.call-done
  463.8 4.9 fusion.3
  468.6 0.0 copy-start.1
  468.6 47.1 %all-gather.11.cloned.1.call-done = f32[1,1,128,3072]{3,1,0,2:T(1,128)} async-done(((f32[1,1,4,3072]{3,1,0,2:T(1,128)}), f32[1,1,128,3072]{3,1,0,2:T(1,128)}) %all-gather.11.cloned.1.call-update) | async-done | bytes 1572880 | tf_op jit(solution)/shard_map/all_gather | solution.py:30
  515.8 0.0 copy-start
  515.8 2.9 fusion.2
  518.7 0.9 dynamic-slice_bitcast_fusion
  519.7 0.7 pad_maximum_fusion.2
  520.3 0.9 dynamic-slice_bitcast_fusion.2
  521.2 0.7 pad_maximum_fusion.1
  521.9 0.0 copy-done.1
  521.9 0.0 copy-done
  521.9 0.6 fusion
  522.5 1.3 pad_maximum_fusion
  (1 shorter events, 0.0 us)
Async XLA Ops:
  7.2 71.3 %all-gather.13.cloned.1.call-start = ((), (), s32[]{:S(2)}) async-start(), calls=%async_computation.2 | async-start | bytes 1622016 | tf_op jit(solution)/shard_map/all_gather | solution.py:29
  8.7 307.2 %all-reduce.4.cloned.1.call-start = ((), (), s32[]{:S(2)}) async-start(), calls=%async_computation.4 | async-start | bytes 6291456 | tf_op jit(solution)/shard_map/psum | solution.py:27
  12.2 0.9 copy-start.2
  12.2 371.2 %all-gather.9.cloned.1.call-start = ((), (), s32[]{:S(2)}) async-start(), calls=%async_computation | async-start | bytes 1622016 | tf_op jit(solution)/shard_map/all_gather | solution.py:29
  12.9 450.8 %all-gather.15.cloned.1.call-start = ((), (), s32[]{:S(2)}) async-start(), calls=%async_computation.3 | async-start | bytes 1622016 | tf_op jit(solution)/shard_map/all_gather | solution.py:30
  13.7 502.0 %all-gather.11.cloned.1.call-start = ((), (), s32[]{:S(2)}) async-start(), calls=%async_computation.1 | async-start | bytes 1622016 | tf_op jit(solution)/shard_map/all_gather | solution.py:30
  468.6 53.3 %copy-start.1 = (bf16[128,3072]{1,0:T(8,128)(2,1)S(1)}, bf16[128,3072]{1,0:T(8,128)(2,1)}, u32[]{:S(2)}) copy-start(bf16[128,3072]{1,0:T(8,128)(2,1)} %get-tuple-element.9) | copy-start | bytes 2359300
  515.8 6.1 %copy-start = (bf16[2,1,1,128,3072]{4,3,2,1,0:T(8,128)(2,1)S(1)}, bf16[2,1,1,128,3072]{4,3,2,1,0:T(8,128)(2,1)}, u32[]{:S(2)}) copy-start(bf16[2,1,1,128,3072]{4,3,2,1,0:T(8,128)(2,1)} %param.3) | copy-start | bytes 4718596
Sparse Core Ops, SparseCore 0:
  9.9 68.5 all-gather.12
  81.7 234.1 all-reduce.3
  318.5 64.8 all-gather.8
  385.3 64.0 all-gather.14
  451.8 63.9 all-gather.10
where the time goes:
time: 531 us; the launch traced here: 530 us
  waiting for transfers between devices  413 us (78%)
  blocking collectives  76 us (14%)
  other arithmetic  20.2 us (4%)
  between operations  15.3 us (3%)
  local copies, waits for them, and re-layouts  5.41 us (1%)
    psum x1, waiting for transfers between devices, shards(): total = lax.psum(own.astype(jnp.float32), 'replica')  237 us
    all_gather x2, waiting for transfers between devices, shards(): lax.all_gather(outer, 'replica', axis=0, tiled=True)  129 us
    psum x1, blocking collectives, clip_factor(): square_sum = lax.psum(jnp.sum(share * share), ('replica', 'mp'))  76 us
    all_gather x2, waiting for transfers between devices, shards(): lax.all_gather(moment, 'replica', axis=0, tiled=True)  47.2 us
  transfers between devices with their start and end apart: 5, of which 4 were waited for; matrix products, arithmetic and copies ran while one was open for 3% of the time, Pallas kernels for 0%

commit v1 on v0

v1 whole, which is shorter than its diff:
```python
import math

import jax
import jax.numpy as jnp
from jax import lax
from jax.sharding import Mesh
from jax.sharding import PartitionSpec as P

CHIPS = ("z", "yl")
SWAP = ((0, 1), (1, 0))


def shards(local_weights, global_params, momentum):
    f32, bf16 = jnp.float32, jnp.bfloat16
    core = lax.axis_index("core")
    other = 1 - core
    chips = lax.axis_size(CHIPS)
    replicas = 2 * chips
    everywhere = chips * lax.axis_size(("x", "yh"))
    rows, width = local_weights.shape[3], local_weights.shape[4]
    share_rows = global_params.shape[2]
    block = rows // chips
    max_norm = 0.5 * math.sqrt(block * width * everywhere)

    weights = local_weights[:, 0, 0]
    state = jnp.stack((global_params[:, 0], momentum[:, 0]), axis=1)
    sent = lax.dynamic_index_in_dim(weights, other, 0, keepdims=False)
    got = lax.ppermute(sent, "core", SWAP)
    state_mine = lax.dynamic_index_in_dim(state, core, 0, keepdims=False)
    state_got = lax.ppermute(
        lax.dynamic_index_in_dim(state, other, 0, keepdims=False), "core", SWAP
    )
    own = lax.dynamic_index_in_dim(weights, core, 0, keepdims=False)
    pair = (own.astype(f32) + got.astype(f32)).astype(bf16)
    pieces = lax.all_to_all(
        pair.reshape(chips, block, width), CHIPS, 0, 0, tiled=True
    )
    total = jnp.sum(pieces.astype(f32), axis=0)
    first = core == 0
    outer, moment = jnp.where(
        first,
        jnp.concatenate((state_mine, state_got), axis=1),
        jnp.concatenate((state_got, state_mine), axis=1),
    )
    pseudo = outer - total / replicas
    part = jnp.sum(pseudo * pseudo)
    parts = lax.all_to_all(
        jnp.broadcast_to(part, (everywhere, 1, 128)),
        ("z", "yl", "x", "yh"),
        0,
        0,
        tiled=True,
    )
    square_sum = jnp.sum(parts[:, 0, 0])
    factor = jnp.minimum(1.0, max_norm / (jnp.sqrt(square_sum) + 1e-06))
    clipped = factor * pseudo
    moment_next = 0.9 * moment + clipped
    outer_next = outer - 0.7 * (clipped + 0.9 * moment_next)
    source = outer_next.astype(bf16)
    gathered = lax.all_to_all(
        jnp.broadcast_to(source, (chips, block, width)), CHIPS, 0, 0, tiled=True
    ).reshape(rows, width)
    swapped = lax.ppermute(gathered, "core", SWAP)

    state_next = jnp.stack((outer_next, moment_next))
    halves = state_next.reshape(2, 2, share_rows, width)
    keep = lax.dynamic_index_in_dim(halves, core, 1, keepdims=False)
    give = lax.dynamic_index_in_dim(halves, other, 1, keepdims=False)
    take = lax.ppermute(give, "core", SWAP)
    state_out = jnp.where(first, jnp.stack((keep, take)), jnp.stack((take, keep)))

    sources = jnp.where(
        first, jnp.stack((gathered, swapped)), jnp.stack((swapped, gathered))
    )
    mixed = (0.5 * weights.astype(f32) + 0.5 * sources.astype(f32)).astype(bf16)
    return (
        mixed[:, None, None],
        state_out[:, 0][:, None],
        state_out[:, 1][:, None],
    )


def solution(mesh):
    fine = Mesh(
        mesh.devices.reshape(8, 2, 2, 4, 2), ("z", "yl", "core", "x", "yh")
    )
    replica, mp = ("z", "yl", "core"), ("x", "yh")
    whole = P(None, replica, mp, None, None)
    outer = P(None, mp, replica, None)
    return jax.shard_map(
        shards,
        mesh=fine,
        in_specs=(whole, outer, outer),
        out_specs=(whole, outer, outer),
        check_vma=False,
    )
```

time: 531 us -> 94.6 us (0.18)
  waiting for transfers between devices: 413 us -> 40.2 us
  blocking collectives: 76 us -> 22.2 us
  starting transfers between devices: 0.21 us -> 22 us
  other arithmetic: 20.2 us -> 4.53 us
  between operations: 15.3 us -> 1.52 us
    psum x1 -> x0, waiting for transfers between devices: 237 us -> none  [shards(): total = lax.psum(own.astype(jnp.float32), 'replica')]
    all_gather x4 -> x0, waiting for transfers between devices: 176 us -> none  [the longest x2 129 us: shards(): lax.all_gather(outer, 'replica', axis=0, tiled=True)]
    psum x1 -> x0, blocking collectives: 76 us -> none  [clip_factor(): square_sum = lax.psum(jnp.sum(share * share), ('replica', 'mp'))]
    all_to_all x0 -> x2, waiting for transfers between devices: none -> 36.2 us  [the longest x1 19 us: shards(): lax.all_to_all(pair.reshape(chips, block, width), CHIPS, 0, 0, tiled=True)]
    all_to_all x0 -> x1, blocking collectives: none -> 22.2 us  [shards(): lax.all_to_all(jnp.broadcast_to(part, (everywhere, 1, 128)), ('z', 'yl',...]
    all_to_all x0 -> x2, starting transfers between devices: none -> 11.2 us  [the longest x1 7.57 us: shards(): lax.all_to_all(pair.reshape(chips, block, width), CHIPS, 0, 0, tiled=True)]
    ppermute x0 -> x4, starting transfers between devices: none -> 10.9 us  [the longest x1 4.77 us: shards(): swapped = lax.ppermute(gathered, 'core', SWAP)]
    convert_element_type x3 -> x2, other arithmetic: 11.2 us -> 1.83 us  [the longest x1 1.79 us: shards(): mixed = (0.5 * weights.astype(f32) + 0.5 * sources.astype(f32)).astype(bf16)]
  transfers between devices with their start and end apart: 5 -> 6, of which waited for: 4 -> 5; matrix products, arithmetic and copies ran while one was open for 3% -> 1% of each run, Pallas kernels for 0% -> 0%
where the time goes in v1:
time: 94.6 us; the launch traced here: 94.2 us
  waiting for transfers between devices  40.2 us (42%)
  blocking collectives  22.2 us (23%)
  starting transfers between devices  22 us (23%)
  other arithmetic  4.53 us (5%)
  local copies, waits for them, and re-layouts  3.79 us (4%)
  between operations  1.52 us (2%)
    all_to_all x1, blocking collectives, shards(): lax.all_to_all(jnp.broadcast_to(part, (everywhere, 1, 128)), ('z', 'yl',...  22.2 us
    all_to_all x1, waiting for transfers between devices, shards(): lax.all_to_all(pair.reshape(chips, block, width), CHIPS, 0, 0, tiled=True)  19 us
    all_to_all x1, waiting for transfers between devices, shards(): lax.all_to_all(jnp.broadcast_to(source, (chips, block, width)), CHIPS, 0,...  17.2 us
    all_to_all x1, starting transfers between devices, shards(): lax.all_to_all(pair.reshape(chips, block, width), CHIPS, 0, 0, tiled=True)  7.57 us
    ppermute x1, starting transfers between devices, shards(): swapped = lax.ppermute(gathered, 'core', SWAP)  4.77 us
    all_to_all x1, starting transfers between devices, shards(): lax.all_to_all(jnp.broadcast_to(source, (chips, block, width)), CHIPS, 0,...  3.61 us
    ppermute x1, starting transfers between devices, shards(): got = lax.ppermute(sent, 'core', SWAP)  3.33 us
    ppermute x1, starting transfers between devices, shards(): take = lax.ppermute(give, 'core', SWAP)  2.02 us
  transfers between devices with their start and end apart: 6, of which 5 were waited for; matrix products, arithmetic and copies ran while one was open for 1% of the time, Pallas kernels for 0%

profile of v1, /device:TPU:1, one launch (start us, length us, event | category | flops | bytes accessed | tf_op | source)
XLA Modules:
  0.0 94.2 jit_solution(1156883499084144655)
XLA Ops:
  0.6 0.0 copy-start
  0.6 1.3 %dynamic-slice_bitcast_fusion = bf16[128,3072]{1,0:T(8,128)(2,1)S(1)} fusion(bf16[2,1,1,128,3072]{4,3,2,1,0:T(8,128)(2,1)} %param.3, s32[]{:T(128)S(6)} %select_n.47), kind=kLoop, calls=%fused_computation.6 | loop fusion | bytes 1572868 | tf_op jit(solution)/shard_map/jit(dynamic_index_in_dim)/squeeze | solution.py:27
  2.0 3.3 %collective-permute-start.1 = (bf16[128,3072]{1,0:T(8,128)(2,1)S(1)}, bf16[128,3072]{1,0:T(8,128)(2,1)S(1)}, u32[]{:S(2)}, u32[]{:S(2)}) collective-permute-start(bf16[128,3072]{1,0:T(8,128)(2,1)S(1)} %dynamic-slice_bitcast_fusion), channel_id=1, source_target_pairs={{0,8},{8,0},{1,9},{9,1},{2,10},{10,2},{3,11},{11,3},{4,12},{12,4},... | collective-permute-start | bytes 2359304 | tf_op jit(solution)/shard_map/ppermute | solution.py:28
  5.3 0.0 copy-start.1
  5.3 0.0 copy-start.2
  5.3 1.9 %collective-permute-done.1 = bf16[128,3072]{1,0:T(8,128)(2,1)S(1)} collective-permute-done((bf16[128,3072]{1,0:T(8,128)(2,1)S(1)}, bf16[128,3072]{1,0:T(8,128)(2,1)S(1)}, u32[]{:S(2)}, u32[]{:S(2)}) %collective-permute-start.1) | collective-permute-done | bytes 786464 | tf_op jit(solution)/shard_map/ppermute | solution.py:28
  7.2 0.0 copy-done
  7.2 1.1 %fusion.1 = bf16[16,8,3072]{2,1,0:T(8,128)(2,1)} fusion(bf16[128,3072]{1,0:T(8,128)(2,1)S(1)} %collective-permute-done.1, bf16[2,1,1,128,3072]{4,3,2,1,0:T(8,128)(2,1)S(1)} %copy-done, s32[]{:T(128)S(6)} %select_n.46), kind=kLoop, calls=%fused_computation.5 | loop fusion | flops 1572864 | bytes 2359300 | tf_op jit(solution)/shard_map/reshape | solution.py:36
  8.3 7.6 %all-to-all-start = ((bf16[16,8,3072]{2,1,0:T(8,128)(2,1)}), bf16[16,8,3072]{2,1,0:T(8,128)(2,1)S(1)}, u32[]{:S(2)}, u32[]{:S(2)}) async-start(bf16[16,8,3072]{2,1,0:T(8,128)(2,1)} %fusion.1), calls=%async_computation | async-start | bytes 1572864 | tf_op jit(solution)/shard_map/all_to_all | solution.py:35
  15.8 0.0 copy-done.1
  15.9 0.0 copy-done.2
  15.9 0.7 collective-permute-start
  16.7 0.9 %collective-permute-done = f32[2,4,3072]{2,1,0:T(4,128)S(1)} collective-permute-done((f32[2,4,3072]{2,1,0:T(4,128)S(1)}, f32[2,4,3072]{2,1,0:T(4,128)S(1)}, u32[]{:S(2)}, u32[]{:S(2)}) %collective-permute-start) | collective-permute-done | bytes 98336 | tf_op jit(solution)/shard_map/ppermute | solution.py:30
  17.6 0.1 maximum_select_fusion.1
  17.7 19.0 %all-to-all-done = bf16[16,8,3072]{2,1,0:T(8,128)(2,1)S(1)} async-done(((bf16[16,8,3072]{2,1,0:T(8,128)(2,1)}), bf16[16,8,3072]{2,1,0:T(8,128)(2,1)S(1)}, u32[]{:S(2)}, u32[]{:S(2)}) %all-to-all-start) | async-done | bytes 786464 | tf_op jit(solution)/shard_map/all_to_all | solution.py:35
  36.7 0.1 convert_reduce_fusion
  36.8 0.6 multiply_reduce_fusion
  37.4 0.7 broadcast_in_dim.7
  38.1 22.2 %all_to_all.15 = f32[128,1,128]{2,1,0:T(1,128)S(1)} all-to-all(f32[128,1,128]{2,1,0:T(1,128)S(1)} %broadcast_in_dim.7), channel_id=1, replica_groups=mesh['z'=8,'yl'=2,'core'=2,'x'=4,'yh'=2] {'z','yl','x','yh'}, dimensions={0} | all-to-all | bytes 131072 | tf_op jit(solution)/shard_map/all_to_all | solution.py:47
  60.3 0.7 slice_reduce_fusion
  61.8 1.0 %broadcast_in_dim.8 = bf16[16,8,3072]{2,1,0:T(8,128)(2,1)} broadcast(bf16[8,3072]{1,0:T(8,128)(2,1)S(1)} %fusion.7), dimensions={1,2} | broadcast | bytes 835584 | tf_op jit(solution)/shard_map/broadcast_in_dim | solution.py:61
  62.7 3.6 %all-to-all-start.2 = ((bf16[16,8,3072]{2,1,0:T(8,128)(2,1)}), bf16[16,8,3072]{2,1,0:T(8,128)(2,1)S(1)}, u32[]{:S(2)}, u32[]{:S(2)}) async-start(bf16[16,8,3072]{2,1,0:T(8,128)(2,1)} %broadcast_in_dim.8), calls=%async_computation.2 | async-start | bytes 1572864 | tf_op jit(solution)/shard_map/all_to_all | solution.py:60
  66.5 2.0 %collective-permute-start.3 = (f32[2,4,3072]{2,1,0:T(4,128)S(1)}, f32[2,4,3072]{2,1,0:T(4,128)S(1)}, u32[]{:S(2)}, u32[]{:S(2)}) collective-permute-start(f32[2,4,3072]{2,1,0:T(4,128)S(1)} %get-tuple-element.8), channel_id=1, source_target_pairs={{0,8},{8,0},{1,9},{9,1},{2,10},{10,2},{3,11},{11,3},{4,12},{12,4},... | collective-permute-start | bytes 294920 | tf_op jit(solution)/shard_map/ppermute | solution.py:69
  68.6 17.2 %all-to-all-done.2 = bf16[16,8,3072]{2,1,0:T(8,128)(2,1)S(1)} async-done(((bf16[16,8,3072]{2,1,0:T(8,128)(2,1)}), bf16[16,8,3072]{2,1,0:T(8,128)(2,1)S(1)}, u32[]{:S(2)}, u32[]{:S(2)}) %all-to-all-start.2) | async-done | bytes 786464 | tf_op jit(solution)/shard_map/all_to_all | solution.py:60
  85.8 4.8 %collective-permute-start.2 = (bf16[128,3072]{1,0:T(8,128)(2,1)S(1)}, bf16[128,3072]{1,0:T(8,128)(2,1)S(1)}, u32[]{:S(2)}, u32[]{:S(2)}) collective-permute-start(bf16[128,3072]{1,0:T(8,128)(2,1)S(1)} %bitcast.47), channel_id=1, source_target_pairs={{0,8},{8,0},{1,9},{9,1},{2,10},{10,2},{3,11},{11,3},{4,12},{12,4},... | collective-permute-start | bytes 2359304 | tf_op jit(solution)/shard_map/ppermute | solution.py:63
  90.5 0.0 collective-permute-done.3
  90.6 0.7 fusion.10
  91.3 1.2 %collective-permute-done.2 = bf16[128,3072]{1,0:T(8,128)(2,1)S(1)} collective-permute-done((bf16[128,3072]{1,0:T(8,128)(2,1)S(1)}, bf16[128,3072]{1,0:T(8,128)(2,1)S(1)}, u32[]{:S(2)}, u32[]{:S(2)}) %collective-permute-start.2) | collective-permute-done | bytes 786464 | tf_op jit(solution)/shard_map/ppermute | solution.py:63
  92.5 1.8 %multiply_convert_fusion = bf16[2,1,1,128,3072]{4,3,2,1,0:T(8,128)(2,1)} fusion(bf16[2,1,1,128,3072]{4,3,2,1,0:T(8,128)(2,1)S(1)} %copy-done, bf16[1,1,1,128,3072]{4,3,2,1,0:T(8,128)(2,1)S(1)} %bitcast.49, bf16[1,1,1,128,3072]{4,3,2,1,0:T(8,128)(2,1)S(1)} %bitcast.48, pred[]{:T(512)S(6)} %eq.3), kind=kLoop, calls=%fused_computation | loop fusion | flops 6291456 | bytes 4718593 | tf_op jit(solution)/shard_map/convert_element_type | solution.py:75
  (11 shorter events, 0.3 us)
Async XLA Ops:
  0.6 6.6 %copy-start = (bf16[2,1,1,128,3072]{4,3,2,1,0:T(8,128)(2,1)S(1)}, bf16[2,1,1,128,3072]{4,3,2,1,0:T(8,128)(2,1)}, u32[]{:S(2)}) copy-start(bf16[2,1,1,128,3072]{4,3,2,1,0:T(8,128)(2,1)} %param.3) | copy-start | bytes 4718596
  2.0 5.2 %collective-permute-start.1 = (bf16[128,3072]{1,0:T(8,128)(2,1)S(1)}, bf16[128,3072]{1,0:T(8,128)(2,1)S(1)}, u32[]{:S(2)}, u32[]{:S(2)}) collective-permute-start(bf16[128,3072]{1,0:T(8,128)(2,1)S(1)} %dynamic-slice_bitcast_fusion), channel_id=1, source_target_pairs={{0,8},{8,0},{1,9},{9,1},{2,10},{10,2},{3,11},{11,3},{4,12},{12,4},... | collective-permute-start | bytes 2359304 | tf_op jit(solution)/shard_map/ppermute | solution.py:28
  5.3 10.6 %copy-start.1 = (f32[2,1,4,3072]{3,2,1,0:T(4,128)S(1)}, f32[2,1,4,3072]{3,2,1,0:T(4,128)}, u32[]{:S(2)}) copy-start(f32[2,1,4,3072]{3,2,1,0:T(4,128)} %param.4) | copy-start | bytes 294916
  5.3 10.6 %copy-start.2 = (f32[2,1,4,3072]{3,2,1,0:T(4,128)S(1)}, f32[2,1,4,3072]{3,2,1,0:T(4,128)}, u32[]{:S(2)}) copy-start(f32[2,1,4,3072]{3,2,1,0:T(4,128)} %param.5) | copy-start | bytes 294916
  8.3 28.4 %all-to-all-start = ((bf16[16,8,3072]{2,1,0:T(8,128)(2,1)}), bf16[16,8,3072]{2,1,0:T(8,128)(2,1)S(1)}, u32[]{:S(2)}, u32[]{:S(2)}) async-start(bf16[16,8,3072]{2,1,0:T(8,128)(2,1)} %fusion.1), calls=%async_computation | async-start | bytes 1572864 | tf_op jit(solution)/shard_map/all_to_all | solution.py:35
  15.9 1.7 %collective-permute-start = (f32[2,4,3072]{2,1,0:T(4,128)S(1)}, f32[2,4,3072]{2,1,0:T(4,128)S(1)}, u32[]{:S(2)}, u32[]{:S(2)}) collective-permute-start(f32[2,4,3072]{2,1,0:T(4,128)S(1)} %get-tuple-element.10), channel_id=1, source_target_pairs={{0,8},{8,0},{1,9},{9,1},{2,10},{10,2},{3,11},{11,3},{4,12},{12,4},... | collective-permute-start | bytes 294920 | tf_op jit(solution)/shard_map/ppermute | solution.py:30
  62.7 23.0 %all-to-all-start.2 = ((bf16[16,8,3072]{2,1,0:T(8,128)(2,1)}), bf16[16,8,3072]{2,1,0:T(8,128)(2,1)S(1)}, u32[]{:S(2)}, u32[]{:S(2)}) async-start(bf16[16,8,3072]{2,1,0:T(8,128)(2,1)} %broadcast_in_dim.8), calls=%async_computation.2 | async-start | bytes 1572864 | tf_op jit(solution)/shard_map/all_to_all | solution.py:60
  66.5 24.0 %collective-permute-start.3 = (f32[2,4,3072]{2,1,0:T(4,128)S(1)}, f32[2,4,3072]{2,1,0:T(4,128)S(1)}, u32[]{:S(2)}, u32[]{:S(2)}) collective-permute-start(f32[2,4,3072]{2,1,0:T(4,128)S(1)} %get-tuple-element.8), channel_id=1, source_target_pairs={{0,8},{8,0},{1,9},{9,1},{2,10},{10,2},{3,11},{11,3},{4,12},{12,4},... | collective-permute-start | bytes 294920 | tf_op jit(solution)/shard_map/ppermute | solution.py:69
  85.8 6.7 %collective-permute-start.2 = (bf16[128,3072]{1,0:T(8,128)(2,1)S(1)}, bf16[128,3072]{1,0:T(8,128)(2,1)S(1)}, u32[]{:S(2)}, u32[]{:S(2)}) collective-permute-start(bf16[128,3072]{1,0:T(8,128)(2,1)S(1)} %bitcast.47), channel_id=1, source_target_pairs={{0,8},{8,0},{1,9},{9,1},{2,10},{10,2},{3,11},{11,3},{4,12},{12,4},... | collective-permute-start | bytes 2359304 | tf_op jit(solution)/shard_map/ppermute | solution.py:63

commit v2 on v1

--- a/solution.py
+++ b/solution.py
@@ -3,17 +3,46 @@
 import jax
 import jax.numpy as jnp
 from jax import lax
+from jax.experimental import pallas as pl
+from jax.experimental.pallas import tpu as pltpu
 from jax.sharding import Mesh
 from jax.sharding import PartitionSpec as P
 
 CHIPS = ("z", "yl")
 SWAP = ((0, 1), (1, 0))
+STEPS = (("z", 8, 4, 8), ("z", 8, 2, 4), ("z", 8, 1, 2), ("yl", 2, 1, 1))
+
+
+def gather(block):
+    held = block[None]
+    for axis, size, step, _ in STEPS:
+        pairs = [(i, i ^ step) for i in range(size)]
+        held = jnp.concatenate((held, lax.ppermute(held, axis, pairs)), axis=0)
+    return held
+
+
+def offsets():
+    places = [0]
+    for _, _, _, jump in STEPS:
+        places = places + [place ^ jump for place in places]
+    return places
+
+
+def mix_kernel(where_ref, weights_ref, mine_ref, theirs_ref, mixed_ref):
+    core, me = where_ref[0], where_ref[1]
+    for place, jump in enumerate(offsets()):
+        chip = me ^ jump
+        for frag, source_ref in ((core, mine_ref), (1 - core, theirs_ref)):
+            own = weights_ref[frag, chip].astype(jnp.float32)
+            source = source_ref[place].astype(jnp.float32)
+            mixed_ref[frag, chip] = (0.5 * own + 0.5 * source).astype(jnp.bfloat16)
 
 
 def shards(local_weights, global_params, momentum):
     f32, bf16 = jnp.float32, jnp.bfloat16
     core = lax.axis_index("core")
     other = 1 - core
+    me = lax.axis_index(CHIPS)
     chips = lax.axis_size(CHIPS)
     replicas = 2 * chips
     everywhere = chips * lax.axis_size(("x", "yh"))
@@ -21,6 +50,7 @@
     share_rows = global_params.shape[2]
     block = rows // chips
     max_norm = 0.5 * math.sqrt(block * width * everywhere)
+    first = core == 0
 
     weights = local_weights[:, 0, 0]
     state = jnp.stack((global_params[:, 0], momentum[:, 0]), axis=1)
@@ -30,19 +60,22 @@
     state_got = lax.ppermute(
         lax.dynamic_index_in_dim(state, other, 0, keepdims=False), "core", SWAP
     )
+    outer, moment = jnp.where(
+        first,
+        jnp.concatenate((state_mine, state_got), axis=1),
+        jnp.concatenate((state_got, state_mine), axis=1),
+    )
+    bases = gather((outer - 0.567 * moment).astype(bf16))
+
     own = lax.dynamic_index_in_dim(weights, core, 0, keepdims=False)
     pair = (own.astype(f32) + got.astype(f32)).astype(bf16)
     pieces = lax.all_to_all(
         pair.reshape(chips, block, width), CHIPS, 0, 0, tiled=True
     )
     total = jnp.sum(pieces.astype(f32), axis=0)
-    first = core == 0
-    outer, moment = jnp.where(
-        first,
-        jnp.concatenate((state_mine, state_got), axis=1),
-        jnp.concatenate((state_got, state_mine), axis=1),
-    )
     pseudo = outer - total / replicas
+    push, bases = lax.optimization_barrier(((1.33 * pseudo).astype(bf16), bases))
+    pushes = gather(push)
     part = jnp.sum(pseudo * pseudo)
     parts = lax.all_to_all(
         jnp.broadcast_to(part, (everywhere, 1, 128)),
@@ -56,11 +89,9 @@
     clipped = factor * pseudo
     moment_next = 0.9 * moment + clipped
     outer_next = outer - 0.7 * (clipped + 0.9 * moment_next)
-    source = outer_next.astype(bf16)
-    gathered = lax.all_to_all(
-        jnp.broadcast_to(source, (chips, block, width)), CHIPS, 0, 0, tiled=True
-    ).reshape(rows, width)
-    swapped = lax.ppermute(gathered, "core", SWAP)
+
+    mine = (bases.astype(f32) - factor * pushes.astype(f32)).astype(bf16)
+    theirs = lax.ppermute(mine, "core", SWAP)
 
     state_next = jnp.stack((outer_next, moment_next))
     halves = state_next.reshape(2, 2, share_rows, width)
@@ -69,12 +100,22 @@
     take = lax.ppermute(give, "core", SWAP)
     state_out = jnp.where(first, jnp.stack((keep, take)), jnp.stack((take, keep)))
 
-    sources = jnp.where(
-        first, jnp.stack((gathered, swapped)), jnp.stack((swapped, gathered))
+    in_vmem = pl.BlockSpec(memory_space=pltpu.VMEM)
+    mixed = pl.pallas_call(
+        mix_kernel,
+        out_shape=jax.ShapeDtypeStruct((2, chips, block, width), bf16),
+        in_specs=[pl.BlockSpec(memory_space=pltpu.SMEM), in_vmem, in_vmem, in_vmem],
+        out_specs=in_vmem,
+        compiler_params=pltpu.CompilerParams(vmem_limit_bytes=32 * 1024 * 1024),
+        name="mix",
+    )(
+        jnp.stack((core, me)).astype(jnp.int32),
+        weights.reshape(2, chips, block, width),
+        mine,
+        theirs,
     )
-    mixed = (0.5 * weights.astype(f32) + 0.5 * sources.astype(f32)).astype(bf16)
     return (
-        mixed[:, None, None],
+        mixed.reshape(local_weights.shape),
         state_out[:, 0][:, None],
         state_out[:, 1][:, None],
     )

time: 94.6 us -> 108 us (1.14)
  starting transfers between devices: 22 us -> 45.4 us
  blocking collectives: 22.2 us -> 0 us
  local copies, waits for them, and re-layouts: 3.79 us -> 11.9 us
  other arithmetic: 4.53 us -> 7.86 us
  Pallas kernels: 0 us -> 2.33 us
  waiting for transfers between devices: 40.2 us -> 38.5 us
    all_to_all x1 -> x0, blocking collectives: 22.2 us -> none  [shards(): lax.all_to_all(jnp.broadcast_to(part, (everywhere, 1, 128)), ('z', 'yl',...]
    ppermute x1 -> x9, waiting for transfers between devices: 1.17 us -> 20.5 us  [the longest x8 19.4 us: gather(): held = jnp.concatenate((held, lax.ppermute(held, axis, pairs)), axis=0)]
    ppermute x1 -> x9, starting transfers between devices: 4.77 us -> 17.9 us  [the longest x8 12 us: gather(): held = jnp.concatenate((held, lax.ppermute(held, axis, pairs)), axis=0)]
    all_to_all x1, waiting for transfers between devices: 19 us -> 9.18 us  [shards(): lax.all_to_all(pair.reshape(chips, block, width), CHIPS, 0, 0, tiled=True)]
    all_to_all x1, waiting for transfers between devices: 17.2 us -> 7.86 us  [shards(): lax.all_to_all(jnp.broadcast_to(part, (everywhere, 1, 128)), ('z', 'yl',...]
    all_to_all x1, starting transfers between devices: 3.61 us -> 12.7 us  [shards(): lax.all_to_all(jnp.broadcast_to(part, (everywhere, 1, 128)), ('z', 'yl',...]
    another operation x3, local copies, waits for them, and re-layouts: 0.07 us -> 4.03 us  [shards(): state_next = jnp.stack((outer_next, moment_next))]
    ppermute x1, starting transfers between devices: 2.02 us -> 5.76 us  [shards(): take = lax.ppermute(give, 'core', SWAP)]
  transfers between devices with their start and end apart: 6 -> 14, of which waited for: 5 -> 7; matrix products, arithmetic and copies ran while one was open for 1% -> 16% of each run, Pallas kernels for 0% -> 0%
where the time goes in v2:
time: 108 us
  starting transfers between devices  45.4 us (42%)
  waiting for transfers between devices  38.5 us (36%)
  local copies, waits for them, and re-layouts  11.9 us (11%)
  other arithmetic  7.86 us (7%)
  Pallas kernels  2.33 us (2%)
  between operations  1.53 us (1%)
    ppermute x8, waiting for transfers between devices, gather(): held = jnp.concatenate((held, lax.ppermute(held, axis, pairs)), axis=0)  19.4 us
    all_to_all x1, starting transfers between devices, shards(): lax.all_to_all(jnp.broadcast_to(part, (everywhere, 1, 128)), ('z', 'yl',...  12.7 us
    ppermute x8, starting transfers between devices, gather(): held = jnp.concatenate((held, lax.ppermute(held, axis, pairs)), axis=0)  12 us
    all_to_all x1, waiting for transfers between devices, shards(): lax.all_to_all(pair.reshape(chips, block, width), CHIPS, 0, 0, tiled=True)  9.18 us
    all_to_all x1, waiting for transfers between devices, shards(): lax.all_to_all(jnp.broadcast_to(part, (everywhere, 1, 128)), ('z', 'yl',...  7.86 us
    ppermute x1, starting transfers between devices, shards(): theirs = lax.ppermute(mine, 'core', SWAP)  5.83 us
    ppermute x1, starting transfers between devices, shards(): take = lax.ppermute(give, 'core', SWAP)  5.76 us
    all_to_all x1, starting transfers between devices, shards(): lax.all_to_all(pair.reshape(chips, block, width), CHIPS, 0, 0, tiled=True)  5.1 us
  transfers between devices with their start and end apart: 14, of which 7 were waited for; matrix products, arithmetic and copies ran while one was open for 16% of the time, Pallas kernels for 0%

profile of v2, /device:TPU:1, one launch (start us, length us, event | category | flops | bytes accessed | tf_op | source)
XLA Modules:
  0.0 107.5 jit_solution(6168414922047101102)
XLA Ops:
  0.6 0.9 constant_dynamic-update-slice_fusion.1
  1.5 0.9 constant_dynamic-update-slice_fusion
  2.4 0.0 copy-start
  2.5 3.3 %collective-permute-start = (f32[2,4,3072]{2,1,0:T(4,128)S(1)}, f32[2,4,3072]{2,1,0:T(4,128)S(1)}, u32[]{:S(2)}, u32[]{:S(2)}) collective-permute-start(f32[2,4,3072]{2,1,0:T(4,128)S(1)} %get-tuple-element.27), channel_id=1, source_target_pairs={{0,8},{8,0},{1,9},{9,1},{2,10},{10,2},{3,11},{11,3},{4,12},{12,4},... | collective-permute-start | bytes 294920 | tf_op jit(solution)/shard_map/ppermute | solution.py:60
  5.8 0.9 collective-permute-done
  6.8 0.1 maximum_select_fusion
  6.9 5.3 %collective-permute-start.2 = (bf16[1,8,3072]{2,1,0:T(8,128)(2,1)S(1)}, bf16[1,8,3072]{2,1,0:T(8,128)(2,1)S(1)}, u32[]{:S(2)}, u32[]{:S(2)}) collective-permute-start(bf16[1,8,3072]{2,1,0:T(8,128)(2,1)S(1)} %get-tuple-element.19), channel_id=1, source_target_pairs={{0,128},{32,160},{64,192},{96,224},{128,0},{160,32},{192,64},{224,... | collective-permute-start | bytes 147464 | tf_op jit(solution)/shard_map/ppermute | solution.py:20
  12.1 2.1 %dynamic-slice_bitcast_fusion = bf16[128,3072]{1,0:T(8,128)(2,1)} fusion(bf16[2,1,1,128,3072]{4,3,2,1,0:T(8,128)(2,1)} %param.3, s32[]{:T(128)S(6)} %select_n.31), kind=kLoop, calls=%fused_computation.5 | loop fusion | bytes 1572868 | tf_op jit(solution)/shard_map/jit(dynamic_index_in_dim)/squeeze | solution.py:57
  14.2 0.6 collective-permute-start.1
  14.8 0.0 collective-permute-done.2
  14.8 1.3 %collective-permute-start.3 = (bf16[2,8,3072]{2,1,0:T(8,128)(2,1)S(1)}, bf16[2,8,3072]{2,1,0:T(8,128)(2,1)S(1)}, u32[]{:S(2)}, u32[]{:S(2)}) collective-permute-start(bf16[2,8,3072]{2,1,0:T(8,128)(2,1)S(1)} %pad_maximum_fusion.4), channel_id=1, source_target_pairs={{0,64},{32,96},{64,0},{96,32},{128,192},{160,224},{192,128},{224,1... | collective-permute-start | bytes 294920 | tf_op jit(solution)/shard_map/ppermute | solution.py:20
  16.1 0.1 pad_add_fusion.where_ref
  16.2 6.0 %collective-permute-done.3 = bf16[2,8,3072]{2,1,0:T(8,128)(2,1)S(1)} collective-permute-done((bf16[2,8,3072]{2,1,0:T(8,128)(2,1)S(1)}, bf16[2,8,3072]{2,1,0:T(8,128)(2,1)S(1)}, u32[]{:S(2)}, u32[]{:S(2)}) %collective-permute-start.3) | collective-permute-done | bytes 98336 | tf_op jit(solution)/shard_map/ppermute | solution.py:20
  22.2 0.7 pad_maximum_fusion.2
  22.9 0.0 collective-permute-start.4
  22.9 0.0 collective-permute-done.1
  22.9 1.1 %fusion.1 = bf16[16,8,3072]{2,1,0:T(8,128)(2,1)} fusion(bf16[128,3072]{1,0:T(8,128)(2,1)S(1)} %collective-permute-done.1, bf16[2,1,1,128,3072]{4,3,2,1,0:T(8,128)(2,1)S(1)} %copy-done, s32[]{:T(128)S(6)} %select_n.30), kind=kLoop, calls=%fused_computation.4 | loop fusion | flops 1572864 | bytes 2359300 | tf_op jit(solution)/shard_map/reshape | solution.py:73
  24.0 5.1 %all-to-all-start = ((bf16[16,8,3072]{2,1,0:T(8,128)(2,1)}), bf16[16,8,3072]{2,1,0:T(8,128)(2,1)S(1)}, u32[]{:S(2)}, u32[]{:S(2)}) async-start(bf16[16,8,3072]{2,1,0:T(8,128)(2,1)} %fusion.1), calls=%async_computation | async-start | bytes 1572864 | tf_op jit(solution)/shard_map/all_to_all | solution.py:72
  29.1 1.0 pad_maximum_fusion
  30.1 1.4 %collective-permute-start.5 = (bf16[8,8,3072]{2,1,0:T(8,128)(2,1)S(1)}, bf16[8,8,3072]{2,1,0:T(8,128)(2,1)S(1)}, u32[]{:S(2)}, u32[]{:S(2)}) collective-permute-start(bf16[8,8,3072]{2,1,0:T(8,128)(2,1)S(1)} %pad_maximum_fusion), channel_id=1, source_target_pairs={{0,16},{16,0},{1,17},{17,1},{2,18},{18,2},{3,19},{19,3},{4,20},{20... | collective-permute-start | bytes 1179656 | tf_op jit(solution)/shard_map/ppermute | solution.py:20
  31.6 0.9 constant_dynamic-update-slice_fusion.3
  32.5 6.9 %collective-permute-done.5 = bf16[8,8,3072]{2,1,0:T(8,128)(2,1)S(1)} collective-permute-done((bf16[8,8,3072]{2,1,0:T(8,128)(2,1)S(1)}, bf16[8,8,3072]{2,1,0:T(8,128)(2,1)S(1)}, u32[]{:S(2)}, u32[]{:S(2)}) %collective-permute-start.5) | collective-permute-done | bytes 393248 | tf_op jit(solution)/shard_map/ppermute | solution.py:20
  39.4 9.2 %all-to-all-done = bf16[16,8,3072]{2,1,0:T(8,128)(2,1)S(1)} async-done(((bf16[16,8,3072]{2,1,0:T(8,128)(2,1)}), bf16[16,8,3072]{2,1,0:T(8,128)(2,1)S(1)}, u32[]{:S(2)}, u32[]{:S(2)}) %all-to-all-start) | async-done | bytes 786464 | tf_op jit(solution)/shard_map/all_to_all | solution.py:72
  48.6 0.1 convert_reduce_fusion
  48.7 0.0 copy-start.1
  48.7 0.6 multiply_reduce_fusion
  49.3 0.0 copy-done.1
  49.3 1.6 %collective-permute-start.6 = (bf16[1,8,3072]{2,1,0:T(8,128)(2,1)S(1)}, bf16[1,8,3072]{2,1,0:T(8,128)(2,1)S(1)}, u32[]{:S(2)}, u32[]{:S(2)}) collective-permute-start(bf16[1,8,3072]{2,1,0:T(8,128)(2,1)S(1)} %bitcast.41), channel_id=1, source_target_pairs={{0,128},{32,160},{64,192},{96,224},{128,0},{160,32},{192,64},{224,... | collective-permute-start | bytes 147464 | tf_op jit(solution)/shard_map/ppermute | solution.py:20
  50.9 1.3 %broadcast_in_dim.7 = f32[128,1,128]{2,1,0:T(1,128)} broadcast(f32[]{:T(128)} %get-tuple-element.20), dimensions={} | broadcast | bytes 65540 | tf_op jit(solution)/shard_map/broadcast_in_dim | solution.py:81
  52.2 12.7 %all-to-all-start.1 = ((f32[128,1,128]{2,1,0:T(1,128)}), f32[128,1,128]{2,1,0:T(1,128)}, u32[]{:S(2)}, u32[]{:S(2)}) async-start(f32[128,1,128]{2,1,0:T(1,128)} %broadcast_in_dim.7), calls=%async_computation.1 | async-start | bytes 131072 | tf_op jit(solution)/shard_map/all_to_all | solution.py:80
  65.0 0.7 pad_maximum_fusion.5
  65.6 1.5 %collective-permute-start.7 = (bf16[2,8,3072]{2,1,0:T(8,128)(2,1)}, bf16[2,8,3072]{2,1,0:T(8,128)(2,1)S(1)}, u32[]{:S(2)}, u32[]{:S(2)}) collective-permute-start(bf16[2,8,3072]{2,1,0:T(8,128)(2,1)} %pad_maximum_fusion.5), channel_id=1, source_target_pairs={{0,64},{32,96},{64,0},{96,32},{128,192},{160,224},{192,128},{224,1... | collective-permute-start | bytes 294920 | tf_op jit(solution)/shard_map/ppermute | solution.py:20
  67.1 7.9 %all-to-all-done.1 = f32[128,1,128]{2,1,0:T(1,128)} async-done(((f32[128,1,128]{2,1,0:T(1,128)}), f32[128,1,128]{2,1,0:T(1,128)}, u32[]{:S(2)}, u32[]{:S(2)}) %all-to-all-start.1) | async-done | bytes 65568 | tf_op jit(solution)/shard_map/all_to_all | solution.py:80
  75.0 1.6 %slice_reduce_fusion = f32[]{:T(128)} fusion(f32[128,1,128]{2,1,0:T(1,128)} %all-to-all-done.1), kind=kLoop, calls=%fused_computation.26 | loop fusion | flops 127 | bytes 516 | tf_op jit(solution)/shard_map/reduce_sum | solution.py:87
  77.3 1.6 %multiply_subtract_fusion = (f32[1,8,3072]{2,1,0:T(8,128)}, f32[1,8,3072]{2,1,0:T(8,128)}) fusion(f32[8,3072]{1,0:T(8,128)} %copy-done.1, f32[2,8,3072]{2,1,0:T(8,128)S(1)} %maximum_select_fusion, f32[]{:T(128)S(6)} %min_shard_map.3), kind=kLoop, calls=%fused_computation.19 | loop fusion | flops 221184 | bytes 491524 | tf_op jit(solution)/shard_map/sub | solution.py:91
  78.9 1.6 %stack.39 = f32[1,2,4,3072]{3,2,1,0:T(4,128)} reshape(f32[1,8,3072]{2,1,0:T(8,128)} %get-tuple-element.16) | data formatting | bytes 196608 | tf_op jit(solution)/shard_map/stack | solution.py:96
  80.5 0.9 constant_dynamic-update-slice_fusion.13
  81.4 1.6 %stack.40 = f32[1,2,4,3072]{3,2,1,0:T(4,128)} reshape(f32[1,8,3072]{2,1,0:T(8,128)} %get-tuple-element.17) | data formatting | bytes 196608 | tf_op jit(solution)/shard_map/stack | solution.py:96
  82.9 0.9 constant_dynamic-update-slice_fusion.12
  83.9 0.8 collective-permute-start.8
  84.7 5.8 %collective-permute-start.11 = (f32[2,4,3072]{2,1,0:T(4,128)S(1)}, f32[2,4,3072]{2,1,0:T(4,128)S(1)}, u32[]{:S(2)}, u32[]{:S(2)}) collective-permute-start(f32[2,4,3072]{2,1,0:T(4,128)S(1)} %get-tuple-element.25), channel_id=1, source_target_pairs={{0,8},{8,0},{1,9},{9,1},{2,10},{10,2},{3,11},{11,3},{4,12},{12,4},... | collective-permute-start | bytes 294920 | tf_op jit(solution)/shard_map/ppermute | solution.py:100
  90.5 0.2 collective-permute-start.9
  90.7 6.5 %collective-permute-done.9 = bf16[8,8,3072]{2,1,0:T(8,128)(2,1)S(1)} collective-permute-done((bf16[8,8,3072]{2,1,0:T(8,128)(2,1)S(1)}, bf16[8,8,3072]{2,1,0:T(8,128)(2,1)S(1)}, u32[]{:S(2)}, u32[]{:S(2)}) %collective-permute-start.9) | collective-permute-done | bytes 393248 | tf_op jit(solution)/shard_map/ppermute | solution.py:20
  97.2 0.2 subtract_convert_fusion.mine_ref
  97.5 5.8 %collective-permute-start.10 = (bf16[16,8,3072]{2,1,0:T(8,128)(2,1)S(1)}, bf16[16,8,3072]{2,1,0:T(8,128)(2,1)S(1)}, u32[]{:S(2)}, u32[]{:S(2)}) collective-permute-start(bf16[16,8,3072]{2,1,0:T(8,128)(2,1)S(1)} %subtract_convert_fusion.mine_ref), channel_id=1, source_target_pairs={{0,8},{8,0},{1,9},{9,1},{2,10},{10,2},{3,11},{11,3},{4,12},{12,4},... | collective-permute-start | bytes 2359304 | tf_op jit(solution)/shard_map/ppermute | solution.py:94
  103.3 0.7 fusion.3
  104.0 1.2 %collective-permute-done.10.theirs_ref = bf16[16,8,3072]{2,1,0:T(8,128)(2,1)S(1)} collective-permute-done((bf16[16,8,3072]{2,1,0:T(8,128)(2,1)S(1)}, bf16[16,8,3072]{2,1,0:T(8,128)(2,1)S(1)}, u32[]{:S(2)}, u32[]{:S(2)}) %collective-permute-start.10) | collective-permute-done | bytes 786464 | tf_op jit(solution)/shard_map/ppermute | solution.py:94
  105.2 2.3 %mix.1 = bf16[2,16,8,3072]{3,2,1,0:T(8,128)(2,1)} custom-call(s32[2]{0:T(128)S(1)} %pad_add_fusion.where_ref, bf16[2,16,8,3072]{3,2,1,0:T(8,128)(2,1)S(1)} %bitcast.39, bf16[16,8,3072]{2,1,0:T(8,128)(2,1)S(1)} %subtract_convert_fusion.mine_ref, bf16[16,8,3072]{2,1,0:T(8,128)(2,1)S(1)} %collective-permute-done.10.theirs_ref), custom_call_target="tpu_custom_call" | custom-call | tf_op jit(solution)/shard_map/mix/pallas_call | solution.py:104
  (21 shorter events, 0.3 us)
Async XLA Ops:
  2.4 20.5 %copy-start = (bf16[2,1,1,128,3072]{4,3,2,1,0:T(8,128)(2,1)S(1)}, bf16[2,1,1,128,3072]{4,3,2,1,0:T(8,128)(2,1)}, u32[]{:S(2)}) copy-start(bf16[2,1,1,128,3072]{4,3,2,1,0:T(8,128)(2,1)} %param.3) | copy-start | bytes 4718596
  2.5 4.3 %collective-permute-start = (f32[2,4,3072]{2,1,0:T(4,128)S(1)}, f32[2,4,3072]{2,1,0:T(4,128)S(1)}, u32[]{:S(2)}, u32[]{:S(2)}) collective-permute-start(f32[2,4,3072]{2,1,0:T(4,128)S(1)} %get-tuple-element.27), channel_id=1, source_target_pairs={{0,8},{8,0},{1,9},{9,1},{2,10},{10,2},{3,11},{11,3},{4,12},{12,4},... | collective-permute-start | bytes 294920 | tf_op jit(solution)/shard_map/ppermute | solution.py:60
  6.9 8.0 %collective-permute-start.2 = (bf16[1,8,3072]{2,1,0:T(8,128)(2,1)S(1)}, bf16[1,8,3072]{2,1,0:T(8,128)(2,1)S(1)}, u32[]{:S(2)}, u32[]{:S(2)}) collective-permute-start(bf16[1,8,3072]{2,1,0:T(8,128)(2,1)S(1)} %get-tuple-element.19), channel_id=1, source_target_pairs={{0,128},{32,160},{64,192},{96,224},{128,0},{160,32},{192,64},{224,... | collective-permute-start | bytes 147464 | tf_op jit(solution)/shard_map/ppermute | solution.py:20
  14.2 8.7 %collective-permute-start.1 = (bf16[128,3072]{1,0:T(8,128)(2,1)}, bf16[128,3072]{1,0:T(8,128)(2,1)S(1)}, u32[]{:S(2)}, u32[]{:S(2)}) collective-permute-start(bf16[128,3072]{1,0:T(8,128)(2,1)} %dynamic-slice_bitcast_fusion), channel_id=1, source_target_pairs={{0,8},{8,0},{1,9},{9,1},{2,10},{10,2},{3,11},{11,3},{4,12},{12,4},... | collective-permute-start | bytes 2359304 | tf_op jit(solution)/shard_map/ppermute | solution.py:58
  14.8 7.3 %collective-permute-start.3 = (bf16[2,8,3072]{2,1,0:T(8,128)(2,1)S(1)}, bf16[2,8,3072]{2,1,0:T(8,128)(2,1)S(1)}, u32[]{:S(2)}, u32[]{:S(2)}) collective-permute-start(bf16[2,8,3072]{2,1,0:T(8,128)(2,1)S(1)} %pad_maximum_fusion.4), channel_id=1, source_target_pairs={{0,64},{32,96},{64,0},{96,32},{128,192},{160,224},{192,128},{224,1... | collective-permute-start | bytes 294920 | tf_op jit(solution)/shard_map/ppermute | solution.py:20
  22.9 6.2 %collective-permute-start.4 = (bf16[4,8,3072]{2,1,0:T(8,128)(2,1)}, bf16[4,8,3072]{2,1,0:T(8,128)(2,1)}, u32[]{:S(2)}, u32[]{:S(2)}) collective-permute-start(bf16[4,8,3072]{2,1,0:T(8,128)(2,1)} %pad_maximum_fusion.2), channel_id=1, source_target_pairs={{0,32},{32,0},{64,96},{96,64},{128,160},{160,128},{192,224},{224,1... | collective-permute-start | bytes 589832 | tf_op jit(solution)/shard_map/ppermute | solution.py:20
  24.0 24.6 %all-to-all-start = ((bf16[16,8,3072]{2,1,0:T(8,128)(2,1)}), bf16[16,8,3072]{2,1,0:T(8,128)(2,1)S(1)}, u32[]{:S(2)}, u32[]{:S(2)}) async-start(bf16[16,8,3072]{2,1,0:T(8,128)(2,1)} %fusion.1), calls=%async_computation | async-start | bytes 1572864 | tf_op jit(solution)/shard_map/all_to_all | solution.py:72
  30.1 9.3 %collective-permute-start.5 = (bf16[8,8,3072]{2,1,0:T(8,128)(2,1)S(1)}, bf16[8,8,3072]{2,1,0:T(8,128)(2,1)S(1)}, u32[]{:S(2)}, u32[]{:S(2)}) collective-permute-start(bf16[8,8,3072]{2,1,0:T(8,128)(2,1)S(1)} %pad_maximum_fusion), channel_id=1, source_target_pairs={{0,16},{16,0},{1,17},{17,1},{2,18},{18,2},{3,19},{19,3},{4,20},{20... | collective-permute-start | bytes 1179656 | tf_op jit(solution)/shard_map/ppermute | solution.py:20
  48.7 0.6 copy-start.1
  49.3 15.6 %collective-permute-start.6 = (bf16[1,8,3072]{2,1,0:T(8,128)(2,1)S(1)}, bf16[1,8,3072]{2,1,0:T(8,128)(2,1)S(1)}, u32[]{:S(2)}, u32[]{:S(2)}) collective-permute-start(bf16[1,8,3072]{2,1,0:T(8,128)(2,1)S(1)} %bitcast.41), channel_id=1, source_target_pairs={{0,128},{32,160},{64,192},{96,224},{128,0},{160,32},{192,64},{224,... | collective-permute-start | bytes 147464 | tf_op jit(solution)/shard_map/ppermute | solution.py:20
  52.2 22.8 %all-to-all-start.1 = ((f32[128,1,128]{2,1,0:T(1,128)}), f32[128,1,128]{2,1,0:T(1,128)}, u32[]{:S(2)}, u32[]{:S(2)}) async-start(f32[128,1,128]{2,1,0:T(1,128)} %broadcast_in_dim.7), calls=%async_computation.1 | async-start | bytes 131072 | tf_op jit(solution)/shard_map/all_to_all | solution.py:80
  65.6 18.2 %collective-permute-start.7 = (bf16[2,8,3072]{2,1,0:T(8,128)(2,1)}, bf16[2,8,3072]{2,1,0:T(8,128)(2,1)S(1)}, u32[]{:S(2)}, u32[]{:S(2)}) collective-permute-start(bf16[2,8,3072]{2,1,0:T(8,128)(2,1)} %pad_maximum_fusion.5), channel_id=1, source_target_pairs={{0,64},{32,96},{64,0},{96,32},{128,192},{160,224},{192,128},{224,1... | collective-permute-start | bytes 294920 | tf_op jit(solution)/shard_map/ppermute | solution.py:20
  83.9 6.5 %collective-permute-start.8 = (bf16[4,8,3072]{2,1,0:T(8,128)(2,1)S(1)}, bf16[4,8,3072]{2,1,0:T(8,128)(2,1)S(1)}, u32[]{:S(2)}, u32[]{:S(2)}) collective-permute-start(bf16[4,8,3072]{2,1,0:T(8,128)(2,1)S(1)} %pad_maximum_fusion.3), channel_id=1, source_target_pairs={{0,32},{32,0},{64,96},{96,64},{128,160},{160,128},{192,224},{224,1... | collective-permute-start | bytes 589832 | tf_op jit(solution)/shard_map/ppermute | solution.py:20
  84.7 18.6 %collective-permute-start.11 = (f32[2,4,3072]{2,1,0:T(4,128)S(1)}, f32[2,4,3072]{2,1,0:T(4,128)S(1)}, u32[]{:S(2)}, u32[]{:S(2)}) collective-permute-start(f32[2,4,3072]{2,1,0:T(4,128)S(1)} %get-tuple-element.25), channel_id=1, source_target_pairs={{0,8},{8,0},{1,9},{9,1},{2,10},{10,2},{3,11},{11,3},{4,12},{12,4},... | collective-permute-start | bytes 294920 | tf_op jit(solution)/shard_map/ppermute | solution.py:100
  90.5 6.7 %collective-permute-start.9 = (bf16[8,8,3072]{2,1,0:T(8,128)(2,1)S(1)}, bf16[8,8,3072]{2,1,0:T(8,128)(2,1)S(1)}, u32[]{:S(2)}, u32[]{:S(2)}) collective-permute-start(bf16[8,8,3072]{2,1,0:T(8,128)(2,1)S(1)} %pad_maximum_fusion.1), channel_id=1, source_target_pairs={{0,16},{16,0},{1,17},{17,1},{2,18},{18,2},{3,19},{19,3},{4,20},{20... | collective-permute-start | bytes 1179656 | tf_op jit(solution)/shard_map/ppermute | solution.py:20
  97.5 7.7 %collective-permute-start.10 = (bf16[16,8,3072]{2,1,0:T(8,128)(2,1)S(1)}, bf16[16,8,3072]{2,1,0:T(8,128)(2,1)S(1)}, u32[]{:S(2)}, u32[]{:S(2)}) collective-permute-start(bf16[16,8,3072]{2,1,0:T(8,128)(2,1)S(1)} %subtract_convert_fusion.mine_ref), channel_id=1, source_target_pairs={{0,8},{8,0},{1,9},{9,1},{2,10},{10,2},{3,11},{11,3},{4,12},{12,4},... | collective-permute-start | bytes 2359304 | tf_op jit(solution)/shard_map/ppermute | solution.py:94

commit v3 on v2

--- a/solution.py
+++ b/solution.py
@@ -10,39 +10,45 @@
 
 CHIPS = ("z", "yl")
 SWAP = ((0, 1), (1, 0))
-STEPS = (("z", 8, 4, 8), ("z", 8, 2, 4), ("z", 8, 1, 2), ("yl", 2, 1, 1))
+STEPS = (4, 2, 1)
 
 
 def gather(block):
     held = block[None]
-    for axis, size, step, _ in STEPS:
-        pairs = [(i, i ^ step) for i in range(size)]
-        held = jnp.concatenate((held, lax.ppermute(held, axis, pairs)), axis=0)
+    for step in STEPS:
+        pairs = [(i, i ^ step) for i in range(8)]
+        held = jnp.concatenate((held, lax.ppermute(held, "z", pairs)), axis=0)
     return held
 
 
 def offsets():
     places = [0]
-    for _, _, _, jump in STEPS:
-        places = places + [place ^ jump for place in places]
+    for step in STEPS:
+        places = places + [place ^ step for place in places]
     return places
 
 
-def mix_kernel(where_ref, weights_ref, mine_ref, theirs_ref, mixed_ref):
-    core, me = where_ref[0], where_ref[1]
+def mix_kernel(where_ref, weights_ref, near_ref, far_ref, near2_ref, far2_ref, mixed_ref):
+    core, z, yl = where_ref[0], where_ref[1], where_ref[2]
     for place, jump in enumerate(offsets()):
-        chip = me ^ jump
-        for frag, source_ref in ((core, mine_ref), (1 - core, theirs_ref)):
-            own = weights_ref[frag, chip].astype(jnp.float32)
+        row = 2 * (z ^ jump)
+        for frag, side, source_ref in (
+            (core, yl, near_ref),
+            (core, 1 - yl, far_ref),
+            (1 - core, yl, near2_ref),
+            (1 - core, 1 - yl, far2_ref),
+        ):
+            own = weights_ref[frag, row + side].astype(jnp.float32)
             source = source_ref[place].astype(jnp.float32)
-            mixed_ref[frag, chip] = (0.5 * own + 0.5 * source).astype(jnp.bfloat16)
+            mixed_ref[frag, row + side] = (0.5 * own + 0.5 * source).astype(
+                jnp.bfloat16
+            )
 
 
 def shards(local_weights, global_params, momentum):
     f32, bf16 = jnp.float32, jnp.bfloat16
     core = lax.axis_index("core")
     other = 1 - core
-    me = lax.axis_index(CHIPS)
     chips = lax.axis_size(CHIPS)
     replicas = 2 * chips
     everywhere = chips * lax.axis_size(("x", "yh"))
@@ -65,33 +71,37 @@
         jnp.concatenate((state_mine, state_got), axis=1),
         jnp.concatenate((state_got, state_mine), axis=1),
     )
-    bases = gather((outer - 0.567 * moment).astype(bf16))
-
     own = lax.dynamic_index_in_dim(weights, core, 0, keepdims=False)
     pair = (own.astype(f32) + got.astype(f32)).astype(bf16)
+    base = (outer - 0.567 * moment).astype(bf16)
+    pair, base = lax.optimization_barrier((pair, base))
     pieces = lax.all_to_all(
         pair.reshape(chips, block, width), CHIPS, 0, 0, tiled=True
     )
+    bases = gather(base)
+    pieces, bases = lax.optimization_barrier((pieces, bases))
     total = jnp.sum(pieces.astype(f32), axis=0)
     pseudo = outer - total / replicas
-    push, bases = lax.optimization_barrier(((1.33 * pseudo).astype(bf16), bases))
-    pushes = gather(push)
     part = jnp.sum(pseudo * pseudo)
     parts = lax.all_to_all(
-        jnp.broadcast_to(part, (everywhere, 1, 128)),
+        jnp.broadcast_to(part, (everywhere, 8, 128)),
         ("z", "yl", "x", "yh"),
         0,
         0,
         tiled=True,
     )
+    pushes = gather((1.33 * pseudo).astype(bf16))
+    parts, pushes = lax.optimization_barrier((parts, pushes))
     square_sum = jnp.sum(parts[:, 0, 0])
     factor = jnp.minimum(1.0, max_norm / (jnp.sqrt(square_sum) + 1e-06))
     clipped = factor * pseudo
     moment_next = 0.9 * moment + clipped
     outer_next = outer - 0.7 * (clipped + 0.9 * moment_next)
 
-    mine = (bases.astype(f32) - factor * pushes.astype(f32)).astype(bf16)
-    theirs = lax.ppermute(mine, "core", SWAP)
+    near = (bases.astype(f32) - factor * pushes.astype(f32)).astype(bf16)
+    far = lax.ppermute(near, "yl", SWAP)
+    near2 = lax.ppermute(near, "core", SWAP)
+    far2 = lax.ppermute(far, "core", SWAP)
 
     state_next = jnp.stack((outer_next, moment_next))
     halves = state_next.reshape(2, 2, share_rows, width)
@@ -104,15 +114,17 @@
     mixed = pl.pallas_call(
         mix_kernel,
         out_shape=jax.ShapeDtypeStruct((2, chips, block, width), bf16),
-        in_specs=[pl.BlockSpec(memory_space=pltpu.SMEM), in_vmem, in_vmem, in_vmem],
+        in_specs=[pl.BlockSpec(memory_space=pltpu.SMEM)] + [in_vmem] * 5,
         out_specs=in_vmem,
         compiler_params=pltpu.CompilerParams(vmem_limit_bytes=32 * 1024 * 1024),
         name="mix",
     )(
-        jnp.stack((core, me)).astype(jnp.int32),
+        jnp.stack((core, lax.axis_index("z"), lax.axis_index("yl"))),
         weights.reshape(2, chips, block, width),
-        mine,
-        theirs,
+        near,
+        far,
+        near2,
+        far2,
     )
     return (
         mixed.reshape(local_weights.shape),

time: 108 us -> 113 us (1.046)
  waiting for transfers between devices: 38.5 us -> 56 us
  local copies, waits for them, and re-layouts: 11.9 us -> 5.4 us
  other arithmetic: 7.86 us -> 4.12 us
  starting transfers between devices: 45.4 us -> 42.8 us
    ppermute x9, waiting for transfers between devices: 20.5 us -> 53.8 us  [the longest x6 44.1 us: gather(): held = jnp.concatenate((held, lax.ppermute(held, 'z', pairs)), axis=0)]
    all_to_all x1, waiting for transfers between devices: 9.18 us -> 0.01 us  [shards(): lax.all_to_all(pair.reshape(chips, block, width), CHIPS, 0, 0, tiled=True)]
    all_to_all x1, waiting for transfers between devices: 7.86 us -> 0.01 us  [shards(): lax.all_to_all(jnp.broadcast_to(part, (everywhere, 8, 128)), ('z', 'yl',...]
    ppermute x9, starting transfers between devices: 17.9 us -> 12.7 us  [the longest x6 10.3 us: gather(): held = jnp.concatenate((held, lax.ppermute(held, 'z', pairs)), axis=0)]
    another operation x3, local copies, waits for them, and re-layouts: 4.03 us -> 0.07 us  [shards(): state_next = jnp.stack((outer_next, moment_next))]
    all_to_all x1, starting transfers between devices: 5.1 us -> 7.57 us  [shards(): lax.all_to_all(pair.reshape(chips, block, width), CHIPS, 0, 0, tiled=True)]
    concatenate x6, other arithmetic: 2.4 us -> 0.15 us  [gather(): held = jnp.concatenate((held, lax.ppermute(held, 'z', pairs)), axis=0)]
    ppermute x1, waiting for transfers between devices: 0.01 us -> 2.15 us  [shards(): got = lax.ppermute(sent, 'core', SWAP)]
  transfers between devices with their start and end apart: 14 -> 14, of which waited for: 7 -> 8; matrix products, arithmetic and copies ran while one was open for 16% -> 4% of each run, Pallas kernels for 0% -> 0%
where the time goes in v3:
time: 113 us; the launch traced here: 112 us
  waiting for transfers between devices  56 us (50%)
  starting transfers between devices  42.8 us (38%)
  local copies, waits for them, and re-layouts  5.4 us (5%)
  other arithmetic  4.12 us (4%)
  Pallas kernels  2.35 us (2%)
  between operations  1.58 us (1%)
    ppermute x6, waiting for transfers between devices, gather(): held = jnp.concatenate((held, lax.ppermute(held, 'z', pairs)), axis=0)  44.1 us
    all_to_all x1, starting transfers between devices, shards(): lax.all_to_all(jnp.broadcast_to(part, (everywhere, 8, 128)), ('z', 'yl',...  14.5 us
    ppermute x6, starting transfers between devices, gather(): held = jnp.concatenate((held, lax.ppermute(held, 'z', pairs)), axis=0)  10.3 us
    ppermute x1, waiting for transfers between devices, shards(): far = lax.ppermute(near, 'yl', SWAP)  9.07 us
    all_to_all x1, starting transfers between devices, shards(): lax.all_to_all(pair.reshape(chips, block, width), CHIPS, 0, 0, tiled=True)  7.57 us
    ppermute x1, starting transfers between devices, shards(): take = lax.ppermute(give, 'core', SWAP)  4.61 us
    ppermute x1, starting transfers between devices, shards(): lax.ppermute(lax.dynamic_index_in_dim(state, other, 0, keepdims=False), '...  3.33 us
    pallas_call x1, Pallas kernels, shards(): pl.pallas_call(mix_kernel, out_shape=jax.ShapeDtypeStruct((2, chips, bloc...  2.35 us
  transfers between devices with their start and end apart: 14, of which 8 were waited for; matrix products, arithmetic and copies ran while one was open for 4% of the time, Pallas kernels for 0%

profile of v3, /device:TPU:1, one launch (start us, length us, event | category | flops | bytes accessed | tf_op | source)
XLA Modules:
  0.0 112.2 jit_solution(12421663301547725590)
XLA Ops:
  0.6 0.0 copy-start
  0.6 1.0 constant_dynamic-update-slice_fusion.1
  1.7 0.9 constant_dynamic-update-slice_fusion
  2.6 3.3 %collective-permute-start.1 = (f32[2,4,3072]{2,1,0:T(4,128)S(1)}, f32[2,4,3072]{2,1,0:T(4,128)S(1)}, u32[]{:S(2)}, u32[]{:S(2)}) collective-permute-start(f32[2,4,3072]{2,1,0:T(4,128)S(1)} %get-tuple-element.31), channel_id=1, source_target_pairs={{0,8},{8,0},{1,9},{9,1},{2,10},{10,2},{3,11},{11,3},{4,12},{12,4},... | collective-permute-start | bytes 294920 | tf_op jit(solution)/shard_map/ppermute | solution.py:66
  5.9 1.2 %dynamic-slice_bitcast_fusion = bf16[128,3072]{1,0:T(8,128)(2,1)S(1)} fusion(bf16[2,1,1,128,3072]{4,3,2,1,0:T(8,128)(2,1)} %param.3, s32[]{:T(128)S(6)} %select_n.30), kind=kLoop, calls=%fused_computation.4 | loop fusion | bytes 1572868 | tf_op jit(solution)/shard_map/jit(dynamic_index_in_dim)/squeeze | solution.py:63
  7.1 0.1 collective-permute-start
  7.2 0.0 collective-permute-done.1
  7.2 0.1 maximum_select_fusion
  7.3 2.1 %collective-permute-done = bf16[128,3072]{1,0:T(8,128)(2,1)S(1)} collective-permute-done((bf16[128,3072]{1,0:T(8,128)(2,1)S(1)}, bf16[128,3072]{1,0:T(8,128)(2,1)S(1)}, u32[]{:S(2)}, u32[]{:S(2)}) %collective-permute-start) | collective-permute-done | bytes 786464 | tf_op jit(solution)/shard_map/ppermute | solution.py:64
  9.5 0.0 copy-done
  9.5 1.1 fusion
  10.6 7.6 %all-to-all-start = ((bf16[16,8,3072]{2,1,0:T(8,128)(2,1)}), bf16[16,8,3072]{2,1,0:T(8,128)(2,1)S(1)}, u32[]{:S(2)}, u32[]{:S(2)}) async-start(bf16[16,8,3072]{2,1,0:T(8,128)(2,1)} %bitcast.10), calls=%async_computation | async-start | bytes 1572864 | tf_op jit(solution)/shard_map/all_to_all | solution.py:78
  18.1 5.3 %collective-permute-start.2 = (bf16[1,8,3072]{2,1,0:T(8,128)(2,1)S(1)}, bf16[1,8,3072]{2,1,0:T(8,128)(2,1)S(1)}, u32[]{:S(2)}, u32[]{:S(2)}) collective-permute-start(bf16[1,8,3072]{2,1,0:T(8,128)(2,1)S(1)} %bitcast.44), channel_id=1, source_target_pairs={{0,128},{32,160},{64,192},{96,224},{128,0},{160,32},{192,64},{224,... | collective-permute-start | bytes 147464 | tf_op jit(solution)/shard_map/ppermute | solution.py:20
  23.4 18.9 %collective-permute-done.2 = bf16[1,8,3072]{2,1,0:T(8,128)(2,1)S(1)} collective-permute-done((bf16[1,8,3072]{2,1,0:T(8,128)(2,1)S(1)}, bf16[1,8,3072]{2,1,0:T(8,128)(2,1)S(1)}, u32[]{:S(2)}, u32[]{:S(2)}) %collective-permute-start.2) | collective-permute-done | bytes 49184 | tf_op jit(solution)/shard_map/ppermute | solution.py:20
  42.3 0.1 collective-permute-start.3
  42.4 4.4 %collective-permute-done.3 = bf16[2,8,3072]{2,1,0:T(8,128)(2,1)S(1)} collective-permute-done((bf16[2,8,3072]{2,1,0:T(8,128)(2,1)S(1)}, bf16[2,8,3072]{2,1,0:T(8,128)(2,1)S(1)}, u32[]{:S(2)}, u32[]{:S(2)}) %collective-permute-start.3) | collective-permute-done | bytes 98336 | tf_op jit(solution)/shard_map/ppermute | solution.py:20
  46.8 1.5 %collective-permute-start.4 = (bf16[4,8,3072]{2,1,0:T(8,128)(2,1)S(1)}, bf16[4,8,3072]{2,1,0:T(8,128)(2,1)S(1)}, u32[]{:S(2)}, u32[]{:S(2)}) collective-permute-start(bf16[4,8,3072]{2,1,0:T(8,128)(2,1)S(1)} %pad_maximum_fusion.2), channel_id=1, source_target_pairs={{0,32},{32,0},{64,96},{96,64},{128,160},{160,128},{192,224},{224,1... | collective-permute-start | bytes 589832 | tf_op jit(solution)/shard_map/ppermute | solution.py:20
  48.2 3.8 %collective-permute-done.4 = bf16[4,8,3072]{2,1,0:T(8,128)(2,1)S(1)} collective-permute-done((bf16[4,8,3072]{2,1,0:T(8,128)(2,1)S(1)}, bf16[4,8,3072]{2,1,0:T(8,128)(2,1)S(1)}, u32[]{:S(2)}, u32[]{:S(2)}) %collective-permute-start.4) | collective-permute-done | bytes 196640 | tf_op jit(solution)/shard_map/ppermute | solution.py:20
  52.1 0.0 all-to-all-done
  52.1 0.1 convert_reduce_fusion
  52.2 1.8 %collective-permute-start.5 = (bf16[1,8,3072]{2,1,0:T(8,128)(2,1)S(1)}, bf16[1,8,3072]{2,1,0:T(8,128)(2,1)S(1)}, u32[]{:S(2)}, u32[]{:S(2)}) collective-permute-start(bf16[1,8,3072]{2,1,0:T(8,128)(2,1)S(1)} %multiply_convert_fusion), channel_id=1, source_target_pairs={{0,128},{32,160},{64,192},{96,224},{128,0},{160,32},{192,64},{224,... | collective-permute-start | bytes 147464 | tf_op jit(solution)/shard_map/ppermute | solution.py:20
  54.0 0.6 fusion.3
  54.6 1.5 %broadcast_in_dim.8 = f32[128,8,128]{2,1,0:T(8,128)} broadcast(f32[]{:T(128)} %fusion.3), dimensions={} | broadcast | bytes 524292 | tf_op jit(solution)/shard_map/broadcast_in_dim | solution.py:87
  56.1 14.5 %all-to-all-start.1 = ((f32[128,8,128]{2,1,0:T(8,128)}), f32[128,8,128]{2,1,0:T(8,128)}, u32[]{:S(2)}, u32[]{:S(2)}) async-start(f32[128,8,128]{2,1,0:T(8,128)} %broadcast_in_dim.8), calls=%async_computation.1 | async-start | bytes 1048576 | tf_op jit(solution)/shard_map/all_to_all | solution.py:86
  70.6 0.0 collective-permute-done.5
  70.6 1.6 %collective-permute-start.6 = (bf16[2,8,3072]{2,1,0:T(8,128)(2,1)S(1)}, bf16[2,8,3072]{2,1,0:T(8,128)(2,1)S(1)}, u32[]{:S(2)}, u32[]{:S(2)}) collective-permute-start(bf16[2,8,3072]{2,1,0:T(8,128)(2,1)S(1)} %pad_maximum_fusion.5), channel_id=1, source_target_pairs={{0,64},{32,96},{64,0},{96,32},{128,192},{160,224},{192,128},{224,1... | collective-permute-start | bytes 294920 | tf_op jit(solution)/shard_map/ppermute | solution.py:20
  72.2 11.1 %collective-permute-done.6 = bf16[2,8,3072]{2,1,0:T(8,128)(2,1)S(1)} collective-permute-done((bf16[2,8,3072]{2,1,0:T(8,128)(2,1)S(1)}, bf16[2,8,3072]{2,1,0:T(8,128)(2,1)S(1)}, u32[]{:S(2)}, u32[]{:S(2)}) %collective-permute-start.6) | collective-permute-done | bytes 98336 | tf_op jit(solution)/shard_map/ppermute | solution.py:20
  83.3 0.1 collective-permute-start.7
  83.4 6.0 %collective-permute-done.7 = bf16[4,8,3072]{2,1,0:T(8,128)(2,1)S(1)} collective-permute-done((bf16[4,8,3072]{2,1,0:T(8,128)(2,1)S(1)}, bf16[4,8,3072]{2,1,0:T(8,128)(2,1)S(1)}, u32[]{:S(2)}, u32[]{:S(2)}) %collective-permute-start.7) | collective-permute-done | bytes 196640 | tf_op jit(solution)/shard_map/ppermute | solution.py:20
  89.4 0.0 all-to-all-done.1
  89.5 1.8 %slice_reduce_fusion = f32[]{:T(128)} fusion(f32[128,8,128]{2,1,0:T(8,128)} %all-to-all-done.1), kind=kLoop, calls=%fused_computation.26 | loop fusion | flops 127 | bytes 516 | tf_op jit(solution)/shard_map/reduce_sum | solution.py:95
  92.2 4.6 %collective-permute-start.11 = (f32[2,4,3072]{2,1,0:T(4,128)S(1)}, f32[2,4,3072]{2,1,0:T(4,128)S(1)}, u32[]{:S(2)}, u32[]{:S(2)}) collective-permute-start(f32[2,4,3072]{2,1,0:T(4,128)S(1)} %get-tuple-element.29), channel_id=1, source_target_pairs={{0,8},{8,0},{1,9},{9,1},{2,10},{10,2},{3,11},{11,3},{4,12},{12,4},... | collective-permute-start | bytes 294920 | tf_op jit(solution)/shard_map/ppermute | solution.py:110
  96.8 0.1 subtract_convert_fusion.near_ref
  96.9 1.3 %collective-permute-start.8 = (bf16[8,8,3072]{2,1,0:T(8,128)(2,1)S(1)}, bf16[8,8,3072]{2,1,0:T(8,128)(2,1)S(1)}, u32[]{:S(2)}, u32[]{:S(2)}) collective-permute-start(bf16[8,8,3072]{2,1,0:T(8,128)(2,1)S(1)} %subtract_convert_fusion.near_ref), channel_id=1, source_target_pairs={{0,16},{16,0},{1,17},{17,1},{2,18},{18,2},{3,19},{19,3},{4,20},{20... | collective-permute-start | bytes 1179656 | tf_op jit(solution)/shard_map/ppermute | solution.py:102
  98.2 0.1 pad_add_fusion.where_ref
  98.3 0.3 collective-permute-start.9
  98.6 0.0 collective-permute-done.11
  98.7 9.1 %collective-permute-done.8.far_ref = bf16[8,8,3072]{2,1,0:T(8,128)(2,1)S(1)} collective-permute-done((bf16[8,8,3072]{2,1,0:T(8,128)(2,1)S(1)}, bf16[8,8,3072]{2,1,0:T(8,128)(2,1)S(1)}, u32[]{:S(2)}, u32[]{:S(2)}) %collective-permute-start.8) | collective-permute-done | bytes 393248 | tf_op jit(solution)/shard_map/ppermute | solution.py:102
  107.7 0.8 collective-permute-start.10
  108.5 0.7 fusion.4
  109.2 0.0 collective-permute-done.9.near2_ref
  109.2 0.7 collective-permute-done.10.far2_ref
  109.9 2.3 %mix.1 = bf16[2,16,8,3072]{3,2,1,0:T(8,128)(2,1)} custom-call(s32[3]{0:T(128)S(1)} %pad_add_fusion.where_ref, bf16[2,16,8,3072]{3,2,1,0:T(8,128)(2,1)S(1)} %bitcast.42, bf16[8,8,3072]{2,1,0:T(8,128)(2,1)S(1)} %subtract_convert_fusion.near_ref, bf16[8,8,3072]{2,1,0:T(8,128)(2,1)S(1)} %collective-permute-done.8.far_ref, ...), custom_call_target="tpu_custom_call" | custom-call | tf_op jit(solution)/shard_map/mix/pallas_call | solution.py:114
  (16 shorter events, 0.4 us)
Async XLA Ops:
  0.6 8.9 %copy-start = (bf16[2,1,1,128,3072]{4,3,2,1,0:T(8,128)(2,1)S(1)}, bf16[2,1,1,128,3072]{4,3,2,1,0:T(8,128)(2,1)}, u32[]{:S(2)}) copy-start(bf16[2,1,1,128,3072]{4,3,2,1,0:T(8,128)(2,1)} %param.3) | copy-start | bytes 4718596
  2.6 4.6 %collective-permute-start.1 = (f32[2,4,3072]{2,1,0:T(4,128)S(1)}, f32[2,4,3072]{2,1,0:T(4,128)S(1)}, u32[]{:S(2)}, u32[]{:S(2)}) collective-permute-start(f32[2,4,3072]{2,1,0:T(4,128)S(1)} %get-tuple-element.31), channel_id=1, source_target_pairs={{0,8},{8,0},{1,9},{9,1},{2,10},{10,2},{3,11},{11,3},{4,12},{12,4},... | collective-permute-start | bytes 294920 | tf_op jit(solution)/shard_map/ppermute | solution.py:66
  7.1 2.4 %collective-permute-start = (bf16[128,3072]{1,0:T(8,128)(2,1)S(1)}, bf16[128,3072]{1,0:T(8,128)(2,1)S(1)}, u32[]{:S(2)}, u32[]{:S(2)}) collective-permute-start(bf16[128,3072]{1,0:T(8,128)(2,1)S(1)} %dynamic-slice_bitcast_fusion), channel_id=1, source_target_pairs={{0,8},{8,0},{1,9},{9,1},{2,10},{10,2},{3,11},{11,3},{4,12},{12,4},... | collective-permute-start | bytes 2359304 | tf_op jit(solution)/shard_map/ppermute | solution.py:64
  10.6 41.5 %all-to-all-start = ((bf16[16,8,3072]{2,1,0:T(8,128)(2,1)}), bf16[16,8,3072]{2,1,0:T(8,128)(2,1)S(1)}, u32[]{:S(2)}, u32[]{:S(2)}) async-start(bf16[16,8,3072]{2,1,0:T(8,128)(2,1)} %bitcast.10), calls=%async_computation | async-start | bytes 1572864 | tf_op jit(solution)/shard_map/all_to_all | solution.py:78
  18.1 24.1 %collective-permute-start.2 = (bf16[1,8,3072]{2,1,0:T(8,128)(2,1)S(1)}, bf16[1,8,3072]{2,1,0:T(8,128)(2,1)S(1)}, u32[]{:S(2)}, u32[]{:S(2)}) collective-permute-start(bf16[1,8,3072]{2,1,0:T(8,128)(2,1)S(1)} %bitcast.44), channel_id=1, source_target_pairs={{0,128},{32,160},{64,192},{96,224},{128,0},{160,32},{192,64},{224,... | collective-permute-start | bytes 147464 | tf_op jit(solution)/shard_map/ppermute | solution.py:20
  42.3 4.5 %collective-permute-start.3 = (bf16[2,8,3072]{2,1,0:T(8,128)(2,1)S(1)}, bf16[2,8,3072]{2,1,0:T(8,128)(2,1)S(1)}, u32[]{:S(2)}, u32[]{:S(2)}) collective-permute-start(bf16[2,8,3072]{2,1,0:T(8,128)(2,1)S(1)} %pad_maximum_fusion.4), channel_id=1, source_target_pairs={{0,64},{32,96},{64,0},{96,32},{128,192},{160,224},{192,128},{224,1... | collective-permute-start | bytes 294920 | tf_op jit(solution)/shard_map/ppermute | solution.py:20
  46.8 5.2 %collective-permute-start.4 = (bf16[4,8,3072]{2,1,0:T(8,128)(2,1)S(1)}, bf16[4,8,3072]{2,1,0:T(8,128)(2,1)S(1)}, u32[]{:S(2)}, u32[]{:S(2)}) collective-permute-start(bf16[4,8,3072]{2,1,0:T(8,128)(2,1)S(1)} %pad_maximum_fusion.2), channel_id=1, source_target_pairs={{0,32},{32,0},{64,96},{96,64},{128,160},{160,128},{192,224},{224,1... | collective-permute-start | bytes 589832 | tf_op jit(solution)/shard_map/ppermute | solution.py:20
  52.2 18.4 %collective-permute-start.5 = (bf16[1,8,3072]{2,1,0:T(8,128)(2,1)S(1)}, bf16[1,8,3072]{2,1,0:T(8,128)(2,1)S(1)}, u32[]{:S(2)}, u32[]{:S(2)}) collective-permute-start(bf16[1,8,3072]{2,1,0:T(8,128)(2,1)S(1)} %multiply_convert_fusion), channel_id=1, source_target_pairs={{0,128},{32,160},{64,192},{96,224},{128,0},{160,32},{192,64},{224,... | collective-permute-start | bytes 147464 | tf_op jit(solution)/shard_map/ppermute | solution.py:20
  56.1 33.4 %all-to-all-start.1 = ((f32[128,8,128]{2,1,0:T(8,128)}), f32[128,8,128]{2,1,0:T(8,128)}, u32[]{:S(2)}, u32[]{:S(2)}) async-start(f32[128,8,128]{2,1,0:T(8,128)} %broadcast_in_dim.8), calls=%async_computation.1 | async-start | bytes 1048576 | tf_op jit(solution)/shard_map/all_to_all | solution.py:86
  70.6 12.7 %collective-permute-start.6 = (bf16[2,8,3072]{2,1,0:T(8,128)(2,1)S(1)}, bf16[2,8,3072]{2,1,0:T(8,128)(2,1)S(1)}, u32[]{:S(2)}, u32[]{:S(2)}) collective-permute-start(bf16[2,8,3072]{2,1,0:T(8,128)(2,1)S(1)} %pad_maximum_fusion.5), channel_id=1, source_target_pairs={{0,64},{32,96},{64,0},{96,32},{128,192},{160,224},{192,128},{224,1... | collective-permute-start | bytes 294920 | tf_op jit(solution)/shard_map/ppermute | solution.py:20
  83.3 6.1 %collective-permute-start.7 = (bf16[4,8,3072]{2,1,0:T(8,128)(2,1)S(1)}, bf16[4,8,3072]{2,1,0:T(8,128)(2,1)S(1)}, u32[]{:S(2)}, u32[]{:S(2)}) collective-permute-start(bf16[4,8,3072]{2,1,0:T(8,128)(2,1)S(1)} %pad_maximum_fusion.3), channel_id=1, source_target_pairs={{0,32},{32,0},{64,96},{96,64},{128,160},{160,128},{192,224},{224,1... | collective-permute-start | bytes 589832 | tf_op jit(solution)/shard_map/ppermute | solution.py:20
  92.2 6.4 %collective-permute-start.11 = (f32[2,4,3072]{2,1,0:T(4,128)S(1)}, f32[2,4,3072]{2,1,0:T(4,128)S(1)}, u32[]{:S(2)}, u32[]{:S(2)}) collective-permute-start(f32[2,4,3072]{2,1,0:T(4,128)S(1)} %get-tuple-element.29), channel_id=1, source_target_pairs={{0,8},{8,0},{1,9},{9,1},{2,10},{10,2},{3,11},{11,3},{4,12},{12,4},... | collective-permute-start | bytes 294920 | tf_op jit(solution)/shard_map/ppermute | solution.py:110
  96.9 10.8 %collective-permute-start.8 = (bf16[8,8,3072]{2,1,0:T(8,128)(2,1)S(1)}, bf16[8,8,3072]{2,1,0:T(8,128)(2,1)S(1)}, u32[]{:S(2)}, u32[]{:S(2)}) collective-permute-start(bf16[8,8,3072]{2,1,0:T(8,128)(2,1)S(1)} %subtract_convert_fusion.near_ref), channel_id=1, source_target_pairs={{0,16},{16,0},{1,17},{17,1},{2,18},{18,2},{3,19},{19,3},{4,20},{20... | collective-permute-start | bytes 1179656 | tf_op jit(solution)/shard_map/ppermute | solution.py:102
  98.3 10.9 %collective-permute-start.9 = (bf16[8,8,3072]{2,1,0:T(8,128)(2,1)S(1)}, bf16[8,8,3072]{2,1,0:T(8,128)(2,1)S(1)}, u32[]{:S(2)}, u32[]{:S(2)}) collective-permute-start(bf16[8,8,3072]{2,1,0:T(8,128)(2,1)S(1)} %subtract_convert_fusion.near_ref), channel_id=1, source_target_pairs={{0,8},{8,0},{1,9},{9,1},{2,10},{10,2},{3,11},{11,3},{4,12},{12,4},... | collective-permute-start | bytes 1179656 | tf_op jit(solution)/shard_map/ppermute | solution.py:103
  107.7 2.2 %collective-permute-start.10 = (bf16[8,8,3072]{2,1,0:T(8,128)(2,1)S(1)}, bf16[8,8,3072]{2,1,0:T(8,128)(2,1)S(1)}, u32[]{:S(2)}, u32[]{:S(2)}) collective-permute-start(bf16[8,8,3072]{2,1,0:T(8,128)(2,1)S(1)} %collective-permute-done.8.far_ref), channel_id=1, source_target_pairs={{0,8},{8,0},{1,9},{9,1},{2,10},{10,2},{3,11},{11,3},{4,12},{12,4},... | collective-permute-start | bytes 1179656 | tf_op jit(solution)/shard_map/ppermute | solution.py:104

commit v4 on v1

v4 whole, which is shorter than its diff:
```python
import functools
import math

import jax
import jax.numpy as jnp
from jax import lax
from jax.experimental import pallas as pl
from jax.experimental.pallas import tpu as pltpu
from jax.sharding import Mesh
from jax.sharding import PartitionSpec as P

CHIPS = ("z", "yl")
PLACES = ((0, 4, 2, 6), (1, 5, 3, 7))


def tied(array, *others):
    return lax.optimization_barrier((array, *others))[0]


def bring(axis, size, jump, array):
    return lax.ppermute(array, axis, [(i, i ^ jump) for i in range(size)])


def near(axis, array):
    return bring(axis, 2, 1, array)


def over_z(array, jump):
    return bring("z", 8, jump, array)


def doubled(held, jump):
    return jnp.concatenate((held, over_z(held, jump)), axis=0)


def summed(axis, size, array):
    return sum((bring(axis, size, jump, array) for jump in (1, 2, 3)), array)


def last_kernel(max_norm, where_ref, weights_ref, outer_ref, moment_ref, sums_ref, *refs):
    core, z, yl = where_ref[0], where_ref[1], where_ref[2]
    pseudo_refs, base_refs, push_refs = refs[:2], refs[2:10], refs[10:18]
    mixed_ref, new_outer_ref, new_moment_ref = refs[18:]
    norms = jnp.sqrt(sums_ref[...])
    factors = jnp.minimum(1.0, max_norm / (norms + 1e-06))
    for at in range(2):
        frag = core if at == 0 else 1 - core
        factor = factors[at : at + 1, :1]
        clipped = factor * pseudo_refs[at][...]
        moment = 0.9 * moment_ref[frag] + clipped
        new_moment_ref[frag] = moment
        new_outer_ref[frag] = outer_ref[frag] - 0.7 * (clipped + 0.9 * moment)
        for part in range(4):
            base_ref, push_ref = base_refs[4 * at + part], push_refs[4 * at + part]
            side = yl if part < 2 else 1 - yl
            for k in range(4):
                chip = 2 * (z ^ PLACES[part % 2][k]) + side
                own = weights_ref[frag, chip].astype(jnp.float32)
                base = base_ref[k].astype(jnp.float32)
                source = base - factor * push_ref[k].astype(jnp.float32)
                source = source.astype(jnp.bfloat16).astype(jnp.float32)
                mixed = 0.5 * own + 0.5 * source
                mixed_ref[frag, chip] = mixed.astype(jnp.bfloat16)


def shards(local_weights, global_params, momentum):
    f32, bf16 = jnp.float32, jnp.bfloat16
    core, yl = lax.axis_index("core"), lax.axis_index("yl")
    other = 1 - core
    first = core == 0
    chips = lax.axis_size(CHIPS)
    replicas = 2 * chips
    everywhere = chips * lax.axis_size(("x", "yh"))
    rows, width = local_weights.shape[3], local_weights.shape[4]
    share_rows = global_params.shape[2]
    block = rows // chips
    max_norm = 0.5 * math.sqrt(block * width * everywhere)

    def pick(array, index, axis=0):
        return lax.dynamic_index_in_dim(array, index, axis, keepdims=False)

    def swapped_rows(array):
        kept = pick(array, core)
        came = near("core", pick(array, other))
        return jnp.where(
            first,
            jnp.concatenate((kept, came), axis=0),
            jnp.concatenate((came, kept), axis=0),
        )

    weights = local_weights[:, 0, 0]
    outer = swapped_rows(global_params[:, 0])
    moment = swapped_rows(momentum[:, 0])
    base = (outer - 0.567 * moment).astype(bf16)[None]
    far = over_z(base, 4)
    got = near("core", pick(weights, other))
    pair = (pick(weights, core).astype(f32) + got.astype(f32)).astype(bf16)

    sides = pair.reshape(chips // 2, 2, block, width)
    give_side = pick(sides, 1 - yl, 1)
    base = jnp.concatenate((base, tied(far, give_side)), axis=0)
    got = near("yl", give_side)
    quad = (pick(sides, yl, 1).astype(f32) + got.astype(f32)).astype(bf16)
    pieces = lax.all_to_all(tied(quad, base), "z", 0, 0, tiled=True)
    base = doubled(base, 2)
    base_far = near("yl", tied(base, quad))
    bases = [base, base_far, near("core", base), near("core", base_far)]
    pieces, *bases = lax.optimization_barrier((pieces, *bases))
    base = bases[0]

    total = jnp.sum(pieces.astype(f32), axis=0)
    pseudo = outer - total / replicas
    push = (1.33 * pseudo).astype(bf16)[None]
    sums = jnp.broadcast_to(jnp.sum(pseudo * pseudo), (1, 128))

    sums = jnp.concatenate((sums, near("core", sums)), axis=0)
    sums = summed(("yl", "yh"), 4, sums)
    push = doubled(push, 4)
    more = over_z(base, 1)
    sums, push, more = lax.optimization_barrier((sums, push, more))

    sums = summed("z", 8, sums)
    push = doubled(push, 2)
    more_far = near("yl", more)
    sums, push, more, more_far = lax.optimization_barrier((sums, push, more, more_far))

    sums = sums + over_z(sums, 4)
    bases += [more, more_far, near("core", more), near("core", more_far)]
    more = over_z(push, 1)
    push_far = near("yl", push)
    halves = pseudo.reshape(2, share_rows, width)
    pseudos = [pick(halves, core), near("core", pick(halves, other))]
    sums, push, more, push_far, pseudos, bases = lax.optimization_barrier(
        (sums, push, more, push_far, pseudos, bases)
    )

    sums = summed("x", 4, sums)
    more_far = near("yl", more)
    pushes = [push, push_far, near("core", push), near("core", push_far)]
    pushes += [more, more_far, near("core", more), near("core", more_far)]
    order = (0, 4, 1, 5, 2, 6, 3, 7)
    sources = [bases[i] for i in order] + [pushes[i] for i in order]

    in_vmem = pl.BlockSpec(memory_space=pltpu.VMEM)
    state = jax.ShapeDtypeStruct((2, share_rows, width), f32)
    mixed, outer_next, moment_next = pl.pallas_call(
        functools.partial(last_kernel, max_norm),
        out_shape=(
            jax.ShapeDtypeStruct((2, chips, block, width), bf16),
            state,
            state,
        ),
        in_specs=[pl.BlockSpec(memory_space=pltpu.SMEM)] + [in_vmem] * 22,
        out_specs=(in_vmem,) * 3,
        compiler_params=pltpu.CompilerParams(vmem_limit_bytes=32 * 1024 * 1024),
        name="last",
    )(
        jnp.stack((core, lax.axis_index("z"), yl)),
        weights.reshape(2, chips, block, width),
        global_params[:, 0],
        momentum[:, 0],
        sums,
        *pseudos,
        *sources,
    )
    return (
        mixed.reshape(local_weights.shape),
        outer_next[:, None],
        moment_next[:, None],
    )


def solution(mesh):
    fine = Mesh(
        mesh.devices.reshape(8, 2, 2, 4, 2), ("z", "yl", "core", "x", "yh")
    )
    replica, mp = ("z", "yl", "core"), ("x", "yh")
    whole = P(None, replica, mp, None, None)
    outer = P(None, mp, replica, None)
    return jax.shard_map(
        shards,
        mesh=fine,
        in_specs=(whole, outer, outer),
        out_specs=(whole, outer, outer),
        check_vma=False,
    )
```

time: 94.6 us -> 99.9 us (1.056)
  starting transfers between devices: 22 us -> 60.2 us
  blocking collectives: 22.2 us -> 0 us
  waiting for transfers between devices: 40.2 us -> 23.7 us
  local copies, waits for them, and re-layouts: 3.79 us -> 7.53 us
  Pallas kernels: 0 us -> 3.39 us
    ppermute x4 -> x34, starting transfers between devices: 10.9 us -> 53.6 us  [bring(): return lax.ppermute(array, axis, [(i, i ^ jump) for i in range(size)])]
    all_to_all x2 -> x1, waiting for transfers between devices: 36.2 us -> 3.79 us  [shards(): pieces = lax.all_to_all(tied(quad, base), 'z', 0, 0, tiled=True)]
    all_to_all x1 -> x0, blocking collectives: 22.2 us -> none  [shards(): lax.all_to_all(jnp.broadcast_to(part, (everywhere, 1, 128)), ('z', 'yl',...]
    ppermute x4 -> x34, waiting for transfers between devices: 4.03 us -> 19.9 us  [bring(): return lax.ppermute(array, axis, [(i, i ^ jump) for i in range(size)])]
    all_to_all x2 -> x1, starting transfers between devices: 11.2 us -> 6.58 us  [shards(): pieces = lax.all_to_all(tied(quad, base), 'z', 0, 0, tiled=True)]
    pallas_call x0 -> x1, Pallas kernels: none -> 3.39 us  [shards(): pl.pallas_call(functools.partial(last_kernel, max_norm), out_shape=(jax.S...]
    unnamed x8 -> x14, local copies, waits for them, and re-layouts: 0.03 us -> 3.23 us
    concatenate x0 -> x2, local copies, waits for them, and re-layouts: none -> 1.48 us  [the longest x1 0.83 us: swapped_rows(): jnp.concatenate((kept, came), axis=0)]
  transfers between devices with their start and end apart: 6 -> 35, of which waited for: 5 -> 17; matrix products, arithmetic and copies ran while one was open for 1% -> 5% of each run, Pallas kernels for 0% -> 0%
where the time goes in v4:
time: 99.9 us; the launch traced here: 99.4 us
  starting transfers between devices  60.2 us (60%)
  waiting for transfers between devices  23.7 us (24%)
  local copies, waits for them, and re-layouts  7.53 us (8%)
  other arithmetic  3.81 us (4%)
  Pallas kernels  3.39 us (3%)
    ppermute x34, starting transfers between devices, bring(): return lax.ppermute(array, axis, [(i, i ^ jump) for i in range(size)])  53.6 us
    ppermute x34, waiting for transfers between devices, bring(): return lax.ppermute(array, axis, [(i, i ^ jump) for i in range(size)])  19.9 us
    all_to_all x1, starting transfers between devices, shards(): pieces = lax.all_to_all(tied(quad, base), 'z', 0, 0, tiled=True)  6.58 us
    all_to_all x1, waiting for transfers between devices, shards(): pieces = lax.all_to_all(tied(quad, base), 'z', 0, 0, tiled=True)  3.79 us
    pallas_call x1, Pallas kernels, shards(): pl.pallas_call(functools.partial(last_kernel, max_norm), out_shape=(jax.S...  3.39 us
    unnamed x14, local copies, waits for them, and re-layouts  3.23 us
    squeeze x4, local copies, waits for them, and re-layouts, pick(): return lax.dynamic_index_in_dim(array, index, axis, keepdims=False)  2.15 us
  transfers between devices with their start and end apart: 35, of which 17 were waited for; matrix products, arithmetic and copies ran while one was open for 5% of the time, Pallas kernels for 0%

profile of v4, /device:TPU:1, one launch (start us, length us, event | category | flops | bytes accessed | tf_op | source)
XLA Modules:
  0.0 99.4 jit_solution(14142445812946392870)
XLA Ops:
  0.7 1.3 %dynamic-slice_bitcast_fusion = bf16[128,3072]{1,0:T(8,128)(2,1)S(1)} fusion(bf16[2,1,1,128,3072]{4,3,2,1,0:T(8,128)(2,1)} %param.3, s32[]{:T(128)S(6)} %select_n.59), kind=kLoop, calls=%fused_computation.5 | loop fusion | bytes 1572868 | tf_op jit(solution)/shard_map/jit(dynamic_index_in_dim)/squeeze | solution.py:80
  2.0 3.3 %collective-permute-start.1 = (bf16[128,3072]{1,0:T(8,128)(2,1)S(1)}, bf16[128,3072]{1,0:T(8,128)(2,1)}, u32[]{:S(2)}, u32[]{:S(2)}) collective-permute-start(bf16[128,3072]{1,0:T(8,128)(2,1)S(1)} %dynamic-slice_bitcast_fusion), channel_id=1, source_target_pairs={{0,8},{8,0},{1,9},{9,1},{2,10},{10,2},{3,11},{11,3},{4,12},{12,4},... | collective-permute-start | bytes 2359304 | tf_op jit(solution)/shard_map/ppermute | solution.py:21
  5.3 0.8 dynamic-slice_bitcast_fusion.5
  7.4 1.3 %fusion = bf16[128,3072]{1,0:T(8,128)(2,1)S(1)} fusion(bf16[128,3072]{1,0:T(8,128)(2,1)} %collective-permute-done.1, bf16[2,1,1,128,3072]{4,3,2,1,0:T(8,128)(2,1)S(1)} %copy-done, s32[]{:T(128)S(6)} %select_n.58), kind=kLoop, calls=%fused_computation.1 | loop fusion | flops 1572864 | bytes 2359300 | tf_op jit(solution)/shard_map/convert_element_type | solution.py:97
  8.7 0.8 dynamic-slice_bitcast_fusion.1
  9.6 6.5 %collective-permute-start.4 = (bf16[1,8,3072]{2,1,0:T(8,128)(2,1)S(1)}, bf16[1,8,3072]{2,1,0:T(8,128)(2,1)S(1)}, u32[]{:S(2)}, u32[]{:S(2)}) collective-permute-start(bf16[1,8,3072]{2,1,0:T(8,128)(2,1)S(1)} %fusion.5), channel_id=1, source_target_pairs={{0,128},{32,160},{64,192},{96,224},{128,0},{160,32},{192,64},{224,... | collective-permute-start | bytes 147464 | tf_op jit(solution)/shard_map/ppermute | solution.py:21
  16.1 1.5 %collective-permute-done.4 = bf16[1,8,3072]{2,1,0:T(8,128)(2,1)S(1)} collective-permute-done((bf16[1,8,3072]{2,1,0:T(8,128)(2,1)S(1)}, bf16[1,8,3072]{2,1,0:T(8,128)(2,1)S(1)}, u32[]{:S(2)}, u32[]{:S(2)}) %collective-permute-start.4) | collective-permute-done | bytes 49184 | tf_op jit(solution)/shard_map/ppermute | solution.py:21
  17.6 1.5 %collective-permute-start.5 = (bf16[2,8,3072]{2,1,0:T(8,128)(2,1)S(1)}, bf16[2,8,3072]{2,1,0:T(8,128)(2,1)S(1)}, u32[]{:S(2)}, u32[]{:S(2)}) collective-permute-start(bf16[2,8,3072]{2,1,0:T(8,128)(2,1)S(1)} %pad_maximum_fusion.2), channel_id=1, source_target_pairs={{0,64},{32,96},{64,0},{96,32},{128,192},{160,224},{192,128},{224,1... | collective-permute-start | bytes 294920 | tf_op jit(solution)/shard_map/ppermute | solution.py:21
  19.2 0.9 collective-permute-done.2
  20.0 0.8 fusion.1
  20.9 6.6 %all-to-all-start = ((bf16[8,8,3072]{2,1,0:T(8,128)(2,1)}), bf16[8,8,3072]{2,1,0:T(8,128)(2,1)S(1)}, u32[]{:S(2)}, u32[]{:S(2)}) async-start(bf16[8,8,3072]{2,1,0:T(8,128)(2,1)} %fusion.1), calls=%async_computation | async-start | bytes 786432 | tf_op jit(solution)/shard_map/all_to_all | solution.py:104
  27.5 1.4 %collective-permute-start.6 = (bf16[4,8,3072]{2,1,0:T(8,128)(2,1)S(1)}, bf16[4,8,3072]{2,1,0:T(8,128)(2,1)S(1)}, u32[]{:S(2)}, u32[]{:S(2)}) collective-permute-start(bf16[4,8,3072]{2,1,0:T(8,128)(2,1)S(1)} %pad_maximum_fusion.refs_2_), channel_id=1, source_target_pairs={{0,16},{16,0},{1,17},{17,1},{2,18},{18,2},{3,19},{19,3},{4,20},{20... | collective-permute-start | bytes 589832 | tf_op jit(solution)/shard_map/ppermute | solution.py:21
  28.9 1.8 %collective-permute-start.7 = (bf16[4,8,3072]{2,1,0:T(8,128)(2,1)S(1)}, bf16[4,8,3072]{2,1,0:T(8,128)(2,1)S(1)}, u32[]{:S(2)}, u32[]{:S(2)}) collective-permute-start(bf16[4,8,3072]{2,1,0:T(8,128)(2,1)S(1)} %pad_maximum_fusion.refs_2_), channel_id=1, source_target_pairs={{0,8},{8,0},{1,9},{9,1},{2,10},{10,2},{3,11},{11,3},{4,12},{12,4},... | collective-permute-start | bytes 589832 | tf_op jit(solution)/shard_map/ppermute | solution.py:21
  30.6 1.5 %collective-permute-done.6.refs_4_ = bf16[4,8,3072]{2,1,0:T(8,128)(2,1)S(1)} collective-permute-done((bf16[4,8,3072]{2,1,0:T(8,128)(2,1)S(1)}, bf16[4,8,3072]{2,1,0:T(8,128)(2,1)S(1)}, u32[]{:S(2)}, u32[]{:S(2)}) %collective-permute-start.6) | collective-permute-done | bytes 196640 | tf_op jit(solution)/shard_map/ppermute | solution.py:21
  32.1 2.9 %collective-permute-start.8 = (bf16[4,8,3072]{2,1,0:T(8,128)(2,1)S(1)}, bf16[4,8,3072]{2,1,0:T(8,128)(2,1)S(1)}, u32[]{:S(2)}, u32[]{:S(2)}) collective-permute-start(bf16[4,8,3072]{2,1,0:T(8,128)(2,1)S(1)} %collective-permute-done.6.refs_4_), channel_id=1, source_target_pairs={{0,8},{8,0},{1,9},{9,1},{2,10},{10,2},{3,11},{11,3},{4,12},{12,4},... | collective-permute-start | bytes 589832 | tf_op jit(solution)/shard_map/ppermute | solution.py:21
  35.0 1.1 %collective-permute-done.8.refs_8_ = bf16[4,8,3072]{2,1,0:T(8,128)(2,1)S(1)} collective-permute-done((bf16[4,8,3072]{2,1,0:T(8,128)(2,1)S(1)}, bf16[4,8,3072]{2,1,0:T(8,128)(2,1)S(1)}, u32[]{:S(2)}, u32[]{:S(2)}) %collective-permute-start.8) | collective-permute-done | bytes 196640 | tf_op jit(solution)/shard_map/ppermute | solution.py:21
  36.1 3.8 %all-to-all-done = bf16[8,8,3072]{2,1,0:T(8,128)(2,1)S(1)} async-done(((bf16[8,8,3072]{2,1,0:T(8,128)(2,1)}), bf16[8,8,3072]{2,1,0:T(8,128)(2,1)S(1)}, u32[]{:S(2)}, u32[]{:S(2)}) %all-to-all-start) | async-done | bytes 393248 | tf_op jit(solution)/shard_map/all_to_all | solution.py:104
  39.9 0.7 multiply_reduce_fusion
  41.2 3.3 %collective-permute-start.9 = (f32[1,128]{1,0:T(1,128)S(1)}, f32[1,128]{1,0:T(1,128)S(1)}, u32[]{:S(2)}, u32[]{:S(2)}) collective-permute-start(f32[1,128]{1,0:T(1,128)S(1)} %broadcast_in_dim.11), channel_id=1, source_target_pairs={{0,8},{8,0},{1,9},{9,1},{2,10},{10,2},{3,11},{11,3},{4,12},{12,4},... | collective-permute-start | bytes 1544 | tf_op jit(solution)/shard_map/ppermute | solution.py:21
  44.5 0.8 collective-permute-done.9
  45.3 0.7 concatenate.88
  46.0 1.4 %collective-permute-start.11 = (f32[2,128]{1,0:T(2,128)S(1)}, f32[2,128]{1,0:T(2,128)S(1)}, u32[]{:S(2)}, u32[]{:S(2)}) collective-permute-start(f32[2,128]{1,0:T(2,128)S(1)} %concatenate.88), channel_id=1, source_target_pairs={{0,16},{1,17},{16,0},{17,1},{2,18},{3,19},{18,2},{19,3},{4,20},{5,... | collective-permute-start | bytes 3080 | tf_op jit(solution)/shard_map/ppermute | solution.py:21
  47.4 1.9 %collective-permute-start.12 = (f32[2,128]{1,0:T(2,128)S(1)}, f32[2,128]{1,0:T(2,128)S(1)}, u32[]{:S(2)}, u32[]{:S(2)}) collective-permute-start(f32[2,128]{1,0:T(2,128)S(1)} %concatenate.88), channel_id=1, source_target_pairs={{0,17},{1,16},{16,1},{17,0},{2,19},{3,18},{18,3},{19,2},{4,21},{5,... | collective-permute-start | bytes 3080 | tf_op jit(solution)/shard_map/ppermute | solution.py:21
  49.3 0.7 collective-permute-start.10
  50.4 1.1 %collective-permute-start.14 = (bf16[4,8,3072]{2,1,0:T(8,128)(2,1)S(1)}, bf16[4,8,3072]{2,1,0:T(8,128)(2,1)S(1)}, u32[]{:S(2)}, u32[]{:S(2)}) collective-permute-start(bf16[4,8,3072]{2,1,0:T(8,128)(2,1)S(1)} %pad_maximum_fusion.refs_2_), channel_id=1, source_target_pairs={{0,32},{32,0},{64,96},{96,64},{128,160},{160,128},{192,224},{224,1... | collective-permute-start | bytes 589832 | tf_op jit(solution)/shard_map/ppermute | solution.py:21
  51.6 1.6 %collective-permute-done.10 = f32[2,128]{1,0:T(2,128)S(1)} collective-permute-done((f32[2,128]{1,0:T(2,128)S(1)}, f32[2,128]{1,0:T(2,128)S(1)}, u32[]{:S(2)}, u32[]{:S(2)}) %collective-permute-start.10) | collective-permute-done | bytes 1056 | tf_op jit(solution)/shard_map/ppermute | solution.py:21
  53.2 0.7 add_add_fusion.2
  53.9 3.3 %collective-permute-done.13 = bf16[1,8,3072]{2,1,0:T(8,128)(2,1)S(1)} collective-permute-done((bf16[1,8,3072]{2,1,0:T(8,128)(2,1)S(1)}, bf16[1,8,3072]{2,1,0:T(8,128)(2,1)S(1)}, u32[]{:S(2)}, u32[]{:S(2)}) %collective-permute-start.13) | collective-permute-done | bytes 49184 | tf_op jit(solution)/shard_map/ppermute | solution.py:21
  57.2 1.1 %collective-permute-done.14.refs_3_ = bf16[4,8,3072]{2,1,0:T(8,128)(2,1)S(1)} collective-permute-done((bf16[4,8,3072]{2,1,0:T(8,128)(2,1)S(1)}, bf16[4,8,3072]{2,1,0:T(8,128)(2,1)S(1)}, u32[]{:S(2)}, u32[]{:S(2)}) %collective-permute-start.14) | collective-permute-done | bytes 196640 | tf_op jit(solution)/shard_map/ppermute | solution.py:21
  58.3 1.9 %collective-permute-start.17 = (f32[2,128]{1,0:T(2,128)S(1)}, f32[2,128]{1,0:T(2,128)S(1)}, u32[]{:S(2)}, u32[]{:S(2)}) collective-permute-start(f32[2,128]{1,0:T(2,128)S(1)} %add_add_fusion.2), channel_id=1, source_target_pairs={{0,96},{32,64},{64,32},{96,0},{128,224},{160,192},{192,160},{224,1... | collective-permute-start | bytes 3080 | tf_op jit(solution)/shard_map/ppermute | solution.py:21
  60.3 1.6 %collective-permute-start.15 = (f32[2,128]{1,0:T(2,128)S(1)}, f32[2,128]{1,0:T(2,128)S(1)}, u32[]{:S(2)}, u32[]{:S(2)}) collective-permute-start(f32[2,128]{1,0:T(2,128)S(1)} %add_add_fusion.2), channel_id=1, source_target_pairs={{0,32},{32,0},{64,96},{96,64},{128,160},{160,128},{192,224},{224,1... | collective-permute-start | bytes 3080 | tf_op jit(solution)/shard_map/ppermute | solution.py:21
  61.9 0.8 collective-permute-start.18
  63.5 3.6 %collective-permute-done.18 = bf16[2,8,3072]{2,1,0:T(8,128)(2,1)S(1)} collective-permute-done((bf16[2,8,3072]{2,1,0:T(8,128)(2,1)S(1)}, bf16[2,8,3072]{2,1,0:T(8,128)(2,1)S(1)}, u32[]{:S(2)}, u32[]{:S(2)}) %collective-permute-start.18) | collective-permute-done | bytes 98336 | tf_op jit(solution)/shard_map/ppermute | solution.py:21
  67.8 1.2 %collective-permute-start.21 = (bf16[4,8,3072]{2,1,0:T(8,128)(2,1)S(1)}, bf16[4,8,3072]{2,1,0:T(8,128)(2,1)}, u32[]{:S(2)}, u32[]{:S(2)}) collective-permute-start(bf16[4,8,3072]{2,1,0:T(8,128)(2,1)S(1)} %pad_maximum_fusion.1.refs_10_), channel_id=1, source_target_pairs={{0,32},{32,0},{64,96},{96,64},{128,160},{160,128},{192,224},{224,1... | collective-permute-start | bytes 589832 | tf_op jit(solution)/shard_map/ppermute | solution.py:21
  69.0 3.2 %collective-permute-start.20 = (f32[2,128]{1,0:T(2,128)S(1)}, f32[2,128]{1,0:T(2,128)S(1)}, u32[]{:S(2)}, u32[]{:S(2)}) collective-permute-start(f32[2,128]{1,0:T(2,128)S(1)} %add_add_fusion.1), channel_id=1, source_target_pairs={{0,128},{32,160},{64,192},{96,224},{128,0},{160,32},{192,64},{224,... | collective-permute-start | bytes 3080 | tf_op jit(solution)/shard_map/ppermute | solution.py:21
  72.2 5.3 %collective-permute-start.24 = (bf16[4,8,3072]{2,1,0:T(8,128)(2,1)S(1)}, bf16[4,8,3072]{2,1,0:T(8,128)(2,1)S(1)}, u32[]{:S(2)}, u32[]{:S(2)}) collective-permute-start(bf16[4,8,3072]{2,1,0:T(8,128)(2,1)S(1)} %collective-permute-done.14.refs_3_), channel_id=1, source_target_pairs={{0,8},{8,0},{1,9},{9,1},{2,10},{10,2},{3,11},{11,3},{4,12},{12,4},... | collective-permute-start | bytes 589832 | tf_op jit(solution)/shard_map/ppermute | solution.py:21
  77.5 4.0 %collective-permute-start.23 = (f32[4,3072]{1,0:T(4,128)S(1)}, f32[4,3072]{1,0:T(4,128)S(1)}, u32[]{:S(2)}, u32[]{:S(2)}) collective-permute-start(f32[4,3072]{1,0:T(4,128)S(1)} %get-tuple-element.72), channel_id=1, source_target_pairs={{0,8},{8,0},{1,9},{9,1},{2,10},{10,2},{3,11},{11,3},{4,12},{12,4},... | collective-permute-start | bytes 147464 | tf_op jit(solution)/shard_map/ppermute | solution.py:21
  81.5 0.9 collective-permute-done.23.refs_1_
  82.4 0.7 copy-done.3
  83.1 0.7 copy-done.5
  84.1 2.5 %collective-permute-start.28 = (f32[2,128]{1,0:T(2,128)S(1)}, f32[2,128]{1,0:T(2,128)S(1)}, u32[]{:S(2)}, u32[]{:S(2)}) collective-permute-start(f32[2,128]{1,0:T(2,128)S(1)} %add.73), channel_id=1, source_target_pairs={{0,6},{2,4},{4,2},{6,0},{1,7},{3,5},{5,3},{7,1},{8,14},{10,12},{12... | collective-permute-start | bytes 3080 | tf_op jit(solution)/shard_map/ppermute | solution.py:21
  87.4 1.5 %collective-permute-start.31 = (bf16[4,8,3072]{2,1,0:T(8,128)(2,1)}, bf16[4,8,3072]{2,1,0:T(8,128)(2,1)S(1)}, u32[]{:S(2)}, u32[]{:S(2)}) collective-permute-start(bf16[4,8,3072]{2,1,0:T(8,128)(2,1)} %collective-permute-done.21.refs_11_), channel_id=1, source_target_pairs={{0,8},{8,0},{1,9},{9,1},{2,10},{10,2},{3,11},{11,3},{4,12},{12,4},... | collective-permute-start | bytes 589832 | tf_op jit(solution)/shard_map/ppermute | solution.py:21
  89.5 1.0 collective-permute-done.27
  90.5 2.1 %collective-permute-start.32 = (bf16[4,8,3072]{2,1,0:T(8,128)(2,1)S(1)}, bf16[4,8,3072]{2,1,0:T(8,128)(2,1)S(1)}, u32[]{:S(2)}, u32[]{:S(2)}) collective-permute-start(bf16[4,8,3072]{2,1,0:T(8,128)(2,1)S(1)} %collective-permute-done.22.refs_12_), channel_id=1, source_target_pairs={{0,8},{8,0},{1,9},{9,1},{2,10},{10,2},{3,11},{11,3},{4,12},{12,4},... | collective-permute-start | bytes 589832 | tf_op jit(solution)/shard_map/ppermute | solution.py:21
  92.6 1.2 %collective-permute-done.32.refs_16_ = bf16[4,8,3072]{2,1,0:T(8,128)(2,1)S(1)} collective-permute-done((bf16[4,8,3072]{2,1,0:T(8,128)(2,1)S(1)}, bf16[4,8,3072]{2,1,0:T(8,128)(2,1)S(1)}, u32[]{:S(2)}, u32[]{:S(2)}) %collective-permute-start.32) | collective-permute-done | bytes 196640 | tf_op jit(solution)/shard_map/ppermute | solution.py:21
  94.2 0.9 copy-done.4
  95.1 0.9 copy-done.6
  96.1 3.4 %last.1 = (bf16[2,16,8,3072]{3,2,1,0:T(8,128)(2,1)}, f32[2,4,3072]{2,1,0:T(4,128)}, f32[2,4,3072]{2,1,0:T(4,128)}) custom-call(s32[3]{0:T(128)S(1)} %pad_add_fusion.where_ref, bf16[2,16,8,3072]{3,2,1,0:T(8,128)(2,1)S(1)} %bitcast.48, f32[2,4,3072]{2,1,0:T(4,128)S(1)} %bitcast.50, f32[2,4,3072]{2,1,0:T(4,128)S(1)} %bitcast.49, ...), custom_call_target="tpu_custom_call" | custom-call | tf_op jit(solution)/shard_map/last/pallas_call | solution.py:146
  (60 shorter events, 6.3 us)
Async XLA Ops:
  0.6 6.7 %copy-start = (bf16[2,1,1,128,3072]{4,3,2,1,0:T(8,128)(2,1)S(1)}, bf16[2,1,1,128,3072]{4,3,2,1,0:T(8,128)(2,1)}, u32[]{:S(2)}) copy-start(bf16[2,1,1,128,3072]{4,3,2,1,0:T(8,128)(2,1)} %param.3) | copy-start | bytes 4718596
  0.6 5.6 %copy-start.2 = (f32[2,1,4,3072]{3,2,1,0:T(4,128)S(1)}, f32[2,1,4,3072]{3,2,1,0:T(4,128)}, u32[]{:S(2)}) copy-start(f32[2,1,4,3072]{3,2,1,0:T(4,128)} %param.4) | copy-start | bytes 294916
  2.0 5.4 %collective-permute-start.1 = (bf16[128,3072]{1,0:T(8,128)(2,1)S(1)}, bf16[128,3072]{1,0:T(8,128)(2,1)}, u32[]{:S(2)}, u32[]{:S(2)}) collective-permute-start(bf16[128,3072]{1,0:T(8,128)(2,1)S(1)} %dynamic-slice_bitcast_fusion), channel_id=1, source_target_pairs={{0,8},{8,0},{1,9},{9,1},{2,10},{10,2},{3,11},{11,3},{4,12},{12,4},... | collective-permute-start | bytes 2359304 | tf_op jit(solution)/shard_map/ppermute | solution.py:21
  6.2 3.3 %collective-permute-start.3 = (f32[4,3072]{1,0:T(4,128)S(1)}, f32[4,3072]{1,0:T(4,128)S(1)}, u32[]{:S(2)}, u32[]{:S(2)}) collective-permute-start(f32[4,3072]{1,0:T(4,128)S(1)} %get-tuple-element.78), channel_id=1, source_target_pairs={{0,8},{8,0},{1,9},{9,1},{2,10},{10,2},{3,11},{11,3},{4,12},{12,4},... | collective-permute-start | bytes 147464 | tf_op jit(solution)/shard_map/ppermute | solution.py:21
  6.3 3.2 %collective-permute-start = (f32[4,3072]{1,0:T(4,128)S(1)}, f32[4,3072]{1,0:T(4,128)S(1)}, u32[]{:S(2)}, u32[]{:S(2)}) collective-permute-start(f32[4,3072]{1,0:T(4,128)S(1)} %get-tuple-element.76), channel_id=1, source_target_pairs={{0,8},{8,0},{1,9},{9,1},{2,10},{10,2},{3,11},{11,3},{4,12},{12,4},... | collective-permute-start | bytes 147464 | tf_op jit(solution)/shard_map/ppermute | solution.py:21
  9.5 10.5 %collective-permute-start.2 = (bf16[8,8,3072]{2,1,0:T(8,128)(2,1)}, bf16[8,8,3072]{2,1,0:T(8,128)(2,1)S(1)}, u32[]{:S(2)}, u32[]{:S(2)}) collective-permute-start(bf16[8,8,3072]{2,1,0:T(8,128)(2,1)} %dynamic-slice_bitcast_fusion.1), channel_id=1, source_target_pairs={{0,16},{16,0},{1,17},{17,1},{2,18},{18,2},{3,19},{19,3},{4,20},{20... | collective-permute-start | bytes 1179656 | tf_op jit(solution)/shard_map/ppermute | solution.py:21
  9.6 8.0 %collective-permute-start.4 = (bf16[1,8,3072]{2,1,0:T(8,128)(2,1)S(1)}, bf16[1,8,3072]{2,1,0:T(8,128)(2,1)S(1)}, u32[]{:S(2)}, u32[]{:S(2)}) collective-permute-start(bf16[1,8,3072]{2,1,0:T(8,128)(2,1)S(1)} %fusion.5), channel_id=1, source_target_pairs={{0,128},{32,160},{64,192},{96,224},{128,0},{160,32},{192,64},{224,... | collective-permute-start | bytes 147464 | tf_op jit(solution)/shard_map/ppermute | solution.py:21
  17.6 9.8 %collective-permute-start.5 = (bf16[2,8,3072]{2,1,0:T(8,128)(2,1)S(1)}, bf16[2,8,3072]{2,1,0:T(8,128)(2,1)S(1)}, u32[]{:S(2)}, u32[]{:S(2)}) collective-permute-start(bf16[2,8,3072]{2,1,0:T(8,128)(2,1)S(1)} %pad_maximum_fusion.2), channel_id=1, source_target_pairs={{0,64},{32,96},{64,0},{96,32},{128,192},{160,224},{192,128},{224,1... | collective-permute-start | bytes 294920 | tf_op jit(solution)/shard_map/ppermute | solution.py:21
  20.9 73.3 %copy-start.1 = (f32[2,1,4,3072]{3,2,1,0:T(4,128)S(1)}, f32[2,1,4,3072]{3,2,1,0:T(4,128)}, u32[]{:S(2)}) copy-start(f32[2,1,4,3072]{3,2,1,0:T(4,128)} %param.5) | copy-start | bytes 294916
  20.9 19.0 %all-to-all-start = ((bf16[8,8,3072]{2,1,0:T(8,128)(2,1)}), bf16[8,8,3072]{2,1,0:T(8,128)(2,1)S(1)}, u32[]{:S(2)}, u32[]{:S(2)}) async-start(bf16[8,8,3072]{2,1,0:T(8,128)(2,1)} %fusion.1), calls=%async_computation | async-start | bytes 786432 | tf_op jit(solution)/shard_map/all_to_all | solution.py:104
  27.5 4.6 %collective-permute-start.6 = (bf16[4,8,3072]{2,1,0:T(8,128)(2,1)S(1)}, bf16[4,8,3072]{2,1,0:T(8,128)(2,1)S(1)}, u32[]{:S(2)}, u32[]{:S(2)}) collective-permute-start(bf16[4,8,3072]{2,1,0:T(8,128)(2,1)S(1)} %pad_maximum_fusion.refs_2_), channel_id=1, source_target_pairs={{0,16},{16,0},{1,17},{17,1},{2,18},{18,2},{3,19},{19,3},{4,20},{20... | collective-permute-start | bytes 589832 | tf_op jit(solution)/shard_map/ppermute | solution.py:21
  28.9 6.1 %collective-permute-start.7 = (bf16[4,8,3072]{2,1,0:T(8,128)(2,1)S(1)}, bf16[4,8,3072]{2,1,0:T(8,128)(2,1)S(1)}, u32[]{:S(2)}, u32[]{:S(2)}) collective-permute-start(bf16[4,8,3072]{2,1,0:T(8,128)(2,1)S(1)} %pad_maximum_fusion.refs_2_), channel_id=1, source_target_pairs={{0,8},{8,0},{1,9},{9,1},{2,10},{10,2},{3,11},{11,3},{4,12},{12,4},... | collective-permute-start | bytes 589832 | tf_op jit(solution)/shard_map/ppermute | solution.py:21
  32.1 4.0 %collective-permute-start.8 = (bf16[4,8,3072]{2,1,0:T(8,128)(2,1)S(1)}, bf16[4,8,3072]{2,1,0:T(8,128)(2,1)S(1)}, u32[]{:S(2)}, u32[]{:S(2)}) collective-permute-start(bf16[4,8,3072]{2,1,0:T(8,128)(2,1)S(1)} %collective-permute-done.6.refs_4_), channel_id=1, source_target_pairs={{0,8},{8,0},{1,9},{9,1},{2,10},{10,2},{3,11},{11,3},{4,12},{12,4},... | collective-permute-start | bytes 589832 | tf_op jit(solution)/shard_map/ppermute | solution.py:21
  41.2 4.1 %collective-permute-start.9 = (f32[1,128]{1,0:T(1,128)S(1)}, f32[1,128]{1,0:T(1,128)S(1)}, u32[]{:S(2)}, u32[]{:S(2)}) collective-permute-start(f32[1,128]{1,0:T(1,128)S(1)} %broadcast_in_dim.11), channel_id=1, source_target_pairs={{0,8},{8,0},{1,9},{9,1},{2,10},{10,2},{3,11},{11,3},{4,12},{12,4},... | collective-permute-start | bytes 1544 | tf_op jit(solution)/shard_map/ppermute | solution.py:21
  46.0 5.6 %collective-permute-start.11 = (f32[2,128]{1,0:T(2,128)S(1)}, f32[2,128]{1,0:T(2,128)S(1)}, u32[]{:S(2)}, u32[]{:S(2)}) collective-permute-start(f32[2,128]{1,0:T(2,128)S(1)} %concatenate.88), channel_id=1, source_target_pairs={{0,16},{1,17},{16,0},{17,1},{2,18},{3,19},{18,2},{19,3},{4,20},{5,... | collective-permute-start | bytes 3080 | tf_op jit(solution)/shard_map/ppermute | solution.py:21
  47.4 4.2 %collective-permute-start.12 = (f32[2,128]{1,0:T(2,128)S(1)}, f32[2,128]{1,0:T(2,128)S(1)}, u32[]{:S(2)}, u32[]{:S(2)}) collective-permute-start(f32[2,128]{1,0:T(2,128)S(1)} %concatenate.88), channel_id=1, source_target_pairs={{0,17},{1,16},{16,1},{17,0},{2,19},{3,18},{18,3},{19,2},{4,21},{5,... | collective-permute-start | bytes 3080 | tf_op jit(solution)/shard_map/ppermute | solution.py:21
  49.3 3.9 %collective-permute-start.10 = (f32[2,128]{1,0:T(2,128)S(1)}, f32[2,128]{1,0:T(2,128)S(1)}, u32[]{:S(2)}, u32[]{:S(2)}) collective-permute-start(f32[2,128]{1,0:T(2,128)S(1)} %concatenate.88), channel_id=1, source_target_pairs={{0,1},{1,0},{16,17},{17,16},{2,3},{3,2},{18,19},{19,18},{4,5},{5,4... | collective-permute-start | bytes 3080 | tf_op jit(solution)/shard_map/ppermute | solution.py:21
  50.1 7.1 %collective-permute-start.13 = (bf16[1,8,3072]{2,1,0:T(8,128)(2,1)S(1)}, bf16[1,8,3072]{2,1,0:T(8,128)(2,1)S(1)}, u32[]{:S(2)}, u32[]{:S(2)}) collective-permute-start(bf16[1,8,3072]{2,1,0:T(8,128)(2,1)S(1)} %fusion.7), channel_id=1, source_target_pairs={{0,128},{32,160},{64,192},{96,224},{128,0},{160,32},{192,64},{224,... | collective-permute-start | bytes 147464 | tf_op jit(solution)/shard_map/ppermute | solution.py:21
  50.4 7.9 %collective-permute-start.14 = (bf16[4,8,3072]{2,1,0:T(8,128)(2,1)S(1)}, bf16[4,8,3072]{2,1,0:T(8,128)(2,1)S(1)}, u32[]{:S(2)}, u32[]{:S(2)}) collective-permute-start(bf16[4,8,3072]{2,1,0:T(8,128)(2,1)S(1)} %pad_maximum_fusion.refs_2_), channel_id=1, source_target_pairs={{0,32},{32,0},{64,96},{96,64},{128,160},{160,128},{192,224},{224,1... | collective-permute-start | bytes 589832 | tf_op jit(solution)/shard_map/ppermute | solution.py:21
  58.3 4.7 %collective-permute-start.17 = (f32[2,128]{1,0:T(2,128)S(1)}, f32[2,128]{1,0:T(2,128)S(1)}, u32[]{:S(2)}, u32[]{:S(2)}) collective-permute-start(f32[2,128]{1,0:T(2,128)S(1)} %add_add_fusion.2), channel_id=1, source_target_pairs={{0,96},{32,64},{64,32},{96,0},{128,224},{160,192},{192,160},{224,1... | collective-permute-start | bytes 3080 | tf_op jit(solution)/shard_map/ppermute | solution.py:21
  60.2 3.3 %collective-permute-start.16 = (f32[2,128]{1,0:T(2,128)S(1)}, f32[2,128]{1,0:T(2,128)S(1)}, u32[]{:S(2)}, u32[]{:S(2)}) collective-permute-start(f32[2,128]{1,0:T(2,128)S(1)} %add_add_fusion.2), channel_id=1, source_target_pairs={{0,64},{32,96},{64,0},{96,32},{128,192},{160,224},{192,128},{224,1... | collective-permute-start | bytes 3080 | tf_op jit(solution)/shard_map/ppermute | solution.py:21
  60.3 3.2 %collective-permute-start.15 = (f32[2,128]{1,0:T(2,128)S(1)}, f32[2,128]{1,0:T(2,128)S(1)}, u32[]{:S(2)}, u32[]{:S(2)}) collective-permute-start(f32[2,128]{1,0:T(2,128)S(1)} %add_add_fusion.2), channel_id=1, source_target_pairs={{0,32},{32,0},{64,96},{96,64},{128,160},{160,128},{192,224},{224,1... | collective-permute-start | bytes 3080 | tf_op jit(solution)/shard_map/ppermute | solution.py:21
  61.9 5.2 %collective-permute-start.18 = (bf16[2,8,3072]{2,1,0:T(8,128)(2,1)S(1)}, bf16[2,8,3072]{2,1,0:T(8,128)(2,1)S(1)}, u32[]{:S(2)}, u32[]{:S(2)}) collective-permute-start(bf16[2,8,3072]{2,1,0:T(8,128)(2,1)S(1)} %pad_maximum_fusion.3), channel_id=1, source_target_pairs={{0,64},{32,96},{64,0},{96,32},{128,192},{160,224},{192,128},{224,1... | collective-permute-start | bytes 294920 | tf_op jit(solution)/shard_map/ppermute | solution.py:21
  62.7 4.5 %collective-permute-start.19 = (bf16[4,8,3072]{2,1,0:T(8,128)(2,1)S(1)}, bf16[4,8,3072]{2,1,0:T(8,128)(2,1)S(1)}, u32[]{:S(2)}, u32[]{:S(2)}) collective-permute-start(bf16[4,8,3072]{2,1,0:T(8,128)(2,1)S(1)} %collective-permute-done.14.refs_3_), channel_id=1, source_target_pairs={{0,16},{16,0},{1,17},{17,1},{2,18},{18,2},{3,19},{19,3},{4,20},{20... | collective-permute-start | bytes 589832 | tf_op jit(solution)/shard_map/ppermute | solution.py:21
  67.2 16.5 %collective-permute-start.22 = (bf16[4,8,3072]{2,1,0:T(8,128)(2,1)S(1)}, bf16[4,8,3072]{2,1,0:T(8,128)(2,1)S(1)}, u32[]{:S(2)}, u32[]{:S(2)}) collective-permute-start(bf16[4,8,3072]{2,1,0:T(8,128)(2,1)S(1)} %pad_maximum_fusion.1.refs_10_), channel_id=1, source_target_pairs={{0,16},{16,0},{1,17},{17,1},{2,18},{18,2},{3,19},{19,3},{4,20},{20... | collective-permute-start | bytes 589832 | tf_op jit(solution)/shard_map/ppermute | solution.py:21
  67.8 16.0 %collective-permute-start.21 = (bf16[4,8,3072]{2,1,0:T(8,128)(2,1)S(1)}, bf16[4,8,3072]{2,1,0:T(8,128)(2,1)}, u32[]{:S(2)}, u32[]{:S(2)}) collective-permute-start(bf16[4,8,3072]{2,1,0:T(8,128)(2,1)S(1)} %pad_maximum_fusion.1.refs_10_), channel_id=1, source_target_pairs={{0,32},{32,0},{64,96},{96,64},{128,160},{160,128},{192,224},{224,1... | collective-permute-start | bytes 589832 | tf_op jit(solution)/shard_map/ppermute | solution.py:21
  69.0 8.5 %collective-permute-start.20 = (f32[2,128]{1,0:T(2,128)S(1)}, f32[2,128]{1,0:T(2,128)S(1)}, u32[]{:S(2)}, u32[]{:S(2)}) collective-permute-start(f32[2,128]{1,0:T(2,128)S(1)} %add_add_fusion.1), channel_id=1, source_target_pairs={{0,128},{32,160},{64,192},{96,224},{128,0},{160,32},{192,64},{224,... | collective-permute-start | bytes 3080 | tf_op jit(solution)/shard_map/ppermute | solution.py:21
  72.2 10.2 %collective-permute-start.24 = (bf16[4,8,3072]{2,1,0:T(8,128)(2,1)S(1)}, bf16[4,8,3072]{2,1,0:T(8,128)(2,1)S(1)}, u32[]{:S(2)}, u32[]{:S(2)}) collective-permute-start(bf16[4,8,3072]{2,1,0:T(8,128)(2,1)S(1)} %collective-permute-done.14.refs_3_), channel_id=1, source_target_pairs={{0,8},{8,0},{1,9},{9,1},{2,10},{10,2},{3,11},{11,3},{4,12},{12,4},... | collective-permute-start | bytes 589832 | tf_op jit(solution)/shard_map/ppermute | solution.py:21
  77.5 5.6 %collective-permute-start.25 = (bf16[4,8,3072]{2,1,0:T(8,128)(2,1)S(1)}, bf16[4,8,3072]{2,1,0:T(8,128)(2,1)S(1)}, u32[]{:S(2)}, u32[]{:S(2)}) collective-permute-start(bf16[4,8,3072]{2,1,0:T(8,128)(2,1)S(1)} %collective-permute-done.19.refs_5_), channel_id=1, source_target_pairs={{0,8},{8,0},{1,9},{9,1},{2,10},{10,2},{3,11},{11,3},{4,12},{12,4},... | collective-permute-start | bytes 589832 | tf_op jit(solution)/shard_map/ppermute | solution.py:21
  77.5 4.9 %collective-permute-start.23 = (f32[4,3072]{1,0:T(4,128)S(1)}, f32[4,3072]{1,0:T(4,128)S(1)}, u32[]{:S(2)}, u32[]{:S(2)}) collective-permute-start(f32[4,3072]{1,0:T(4,128)S(1)} %get-tuple-element.72), channel_id=1, source_target_pairs={{0,8},{8,0},{1,9},{9,1},{2,10},{10,2},{3,11},{11,3},{4,12},{12,4},... | collective-permute-start | bytes 147464 | tf_op jit(solution)/shard_map/ppermute | solution.py:21
  82.4 0.7 copy-start.3
  83.1 0.7 copy-start.5
  83.8 8.8 %collective-permute-start.29 = (bf16[4,8,3072]{2,1,0:T(8,128)(2,1)}, bf16[4,8,3072]{2,1,0:T(8,128)(2,1)}, u32[]{:S(2)}, u32[]{:S(2)}) collective-permute-start(bf16[4,8,3072]{2,1,0:T(8,128)(2,1)} %collective-permute-done.21.refs_11_), channel_id=1, source_target_pairs={{0,16},{16,0},{1,17},{17,1},{2,18},{18,2},{3,19},{19,3},{4,20},{20... | collective-permute-start | bytes 589832 | tf_op jit(solution)/shard_map/ppermute | solution.py:21
  84.1 4.8 %collective-permute-start.28 = (f32[2,128]{1,0:T(2,128)S(1)}, f32[2,128]{1,0:T(2,128)S(1)}, u32[]{:S(2)}, u32[]{:S(2)}) collective-permute-start(f32[2,128]{1,0:T(2,128)S(1)} %add.73), channel_id=1, source_target_pairs={{0,6},{2,4},{4,2},{6,0},{1,7},{3,5},{5,3},{7,1},{8,14},{10,12},{12... | collective-permute-start | bytes 3080 | tf_op jit(solution)/shard_map/ppermute | solution.py:21
  86.6 3.9 %collective-permute-start.27 = (f32[2,128]{1,0:T(2,128)S(1)}, f32[2,128]{1,0:T(2,128)S(1)}, u32[]{:S(2)}, u32[]{:S(2)}) collective-permute-start(f32[2,128]{1,0:T(2,128)S(1)} %add.73), channel_id=1, source_target_pairs={{0,4},{2,6},{4,0},{6,2},{1,5},{3,7},{5,1},{7,3},{8,12},{10,14},{12... | collective-permute-start | bytes 3080 | tf_op jit(solution)/shard_map/ppermute | solution.py:21
  87.1 5.5 %collective-permute-start.26 = (f32[2,128]{1,0:T(2,128)S(1)}, f32[2,128]{1,0:T(2,128)S(1)}, u32[]{:S(2)}, u32[]{:S(2)}) collective-permute-start(f32[2,128]{1,0:T(2,128)S(1)} %add.73), channel_id=1, source_target_pairs={{0,2},{2,0},{4,6},{6,4},{1,3},{3,1},{5,7},{7,5},{8,10},{10,8},{12,... | collective-permute-start | bytes 3080 | tf_op jit(solution)/shard_map/ppermute | solution.py:21
  87.4 6.4 %collective-permute-start.31 = (bf16[4,8,3072]{2,1,0:T(8,128)(2,1)}, bf16[4,8,3072]{2,1,0:T(8,128)(2,1)S(1)}, u32[]{:S(2)}, u32[]{:S(2)}) collective-permute-start(bf16[4,8,3072]{2,1,0:T(8,128)(2,1)} %collective-permute-done.21.refs_11_), channel_id=1, source_target_pairs={{0,8},{8,0},{1,9},{9,1},{2,10},{10,2},{3,11},{11,3},{4,12},{12,4},... | collective-permute-start | bytes 589832 | tf_op jit(solution)/shard_map/ppermute | solution.py:21
  88.9 3.7 %collective-permute-start.30 = (bf16[4,8,3072]{2,1,0:T(8,128)(2,1)S(1)}, bf16[4,8,3072]{2,1,0:T(8,128)(2,1)S(1)}, u32[]{:S(2)}, u32[]{:S(2)}) collective-permute-start(bf16[4,8,3072]{2,1,0:T(8,128)(2,1)S(1)} %pad_maximum_fusion.1.refs_10_), channel_id=1, source_target_pairs={{0,8},{8,0},{1,9},{9,1},{2,10},{10,2},{3,11},{11,3},{4,12},{12,4},... | collective-permute-start | bytes 589832 | tf_op jit(solution)/shard_map/ppermute | solution.py:21
  90.5 3.3 %collective-permute-start.32 = (bf16[4,8,3072]{2,1,0:T(8,128)(2,1)S(1)}, bf16[4,8,3072]{2,1,0:T(8,128)(2,1)S(1)}, u32[]{:S(2)}, u32[]{:S(2)}) collective-permute-start(bf16[4,8,3072]{2,1,0:T(8,128)(2,1)S(1)} %collective-permute-done.22.refs_12_), channel_id=1, source_target_pairs={{0,8},{8,0},{1,9},{9,1},{2,10},{10,2},{3,11},{11,3},{4,12},{12,4},... | collective-permute-start | bytes 589832 | tf_op jit(solution)/shard_map/ppermute | solution.py:21
  92.5 1.7 %collective-permute-start.33 = (bf16[4,8,3072]{2,1,0:T(8,128)(2,1)}, bf16[4,8,3072]{2,1,0:T(8,128)(2,1)S(1)}, u32[]{:S(2)}, u32[]{:S(2)}) collective-permute-start(bf16[4,8,3072]{2,1,0:T(8,128)(2,1)} %collective-permute-done.29.refs_13_), channel_id=1, source_target_pairs={{0,8},{8,0},{1,9},{9,1},{2,10},{10,2},{3,11},{11,3},{4,12},{12,4},... | collective-permute-start | bytes 589832 | tf_op jit(solution)/shard_map/ppermute | solution.py:21
  94.2 0.9 copy-start.4
  95.1 0.9 copy-start.6

commit v5 on v1

v5 whole, which is shorter than its diff:
```python
import functools
import math

import jax
import jax.numpy as jnp
from jax import lax
from jax.experimental import pallas as pl
from jax.experimental.pallas import tpu as pltpu
from jax.sharding import Mesh
from jax.sharding import PartitionSpec as P

CHIPS = ("z", "yl")
EXCHANGES = (
    ("x", ((0, 1), (2, 3))),
    ("x", ((1, 2), (3, 0))),
    ("yl", ((0, 1),)),
    (("yl", "yh"), ((2, 1), (3, 0))),
    ("z", ((0, 1), (2, 3), (4, 5), (6, 7))),
    ("z", ((1, 2), (3, 4), (5, 6), (7, 0))),
    ("z", ((2, 5), (1, 6), (3, 0), (4, 7))),
)


def swap(axis, pairs, array):
    return lax.ppermute(array, axis, pairs + tuple(pair[::-1] for pair in pairs))


def over_core(array):
    return swap("core", ((0, 1),), array)


SPLIT = 2048


def total_kernel(
    replicas,
    total_ref,
    outer_ref,
    base_ref,
    pseudo_ref,
    sums_ref,
    packs_hbm,
    pack_ref,
    out_sems,
):
    width = outer_ref.shape[1]
    pseudo = outer_ref[...] - total_ref[...] / replicas
    pack_ref[:, :width] = (1.33 * pseudo).astype(jnp.bfloat16)
    pack_ref[:, width:] = base_ref[:, SPLIT:]
    copies = [
        pltpu.make_async_copy(pack_ref, packs_hbm.at[chip], out_sems.at[chip])
        for chip in range(packs_hbm.shape[0])
    ]
    for copy in copies:
        copy.start()
    pseudo_ref[...] = pseudo
    square_sum = jnp.sum(jnp.sum(pseudo * pseudo, axis=0, keepdims=True), keepdims=True)
    sums_ref[...] = jnp.broadcast_to(square_sum, sums_ref.shape)
    for copy in copies:
        copy.wait()


def last_kernel(
    max_norm,
    core_ref,
    weights_ref,
    outer_ref,
    moment_ref,
    sums_ref,
    sums2_ref,
    pseudo_ref,
    pseudo2_ref,
    packs_ref,
    packs2_ref,
    bases_hbm,
    mixed_hbm,
    new_outer_ref,
    new_moment_ref,
    bases_ref,
    mixed_ref,
    in_sems,
    out_sems,
):
    core = core_ref[0]
    chips, _, width = weights_ref.shape[1:]
    parts = out_sems.shape[0]
    step = chips // parts
    loads = []
    for part in range(parts):
        some = pl.ds(part * step, step)
        loads.append(
            pltpu.make_async_copy(
                bases_hbm.at[some], bases_ref.at[some], in_sems.at[part]
            )
        )
        loads[-1].start()
    sides = []
    for frag, square_sum_ref, rows_ref, pack_ref in (
        (core, sums_ref, pseudo_ref, packs_ref),
        (1 - core, sums2_ref, pseudo2_ref, packs2_ref),
    ):
        norms = jnp.sqrt(square_sum_ref[...])
        factor = jnp.minimum(1.0, max_norm / (norms + 1e-06))[:, :1]
        sides.append((frag, factor, pack_ref))
        clipped = factor * rows_ref[...]
        moment = 0.9 * moment_ref[frag] + clipped
        new_moment_ref[frag] = moment
        new_outer_ref[frag] = outer_ref[frag] - 0.7 * (clipped + 0.9 * moment)
    stores = []
    for part in range(parts):
        loads[part].wait()
        for at, (frag, factor, pack_ref) in enumerate(sides):
            for chip in range(part * step, part * step + step):
                for low, high, base in (
                    (0, SPLIT, bases_ref[chip, frag]),
                    (SPLIT, width, pack_ref[chip, :, width:]),
                ):
                    own = weights_ref[frag, chip, :, low:high].astype(jnp.float32)
                    push = pack_ref[chip, :, low:high].astype(jnp.float32)
                    source = base.astype(jnp.float32) - factor * push
                    source = source.astype(jnp.bfloat16).astype(jnp.float32)
                    mixed = 0.5 * (own + source)
                    mixed_ref[at, chip, :, low:high] = mixed.astype(jnp.bfloat16)
            some = pl.ds(part * step, step)
            stores.append(
                pltpu.make_async_copy(
                    mixed_ref.at[at, some],
                    mixed_hbm.at[frag, some],
                    out_sems.at[part, at],
                )
            )
            stores[-1].start()
    for store in stores:
        store.wait()


def shards(local_weights, global_params, momentum):
    f32, bf16 = jnp.float32, jnp.bfloat16
    core = lax.axis_index("core")
    other = 1 - core
    first = core == 0
    chips = lax.axis_size(CHIPS)
    replicas = 2 * chips
    everywhere = chips * lax.axis_size(("x", "yh"))
    rows, width = local_weights.shape[3], local_weights.shape[4]
    share_rows = global_params.shape[2]
    block = rows // chips
    max_norm = 0.5 * math.sqrt(block * width * everywhere)

    def pick(array, index, axis=0):
        return lax.dynamic_index_in_dim(array, index, axis, keepdims=False)

    def swapped_rows(array):
        kept = pick(array, core)
        came = over_core(pick(array, other))
        return jnp.where(
            first,
            jnp.concatenate((kept, came), axis=0),
            jnp.concatenate((came, kept), axis=0),
        )

    weights = local_weights[:, 0, 0]
    outer = swapped_rows(global_params[:, 0])
    moment = swapped_rows(momentum[:, 0])
    base = (outer - 0.567 * moment).astype(bf16)
    got = over_core(pick(weights, other))
    in_vmem = pl.BlockSpec(memory_space=pltpu.VMEM)
    in_hbm = pl.BlockSpec(memory_space=pl.ANY)
    in_smem = pl.BlockSpec(memory_space=pltpu.SMEM)
    pair = (pick(weights, core).astype(f32) + got.astype(f32)).astype(bf16)
    pair, base = lax.optimization_barrier((pair, base))
    bases = lax.all_gather(
        base[:, :SPLIT], ("z", "yl", "core"), axis=0, tiled=False
    )
    pieces = lax.all_to_all(
        pair.reshape(chips, block, width), CHIPS, 0, 0, tiled=True
    )
    extended = 2 * width - SPLIT
    pseudo, sums, pack = pl.pallas_call(
        functools.partial(total_kernel, replicas),
        out_shape=(
            pltpu.VMEM((block, width), f32),
            pltpu.VMEM((1, 128), f32),
            jax.ShapeDtypeStruct((chips, block, extended), bf16),
        ),
        in_specs=[in_vmem] * 3,
        out_specs=(in_vmem, in_vmem, in_hbm),
        scratch_shapes=[
            pltpu.VMEM((block, extended), bf16),
            pltpu.SemaphoreType.DMA((chips,)),
        ],
        name="total",
    )(jnp.sum(pieces.astype(f32), axis=0), outer, base)
    packs = lax.all_to_all(pack, CHIPS, 0, 0, tiled=True)
    halves = pseudo.reshape(2, share_rows, width)
    pseudo2 = over_core(pick(halves, other))
    for step, (axis, pairs) in enumerate(EXCHANGES):
        if step == 5:
            sums, bases = lax.optimization_barrier((sums, bases))
        if step == 6:
            sums, packs = lax.optimization_barrier((sums, packs))
        sums = sums + swap(axis, pairs, sums)
    packs2 = over_core(packs)
    sums2 = over_core(sums)

    state = jax.ShapeDtypeStruct((2, share_rows, width), f32)
    mixed, outer_next, moment_next = pl.pallas_call(
        functools.partial(last_kernel, max_norm),
        out_shape=(
            jax.ShapeDtypeStruct((2, chips, block, width), bf16),
            state,
            state,
        ),
        in_specs=[in_smem] + [in_vmem] * 9 + [in_hbm],
        out_specs=(in_hbm, in_vmem, in_vmem),
        scratch_shapes=[
            pltpu.VMEM((chips, 2, block, SPLIT), bf16),
            pltpu.VMEM((2, chips, block, width), bf16),
            pltpu.SemaphoreType.DMA((4,)),
            pltpu.SemaphoreType.DMA((4, 2)),
        ],
        compiler_params=pltpu.CompilerParams(vmem_limit_bytes=16 * 1024 * 1024),
        name="last",
    )(
        core[None],
        weights.reshape(2, chips, block, width),
        global_params[:, 0],
        momentum[:, 0],
        sums,
        sums2,
        pick(halves, core),
        pseudo2,
        packs,
        packs2,
        pltpu.with_memory_space_constraint(
            bases.reshape(chips, 2, block, SPLIT), pltpu.HBM
        ),
    )
    return (
        mixed.reshape(local_weights.shape),
        outer_next[:, None],
        moment_next[:, None],
    )


def solution(mesh):
    fine = Mesh(
        mesh.devices.reshape(8, 2, 2, 4, 2), ("z", "yl", "core", "x", "yh")
    )
    replica, mp = ("z", "yl", "core"), ("x", "yh")
    whole = P(None, replica, mp, None, None)
    outer = P(None, mp, replica, None)
    return jax.shard_map(
        shards,
        mesh=fine,
        in_specs=(whole, outer, outer),
        out_specs=(whole, outer, outer),
        check_vma=False,
    )
```

time: 94.6 us -> 123 us (1.30)
  waiting for transfers between devices: 40.2 us -> 64 us
  blocking collectives: 22.2 us -> 0 us
  between operations: 1.52 us -> 14.1 us
  starting transfers between devices: 22 us -> 32.4 us
  Pallas kernels: 0 us -> 6.71 us
  other arithmetic: 4.53 us -> 2.56 us
    all_to_all x1 -> x0, blocking collectives: 22.2 us -> none  [shards(): lax.all_to_all(jnp.broadcast_to(part, (everywhere, 1, 128)), ('z', 'yl',...]
    all_gather x0 -> x1, waiting for transfers between devices: none -> 20.5 us  [shards(): lax.all_gather(base[:, :SPLIT], ('z', 'yl', 'core'), axis=0, tiled=False)]
    ppermute x4 -> x13, waiting for transfers between devices: 4.03 us -> 23.4 us  [swap(): lax.ppermute(array, axis, pairs + tuple((pair[::-1] for pair in pairs)))]
    all_to_all x1, waiting for transfers between devices: 17.2 us -> 0.01 us  [shards(): packs = lax.all_to_all(pack, CHIPS, 0, 0, tiled=True)]
    ppermute x4 -> x13, starting transfers between devices: 10.9 us -> 19.2 us  [swap(): lax.ppermute(array, axis, pairs + tuple((pair[::-1] for pair in pairs)))]
    pallas_call x0 -> x2, Pallas kernels: none -> 6.71 us  [the longest x1 4.62 us: shards(): pl.pallas_call(functools.partial(last_kernel, max_norm), out_shape=(jax.S...]
    all_to_all x1, starting transfers between devices: 3.61 us -> 5.59 us  [shards(): packs = lax.all_to_all(pack, CHIPS, 0, 0, tiled=True)]
    broadcast_in_dim x2 -> x0, local copies, waits for them, and re-layouts: 1.64 us -> none  [the longest x1 0.96 us: shards(): jnp.broadcast_to(source, (chips, block, width))]
  transfers between devices with their start and end apart: 6 -> 16, of which waited for: 5 -> 12; matrix products, arithmetic and copies ran while one was open for 1% -> 2% of each run, Pallas kernels for 0% -> 2%
where the time goes in v5:
time: 123 us
  waiting for transfers between devices  64 us (52%)
  starting transfers between devices  32.4 us (26%)
  between operations  14.1 us (11%)
  Pallas kernels  6.71 us (5%)
  local copies, waits for them, and re-layouts  2.85 us (2%)
  other arithmetic  2.56 us (2%)
    ppermute x13, waiting for transfers between devices, swap(): lax.ppermute(array, axis, pairs + tuple((pair[::-1] for pair in pairs)))  23.4 us
    all_gather x1, waiting for transfers between devices, shards(): lax.all_gather(base[:, :SPLIT], ('z', 'yl', 'core'), axis=0, tiled=False)  20.5 us
    all_to_all x1, waiting for transfers between devices, shards(): lax.all_to_all(pair.reshape(chips, block, width), CHIPS, 0, 0, tiled=True)  20.1 us
    ppermute x13, starting transfers between devices, swap(): lax.ppermute(array, axis, pairs + tuple((pair[::-1] for pair in pairs)))  19.2 us
    all_to_all x1, starting transfers between devices, shards(): lax.all_to_all(pair.reshape(chips, block, width), CHIPS, 0, 0, tiled=True)  7.57 us
    all_to_all x1, starting transfers between devices, shards(): packs = lax.all_to_all(pack, CHIPS, 0, 0, tiled=True)  5.59 us
    pallas_call x1, Pallas kernels, shards(): pl.pallas_call(functools.partial(last_kernel, max_norm), out_shape=(jax.S...  4.62 us
  transfers between devices with their start and end apart: 16, of which 12 were waited for; matrix products, arithmetic and copies ran while one was open for 2% of the time, Pallas kernels for 2%

profile of v5, /device:TPU:1, one launch (start us, length us, event | category | flops | bytes accessed | tf_op | source)
XLA Modules:
  0.0 122.6 jit_solution(13071678404072982451)
XLA Ops:
  7.2 0.0 copy-start
  7.2 0.0 copy-start.2
  7.2 1.3 %dynamic-slice_bitcast_fusion = bf16[128,3072]{1,0:T(8,128)(2,1)S(1)} fusion(bf16[2,1,1,128,3072]{4,3,2,1,0:T(8,128)(2,1)} %param.3, s32[]{:T(128)S(6)} %select_n.27), kind=kLoop, calls=%fused_computation.3 | loop fusion | bytes 1572868 | tf_op jit(solution)/shard_map/jit(dynamic_index_in_dim)/squeeze | solution.py:151
  8.5 3.3 %collective-permute-start = (bf16[128,3072]{1,0:T(8,128)(2,1)S(1)}, bf16[128,3072]{1,0:T(8,128)(2,1)S(1)}, u32[]{:S(2)}, u32[]{:S(2)}) collective-permute-start(bf16[128,3072]{1,0:T(8,128)(2,1)S(1)} %dynamic-slice_bitcast_fusion), channel_id=1, source_target_pairs={{0,8},{8,0},{1,9},{9,1},{2,10},{10,2},{3,11},{11,3},{4,12},{12,4},... | collective-permute-start | bytes 2359304 | tf_op jit(solution)/shard_map/ppermute | solution.py:25
  11.9 0.8 dynamic-slice_bitcast_fusion.5
  12.7 0.1 collective-permute-start.1
  12.8 0.0 copy-done.2
  12.8 0.6 collective-permute-start.2
  13.4 0.6 collective-permute-done.1
  14.0 0.3 collective-permute-done.2
  14.3 0.7 maximum_select_fusion
  15.0 0.0 copy-start.3
  15.0 0.0 collective-permute-done
  15.0 0.0 copy-done
  15.0 1.1 fusion
  16.1 7.6 %all-to-all-start = ((bf16[16,8,3072]{2,1,0:T(8,128)(2,1)}), bf16[16,8,3072]{2,1,0:T(8,128)(2,1)S(1)}, u32[]{:S(2)}, u32[]{:S(2)}) async-start(bf16[16,8,3072]{2,1,0:T(8,128)(2,1)} %bitcast.10), calls=%async_computation | async-start | bytes 1572864 | tf_op jit(solution)/shard_map/all_to_all | solution.py:175
  23.6 0.0 all-gather.3.cloned.1.call-start
  23.7 0.0 copy-done.3
  23.7 0.6 slice.3
  24.3 0.1 all-gather.3.cloned.1.call-update
  24.4 20.1 %all-to-all-done = bf16[16,8,3072]{2,1,0:T(8,128)(2,1)S(1)} async-done(((bf16[16,8,3072]{2,1,0:T(8,128)(2,1)}), bf16[16,8,3072]{2,1,0:T(8,128)(2,1)S(1)}, u32[]{:S(2)}, u32[]{:S(2)}) %all-to-all-start) | async-done | bytes 786464 | tf_op jit(solution)/shard_map/all_to_all | solution.py:175
  44.4 0.7 convert_reduce_fusion.total_ref
  45.2 2.1 %total.1 = (f32[8,3072]{1,0:T(8,128)S(1)}, f32[1,128]{1,0:T(1,128)S(1)}, bf16[16,8,4096]{2,1,0:T(8,128)(2,1)}) custom-call(f32[8,3072]{1,0:T(8,128)} %convert_reduce_fusion.total_ref, f32[8,3072]{1,0:T(8,128)} %get-tuple-element.32.outer_ref, bf16[8,3072]{1,0:T(8,128)(2,1)} %copy-done.3), custom_call_target="tpu_custom_call" | custom-call | tf_op jit(solution)/shard_map/total/pallas_call | solution.py:179
  47.3 5.6 %all-to-all-start.1 = ((bf16[16,8,4096]{2,1,0:T(8,128)(2,1)}), bf16[16,8,4096]{2,1,0:T(8,128)(2,1)S(1)}, u32[]{:S(2)}, u32[]{:S(2)}) async-start(bf16[16,8,4096]{2,1,0:T(8,128)(2,1)} %get-tuple-element.19), calls=%async_computation.1 | async-start | bytes 2097152 | tf_op jit(solution)/shard_map/all_to_all | solution.py:194
  52.9 1.3 %collective-permute-start.3 = (f32[1,128]{1,0:T(1,128)S(1)}, f32[1,128]{1,0:T(1,128)S(1)}, u32[]{:S(2)}, u32[]{:S(2)}) collective-permute-start(f32[1,128]{1,0:T(1,128)S(1)} %get-tuple-element.17), channel_id=1, source_target_pairs={{0,2},{4,6},{2,0},{6,4},{1,3},{5,7},{3,1},{7,5},{8,10},{12,14},{10... | collective-permute-start | bytes 1544 | tf_op jit(solution)/shard_map/ppermute | solution.py:25
  54.2 1.2 collective-permute-done.3
  55.4 2.5 %collective-permute-start.4 = (f32[1,128]{1,0:T(1,128)S(1)}, f32[1,128]{1,0:T(1,128)S(1)}, u32[]{:S(2)}, u32[]{:S(2)}) collective-permute-start(f32[1,128]{1,0:T(1,128)S(1)} %add.42), channel_id=1, source_target_pairs={{2,4},{6,0},{4,2},{0,6},{3,5},{7,1},{5,3},{1,7},{10,12},{14,8},{12... | collective-permute-start | bytes 1544 | tf_op jit(solution)/shard_map/ppermute | solution.py:25
  57.9 1.1 collective-permute-done.4
  59.0 1.5 %collective-permute-start.5 = (f32[1,128]{1,0:T(1,128)S(1)}, f32[1,128]{1,0:T(1,128)S(1)}, u32[]{:S(2)}, u32[]{:S(2)}) collective-permute-start(f32[1,128]{1,0:T(1,128)S(1)} %add.43), channel_id=1, source_target_pairs={{0,16},{16,0},{1,17},{17,1},{2,18},{18,2},{3,19},{19,3},{4,20},{20... | collective-permute-start | bytes 1544 | tf_op jit(solution)/shard_map/ppermute | solution.py:25
  60.5 1.2 collective-permute-done.5
  61.7 2.8 %collective-permute-start.6 = (f32[1,128]{1,0:T(1,128)S(1)}, f32[1,128]{1,0:T(1,128)S(1)}, u32[]{:S(2)}, u32[]{:S(2)}) collective-permute-start(f32[1,128]{1,0:T(1,128)S(1)} %add.44), channel_id=1, source_target_pairs={{16,1},{17,0},{1,16},{0,17},{18,3},{19,2},{3,18},{2,19},{20,5},{21... | collective-permute-start | bytes 1544 | tf_op jit(solution)/shard_map/ppermute | solution.py:25
  64.5 1.2 collective-permute-done.6
  65.7 1.7 %collective-permute-start.7 = (f32[1,128]{1,0:T(1,128)S(1)}, f32[1,128]{1,0:T(1,128)S(1)}, u32[]{:S(2)}, u32[]{:S(2)}) collective-permute-start(f32[1,128]{1,0:T(1,128)S(1)} %add.45), channel_id=1, source_target_pairs={{0,32},{64,96},{128,160},{192,224},{32,0},{96,64},{160,128},{224,1... | collective-permute-start | bytes 1544 | tf_op jit(solution)/shard_map/ppermute | solution.py:25
  67.4 11.4 %collective-permute-done.7 = f32[1,128]{1,0:T(1,128)S(1)} collective-permute-done((f32[1,128]{1,0:T(1,128)S(1)}, f32[1,128]{1,0:T(1,128)S(1)}, u32[]{:S(2)}, u32[]{:S(2)}) %collective-permute-start.7) | collective-permute-done | bytes 544 | tf_op jit(solution)/shard_map/ppermute | solution.py:25
  78.8 20.5 %all-gather.3.cloned.1.call-done = bf16[256,2048]{1,0:T(8,128)(2,1)} async-done(((bf16[8,2048]{1,0:T(8,128)(2,1)}), bf16[256,2048]{1,0:T(8,128)(2,1)}) %all-gather.3.cloned.1.call-update) | async-done | bytes 1048592 | tf_op jit(solution)/shard_map/all_gather | solution.py:172
  99.3 1.3 %collective-permute-start.8 = (f32[1,128]{1,0:T(1,128)S(1)}, f32[1,128]{1,0:T(1,128)S(1)}, u32[]{:S(2)}, u32[]{:S(2)}) collective-permute-start(f32[1,128]{1,0:T(1,128)S(1)} %add.46), channel_id=1, source_target_pairs={{32,64},{96,128},{160,192},{224,0},{64,32},{128,96},{192,160},{0,2... | collective-permute-start | bytes 1544 | tf_op jit(solution)/shard_map/ppermute | solution.py:25
  100.6 2.3 %collective-permute-done.8 = f32[1,128]{1,0:T(1,128)S(1)} collective-permute-done((f32[1,128]{1,0:T(1,128)S(1)}, f32[1,128]{1,0:T(1,128)S(1)}, u32[]{:S(2)}, u32[]{:S(2)}) %collective-permute-start.8) | collective-permute-done | bytes 544 | tf_op jit(solution)/shard_map/ppermute | solution.py:25
  102.9 0.0 all-to-all-done.1.packs_ref
  102.9 1.4 %collective-permute-start.12 = (bf16[16,8,4096]{2,1,0:T(8,128)(2,1)S(1)}, bf16[16,8,4096]{2,1,0:T(8,128)(2,1)}, u32[]{:S(2)}, u32[]{:S(2)}) collective-permute-start(bf16[16,8,4096]{2,1,0:T(8,128)(2,1)S(1)} %all-to-all-done.1.packs_ref), channel_id=1, source_target_pairs={{0,8},{8,0},{1,9},{9,1},{2,10},{10,2},{3,11},{11,3},{4,12},{12,4},... | collective-permute-start | bytes 3145736 | tf_op jit(solution)/shard_map/ppermute | solution.py:25
  104.4 0.1 collective-permute-start.11
  104.5 1.1 collective-permute-start.9
  105.6 3.1 %collective-permute-done.9 = f32[1,128]{1,0:T(1,128)S(1)} collective-permute-done((f32[1,128]{1,0:T(1,128)S(1)}, f32[1,128]{1,0:T(1,128)S(1)}, u32[]{:S(2)}, u32[]{:S(2)}) %collective-permute-start.9) | collective-permute-done | bytes 544 | tf_op jit(solution)/shard_map/ppermute | solution.py:25
  108.8 1.6 %collective-permute-start.10 = (f32[1,128]{1,0:T(1,128)S(1)}, f32[1,128]{1,0:T(1,128)S(1)}, u32[]{:S(2)}, u32[]{:S(2)}) collective-permute-start(f32[1,128]{1,0:T(1,128)S(1)} %add.48.sums_ref), channel_id=1, source_target_pairs={{0,8},{8,0},{1,9},{9,1},{2,10},{10,2},{3,11},{11,3},{4,12},{12,4},... | collective-permute-start | bytes 1544 | tf_op jit(solution)/shard_map/ppermute | solution.py:25
  110.3 0.0 collective-permute-done.11.pseudo2_ref
  110.3 0.8 collective-permute-done.10.sums2_ref
  111.2 0.0 collective-permute-done.12.packs2_ref
  111.2 0.0 copy-done.1
  111.2 4.6 %last.1 = (bf16[2,16,8,3072]{3,2,1,0:T(8,128)(2,1)}, f32[2,4,3072]{2,1,0:T(4,128)}, f32[2,4,3072]{2,1,0:T(4,128)}) custom-call(s32[1]{0:T(128)} %bitcast.core_ref, bf16[2,16,8,3072]{3,2,1,0:T(8,128)(2,1)S(1)} %bitcast.33, f32[2,4,3072]{2,1,0:T(4,128)S(1)} %bitcast.34, f32[2,4,3072]{2,1,0:T(4,128)S(1)} %bitcast.35, f32[1,128]{1,0:T(1,128)S(1)} %add.48.sums_ref, ...), custom_call_target="tpu_custom_call" | custom-call | tf_op jit(solution)/shard_map/last/pallas_call | solution.py:207
  (11 shorter events, 0.1 us)
Async XLA Ops:
  7.2 7.8 %copy-start = (bf16[2,1,1,128,3072]{4,3,2,1,0:T(8,128)(2,1)S(1)}, bf16[2,1,1,128,3072]{4,3,2,1,0:T(8,128)(2,1)}, u32[]{:S(2)}) copy-start(bf16[2,1,1,128,3072]{4,3,2,1,0:T(8,128)(2,1)} %param.3) | copy-start | bytes 4718596
  7.2 5.6 %copy-start.2 = (f32[2,1,4,3072]{3,2,1,0:T(4,128)S(1)}, f32[2,1,4,3072]{3,2,1,0:T(4,128)}, u32[]{:S(2)}) copy-start(f32[2,1,4,3072]{3,2,1,0:T(4,128)} %param.5) | copy-start | bytes 294916
  8.5 6.5 %collective-permute-start = (bf16[128,3072]{1,0:T(8,128)(2,1)S(1)}, bf16[128,3072]{1,0:T(8,128)(2,1)S(1)}, u32[]{:S(2)}, u32[]{:S(2)}) collective-permute-start(bf16[128,3072]{1,0:T(8,128)(2,1)S(1)} %dynamic-slice_bitcast_fusion), channel_id=1, source_target_pairs={{0,8},{8,0},{1,9},{9,1},{2,10},{10,2},{3,11},{11,3},{4,12},{12,4},... | collective-permute-start | bytes 2359304 | tf_op jit(solution)/shard_map/ppermute | solution.py:25
  12.7 1.3 %collective-permute-start.1 = (f32[4,3072]{1,0:T(4,128)S(1)}, f32[4,3072]{1,0:T(4,128)S(1)}, u32[]{:S(2)}, u32[]{:S(2)}) collective-permute-start(f32[4,3072]{1,0:T(4,128)S(1)} %get-tuple-element.34), channel_id=1, source_target_pairs={{0,8},{8,0},{1,9},{9,1},{2,10},{10,2},{3,11},{11,3},{4,12},{12,4},... | collective-permute-start | bytes 147464 | tf_op jit(solution)/shard_map/ppermute | solution.py:25
  12.8 1.4 %collective-permute-start.2 = (f32[4,3072]{1,0:T(4,128)S(1)}, f32[4,3072]{1,0:T(4,128)S(1)}, u32[]{:S(2)}, u32[]{:S(2)}) collective-permute-start(f32[4,3072]{1,0:T(4,128)S(1)} %get-tuple-element.37), channel_id=1, source_target_pairs={{0,8},{8,0},{1,9},{9,1},{2,10},{10,2},{3,11},{11,3},{4,12},{12,4},... | collective-permute-start | bytes 147464 | tf_op jit(solution)/shard_map/ppermute | solution.py:25
  15.0 8.7 %copy-start.3 = (bf16[8,3072]{1,0:T(8,128)(2,1)}, bf16[8,3072]{1,0:T(8,128)(2,1)S(1)}, u32[]{:S(2)}) copy-start(bf16[8,3072]{1,0:T(8,128)(2,1)S(1)} %get-tuple-element.16.base_ref) | copy-start | bytes 147460
  16.1 28.4 %all-to-all-start = ((bf16[16,8,3072]{2,1,0:T(8,128)(2,1)}), bf16[16,8,3072]{2,1,0:T(8,128)(2,1)S(1)}, u32[]{:S(2)}, u32[]{:S(2)}) async-start(bf16[16,8,3072]{2,1,0:T(8,128)(2,1)} %bitcast.10), calls=%async_computation | async-start | bytes 1572864 | tf_op jit(solution)/shard_map/all_to_all | solution.py:175
  23.6 75.7 %all-gather.3.cloned.1.call-start = ((), (), s32[]{:S(2)}) async-start(), calls=%async_computation.2 | async-start | bytes 1081344 | tf_op jit(solution)/shard_map/all_gather | solution.py:172
  45.2 66.0 %copy-start.1 = (f32[2,1,4,3072]{3,2,1,0:T(4,128)S(1)}, f32[2,1,4,3072]{3,2,1,0:T(4,128)}, u32[]{:S(2)}) copy-start(f32[2,1,4,3072]{3,2,1,0:T(4,128)} %param.4) | copy-start | bytes 294916
  47.3 55.6 %all-to-all-start.1 = ((bf16[16,8,4096]{2,1,0:T(8,128)(2,1)}), bf16[16,8,4096]{2,1,0:T(8,128)(2,1)S(1)}, u32[]{:S(2)}, u32[]{:S(2)}) async-start(bf16[16,8,4096]{2,1,0:T(8,128)(2,1)} %get-tuple-element.19), calls=%async_computation.1 | async-start | bytes 2097152 | tf_op jit(solution)/shard_map/all_to_all | solution.py:194
  52.9 2.5 %collective-permute-start.3 = (f32[1,128]{1,0:T(1,128)S(1)}, f32[1,128]{1,0:T(1,128)S(1)}, u32[]{:S(2)}, u32[]{:S(2)}) collective-permute-start(f32[1,128]{1,0:T(1,128)S(1)} %get-tuple-element.17), channel_id=1, source_target_pairs={{0,2},{4,6},{2,0},{6,4},{1,3},{5,7},{3,1},{7,5},{8,10},{12,14},{10... | collective-permute-start | bytes 1544 | tf_op jit(solution)/shard_map/ppermute | solution.py:25
  55.4 3.6 %collective-permute-start.4 = (f32[1,128]{1,0:T(1,128)S(1)}, f32[1,128]{1,0:T(1,128)S(1)}, u32[]{:S(2)}, u32[]{:S(2)}) collective-permute-start(f32[1,128]{1,0:T(1,128)S(1)} %add.42), channel_id=1, source_target_pairs={{2,4},{6,0},{4,2},{0,6},{3,5},{7,1},{5,3},{1,7},{10,12},{14,8},{12... | collective-permute-start | bytes 1544 | tf_op jit(solution)/shard_map/ppermute | solution.py:25
  59.0 2.7 %collective-permute-start.5 = (f32[1,128]{1,0:T(1,128)S(1)}, f32[1,128]{1,0:T(1,128)S(1)}, u32[]{:S(2)}, u32[]{:S(2)}) collective-permute-start(f32[1,128]{1,0:T(1,128)S(1)} %add.43), channel_id=1, source_target_pairs={{0,16},{16,0},{1,17},{17,1},{2,18},{18,2},{3,19},{19,3},{4,20},{20... | collective-permute-start | bytes 1544 | tf_op jit(solution)/shard_map/ppermute | solution.py:25
  61.7 4.0 %collective-permute-start.6 = (f32[1,128]{1,0:T(1,128)S(1)}, f32[1,128]{1,0:T(1,128)S(1)}, u32[]{:S(2)}, u32[]{:S(2)}) collective-permute-start(f32[1,128]{1,0:T(1,128)S(1)} %add.44), channel_id=1, source_target_pairs={{16,1},{17,0},{1,16},{0,17},{18,3},{19,2},{3,18},{2,19},{20,5},{21... | collective-permute-start | bytes 1544 | tf_op jit(solution)/shard_map/ppermute | solution.py:25
  65.7 13.1 %collective-permute-start.7 = (f32[1,128]{1,0:T(1,128)S(1)}, f32[1,128]{1,0:T(1,128)S(1)}, u32[]{:S(2)}, u32[]{:S(2)}) collective-permute-start(f32[1,128]{1,0:T(1,128)S(1)} %add.45), channel_id=1, source_target_pairs={{0,32},{64,96},{128,160},{192,224},{32,0},{96,64},{160,128},{224,1... | collective-permute-start | bytes 1544 | tf_op jit(solution)/shard_map/ppermute | solution.py:25
  99.3 3.6 %collective-permute-start.8 = (f32[1,128]{1,0:T(1,128)S(1)}, f32[1,128]{1,0:T(1,128)S(1)}, u32[]{:S(2)}, u32[]{:S(2)}) collective-permute-start(f32[1,128]{1,0:T(1,128)S(1)} %add.46), channel_id=1, source_target_pairs={{32,64},{96,128},{160,192},{224,0},{64,32},{128,96},{192,160},{0,2... | collective-permute-start | bytes 1544 | tf_op jit(solution)/shard_map/ppermute | solution.py:25
  102.9 8.2 %collective-permute-start.12 = (bf16[16,8,4096]{2,1,0:T(8,128)(2,1)S(1)}, bf16[16,8,4096]{2,1,0:T(8,128)(2,1)}, u32[]{:S(2)}, u32[]{:S(2)}) collective-permute-start(bf16[16,8,4096]{2,1,0:T(8,128)(2,1)S(1)} %all-to-all-done.1.packs_ref), channel_id=1, source_target_pairs={{0,8},{8,0},{1,9},{9,1},{2,10},{10,2},{3,11},{11,3},{4,12},{12,4},... | collective-permute-start | bytes 3145736 | tf_op jit(solution)/shard_map/ppermute | solution.py:25
  104.4 5.9 %collective-permute-start.11 = (f32[4,3072]{1,0:T(4,128)S(1)}, f32[4,3072]{1,0:T(4,128)S(1)}, u32[]{:S(2)}, u32[]{:S(2)}) collective-permute-start(f32[4,3072]{1,0:T(4,128)S(1)} %get-tuple-element.30), channel_id=1, source_target_pairs={{0,8},{8,0},{1,9},{9,1},{2,10},{10,2},{3,11},{11,3},{4,12},{12,4},... | collective-permute-start | bytes 147464 | tf_op jit(solution)/shard_map/ppermute | solution.py:25
  104.5 4.3 %collective-permute-start.9 = (f32[1,128]{1,0:T(1,128)S(1)}, f32[1,128]{1,0:T(1,128)S(1)}, u32[]{:S(2)}, u32[]{:S(2)}) collective-permute-start(f32[1,128]{1,0:T(1,128)S(1)} %add.47), channel_id=1, source_target_pairs={{64,160},{32,192},{96,0},{128,224},{160,64},{192,32},{0,96},{224,1... | collective-permute-start | bytes 1544 | tf_op jit(solution)/shard_map/ppermute | solution.py:25
  108.8 2.4 %collective-permute-start.10 = (f32[1,128]{1,0:T(1,128)S(1)}, f32[1,128]{1,0:T(1,128)S(1)}, u32[]{:S(2)}, u32[]{:S(2)}) collective-permute-start(f32[1,128]{1,0:T(1,128)S(1)} %add.48.sums_ref), channel_id=1, source_target_pairs={{0,8},{8,0},{1,9},{9,1},{2,10},{10,2},{3,11},{11,3},{4,12},{12,4},... | collective-permute-start | bytes 1544 | tf_op jit(solution)/shard_map/ppermute | solution.py:25
Sparse Core Ops, SparseCore 0:
  26.3 72.9 all-gather.2

commit v6 on v1

v6 whole, which is shorter than its diff:
```python
import functools
import math

import jax
import jax.numpy as jnp
from jax import lax
from jax.experimental import pallas as pl
from jax.experimental.pallas import tpu as pltpu
from jax.sharding import Mesh
from jax.sharding import PartitionSpec as P

CHIPS = ("z", "yl")
EVERYWHERE = ("z", "yl", "x", "yh")
NEAR, NEXT = (0, 4, 2, 6), (1, 5, 3, 7)
LINES = 1
ANY = pl.BlockSpec(memory_space=pl.ANY)
SMEM = pl.BlockSpec(memory_space=pltpu.SMEM)
SMALL = pltpu.CompilerParams(vmem_limit_bytes=12 * 1024 * 1024)
VMEM = pl.BlockSpec(memory_space=pltpu.VMEM)


def over(axis, size, jump, array):
    return lax.ppermute(array, axis, [(i, i ^ jump) for i in range(size)])


def over_core(array):
    return over("core", 2, 1, array)


def over_y(array):
    return over("yl", 2, 1, array)


def over_z(array, jump):
    return over("z", 8, jump, array)


def total_kernel(
    replicas, total_ref, outer_ref, moment_ref, pseudo_ref, pack_ref, sums_hbm, sums_ref, sem
):
    outer = outer_ref[...]
    pseudo = outer - total_ref[...] / replicas
    square_sum = jnp.sum(jnp.sum(pseudo * pseudo, axis=0, keepdims=True), keepdims=True)
    sums_ref[...] = jnp.broadcast_to(square_sum[None], sums_ref.shape)
    copy = pltpu.make_async_copy(sums_ref, sums_hbm, sem)
    copy.start()
    pseudo_ref[...] = pseudo
    pack_ref[0] = (outer - 0.567 * moment_ref[...]).astype(jnp.bfloat16)
    pack_ref[1] = (1.33 * pseudo).astype(jnp.bfloat16)
    copy.wait()


def source_kernel(max_norm, sums_ref, *refs):
    source_ref, factor_ref = refs[-2:]
    square_sum = jnp.sum(sums_ref[:, 0, :], axis=0, keepdims=True)
    factor = jnp.minimum(1.0, max_norm / (jnp.sqrt(square_sum) + 1e-06))
    factor_ref[...] = factor
    for place, pack_ref in enumerate(refs[:-2]):
        base = pack_ref[0].astype(jnp.float32)
        push = pack_ref[1].astype(jnp.float32)
        source_ref[place] = (base - factor[:, :1] * push).astype(jnp.bfloat16)


def state_kernel(
    core,
    outer_ref,
    moment_ref,
    factor_ref,
    factor2_ref,
    pseudo_ref,
    pseudo2_ref,
    new_outer_ref,
    new_moment_ref,
):
    for frag, scale_ref, rows_ref in (
        (core, factor_ref, pseudo_ref),
        (1 - core, factor2_ref, pseudo2_ref),
    ):
        clipped = scale_ref[:, :1] * rows_ref[...]
        moment = 0.9 * moment_ref[frag] + clipped
        new_moment_ref[frag] = moment
        new_outer_ref[frag] = outer_ref[frag] - 0.7 * (clipped + 0.9 * moment)


def mix_kernel(jobs, where_ref, weights_ref, *refs):
    core, z, yl = where_ref[0], where_ref[1], where_ref[2]
    mixed_hbm, mixed_ref, sems = refs[-3:]
    stores = []
    for number, (other_frag, other_side, places) in enumerate(jobs):
        frag = 1 - core if other_frag else core
        side = 1 - yl if other_side else yl
        for k, jump in enumerate(places):
            chip = 2 * (z ^ jump) + side
            own = weights_ref[frag, chip].astype(jnp.float32)
            source = refs[number][k].astype(jnp.float32)
            mixed_ref[number, k] = (0.5 * own + 0.5 * source).astype(jnp.bfloat16)
            stores.append(
                pltpu.make_async_copy(
                    mixed_ref.at[number, k], mixed_hbm.at[frag, chip], sems.at[number, k]
                )
            )
            stores[-1].start()
    for store in stores:
        store.wait()


def shards(local_weights, global_params, momentum):
    f32, bf16 = jnp.float32, jnp.bfloat16
    core, z, yl = (lax.axis_index(axis) for axis in ("core", "z", "yl"))
    other = 1 - core
    first = core == 0
    chips = lax.axis_size(CHIPS)
    replicas = 2 * chips
    everywhere = lax.axis_size(EVERYWHERE)
    rows, width = local_weights.shape[3], local_weights.shape[4]
    share_rows = global_params.shape[2]
    block = rows // chips
    max_norm = 0.5 * math.sqrt(block * width * everywhere)

    def pick(array, index, axis=0):
        return lax.dynamic_index_in_dim(array, index, axis, keepdims=False)

    def swapped_rows(array):
        kept = pick(array, core)
        came = over_core(pick(array, other))
        return jnp.where(
            first,
            jnp.concatenate((kept, came), axis=0),
            jnp.concatenate((came, kept), axis=0),
        )

    weights = local_weights[:, 0, 0]
    outer = swapped_rows(global_params[:, 0])
    moment = swapped_rows(momentum[:, 0])
    got = over_core(pick(weights, other))
    pair = (pick(weights, core).astype(f32) + got.astype(f32)).astype(bf16)
    pieces = lax.all_to_all(
        pair.reshape(chips, block, width), CHIPS, 0, 0, tiled=True
    )
    pseudo, pack, sums = pl.pallas_call(
        functools.partial(total_kernel, replicas),
        out_shape=(
            pltpu.VMEM((block, width), f32),
            pltpu.VMEM((2, block, width), bf16),
            jax.ShapeDtypeStruct((everywhere, LINES, 128), f32),
        ),
        in_specs=[VMEM] * 3,
        out_specs=(VMEM, VMEM, ANY),
        scratch_shapes=[
            pltpu.VMEM((everywhere, LINES, 128), f32),
            pltpu.SemaphoreType.DMA,
        ],
        compiler_params=SMALL,
        name="total",
    )(jnp.sum(pieces.astype(f32), axis=0), outer, moment)

    sums = lax.all_to_all(sums, EVERYWHERE, 0, 0, tiled=True)
    packs = [over_z(pack, jump) for jump in NEAR[1:]]
    halves = pseudo.reshape(2, share_rows, width)
    pseudo2 = over_core(pick(halves, other))
    packs, pseudo2 = lax.optimization_barrier((packs, pseudo2))
    near, factor = pl.pallas_call(
        functools.partial(source_kernel, max_norm),
        out_shape=(
            pltpu.VMEM((len(NEAR), block, width), bf16),
            pltpu.VMEM((1, 128), f32),
        ),
        in_specs=[VMEM] * (1 + len(NEAR)),
        out_specs=(VMEM, VMEM),
        compiler_params=SMALL,
        name="source",
    )(sums, pack, *packs)

    far = over_y(near)
    after = over_z(near, 1)
    after_far = over_y(after)
    factor2 = over_core(factor)

    where = jnp.stack((core, z, yl))
    blocks = weights.reshape(2, chips, block, width)

    jobs = (
        (False, False, NEAR),
        (True, False, NEAR),
        (False, True, NEAR),
        (True, True, NEAR),
        (False, False, NEXT),
        (True, False, NEXT),
    )
    last_jobs = ((False, True, NEXT), (True, True, NEXT))

    def scratch(number):
        return [
            pltpu.VMEM((number, len(NEAR), block, width), bf16),
            pltpu.SemaphoreType.DMA((number, len(NEAR))),
        ]

    def mix_and_state(where_ref, weights_ref, *refs):
        count = len(jobs)
        states, (mixed_hbm, *news), room = refs[count:-5], refs[-5:-2], refs[-2:]
        mix_kernel(jobs, where_ref, weights_ref, *refs[:count], mixed_hbm, *room)
        state_kernel(where_ref[0], *states, *news)

    def mix_last(where_ref, weights_ref, *refs):
        mix_kernel(last_jobs, where_ref, weights_ref, *refs[:2], *refs[-3:])

    state = jax.ShapeDtypeStruct((2, share_rows, width), f32)
    mixed_type = jax.ShapeDtypeStruct(blocks.shape, bf16)
    mixed, outer_next, moment_next = pl.pallas_call(
        mix_and_state,
        out_shape=(mixed_type, state, state),
        in_specs=[SMEM] + [VMEM] * (1 + len(jobs) + 6),
        out_specs=(ANY, VMEM, VMEM),
        scratch_shapes=scratch(len(jobs)),
        compiler_params=SMALL,
        name="mix",
    )(
        where,
        blocks,
        near,
        over_core(near),
        far,
        over_core(far),
        after,
        over_core(after),
        global_params[:, 0],
        momentum[:, 0],
        factor,
        factor2,
        pick(halves, core),
        pseudo2,
    )
    after_far, mixed = lax.optimization_barrier((after_far, mixed))
    mixed = pl.pallas_call(
        mix_last,
        out_shape=mixed_type,
        in_specs=[SMEM, VMEM, VMEM, VMEM, ANY],
        out_specs=ANY,
        scratch_shapes=scratch(len(last_jobs)),
        input_output_aliases={4: 0},
        compiler_params=SMALL,
        name="mix_last",
    )(where, blocks, after_far, over_core(after_far), mixed)
    return (
        mixed.reshape(local_weights.shape),
        outer_next[:, None],
        moment_next[:, None],
    )


def solution(mesh):
    fine = Mesh(
        mesh.devices.reshape(8, 2, 2, 4, 2), ("z", "yl", "core", "x", "yh")
    )
    replica, mp = ("z", "yl", "core"), ("x", "yh")
    whole = P(None, replica, mp, None, None)
    outer = P(None, mp, replica, None)
    return jax.shard_map(
        shards,
        mesh=fine,
        in_specs=(whole, outer, outer),
        out_specs=(whole, outer, outer),
        check_vma=False,
    )
```

time: 94.6 us -> 84.9 us (0.90)
  blocking collectives: 22.2 us -> 0 us
  starting transfers between devices: 22 us -> 42.3 us
  waiting for transfers between devices: 40.2 us -> 33.9 us
  Pallas kernels: 0 us -> 5.06 us
  other arithmetic: 4.53 us -> 1.34 us
  local copies, waits for them, and re-layouts: 3.79 us -> 1.39 us
    all_to_all x1 -> x0, blocking collectives: 22.2 us -> none  [shards(): lax.all_to_all(jnp.broadcast_to(part, (everywhere, 1, 128)), ('z', 'yl',...]
    ppermute x4 -> x15, starting transfers between devices: 10.9 us -> 22.7 us  [over(): return lax.ppermute(array, axis, [(i, i ^ jump) for i in range(size)])]
    all_to_all x1, waiting for transfers between devices: 17.2 us -> 7.49 us  [shards(): sums = lax.all_to_all(sums, EVERYWHERE, 0, 0, tiled=True)]
    all_to_all x1, starting transfers between devices: 3.61 us -> 12 us  [shards(): sums = lax.all_to_all(sums, EVERYWHERE, 0, 0, tiled=True)]
    pallas_call x0 -> x4, Pallas kernels: none -> 5.06 us  [the longest x1 2.64 us: shards(): pl.pallas_call(mix_and_state, out_shape=(mixed_type, state, state), in_sp...]
    ppermute x4 -> x15, waiting for transfers between devices: 4.03 us -> 7.7 us  [over(): return lax.ppermute(array, axis, [(i, i ^ jump) for i in range(size)])]
    convert_element_type x2 -> x0, other arithmetic: 1.83 us -> none  [the longest x1 1.79 us: shards(): mixed = (0.5 * weights.astype(f32) + 0.5 * sources.astype(f32)).astype(bf16)]
    broadcast_in_dim x2 -> x0, local copies, waits for them, and re-layouts: 1.64 us -> none  [the longest x1 0.96 us: shards(): jnp.broadcast_to(source, (chips, block, width))]
  transfers between devices with their start and end apart: 6 -> 17, of which waited for: 5 -> 10; matrix products, arithmetic and copies ran while one was open for 1% -> 0% of each run, Pallas kernels for 0% -> 3%
where the time goes in v6:
time: 84.9 us; the launch traced here: 84.7 us
  starting transfers between devices  42.3 us (50%)
  waiting for transfers between devices  33.9 us (40%)
  Pallas kernels  5.06 us (6%)
  local copies, waits for them, and re-layouts  1.39 us (2%)
  other arithmetic  1.34 us (2%)
    ppermute x15, starting transfers between devices, over(): return lax.ppermute(array, axis, [(i, i ^ jump) for i in range(size)])  22.7 us
    all_to_all x1, waiting for transfers between devices, shards(): lax.all_to_all(pair.reshape(chips, block, width), CHIPS, 0, 0, tiled=True)  18.7 us
    all_to_all x1, starting transfers between devices, shards(): sums = lax.all_to_all(sums, EVERYWHERE, 0, 0, tiled=True)  12 us
    ppermute x15, waiting for transfers between devices, over(): return lax.ppermute(array, axis, [(i, i ^ jump) for i in range(size)])  7.7 us
    all_to_all x1, starting transfers between devices, shards(): lax.all_to_all(pair.reshape(chips, block, width), CHIPS, 0, 0, tiled=True)  7.57 us
    all_to_all x1, waiting for transfers between devices, shards(): sums = lax.all_to_all(sums, EVERYWHERE, 0, 0, tiled=True)  7.49 us
    pallas_call x1, Pallas kernels, shards(): pl.pallas_call(mix_and_state, out_shape=(mixed_type, state, state), in_sp...  2.64 us
  transfers between devices with their start and end apart: 17, of which 10 were waited for; matrix products, arithmetic and copies ran while one was open for 0% of the time, Pallas kernels for 3%

profile of v6, /device:TPU:1, one launch (start us, length us, event | category | flops | bytes accessed | tf_op | source)
XLA Modules:
  0.0 84.7 jit_solution(5532827664141405289)
XLA Ops:
  0.6 0.0 copy-start
  0.6 1.3 %dynamic-slice_bitcast_fusion = bf16[128,3072]{1,0:T(8,128)(2,1)S(1)} fusion(bf16[2,1,1,128,3072]{4,3,2,1,0:T(8,128)(2,1)} %param.3, s32[]{:T(128)S(6)} %select_n.27), kind=kLoop, calls=%fused_computation.4 | loop fusion | bytes 1572868 | tf_op jit(solution)/shard_map/jit(dynamic_index_in_dim)/squeeze | solution.py:121
  2.0 3.3 %collective-permute-start = (bf16[128,3072]{1,0:T(8,128)(2,1)S(1)}, bf16[128,3072]{1,0:T(8,128)(2,1)S(1)}, u32[]{:S(2)}, u32[]{:S(2)}) collective-permute-start(bf16[128,3072]{1,0:T(8,128)(2,1)S(1)} %dynamic-slice_bitcast_fusion), channel_id=1, source_target_pairs={{0,8},{8,0},{1,9},{9,1},{2,10},{10,2},{3,11},{11,3},{4,12},{12,4},... | collective-permute-start | bytes 2359304 | tf_op jit(solution)/shard_map/ppermute | solution.py:23
  5.3 0.0 copy-start.1
  5.3 0.0 copy-start.2
  5.3 1.9 %collective-permute-done = bf16[128,3072]{1,0:T(8,128)(2,1)S(1)} collective-permute-done((bf16[128,3072]{1,0:T(8,128)(2,1)S(1)}, bf16[128,3072]{1,0:T(8,128)(2,1)S(1)}, u32[]{:S(2)}, u32[]{:S(2)}) %collective-permute-start) | collective-permute-done | bytes 786464 | tf_op jit(solution)/shard_map/ppermute | solution.py:23
  7.2 0.0 copy-done
  7.2 1.1 %fusion.1 = bf16[16,8,3072]{2,1,0:T(8,128)(2,1)} fusion(bf16[128,3072]{1,0:T(8,128)(2,1)S(1)} %collective-permute-done, bf16[2,1,1,128,3072]{4,3,2,1,0:T(8,128)(2,1)S(1)} %copy-done, s32[]{:T(128)S(6)} %select_n.26), kind=kLoop, calls=%fused_computation.3 | loop fusion | flops 1572864 | bytes 2359300 | tf_op jit(solution)/shard_map/reshape | solution.py:138
  8.3 7.6 %all-to-all-start = ((bf16[16,8,3072]{2,1,0:T(8,128)(2,1)}), bf16[16,8,3072]{2,1,0:T(8,128)(2,1)S(1)}, u32[]{:S(2)}, u32[]{:S(2)}) async-start(bf16[16,8,3072]{2,1,0:T(8,128)(2,1)} %fusion.1), calls=%async_computation | async-start | bytes 1572864 | tf_op jit(solution)/shard_map/all_to_all | solution.py:137
  15.8 0.0 copy-done.1
  15.9 0.7 collective-permute-start.1
  16.6 0.0 copy-done.2
  16.6 0.1 collective-permute-start.2
  16.8 0.7 collective-permute-done.1
  17.5 0.4 collective-permute-done.2
  18.0 18.7 %all-to-all-done = bf16[16,8,3072]{2,1,0:T(8,128)(2,1)S(1)} async-done(((bf16[16,8,3072]{2,1,0:T(8,128)(2,1)}), bf16[16,8,3072]{2,1,0:T(8,128)(2,1)S(1)}, u32[]{:S(2)}, u32[]{:S(2)}) %all-to-all-start) | async-done | bytes 786464 | tf_op jit(solution)/shard_map/all_to_all | solution.py:137
  36.7 0.1 convert_reduce_fusion.total_ref
  36.8 0.8 total.1
  37.6 2.4 %collective-permute-start.5 = (bf16[2,8,3072]{2,1,0:T(8,128)(2,1)S(1)}, bf16[2,8,3072]{2,1,0:T(8,128)(2,1)S(1)}, u32[]{:S(2)}, u32[]{:S(2)}) collective-permute-start(bf16[2,8,3072]{2,1,0:T(8,128)(2,1)S(1)} %get-tuple-element.18.refs_0_), channel_id=1, source_target_pairs={{0,192},{32,224},{64,128},{96,160},{128,64},{160,96},{192,0},{224,... | collective-permute-start | bytes 294920 | tf_op jit(solution)/shard_map/ppermute | solution.py:23
  40.0 1.4 %collective-permute-start.4 = (bf16[2,8,3072]{2,1,0:T(8,128)(2,1)S(1)}, bf16[2,8,3072]{2,1,0:T(8,128)(2,1)S(1)}, u32[]{:S(2)}, u32[]{:S(2)}) collective-permute-start(bf16[2,8,3072]{2,1,0:T(8,128)(2,1)S(1)} %get-tuple-element.18.refs_0_), channel_id=1, source_target_pairs={{0,64},{32,96},{64,0},{96,32},{128,192},{160,224},{192,128},{224,1... | collective-permute-start | bytes 294920 | tf_op jit(solution)/shard_map/ppermute | solution.py:23
  41.3 2.2 %collective-permute-start.3 = (bf16[2,8,3072]{2,1,0:T(8,128)(2,1)S(1)}, bf16[2,8,3072]{2,1,0:T(8,128)(2,1)S(1)}, u32[]{:S(2)}, u32[]{:S(2)}) collective-permute-start(bf16[2,8,3072]{2,1,0:T(8,128)(2,1)S(1)} %get-tuple-element.18.refs_0_), channel_id=1, source_target_pairs={{0,128},{32,160},{64,192},{96,224},{128,0},{160,32},{192,64},{224,... | collective-permute-start | bytes 294920 | tf_op jit(solution)/shard_map/ppermute | solution.py:23
  43.5 12.0 %all-to-all-start.1 = ((f32[128,1,128]{2,1,0:T(1,128)}), f32[128,1,128]{2,1,0:T(1,128)S(1)}, u32[]{:S(2)}, u32[]{:S(2)}) async-start(f32[128,1,128]{2,1,0:T(1,128)} %get-tuple-element.17), calls=%async_computation.1 | async-start | bytes 131072 | tf_op jit(solution)/shard_map/all_to_all | solution.py:157
  55.6 1.7 %collective-permute-start.6 = (f32[4,3072]{1,0:T(4,128)S(1)}, f32[4,3072]{1,0:T(4,128)S(1)}, u32[]{:S(2)}, u32[]{:S(2)}) collective-permute-start(f32[4,3072]{1,0:T(4,128)S(1)} %get-tuple-element.35), channel_id=1, source_target_pairs={{0,8},{8,0},{1,9},{9,1},{2,10},{10,2},{3,11},{11,3},{4,12},{12,4},... | collective-permute-start | bytes 147464 | tf_op jit(solution)/shard_map/ppermute | solution.py:23
  57.3 0.9 %collective-permute-done.6.refs_11_ = f32[4,3072]{1,0:T(4,128)S(1)} collective-permute-done((f32[4,3072]{1,0:T(4,128)S(1)}, f32[4,3072]{1,0:T(4,128)S(1)}, u32[]{:S(2)}, u32[]{:S(2)}) %collective-permute-start.6) | collective-permute-done | bytes 49184 | tf_op jit(solution)/shard_map/ppermute | solution.py:23
  58.2 0.0 collective-permute-done.5.refs_3_
  58.2 0.0 collective-permute-done.4.refs_2_
  58.2 0.0 collective-permute-done.3.refs_1_
  58.2 7.5 %all-to-all-done.1.sums_ref = f32[128,1,128]{2,1,0:T(1,128)S(1)} async-done(((f32[128,1,128]{2,1,0:T(1,128)}), f32[128,1,128]{2,1,0:T(1,128)S(1)}, u32[]{:S(2)}, u32[]{:S(2)}) %all-to-all-start.1) | async-done | bytes 65568 | tf_op jit(solution)/shard_map/all_to_all | solution.py:157
  65.7 0.2 source.1
  65.9 0.3 collective-permute-start.10
  66.2 0.5 collective-permute-start.7
  66.7 3.3 %collective-permute-start.9 = (bf16[4,8,3072]{2,1,0:T(8,128)(2,1)S(1)}, bf16[4,8,3072]{2,1,0:T(8,128)(2,1)S(1)}, u32[]{:S(2)}, u32[]{:S(2)}) collective-permute-start(bf16[4,8,3072]{2,1,0:T(8,128)(2,1)S(1)} %get-tuple-element.23.refs_0_), channel_id=1, source_target_pairs={{0,8},{8,0},{1,9},{9,1},{2,10},{10,2},{3,11},{11,3},{4,12},{12,4},... | collective-permute-start | bytes 589832 | tf_op jit(solution)/shard_map/ppermute | solution.py:23
  70.0 0.4 collective-permute-done.10.refs_2_
  70.5 3.9 %collective-permute-start.11 = (bf16[4,8,3072]{2,1,0:T(8,128)(2,1)S(1)}, bf16[4,8,3072]{2,1,0:T(8,128)(2,1)S(1)}, u32[]{:S(2)}, u32[]{:S(2)}) collective-permute-start(bf16[4,8,3072]{2,1,0:T(8,128)(2,1)S(1)} %collective-permute-done.10.refs_2_), channel_id=1, source_target_pairs={{0,8},{8,0},{1,9},{9,1},{2,10},{10,2},{3,11},{11,3},{4,12},{12,4},... | collective-permute-start | bytes 589832 | tf_op jit(solution)/shard_map/ppermute | solution.py:23
  74.4 0.0 collective-permute-done.7.refs_4_
  74.4 0.5 collective-permute-start.12
  74.9 1.3 %collective-permute-start.8 = (bf16[4,8,3072]{2,1,0:T(8,128)(2,1)S(1)}, bf16[4,8,3072]{2,1,0:T(8,128)(2,1)S(1)}, u32[]{:S(2)}, u32[]{:S(2)}) collective-permute-start(bf16[4,8,3072]{2,1,0:T(8,128)(2,1)S(1)} %collective-permute-done.7.refs_4_), channel_id=1, source_target_pairs={{0,16},{16,0},{1,17},{17,1},{2,18},{18,2},{3,19},{19,3},{4,20},{20... | collective-permute-start | bytes 589832 | tf_op jit(solution)/shard_map/ppermute | solution.py:23
  76.1 0.3 collective-permute-start.13
  76.4 0.1 pad_add_fusion.where_ref
  76.5 0.8 collective-permute-done.13.refs_9_
  77.3 0.0 collective-permute-done.9.refs_1_
  77.3 0.0 collective-permute-done.11.refs_3_
  77.3 0.0 collective-permute-done.12.refs_5_
  77.3 2.6 %mix.1 = (bf16[2,16,8,3072]{3,2,1,0:T(8,128)(2,1)}, f32[2,4,3072]{2,1,0:T(4,128)}, f32[2,4,3072]{2,1,0:T(4,128)}) custom-call(s32[3]{0:T(128)S(1)} %pad_add_fusion.where_ref, bf16[2,16,8,3072]{3,2,1,0:T(8,128)(2,1)S(1)} %bitcast.34, bf16[4,8,3072]{2,1,0:T(8,128)(2,1)S(1)} %get-tuple-element.23.refs_0_, ...), custom_call_target="tpu_custom_call" | custom-call | tf_op jit(solution)/shard_map/mix/pallas_call | solution.py:209
  79.9 1.5 %collective-permute-done.8.refs_0_ = bf16[4,8,3072]{2,1,0:T(8,128)(2,1)S(1)} collective-permute-done((bf16[4,8,3072]{2,1,0:T(8,128)(2,1)S(1)}, bf16[4,8,3072]{2,1,0:T(8,128)(2,1)S(1)}, u32[]{:S(2)}, u32[]{:S(2)}) %collective-permute-start.8) | collective-permute-done | bytes 196640 | tf_op jit(solution)/shard_map/ppermute | solution.py:23
  81.4 0.8 collective-permute-start.14
  82.2 1.1 %collective-permute-done.14.refs_1_ = bf16[4,8,3072]{2,1,0:T(8,128)(2,1)S(1)} collective-permute-done((bf16[4,8,3072]{2,1,0:T(8,128)(2,1)S(1)}, bf16[4,8,3072]{2,1,0:T(8,128)(2,1)S(1)}, u32[]{:S(2)}, u32[]{:S(2)}) %collective-permute-start.14) | collective-permute-done | bytes 196640 | tf_op jit(solution)/shard_map/ppermute | solution.py:23
  83.3 1.4 %mix_last.1 = bf16[2,16,8,3072]{3,2,1,0:T(8,128)(2,1)} custom-call(s32[3]{0:T(128)S(1)} %pad_add_fusion.where_ref, bf16[2,16,8,3072]{3,2,1,0:T(8,128)(2,1)S(1)} %bitcast.35, bf16[4,8,3072]{2,1,0:T(8,128)(2,1)S(1)} %collective-permute-done.8.refs_0_, bf16[4,8,3072]{2,1,0:T(8,128)(2,1)S(1)} %collective-permute-done.14.refs_1_, ...), custom_call_target="tpu_custom_call", output_to_operand_aliasing={{}: (4, {})} | custom-call | tf_op jit(solution)/shard_map/mix_last/pallas_call | solution.py:234
  (6 shorter events, 0.2 us)
Async XLA Ops:
  0.6 6.6 %copy-start = (bf16[2,1,1,128,3072]{4,3,2,1,0:T(8,128)(2,1)S(1)}, bf16[2,1,1,128,3072]{4,3,2,1,0:T(8,128)(2,1)}, u32[]{:S(2)}) copy-start(bf16[2,1,1,128,3072]{4,3,2,1,0:T(8,128)(2,1)} %param.3) | copy-start | bytes 4718596
  2.0 5.2 %collective-permute-start = (bf16[128,3072]{1,0:T(8,128)(2,1)S(1)}, bf16[128,3072]{1,0:T(8,128)(2,1)S(1)}, u32[]{:S(2)}, u32[]{:S(2)}) collective-permute-start(bf16[128,3072]{1,0:T(8,128)(2,1)S(1)} %dynamic-slice_bitcast_fusion), channel_id=1, source_target_pairs={{0,8},{8,0},{1,9},{9,1},{2,10},{10,2},{3,11},{11,3},{4,12},{12,4},... | collective-permute-start | bytes 2359304 | tf_op jit(solution)/shard_map/ppermute | solution.py:23
  5.3 10.6 %copy-start.1 = (f32[2,1,4,3072]{3,2,1,0:T(4,128)S(1)}, f32[2,1,4,3072]{3,2,1,0:T(4,128)}, u32[]{:S(2)}) copy-start(f32[2,1,4,3072]{3,2,1,0:T(4,128)} %param.4) | copy-start | bytes 294916
  5.3 11.3 %copy-start.2 = (f32[2,1,4,3072]{3,2,1,0:T(4,128)S(1)}, f32[2,1,4,3072]{3,2,1,0:T(4,128)}, u32[]{:S(2)}) copy-start(f32[2,1,4,3072]{3,2,1,0:T(4,128)} %param.5) | copy-start | bytes 294916
  8.3 28.4 %all-to-all-start = ((bf16[16,8,3072]{2,1,0:T(8,128)(2,1)}), bf16[16,8,3072]{2,1,0:T(8,128)(2,1)S(1)}, u32[]{:S(2)}, u32[]{:S(2)}) async-start(bf16[16,8,3072]{2,1,0:T(8,128)(2,1)} %fusion.1), calls=%async_computation | async-start | bytes 1572864 | tf_op jit(solution)/shard_map/all_to_all | solution.py:137
  15.9 1.6 %collective-permute-start.1 = (f32[4,3072]{1,0:T(4,128)S(1)}, f32[4,3072]{1,0:T(4,128)S(1)}, u32[]{:S(2)}, u32[]{:S(2)}) collective-permute-start(f32[4,3072]{1,0:T(4,128)S(1)} %get-tuple-element.39), channel_id=1, source_target_pairs={{0,8},{8,0},{1,9},{9,1},{2,10},{10,2},{3,11},{11,3},{4,12},{12,4},... | collective-permute-start | bytes 147464 | tf_op jit(solution)/shard_map/ppermute | solution.py:23
  16.6 1.3 %collective-permute-start.2 = (f32[4,3072]{1,0:T(4,128)S(1)}, f32[4,3072]{1,0:T(4,128)S(1)}, u32[]{:S(2)}, u32[]{:S(2)}) collective-permute-start(f32[4,3072]{1,0:T(4,128)S(1)} %get-tuple-element.37), channel_id=1, source_target_pairs={{0,8},{8,0},{1,9},{9,1},{2,10},{10,2},{3,11},{11,3},{4,12},{12,4},... | collective-permute-start | bytes 147464 | tf_op jit(solution)/shard_map/ppermute | solution.py:23
  37.6 20.5 %collective-permute-start.5 = (bf16[2,8,3072]{2,1,0:T(8,128)(2,1)S(1)}, bf16[2,8,3072]{2,1,0:T(8,128)(2,1)S(1)}, u32[]{:S(2)}, u32[]{:S(2)}) collective-permute-start(bf16[2,8,3072]{2,1,0:T(8,128)(2,1)S(1)} %get-tuple-element.18.refs_0_), channel_id=1, source_target_pairs={{0,192},{32,224},{64,128},{96,160},{128,64},{160,96},{192,0},{224,... | collective-permute-start | bytes 294920 | tf_op jit(solution)/shard_map/ppermute | solution.py:23
  40.0 18.2 %collective-permute-start.4 = (bf16[2,8,3072]{2,1,0:T(8,128)(2,1)S(1)}, bf16[2,8,3072]{2,1,0:T(8,128)(2,1)S(1)}, u32[]{:S(2)}, u32[]{:S(2)}) collective-permute-start(bf16[2,8,3072]{2,1,0:T(8,128)(2,1)S(1)} %get-tuple-element.18.refs_0_), channel_id=1, source_target_pairs={{0,64},{32,96},{64,0},{96,32},{128,192},{160,224},{192,128},{224,1... | collective-permute-start | bytes 294920 | tf_op jit(solution)/shard_map/ppermute | solution.py:23
  41.3 16.8 %collective-permute-start.3 = (bf16[2,8,3072]{2,1,0:T(8,128)(2,1)S(1)}, bf16[2,8,3072]{2,1,0:T(8,128)(2,1)S(1)}, u32[]{:S(2)}, u32[]{:S(2)}) collective-permute-start(bf16[2,8,3072]{2,1,0:T(8,128)(2,1)S(1)} %get-tuple-element.18.refs_0_), channel_id=1, source_target_pairs={{0,128},{32,160},{64,192},{96,224},{128,0},{160,32},{192,64},{224,... | collective-permute-start | bytes 294920 | tf_op jit(solution)/shard_map/ppermute | solution.py:23
  43.5 22.2 %all-to-all-start.1 = ((f32[128,1,128]{2,1,0:T(1,128)}), f32[128,1,128]{2,1,0:T(1,128)S(1)}, u32[]{:S(2)}, u32[]{:S(2)}) async-start(f32[128,1,128]{2,1,0:T(1,128)} %get-tuple-element.17), calls=%async_computation.1 | async-start | bytes 131072 | tf_op jit(solution)/shard_map/all_to_all | solution.py:157
  55.6 2.6 %collective-permute-start.6 = (f32[4,3072]{1,0:T(4,128)S(1)}, f32[4,3072]{1,0:T(4,128)S(1)}, u32[]{:S(2)}, u32[]{:S(2)}) collective-permute-start(f32[4,3072]{1,0:T(4,128)S(1)} %get-tuple-element.35), channel_id=1, source_target_pairs={{0,8},{8,0},{1,9},{9,1},{2,10},{10,2},{3,11},{11,3},{4,12},{12,4},... | collective-permute-start | bytes 147464 | tf_op jit(solution)/shard_map/ppermute | solution.py:23
  65.9 4.6 %collective-permute-start.10 = (bf16[4,8,3072]{2,1,0:T(8,128)(2,1)S(1)}, bf16[4,8,3072]{2,1,0:T(8,128)(2,1)S(1)}, u32[]{:S(2)}, u32[]{:S(2)}) collective-permute-start(bf16[4,8,3072]{2,1,0:T(8,128)(2,1)S(1)} %get-tuple-element.23.refs_0_), channel_id=1, source_target_pairs={{0,16},{16,0},{1,17},{17,1},{2,18},{18,2},{3,19},{19,3},{4,20},{20... | collective-permute-start | bytes 589832 | tf_op jit(solution)/shard_map/ppermute | solution.py:23
  66.2 8.2 %collective-permute-start.7 = (bf16[4,8,3072]{2,1,0:T(8,128)(2,1)S(1)}, bf16[4,8,3072]{2,1,0:T(8,128)(2,1)S(1)}, u32[]{:S(2)}, u32[]{:S(2)}) collective-permute-start(bf16[4,8,3072]{2,1,0:T(8,128)(2,1)S(1)} %get-tuple-element.23.refs_0_), channel_id=1, source_target_pairs={{0,32},{32,0},{64,96},{96,64},{128,160},{160,128},{192,224},{224,1... | collective-permute-start | bytes 589832 | tf_op jit(solution)/shard_map/ppermute | solution.py:23
  66.7 10.6 %collective-permute-start.9 = (bf16[4,8,3072]{2,1,0:T(8,128)(2,1)S(1)}, bf16[4,8,3072]{2,1,0:T(8,128)(2,1)S(1)}, u32[]{:S(2)}, u32[]{:S(2)}) collective-permute-start(bf16[4,8,3072]{2,1,0:T(8,128)(2,1)S(1)} %get-tuple-element.23.refs_0_), channel_id=1, source_target_pairs={{0,8},{8,0},{1,9},{9,1},{2,10},{10,2},{3,11},{11,3},{4,12},{12,4},... | collective-permute-start | bytes 589832 | tf_op jit(solution)/shard_map/ppermute | solution.py:23
  70.5 6.8 %collective-permute-start.11 = (bf16[4,8,3072]{2,1,0:T(8,128)(2,1)S(1)}, bf16[4,8,3072]{2,1,0:T(8,128)(2,1)S(1)}, u32[]{:S(2)}, u32[]{:S(2)}) collective-permute-start(bf16[4,8,3072]{2,1,0:T(8,128)(2,1)S(1)} %collective-permute-done.10.refs_2_), channel_id=1, source_target_pairs={{0,8},{8,0},{1,9},{9,1},{2,10},{10,2},{3,11},{11,3},{4,12},{12,4},... | collective-permute-start | bytes 589832 | tf_op jit(solution)/shard_map/ppermute | solution.py:23
  74.4 2.9 %collective-permute-start.12 = (bf16[4,8,3072]{2,1,0:T(8,128)(2,1)S(1)}, bf16[4,8,3072]{2,1,0:T(8,128)(2,1)S(1)}, u32[]{:S(2)}, u32[]{:S(2)}) collective-permute-start(bf16[4,8,3072]{2,1,0:T(8,128)(2,1)S(1)} %collective-permute-done.7.refs_4_), channel_id=1, source_target_pairs={{0,8},{8,0},{1,9},{9,1},{2,10},{10,2},{3,11},{11,3},{4,12},{12,4},... | collective-permute-start | bytes 589832 | tf_op jit(solution)/shard_map/ppermute | solution.py:23
  74.9 6.5 %collective-permute-start.8 = (bf16[4,8,3072]{2,1,0:T(8,128)(2,1)S(1)}, bf16[4,8,3072]{2,1,0:T(8,128)(2,1)S(1)}, u32[]{:S(2)}, u32[]{:S(2)}) collective-permute-start(bf16[4,8,3072]{2,1,0:T(8,128)(2,1)S(1)} %collective-permute-done.7.refs_4_), channel_id=1, source_target_pairs={{0,16},{16,0},{1,17},{17,1},{2,18},{18,2},{3,19},{19,3},{4,20},{20... | collective-permute-start | bytes 589832 | tf_op jit(solution)/shard_map/ppermute | solution.py:23
  76.1 1.1 %collective-permute-start.13 = (f32[1,128]{1,0:T(1,128)S(1)}, f32[1,128]{1,0:T(1,128)S(1)}, u32[]{:S(2)}, u32[]{:S(2)}) collective-permute-start(f32[1,128]{1,0:T(1,128)S(1)} %get-tuple-element.24.refs_8_), channel_id=1, source_target_pairs={{0,8},{8,0},{1,9},{9,1},{2,10},{10,2},{3,11},{11,3},{4,12},{12,4},... | collective-permute-start | bytes 1544 | tf_op jit(solution)/shard_map/ppermute | solution.py:23
  81.4 1.9 %collective-permute-start.14 = (bf16[4,8,3072]{2,1,0:T(8,128)(2,1)S(1)}, bf16[4,8,3072]{2,1,0:T(8,128)(2,1)S(1)}, u32[]{:S(2)}, u32[]{:S(2)}) collective-permute-start(bf16[4,8,3072]{2,1,0:T(8,128)(2,1)S(1)} %collective-permute-done.8.refs_0_), channel_id=1, source_target_pairs={{0,8},{8,0},{1,9},{9,1},{2,10},{10,2},{3,11},{11,3},{4,12},{12,4},... | collective-permute-start | bytes 589832 | tf_op jit(solution)/shard_map/ppermute | solution.py:23

commit v7 on v6

v7 whole, which is shorter than its diff:
```python
import functools
import math

import jax
import jax.numpy as jnp
from jax import lax
from jax.experimental import pallas as pl
from jax.experimental.pallas import tpu as pltpu
from jax.sharding import Mesh
from jax.sharding import PartitionSpec as P

CHIPS = ("zh", "zl", "yl")
EVERYWHERE = ("zh", "zl", "yl", "x", "yh")
GROUPS = ("zl", "yl", "x", "yh")
JUMPS = (0, 2, 1, 3)
EXTRA = 128
PARTS = 4
ANY = pl.BlockSpec(memory_space=pl.ANY)
SMEM = pl.BlockSpec(memory_space=pltpu.SMEM)
SMALL = pltpu.CompilerParams(vmem_limit_bytes=12 * 1024 * 1024)
VMEM = pl.BlockSpec(memory_space=pltpu.VMEM)


def over(axis, size, jump, array):
    return lax.ppermute(array, axis, [(i, i ^ jump) for i in range(size)])


def over_core(array):
    return over("core", 2, 1, array)


def over_y(array):
    return over("yl", 2, 1, array)


def over_z(array):
    return over("zl", 2, 1, array)


def cut_kernel(which_ref, weights_hbm, cut_ref, sems):
    step = cut_ref.shape[0] // PARTS
    copies = []
    for part in range(PARTS):
        some = pl.ds(part * step, step)
        copies.append(
            pltpu.make_async_copy(
                weights_hbm.at[which_ref[0], some], cut_ref.at[some], sems.at[part]
            )
        )
        copies[-1].start()
    for copy in copies:
        copy.wait()


def pair_kernel(core_ref, weights_ref, got_ref, pair_hbm, pair_ref, sems):
    step = got_ref.shape[0] // PARTS
    copies = []
    for part in range(PARTS):
        some = pl.ds(part * step, step)
        own = weights_ref[core_ref[0], some].astype(jnp.float32)
        pair = own + got_ref[some].astype(jnp.float32)
        pair_ref[some] = pair.astype(jnp.bfloat16)
        copies.append(
            pltpu.make_async_copy(
                pair_ref.at[some], pair_hbm.at[some], sems.at[part]
            )
        )
        copies[-1].start()
    for copy in copies:
        copy.wait()


def total_kernel(replicas, total_ref, outer_ref, moment_ref, pseudo_ref, pack_ref):
    outer = outer_ref[...]
    width = outer.shape[1]
    pseudo = outer - total_ref[...] / replicas
    pseudo_ref[...] = pseudo
    pack_ref[0, :, :width] = (outer - 0.567 * moment_ref[...]).astype(jnp.bfloat16)
    pack_ref[1, :, :width] = (1.33 * pseudo).astype(jnp.bfloat16)
    square_sum = jnp.sum(jnp.sum(pseudo * pseudo, axis=0, keepdims=True), keepdims=True)
    high = square_sum.astype(jnp.bfloat16).astype(jnp.float32)
    middle = (square_sum - high).astype(jnp.bfloat16).astype(jnp.float32)
    low = square_sum - high - middle
    shape = (outer.shape[0], EXTRA)
    row = lax.broadcasted_iota(jnp.int32, shape, 0)
    lines = jnp.where(row == 0, high, jnp.where(row == 1, middle, low))
    lines = jnp.where(row < 3, lines, 0.0).astype(jnp.bfloat16)
    pack_ref[0, :, width:] = lines
    pack_ref[1, :, width:] = lines


def join_kernel(*refs):
    pack_refs = refs[: len(JUMPS)]
    joined_ref, sums_hbm, sums_ref, sem = refs[len(JUMPS) :]
    width = joined_ref.shape[3]
    lines = sum(ref[0, :, width:].astype(jnp.float32) for ref in pack_refs)
    sums_ref[...] = jnp.broadcast_to(
        jnp.sum(lines, axis=0, keepdims=True)[None], sums_ref.shape
    )
    copy = pltpu.make_async_copy(sums_ref, sums_hbm, sem)
    copy.start()
    for place, ref in enumerate(pack_refs):
        joined_ref[place] = ref[:, :, :width]
    copy.wait()


def source_kernel(max_norm, sums_ref, *refs):
    joined_refs, (source_ref, factor_ref) = refs[:-2], refs[-2:]
    square_sum = jnp.sum(sums_ref[:, 0, :], axis=0, keepdims=True)
    factor = jnp.minimum(1.0, max_norm / (jnp.sqrt(square_sum) + 1e-06))
    factor_ref[...] = factor
    for number, joined_ref in enumerate(joined_refs):
        for place in range(len(JUMPS)):
            base = joined_ref[place, 0].astype(jnp.float32)
            push = joined_ref[place, 1].astype(jnp.float32)
            source = base - factor[:, :1] * push
            source_ref[number, place] = source.astype(jnp.bfloat16)


def state_kernel(
    core,
    outer_ref,
    moment_ref,
    factor_ref,
    factor2_ref,
    pseudo_ref,
    pseudo2_ref,
    new_outer_ref,
    new_moment_ref,
):
    for frag, scale_ref, rows_ref in (
        (core, factor_ref, pseudo_ref),
        (1 - core, factor2_ref, pseudo2_ref),
    ):
        clipped = scale_ref[:, :1] * rows_ref[...]
        moment = 0.9 * moment_ref[frag] + clipped
        new_moment_ref[frag] = moment
        new_outer_ref[frag] = outer_ref[frag] - 0.7 * (clipped + 0.9 * moment)


def mix_kernel(jobs, where_ref, weights_ref, *refs):
    core, zh, zl, yl = (where_ref[i] for i in range(4))
    mixed_hbm, mixed_ref, sems = refs
    stores = []
    for number, (source_ref, other_frag, other_z, other_y) in enumerate(jobs):
        frag = 1 - core if other_frag else core
        low = (1 - zl if other_z else zl) * 2 + (1 - yl if other_y else yl)
        for k, jump in enumerate(JUMPS):
            chip = 4 * (zh ^ jump) + low
            own = weights_ref[frag, chip].astype(jnp.float32)
            source = source_ref[k].astype(jnp.float32)
            mixed_ref[number, k] = (0.5 * own + 0.5 * source).astype(jnp.bfloat16)
            stores.append(
                pltpu.make_async_copy(
                    mixed_ref.at[number, k], mixed_hbm.at[frag, chip], sems.at[number, k]
                )
            )
            stores[-1].start()
    for store in stores:
        store.wait()


def shards(local_weights, global_params, momentum):
    f32, bf16 = jnp.float32, jnp.bfloat16
    core = lax.axis_index("core")
    other = 1 - core
    first = core == 0
    chips = lax.axis_size(CHIPS)
    replicas = 2 * chips
    everywhere = lax.axis_size(EVERYWHERE)
    rows, width = local_weights.shape[3], local_weights.shape[4]
    share_rows = global_params.shape[2]
    block = rows // chips
    max_norm = 0.5 * math.sqrt(block * width * everywhere)

    def pick(array, index, axis=0):
        return lax.dynamic_index_in_dim(array, index, axis, keepdims=False)

    def swapped_rows(array):
        kept = pick(array, core)
        came = over_core(pick(array, other))
        return jnp.where(
            first,
            jnp.concatenate((kept, came), axis=0),
            jnp.concatenate((came, kept), axis=0),
        )

    weights = local_weights[:, 0, 0]
    outer = swapped_rows(global_params[:, 0])
    moment = swapped_rows(momentum[:, 0])
    sent = pl.pallas_call(
        cut_kernel,
        out_shape=pltpu.VMEM((rows, width), bf16),
        in_specs=[SMEM, ANY],
        out_specs=VMEM,
        scratch_shapes=[pltpu.SemaphoreType.DMA((PARTS,))],
        compiler_params=SMALL,
        name="cut",
    )(other[None], pltpu.with_memory_space_constraint(weights, pltpu.HBM))
    pair = pl.pallas_call(
        pair_kernel,
        out_shape=jax.ShapeDtypeStruct((rows, width), bf16),
        in_specs=[SMEM, VMEM, VMEM],
        out_specs=ANY,
        scratch_shapes=[
            pltpu.VMEM((rows, width), bf16),
            pltpu.SemaphoreType.DMA((PARTS,)),
        ],
        compiler_params=SMALL,
        name="pair",
    )(core[None], weights, over_core(sent))
    pieces = lax.all_to_all(
        pair.reshape(chips, block, width), CHIPS, 0, 0, tiled=True
    )
    pseudo, pack = pl.pallas_call(
        functools.partial(total_kernel, replicas),
        out_shape=(
            pltpu.VMEM((block, width), f32),
            pltpu.VMEM((2, block, width + EXTRA), bf16),
        ),
        in_specs=[VMEM] * 3,
        out_specs=(VMEM, VMEM),
        compiler_params=SMALL,
        name="total",
    )(jnp.sum(pieces.astype(f32), axis=0), outer, moment)
    halves = pseudo.reshape(2, share_rows, width)
    pseudo2 = over_core(pick(halves, other))

    packs = [pack] + [over("zh", 4, jump, pack) for jump in JUMPS[1:]]
    packs, pseudo2 = lax.optimization_barrier((packs, pseudo2))
    groups = lax.axis_size(GROUPS)
    joined, sums = pl.pallas_call(
        join_kernel,
        out_shape=(
            pltpu.VMEM((len(JUMPS), 2, block, width), bf16),
            jax.ShapeDtypeStruct((groups, 1, EXTRA), f32),
        ),
        in_specs=[VMEM] * len(JUMPS),
        out_specs=(VMEM, ANY),
        scratch_shapes=[
            pltpu.VMEM((groups, 1, EXTRA), f32),
            pltpu.SemaphoreType.DMA,
        ],
        compiler_params=SMALL,
        name="join",
    )(*packs)

    sums = lax.all_to_all(sums, GROUPS, 0, 0, tiled=True)
    after = over_z(joined)
    far = over_y(joined)
    sources, factor = pl.pallas_call(
        functools.partial(source_kernel, max_norm),
        out_shape=(
            pltpu.VMEM((3, len(JUMPS), block, width), bf16),
            pltpu.VMEM((1, EXTRA), f32),
        ),
        in_specs=[VMEM] * 4,
        out_specs=(VMEM, VMEM),
        compiler_params=SMALL,
        name="source",
    )(sums, joined, after, far)

    left = over_y(sources[1, :, :, : width // 2])
    right = over_z(sources[2, :, :, width // 2 :])
    sources2 = over_core(sources)
    factor2 = over_core(factor)

    where = jnp.stack([core] + [lax.axis_index(axis) for axis in CHIPS])
    blocks = weights.reshape(2, chips, block, width)

    def scratch(number):
        return [
            pltpu.VMEM((number, len(JUMPS), block, width), bf16),
            pltpu.SemaphoreType.DMA((number, len(JUMPS))),
        ]

    def mix_and_state(where_ref, weights_ref, sources_ref, sources2_ref, *refs):
        states, (mixed_hbm, *news), room = refs[:6], refs[6:9], refs[9:]
        jobs = [
            (ref.at[number], ref is sources2_ref, number == 1, number == 2)
            for number in range(3)
            for ref in (sources_ref, sources2_ref)
        ]
        mix_kernel(jobs, where_ref, weights_ref, mixed_hbm, *room)
        state_kernel(where_ref[0], *states, *news)

    def mix_last(where_ref, weights_ref, source_ref, source2_ref, _, *refs):
        jobs = [(source_ref, False, True, True), (source2_ref, True, True, True)]
        mix_kernel(jobs, where_ref, weights_ref, *refs)

    state = jax.ShapeDtypeStruct((2, share_rows, width), f32)
    mixed_type = jax.ShapeDtypeStruct(blocks.shape, bf16)
    mixed, outer_next, moment_next = pl.pallas_call(
        mix_and_state,
        out_shape=(mixed_type, state, state),
        in_specs=[SMEM] + [VMEM] * 9,
        out_specs=(ANY, VMEM, VMEM),
        scratch_shapes=scratch(6),
        compiler_params=SMALL,
        name="mix",
    )(
        where,
        blocks,
        sources,
        sources2,
        global_params[:, 0],
        momentum[:, 0],
        factor,
        factor2,
        pick(halves, core),
        pseudo2,
    )
    left, right, mixed = lax.optimization_barrier((left, right, mixed))
    diagonal = jnp.concatenate((left, right), axis=2)
    mixed = pl.pallas_call(
        mix_last,
        out_shape=mixed_type,
        in_specs=[SMEM, VMEM, VMEM, VMEM, ANY],
        out_specs=ANY,
        scratch_shapes=scratch(2),
        input_output_aliases={4: 0},
        compiler_params=SMALL,
        name="mix_last",
    )(where, blocks, diagonal, over_core(diagonal), mixed)
    return (
        mixed.reshape(local_weights.shape),
        outer_next[:, None],
        moment_next[:, None],
    )


def solution(mesh):
    fine = Mesh(
        mesh.devices.reshape(4, 2, 2, 2, 4, 2), ("zh", "zl", "yl", "core", "x", "yh")
    )
    replica, mp = ("zh", "zl", "yl", "core"), ("x", "yh")
    whole = P(None, replica, mp, None, None)
    outer = P(None, mp, replica, None)
    return jax.shard_map(
        shards,
        mesh=fine,
        in_specs=(whole, outer, outer),
        out_specs=(whole, outer, outer),
        check_vma=False,
    )
```

time: 84.9 us -> 79.2 us (0.933)
  blocking collectives: 0 us -> 13.7 us
  starting transfers between devices: 42.3 us -> 31.8 us
  waiting for transfers between devices: 33.9 us -> 25.3 us
  Pallas kernels: 5.06 us -> 6.94 us
  local copies, waits for them, and re-layouts: 1.39 us -> 0.12 us
  other arithmetic: 1.34 us -> 0.27 us
    all_to_all x0 -> x1, blocking collectives: none -> 13.7 us  [shards(): sums = lax.all_to_all(sums, GROUPS, 0, 0, tiled=True)]
    all_to_all x1 -> x0, starting transfers between devices: 12 us -> none  [shards(): sums = lax.all_to_all(sums, EVERYWHERE, 0, 0, tiled=True)]
    all_to_all x1 -> x0, waiting for transfers between devices: 7.49 us -> none  [shards(): sums = lax.all_to_all(sums, EVERYWHERE, 0, 0, tiled=True)]
    pallas_call x0 -> x3, Pallas kernels: none -> 2.39 us  [the longest x1 1.36 us: shards(): pl.pallas_call(cut_kernel, out_shape=pltpu.VMEM((rows, width), bf16), in_...]
    ppermute x15 -> x14, starting transfers between devices: 22.7 us -> 24.1 us  [over(): return lax.ppermute(array, axis, [(i, i ^ jump) for i in range(size)])]
    squeeze x4 -> x3, local copies, waits for them, and re-layouts: 1.35 us -> 0.04 us  [pick(): return lax.dynamic_index_in_dim(array, index, axis, keepdims=False)]
    reshape x1 -> x0, other arithmetic: 1.07 us -> none  [shards(): pair.reshape(chips, block, width)]
    ppermute x15 -> x14, waiting for transfers between devices: 7.7 us -> 6.65 us  [over(): return lax.ppermute(array, axis, [(i, i ^ jump) for i in range(size)])]
  transfers between devices with their start and end apart: 17 -> 15, of which waited for: 10 -> 8; matrix products, arithmetic and copies ran while one was open for 0% -> 0% of each run, Pallas kernels for 3% -> 3%
where the time goes in v7:
time: 79.2 us; the launch traced here: 78.9 us
  starting transfers between devices  31.8 us (40%)
  waiting for transfers between devices  25.3 us (32%)
  blocking collectives  13.7 us (17%)
  Pallas kernels  6.94 us (9%)
  between operations  0.8 us (1%)
    ppermute x14, starting transfers between devices, over(): return lax.ppermute(array, axis, [(i, i ^ jump) for i in range(size)])  24.1 us
    all_to_all x1, waiting for transfers between devices, shards(): lax.all_to_all(pair.reshape(chips, block, width), CHIPS, 0, 0, tiled=True)  18.7 us
    all_to_all x1, blocking collectives, shards(): sums = lax.all_to_all(sums, GROUPS, 0, 0, tiled=True)  13.7 us
    all_to_all x1, starting transfers between devices, shards(): lax.all_to_all(pair.reshape(chips, block, width), CHIPS, 0, 0, tiled=True)  7.71 us
    ppermute x14, waiting for transfers between devices, over(): return lax.ppermute(array, axis, [(i, i ^ jump) for i in range(size)])  6.65 us
    pallas_call x1, Pallas kernels, shards(): pl.pallas_call(mix_and_state, out_shape=(mixed_type, state, state), in_sp...  2.7 us
  transfers between devices with their start and end apart: 15, of which 8 were waited for; matrix products, arithmetic and copies ran while one was open for 0% of the time, Pallas kernels for 3%

profile of v7, /device:TPU:1, one launch (start us, length us, event | category | flops | bytes accessed | tf_op | source)
XLA Modules:
  0.0 78.9 jit_solution(5713215351649402415)
XLA Ops:
  0.6 0.0 copy-start
  0.6 1.4 %cut.1 = bf16[128,3072]{1,0:T(8,128)(2,1)S(1)} custom-call(s32[1]{0:T(128)} %bitcast.6.which_ref, bf16[2,128,3072]{2,1,0:T(8,128)(2,1)} %bitcast.35), custom_call_target="tpu_custom_call" | custom-call | tf_op jit(solution)/shard_map/cut/pallas_call | solution.py:191
  2.0 3.3 %collective-permute-start = (bf16[128,3072]{1,0:T(8,128)(2,1)S(1)}, bf16[128,3072]{1,0:T(8,128)(2,1)S(1)}, u32[]{:S(2)}, u32[]{:S(2)}) collective-permute-start(bf16[128,3072]{1,0:T(8,128)(2,1)S(1)} %cut.1), channel_id=1, source_target_pairs={{0,8},{8,0},{1,9},{9,1},{2,10},{10,2},{3,11},{11,3},{4,12},{12,4},... | collective-permute-start | bytes 2359304 | tf_op jit(solution)/shard_map/ppermute | solution.py:25
  5.3 1.9 %collective-permute-done.got_ref = bf16[128,3072]{1,0:T(8,128)(2,1)S(1)} collective-permute-done((bf16[128,3072]{1,0:T(8,128)(2,1)S(1)}, bf16[128,3072]{1,0:T(8,128)(2,1)S(1)}, u32[]{:S(2)}, u32[]{:S(2)}) %collective-permute-start) | collective-permute-done | bytes 786464 | tf_op jit(solution)/shard_map/ppermute | solution.py:25
  7.3 0.0 copy-done
  7.3 1.0 %pair.1 = bf16[128,3072]{1,0:T(8,128)(2,1)} custom-call(s32[1]{0:T(128)} %bitcast.core_ref, bf16[2,128,3072]{2,1,0:T(8,128)(2,1)S(1)} %bitcast.36, bf16[128,3072]{1,0:T(8,128)(2,1)S(1)} %collective-permute-done.got_ref), custom_call_target="tpu_custom_call" | custom-call | tf_op jit(solution)/shard_map/pair/pallas_call | solution.py:200
  8.2 0.0 copy-start.1
  8.2 0.0 copy-start.2
  8.2 7.7 %all-to-all-start = ((bf16[16,8,3072]{2,1,0:T(8,128)(2,1)}), bf16[16,8,3072]{2,1,0:T(8,128)(2,1)S(1)}, u32[]{:S(2)}, u32[]{:S(2)}) async-start(bf16[16,8,3072]{2,1,0:T(8,128)(2,1)} %bitcast.7), calls=%async_computation | async-start | bytes 1572864 | tf_op jit(solution)/shard_map/all_to_all | solution.py:212
  16.0 0.0 copy-done.1
  16.0 0.7 collective-permute-start.1
  16.7 0.0 copy-done.2
  16.8 0.1 collective-permute-start.2
  16.9 0.7 collective-permute-done.1
  17.7 0.4 collective-permute-done.2
  18.1 18.7 %all-to-all-done = bf16[16,8,3072]{2,1,0:T(8,128)(2,1)S(1)} async-done(((bf16[16,8,3072]{2,1,0:T(8,128)(2,1)}), bf16[16,8,3072]{2,1,0:T(8,128)(2,1)S(1)}, u32[]{:S(2)}, u32[]{:S(2)}) %all-to-all-start) | async-done | bytes 786464 | tf_op jit(solution)/shard_map/all_to_all | solution.py:212
  36.8 0.1 convert_reduce_fusion.total_ref
  36.9 0.2 total.1
  37.1 2.4 %collective-permute-start.5 = (bf16[2,8,3200]{2,1,0:T(8,128)(2,1)S(1)}, bf16[2,8,3200]{2,1,0:T(8,128)(2,1)S(1)}, u32[]{:S(2)}, u32[]{:S(2)}) collective-permute-start(bf16[2,8,3200]{2,1,0:T(8,128)(2,1)S(1)} %get-tuple-element.22.refs_0_), channel_id=1, source_target_pairs={{0,192},{64,128},{128,64},{192,0},{1,193},{65,129},{129,65},{193,1... | collective-permute-start | bytes 307208 | tf_op jit(solution)/shard_map/ppermute | solution.py:25
  39.4 1.4 %collective-permute-start.4 = (bf16[2,8,3200]{2,1,0:T(8,128)(2,1)S(1)}, bf16[2,8,3200]{2,1,0:T(8,128)(2,1)S(1)}, u32[]{:S(2)}, u32[]{:S(2)}) collective-permute-start(bf16[2,8,3200]{2,1,0:T(8,128)(2,1)S(1)} %get-tuple-element.22.refs_0_), channel_id=1, source_target_pairs={{0,64},{64,0},{128,192},{192,128},{1,65},{65,1},{129,193},{193,129... | collective-permute-start | bytes 307208 | tf_op jit(solution)/shard_map/ppermute | solution.py:25
  40.8 2.2 %collective-permute-start.3 = (bf16[2,8,3200]{2,1,0:T(8,128)(2,1)S(1)}, bf16[2,8,3200]{2,1,0:T(8,128)(2,1)S(1)}, u32[]{:S(2)}, u32[]{:S(2)}) collective-permute-start(bf16[2,8,3200]{2,1,0:T(8,128)(2,1)S(1)} %get-tuple-element.22.refs_0_), channel_id=1, source_target_pairs={{0,128},{64,192},{128,0},{192,64},{1,129},{65,193},{129,1},{193,65... | collective-permute-start | bytes 307208 | tf_op jit(solution)/shard_map/ppermute | solution.py:25
  43.0 4.2 %collective-permute-start.6 = (f32[4,3072]{1,0:T(4,128)S(1)}, f32[4,3072]{1,0:T(4,128)S(1)}, u32[]{:S(2)}, u32[]{:S(2)}) collective-permute-start(f32[4,3072]{1,0:T(4,128)S(1)} %get-tuple-element.43), channel_id=1, source_target_pairs={{0,8},{8,0},{1,9},{9,1},{2,10},{10,2},{3,11},{11,3},{4,12},{12,4},... | collective-permute-start | bytes 147464 | tf_op jit(solution)/shard_map/ppermute | solution.py:25
  47.2 0.9 %collective-permute-done.6.refs_5_ = f32[4,3072]{1,0:T(4,128)S(1)} collective-permute-done((f32[4,3072]{1,0:T(4,128)S(1)}, f32[4,3072]{1,0:T(4,128)S(1)}, u32[]{:S(2)}, u32[]{:S(2)}) %collective-permute-start.6) | collective-permute-done | bytes 49184 | tf_op jit(solution)/shard_map/ppermute | solution.py:25
  48.1 0.0 collective-permute-done.5.refs_3_
  48.1 0.0 collective-permute-done.4.refs_2_
  48.1 0.9 %collective-permute-done.3.refs_1_ = bf16[2,8,3200]{2,1,0:T(8,128)(2,1)S(1)} collective-permute-done((bf16[2,8,3200]{2,1,0:T(8,128)(2,1)S(1)}, bf16[2,8,3200]{2,1,0:T(8,128)(2,1)S(1)}, u32[]{:S(2)}, u32[]{:S(2)}) %collective-permute-start.3) | collective-permute-done | bytes 102432 | tf_op jit(solution)/shard_map/ppermute | solution.py:25
  49.0 0.1 join.1
  49.1 1.2 %collective-permute-start.8 = (bf16[4,2,8,3072]{3,2,1,0:T(8,128)(2,1)S(1)}, bf16[4,2,8,3072]{3,2,1,0:T(8,128)(2,1)S(1)}, u32[]{:S(2)}, u32[]{:S(2)}) collective-permute-start(bf16[4,2,8,3072]{3,2,1,0:T(8,128)(2,1)S(1)} %get-tuple-element.27.refs_0_), channel_id=1, source_target_pairs={{0,16},{16,0},{1,17},{17,1},{2,18},{18,2},{3,19},{19,3},{4,20},{20... | collective-permute-start | bytes 1179656 | tf_op jit(solution)/shard_map/ppermute | solution.py:25
  50.3 2.1 %collective-permute-start.7 = (bf16[4,2,8,3072]{3,2,1,0:T(8,128)(2,1)S(1)}, bf16[4,2,8,3072]{3,2,1,0:T(8,128)(2,1)S(1)}, u32[]{:S(2)}, u32[]{:S(2)}) collective-permute-start(bf16[4,2,8,3072]{3,2,1,0:T(8,128)(2,1)S(1)} %get-tuple-element.27.refs_0_), channel_id=1, source_target_pairs={{0,32},{32,0},{1,33},{33,1},{2,34},{34,2},{3,35},{35,3},{4,36},{36... | collective-permute-start | bytes 1179656 | tf_op jit(solution)/shard_map/ppermute | solution.py:25
  52.4 13.7 %all_to_all.10.sums_ref = f32[32,1,128]{2,1,0:T(1,128)S(1)} all-to-all(f32[32,1,128]{2,1,0:T(1,128)S(1)} %get-tuple-element.26), channel_id=1, replica_groups=mesh['zh'=4,'zl'=2,'yl'=2,'core'=2,'x'=4,'yh'=2] {'zl','yl','x','yh'}, dimensions={0} | all-to-all | bytes 32768 | tf_op jit(solution)/shard_map/all_to_all | solution.py:248
  66.1 0.0 collective-permute-done.8.refs_2_
  66.1 0.0 collective-permute-done.7.refs_1_
  66.1 0.3 source.1
  66.4 4.2 %collective-permute-start.11 = (bf16[3,4,8,3072]{3,2,1,0:T(8,128)(2,1)S(1)}, bf16[3,4,8,3072]{3,2,1,0:T(8,128)(2,1)S(1)}, u32[]{:S(2)}, u32[]{:S(2)}) collective-permute-start(bf16[3,4,8,3072]{3,2,1,0:T(8,128)(2,1)S(1)} %get-tuple-element.28.sources_ref), channel_id=1, source_target_pairs={{0,8},{8,0},{1,9},{9,1},{2,10},{10,2},{3,11},{11,3},{4,12},{12,4},... | collective-permute-start | bytes 1769480 | tf_op jit(solution)/shard_map/ppermute | solution.py:25
  70.5 0.1 collective-permute-start.12
  70.7 0.4 collective-permute-start.10
  71.1 0.3 collective-permute-start.9
  71.4 0.1 pad_add_fusion.where_ref
  71.5 0.7 collective-permute-done.12.refs_3_
  72.2 0.0 collective-permute-done.11.sources2_ref
  72.2 2.7 %mix.1 = (bf16[2,16,8,3072]{3,2,1,0:T(8,128)(2,1)}, f32[2,4,3072]{2,1,0:T(4,128)}, f32[2,4,3072]{2,1,0:T(4,128)}) custom-call(s32[4]{0:T(128)S(1)} %pad_add_fusion.where_ref, bf16[2,16,8,3072]{3,2,1,0:T(8,128)(2,1)S(1)} %bitcast.37, bf16[3,4,8,3072]{3,2,1,0:T(8,128)(2,1)S(1)} %get-tuple-element.28.sources_ref, ...), custom_call_target="tpu_custom_call" | custom-call | tf_op jit(solution)/shard_map/mix/pallas_call | solution.py:293
  74.9 0.0 collective-permute-done.10
  74.9 0.0 collective-permute-done.9
  74.9 1.5 %collective-permute-start.13 = (bf16[4,8,3072]{2,1,0:T(8,128)(2,1)S(1)}, bf16[4,8,3072]{2,1,0:T(8,128)(2,1)S(1)}, u32[]{:S(2)}, u32[]{:S(2)}) collective-permute-start(bf16[4,8,3072]{2,1,0:T(8,128)(2,1)S(1)} %constant_dynamic-update-slice_fusion.source_ref), channel_id=1, source_target_pairs={{0,8},{8,0},{1,9},{9,1},{2,10},{10,2},{3,11},{11,3},{4,12},{12,4},... | collective-permute-start | bytes 589832 | tf_op jit(solution)/shard_map/ppermute | solution.py:25
  76.5 1.1 %collective-permute-done.13.source2_ref = bf16[4,8,3072]{2,1,0:T(8,128)(2,1)S(1)} collective-permute-done((bf16[4,8,3072]{2,1,0:T(8,128)(2,1)S(1)}, bf16[4,8,3072]{2,1,0:T(8,128)(2,1)S(1)}, u32[]{:S(2)}, u32[]{:S(2)}) %collective-permute-start.13) | collective-permute-done | bytes 196640 | tf_op jit(solution)/shard_map/ppermute | solution.py:25
  77.5 1.4 %mix_last.1 = bf16[2,16,8,3072]{3,2,1,0:T(8,128)(2,1)} custom-call(s32[4]{0:T(128)S(1)} %pad_add_fusion.where_ref, bf16[2,16,8,3072]{3,2,1,0:T(8,128)(2,1)S(1)} %bitcast.38, bf16[4,8,3072]{2,1,0:T(8,128)(2,1)S(1)} %constant_dynamic-update-slice_fusion.source_ref, ...), custom_call_target="tpu_custom_call", output_to_operand_aliasing={{}: (4, {})} | custom-call | tf_op jit(solution)/shard_map/mix_last/pallas_call | solution.py:315
  (9 shorter events, 0.2 us)
Async XLA Ops:
  0.6 6.6 %copy-start = (bf16[2,1,1,128,3072]{4,3,2,1,0:T(8,128)(2,1)S(1)}, bf16[2,1,1,128,3072]{4,3,2,1,0:T(8,128)(2,1)}, u32[]{:S(2)}) copy-start(bf16[2,1,1,128,3072]{4,3,2,1,0:T(8,128)(2,1)} %param.3) | copy-start | bytes 4718596
  2.0 5.2 %collective-permute-start = (bf16[128,3072]{1,0:T(8,128)(2,1)S(1)}, bf16[128,3072]{1,0:T(8,128)(2,1)S(1)}, u32[]{:S(2)}, u32[]{:S(2)}) collective-permute-start(bf16[128,3072]{1,0:T(8,128)(2,1)S(1)} %cut.1), channel_id=1, source_target_pairs={{0,8},{8,0},{1,9},{9,1},{2,10},{10,2},{3,11},{11,3},{4,12},{12,4},... | collective-permute-start | bytes 2359304 | tf_op jit(solution)/shard_map/ppermute | solution.py:25
  8.2 7.7 %copy-start.1 = (f32[2,1,4,3072]{3,2,1,0:T(4,128)S(1)}, f32[2,1,4,3072]{3,2,1,0:T(4,128)}, u32[]{:S(2)}) copy-start(f32[2,1,4,3072]{3,2,1,0:T(4,128)} %param.4) | copy-start | bytes 294916
  8.2 8.5 %copy-start.2 = (f32[2,1,4,3072]{3,2,1,0:T(4,128)S(1)}, f32[2,1,4,3072]{3,2,1,0:T(4,128)}, u32[]{:S(2)}) copy-start(f32[2,1,4,3072]{3,2,1,0:T(4,128)} %param.5) | copy-start | bytes 294916
  8.2 28.5 %all-to-all-start = ((bf16[16,8,3072]{2,1,0:T(8,128)(2,1)}), bf16[16,8,3072]{2,1,0:T(8,128)(2,1)S(1)}, u32[]{:S(2)}, u32[]{:S(2)}) async-start(bf16[16,8,3072]{2,1,0:T(8,128)(2,1)} %bitcast.7), calls=%async_computation | async-start | bytes 1572864 | tf_op jit(solution)/shard_map/all_to_all | solution.py:212
  16.0 1.6 %collective-permute-start.1 = (f32[4,3072]{1,0:T(4,128)S(1)}, f32[4,3072]{1,0:T(4,128)S(1)}, u32[]{:S(2)}, u32[]{:S(2)}) collective-permute-start(f32[4,3072]{1,0:T(4,128)S(1)} %get-tuple-element.47), channel_id=1, source_target_pairs={{0,8},{8,0},{1,9},{9,1},{2,10},{10,2},{3,11},{11,3},{4,12},{12,4},... | collective-permute-start | bytes 147464 | tf_op jit(solution)/shard_map/ppermute | solution.py:25
  16.8 1.3 %collective-permute-start.2 = (f32[4,3072]{1,0:T(4,128)S(1)}, f32[4,3072]{1,0:T(4,128)S(1)}, u32[]{:S(2)}, u32[]{:S(2)}) collective-permute-start(f32[4,3072]{1,0:T(4,128)S(1)} %get-tuple-element.45), channel_id=1, source_target_pairs={{0,8},{8,0},{1,9},{9,1},{2,10},{10,2},{3,11},{11,3},{4,12},{12,4},... | collective-permute-start | bytes 147464 | tf_op jit(solution)/shard_map/ppermute | solution.py:25
  37.1 11.0 %collective-permute-start.5 = (bf16[2,8,3200]{2,1,0:T(8,128)(2,1)S(1)}, bf16[2,8,3200]{2,1,0:T(8,128)(2,1)S(1)}, u32[]{:S(2)}, u32[]{:S(2)}) collective-permute-start(bf16[2,8,3200]{2,1,0:T(8,128)(2,1)S(1)} %get-tuple-element.22.refs_0_), channel_id=1, source_target_pairs={{0,192},{64,128},{128,64},{192,0},{1,193},{65,129},{129,65},{193,1... | collective-permute-start | bytes 307208 | tf_op jit(solution)/shard_map/ppermute | solution.py:25
  39.4 8.7 %collective-permute-start.4 = (bf16[2,8,3200]{2,1,0:T(8,128)(2,1)S(1)}, bf16[2,8,3200]{2,1,0:T(8,128)(2,1)S(1)}, u32[]{:S(2)}, u32[]{:S(2)}) collective-permute-start(bf16[2,8,3200]{2,1,0:T(8,128)(2,1)S(1)} %get-tuple-element.22.refs_0_), channel_id=1, source_target_pairs={{0,64},{64,0},{128,192},{192,128},{1,65},{65,1},{129,193},{193,129... | collective-permute-start | bytes 307208 | tf_op jit(solution)/shard_map/ppermute | solution.py:25
  40.8 8.2 %collective-permute-start.3 = (bf16[2,8,3200]{2,1,0:T(8,128)(2,1)S(1)}, bf16[2,8,3200]{2,1,0:T(8,128)(2,1)S(1)}, u32[]{:S(2)}, u32[]{:S(2)}) collective-permute-start(bf16[2,8,3200]{2,1,0:T(8,128)(2,1)S(1)} %get-tuple-element.22.refs_0_), channel_id=1, source_target_pairs={{0,128},{64,192},{128,0},{192,64},{1,129},{65,193},{129,1},{193,65... | collective-permute-start | bytes 307208 | tf_op jit(solution)/shard_map/ppermute | solution.py:25
  43.0 5.1 %collective-permute-start.6 = (f32[4,3072]{1,0:T(4,128)S(1)}, f32[4,3072]{1,0:T(4,128)S(1)}, u32[]{:S(2)}, u32[]{:S(2)}) collective-permute-start(f32[4,3072]{1,0:T(4,128)S(1)} %get-tuple-element.43), channel_id=1, source_target_pairs={{0,8},{8,0},{1,9},{9,1},{2,10},{10,2},{3,11},{11,3},{4,12},{12,4},... | collective-permute-start | bytes 147464 | tf_op jit(solution)/shard_map/ppermute | solution.py:25
  49.1 17.0 %collective-permute-start.8 = (bf16[4,2,8,3072]{3,2,1,0:T(8,128)(2,1)S(1)}, bf16[4,2,8,3072]{3,2,1,0:T(8,128)(2,1)S(1)}, u32[]{:S(2)}, u32[]{:S(2)}) collective-permute-start(bf16[4,2,8,3072]{3,2,1,0:T(8,128)(2,1)S(1)} %get-tuple-element.27.refs_0_), channel_id=1, source_target_pairs={{0,16},{16,0},{1,17},{17,1},{2,18},{18,2},{3,19},{19,3},{4,20},{20... | collective-permute-start | bytes 1179656 | tf_op jit(solution)/shard_map/ppermute | solution.py:25
  50.3 15.8 %collective-permute-start.7 = (bf16[4,2,8,3072]{3,2,1,0:T(8,128)(2,1)S(1)}, bf16[4,2,8,3072]{3,2,1,0:T(8,128)(2,1)S(1)}, u32[]{:S(2)}, u32[]{:S(2)}) collective-permute-start(bf16[4,2,8,3072]{3,2,1,0:T(8,128)(2,1)S(1)} %get-tuple-element.27.refs_0_), channel_id=1, source_target_pairs={{0,32},{32,0},{1,33},{33,1},{2,34},{34,2},{3,35},{35,3},{4,36},{36... | collective-permute-start | bytes 1179656 | tf_op jit(solution)/shard_map/ppermute | solution.py:25
  66.4 5.8 %collective-permute-start.11 = (bf16[3,4,8,3072]{3,2,1,0:T(8,128)(2,1)S(1)}, bf16[3,4,8,3072]{3,2,1,0:T(8,128)(2,1)S(1)}, u32[]{:S(2)}, u32[]{:S(2)}) collective-permute-start(bf16[3,4,8,3072]{3,2,1,0:T(8,128)(2,1)S(1)} %get-tuple-element.28.sources_ref), channel_id=1, source_target_pairs={{0,8},{8,0},{1,9},{9,1},{2,10},{10,2},{3,11},{11,3},{4,12},{12,4},... | collective-permute-start | bytes 1769480 | tf_op jit(solution)/shard_map/ppermute | solution.py:25
  70.5 1.6 %collective-permute-start.12 = (f32[1,128]{1,0:T(1,128)S(1)}, f32[1,128]{1,0:T(1,128)S(1)}, u32[]{:S(2)}, u32[]{:S(2)}) collective-permute-start(f32[1,128]{1,0:T(1,128)S(1)} %get-tuple-element.29.refs_2_), channel_id=1, source_target_pairs={{0,8},{8,0},{1,9},{9,1},{2,10},{10,2},{3,11},{11,3},{4,12},{12,4},... | collective-permute-start | bytes 1544 | tf_op jit(solution)/shard_map/ppermute | solution.py:25
  70.7 4.2 %collective-permute-start.10 = (bf16[4,8,1536]{2,1,0:T(8,128)(2,1)S(1)}, bf16[4,8,1536]{2,1,0:T(8,128)(2,1)S(1)}, u32[]{:S(2)}, u32[]{:S(2)}) collective-permute-start(bf16[4,8,1536]{2,1,0:T(8,128)(2,1)S(1)} %get-tuple-element.40), channel_id=1, source_target_pairs={{0,32},{32,0},{1,33},{33,1},{2,34},{34,2},{3,35},{35,3},{4,36},{36... | collective-permute-start | bytes 294920 | tf_op jit(solution)/shard_map/ppermute | solution.py:25
  71.1 3.8 %collective-permute-start.9 = (bf16[4,8,1536]{2,1,0:T(8,128)(2,1)S(1)}, bf16[4,8,1536]{2,1,0:T(8,128)(2,1)S(1)}, u32[]{:S(2)}, u32[]{:S(2)}) collective-permute-start(bf16[4,8,1536]{2,1,0:T(8,128)(2,1)S(1)} %get-tuple-element.41), channel_id=1, source_target_pairs={{0,16},{16,0},{1,17},{17,1},{2,18},{18,2},{3,19},{19,3},{4,20},{20... | collective-permute-start | bytes 294920 | tf_op jit(solution)/shard_map/ppermute | solution.py:25
  74.9 2.6 %collective-permute-start.13 = (bf16[4,8,3072]{2,1,0:T(8,128)(2,1)S(1)}, bf16[4,8,3072]{2,1,0:T(8,128)(2,1)S(1)}, u32[]{:S(2)}, u32[]{:S(2)}) collective-permute-start(bf16[4,8,3072]{2,1,0:T(8,128)(2,1)S(1)} %constant_dynamic-update-slice_fusion.source_ref), channel_id=1, source_target_pairs={{0,8},{8,0},{1,9},{9,1},{2,10},{10,2},{3,11},{11,3},{4,12},{12,4},... | collective-permute-start | bytes 589832 | tf_op jit(solution)/shard_map/ppermute | solution.py:25

commit v8 on v7

--- a/solution.py
+++ b/solution.py
@@ -52,39 +52,80 @@
         copy.wait()
 
 
-def pair_kernel(core_ref, weights_ref, got_ref, pair_hbm, pair_ref, sems):
-    step = got_ref.shape[0] // PARTS
-    copies = []
-    for part in range(PARTS):
-        some = pl.ds(part * step, step)
-        own = weights_ref[core_ref[0], some].astype(jnp.float32)
-        pair = own + got_ref[some].astype(jnp.float32)
-        pair_ref[some] = pair.astype(jnp.bfloat16)
-        copies.append(
-            pltpu.make_async_copy(
-                pair_ref.at[some], pair_hbm.at[some], sems.at[part]
+def pair_of(weights_ref, got_ref, core, at, columns):
+    own = weights_ref[(core, *at)][:, columns].astype(jnp.float32)
+    return own + got_ref[at][:, columns].astype(jnp.float32)
+
+
+def first_kernel(where_ref, weights_ref, got_ref, left_ref, right_ref):
+    core, zl, yl = where_ref[0], where_ref[2], where_ref[3]
+    half = left_ref.shape[3]
+    for zh in range(4):
+        for bit in range(2):
+            pair = pair_of(weights_ref, got_ref, core, (zh, bit, 1 - yl), slice(0, half))
+            left_ref[zh, bit] = pair.astype(jnp.bfloat16)
+            pair = pair_of(
+                weights_ref, got_ref, core, (zh, 1 - zl, bit), slice(half, None)
             )
-        )
-        copies[-1].start()
-    for copy in copies:
-        copy.wait()
-
-
-def total_kernel(replicas, total_ref, outer_ref, moment_ref, pseudo_ref, pack_ref):
+            right_ref[zh, bit] = pair.astype(jnp.bfloat16)
+
+
+def second_kernel(where_ref, weights_ref, got_ref, left_ref, right_ref, left2_ref, right2_ref):
+    core, zl, yl = where_ref[0], where_ref[2], where_ref[3]
+    half = left_ref.shape[3]
+    for zh in range(4):
+        pair = pair_of(weights_ref, got_ref, core, (zh, 1 - zl, yl), slice(0, half))
+        quad = pair + left_ref[zh, 1 - zl].astype(jnp.float32)
+        left2_ref[zh] = quad.astype(jnp.bfloat16)
+        pair = pair_of(weights_ref, got_ref, core, (zh, zl, 1 - yl), slice(half, None))
+        quad = pair + right_ref[zh, 1 - yl].astype(jnp.float32)
+        right2_ref[zh] = quad.astype(jnp.bfloat16)
+
+
+def third_kernel(
+    where_ref, weights_ref, got_ref, left_ref, right_ref, left2_ref, right2_ref, *outs
+):
+    core, zh, zl, yl = (where_ref[i] for i in range(4))
+    half = left_ref.shape[3]
+    for jump, out_ref in zip(JUMPS, outs):
+        to = zh ^ jump
+        at = (to, zl, yl)
+        left = pair_of(weights_ref, got_ref, core, at, slice(0, half))
+        left += left_ref[to, zl].astype(jnp.float32)
+        left += left2_ref[to].astype(jnp.float32)
+        right = pair_of(weights_ref, got_ref, core, at, slice(half, None))
+        right += right_ref[to, yl].astype(jnp.float32)
+        right += right2_ref[to].astype(jnp.float32)
+        out_ref[:, :half] = left.astype(out_ref.dtype)
+        out_ref[:, half:] = right.astype(out_ref.dtype)
+
+
+def split_lines(value, rows):
+    high = value.astype(jnp.bfloat16).astype(jnp.float32)
+    middle = (value - high).astype(jnp.bfloat16).astype(jnp.float32)
+    low = value - high - middle
+    row = lax.broadcasted_iota(jnp.int32, (rows, EXTRA), 0)
+    lines = jnp.where(row == 0, high, jnp.where(row == 1, middle, low))
+    return jnp.where(row < 3, lines, 0.0).astype(jnp.bfloat16)
+
+
+def joined_lines(lines):
+    return jnp.sum(lines.astype(jnp.float32), axis=0, keepdims=True)
+
+
+def total_kernel(replicas, outer_ref, moment_ref, own_ref, *refs):
+    pseudo_ref, pack_ref = refs[-2:]
     outer = outer_ref[...]
     width = outer.shape[1]
-    pseudo = outer - total_ref[...] / replicas
+    total = own_ref[...]
+    for ref in refs[:-2]:
+        total += ref[...].astype(jnp.float32)
+    pseudo = outer - total / replicas
     pseudo_ref[...] = pseudo
     pack_ref[0, :, :width] = (outer - 0.567 * moment_ref[...]).astype(jnp.bfloat16)
     pack_ref[1, :, :width] = (1.33 * pseudo).astype(jnp.bfloat16)
     square_sum = jnp.sum(jnp.sum(pseudo * pseudo, axis=0, keepdims=True), keepdims=True)
-    high = square_sum.astype(jnp.bfloat16).astype(jnp.float32)
-    middle = (square_sum - high).astype(jnp.bfloat16).astype(jnp.float32)
-    low = square_sum - high - middle
-    shape = (outer.shape[0], EXTRA)
-    row = lax.broadcasted_iota(jnp.int32, shape, 0)
-    lines = jnp.where(row == 0, high, jnp.where(row == 1, middle, low))
-    lines = jnp.where(row < 3, lines, 0.0).astype(jnp.bfloat16)
+    lines = split_lines(square_sum, outer.shape[0])
     pack_ref[0, :, width:] = lines
     pack_ref[1, :, width:] = lines
 
@@ -93,10 +134,8 @@
     pack_refs = refs[: len(JUMPS)]
     joined_ref, sums_hbm, sums_ref, sem = refs[len(JUMPS) :]
     width = joined_ref.shape[3]
-    lines = sum(ref[0, :, width:].astype(jnp.float32) for ref in pack_refs)
-    sums_ref[...] = jnp.broadcast_to(
-        jnp.sum(lines, axis=0, keepdims=True)[None], sums_ref.shape
-    )
+    square_sum = sum(joined_lines(ref[0, :, width:]) for ref in pack_refs)
+    sums_ref[...] = jnp.broadcast_to(square_sum[None], sums_ref.shape)
     copy = pltpu.make_async_copy(sums_ref, sums_hbm, sem)
     copy.start()
     for place, ref in enumerate(pack_refs):
@@ -105,34 +144,38 @@
 
 
 def source_kernel(max_norm, sums_ref, *refs):
-    joined_refs, (source_ref, factor_ref) = refs[:-2], refs[-2:]
-    square_sum = jnp.sum(sums_ref[:, 0, :], axis=0, keepdims=True)
+    joined_refs, source_ref = refs[:-1], refs[-1]
+    rows, width = joined_refs[0].shape[2:]
+    square_sum = jnp.sum(sums_ref[:, 0, :1], axis=0, keepdims=True)
     factor = jnp.minimum(1.0, max_norm / (jnp.sqrt(square_sum) + 1e-06))
-    factor_ref[...] = factor
+    lines = split_lines(factor, rows)
     for number, joined_ref in enumerate(joined_refs):
         for place in range(len(JUMPS)):
             base = joined_ref[place, 0].astype(jnp.float32)
             push = joined_ref[place, 1].astype(jnp.float32)
-            source = base - factor[:, :1] * push
-            source_ref[number, place] = source.astype(jnp.bfloat16)
+            source = base - factor * push
+            source_ref[number, place, :, :width] = source.astype(jnp.bfloat16)
+            source_ref[number, place, :, width:] = lines
 
 
 def state_kernel(
     core,
+    sources_ref,
+    sources2_ref,
     outer_ref,
     moment_ref,
-    factor_ref,
-    factor2_ref,
     pseudo_ref,
     pseudo2_ref,
     new_outer_ref,
     new_moment_ref,
 ):
-    for frag, scale_ref, rows_ref in (
-        (core, factor_ref, pseudo_ref),
-        (1 - core, factor2_ref, pseudo2_ref),
+    width = pseudo_ref.shape[1]
+    for frag, lines_ref, rows_ref in (
+        (core, sources_ref, pseudo_ref),
+        (1 - core, sources2_ref, pseudo2_ref),
     ):
-        clipped = scale_ref[:, :1] * rows_ref[...]
+        factor = joined_lines(lines_ref[0, 0, :, width:])[:, :1]
+        clipped = factor * rows_ref[...]
         moment = 0.9 * moment_ref[frag] + clipped
         new_moment_ref[frag] = moment
         new_outer_ref[frag] = outer_ref[frag] - 0.7 * (clipped + 0.9 * moment)
@@ -148,7 +191,7 @@
         for k, jump in enumerate(JUMPS):
             chip = 4 * (zh ^ jump) + low
             own = weights_ref[frag, chip].astype(jnp.float32)
-            source = source_ref[k].astype(jnp.float32)
+            source = source_ref[k, :, : own.shape[1]].astype(jnp.float32)
             mixed_ref[number, k] = (0.5 * own + 0.5 * source).astype(jnp.bfloat16)
             stores.append(
                 pltpu.make_async_copy(
@@ -197,32 +240,51 @@
         compiler_params=SMALL,
         name="cut",
     )(other[None], pltpu.with_memory_space_constraint(weights, pltpu.HBM))
-    pair = pl.pallas_call(
-        pair_kernel,
-        out_shape=jax.ShapeDtypeStruct((rows, width), bf16),
-        in_specs=[SMEM, VMEM, VMEM],
-        out_specs=ANY,
-        scratch_shapes=[
-            pltpu.VMEM((rows, width), bf16),
-            pltpu.SemaphoreType.DMA((PARTS,)),
-        ],
-        compiler_params=SMALL,
-        name="pair",
-    )(core[None], weights, over_core(sent))
-    pieces = lax.all_to_all(
-        pair.reshape(chips, block, width), CHIPS, 0, 0, tiled=True
-    )
+    where = jnp.stack([core] + [lax.axis_index(axis) for axis in CHIPS])
+    sizes = tuple(lax.axis_size(axis) for axis in CHIPS)
+    half = width // 2
+    spread = weights.reshape(2, *sizes, block, width)
+    got = over_core(sent).reshape(*sizes, block, width)
+
+    def reduced(kernel, outs, *given):
+        return pl.pallas_call(
+            kernel,
+            out_shape=outs,
+            in_specs=[SMEM] + [VMEM] * (2 + len(given)),
+            out_specs=(VMEM,) * len(outs),
+            compiler_params=SMALL,
+            name="reduced",
+        )(where, spread, got, *given)
+
+    left, right = reduced(
+        first_kernel, (pltpu.VMEM((sizes[0], 2, block, half), bf16),) * 2
+    )
+    left, right = over_y(left), over_z(right)
+    left2, right2 = reduced(
+        second_kernel, (pltpu.VMEM((sizes[0], block, half), bf16),) * 2, left, right
+    )
+    left2, right2 = over_z(left2), over_y(right2)
+    own, *sums = reduced(
+        third_kernel,
+        (pltpu.VMEM((block, width), f32),)
+        + (pltpu.VMEM((block, width), bf16),) * (len(JUMPS) - 1),
+        left,
+        right,
+        left2,
+        right2,
+    )
+    sums = [over("zh", 4, jump, one) for jump, one in zip(JUMPS[1:], sums)]
     pseudo, pack = pl.pallas_call(
         functools.partial(total_kernel, replicas),
         out_shape=(
             pltpu.VMEM((block, width), f32),
             pltpu.VMEM((2, block, width + EXTRA), bf16),
         ),
-        in_specs=[VMEM] * 3,
+        in_specs=[VMEM] * (2 + len(JUMPS)),
         out_specs=(VMEM, VMEM),
         compiler_params=SMALL,
         name="total",
-    )(jnp.sum(pieces.astype(f32), axis=0), outer, moment)
+    )(outer, moment, own, *sums)
     halves = pseudo.reshape(2, share_rows, width)
     pseudo2 = over_core(pick(halves, other))
 
@@ -248,24 +310,19 @@
     sums = lax.all_to_all(sums, GROUPS, 0, 0, tiled=True)
     after = over_z(joined)
     far = over_y(joined)
-    sources, factor = pl.pallas_call(
+    sources = pl.pallas_call(
         functools.partial(source_kernel, max_norm),
-        out_shape=(
-            pltpu.VMEM((3, len(JUMPS), block, width), bf16),
-            pltpu.VMEM((1, EXTRA), f32),
-        ),
+        out_shape=pltpu.VMEM((3, len(JUMPS), block, width + EXTRA), bf16),
         in_specs=[VMEM] * 4,
-        out_specs=(VMEM, VMEM),
+        out_specs=VMEM,
         compiler_params=SMALL,
         name="source",
     )(sums, joined, after, far)
 
     left = over_y(sources[1, :, :, : width // 2])
-    right = over_z(sources[2, :, :, width // 2 :])
+    right = over_z(sources[2, :, :, width // 2 : width])
     sources2 = over_core(sources)
-    factor2 = over_core(factor)
-
-    where = jnp.stack([core] + [lax.axis_index(axis) for axis in CHIPS])
+
     blocks = weights.reshape(2, chips, block, width)
 
     def scratch(number):
@@ -275,14 +332,14 @@
         ]
 
     def mix_and_state(where_ref, weights_ref, sources_ref, sources2_ref, *refs):
-        states, (mixed_hbm, *news), room = refs[:6], refs[6:9], refs[9:]
+        states, (mixed_hbm, *news), room = refs[:4], refs[4:7], refs[7:]
         jobs = [
             (ref.at[number], ref is sources2_ref, number == 1, number == 2)
             for number in range(3)
             for ref in (sources_ref, sources2_ref)
         ]
         mix_kernel(jobs, where_ref, weights_ref, mixed_hbm, *room)
-        state_kernel(where_ref[0], *states, *news)
+        state_kernel(where_ref[0], sources_ref, sources2_ref, *states, *news)
 
     def mix_last(where_ref, weights_ref, source_ref, source2_ref, _, *refs):
         jobs = [(source_ref, False, True, True), (source2_ref, True, True, True)]
@@ -293,7 +350,7 @@
     mixed, outer_next, moment_next = pl.pallas_call(
         mix_and_state,
         out_shape=(mixed_type, state, state),
-        in_specs=[SMEM] + [VMEM] * 9,
+        in_specs=[SMEM] + [VMEM] * 7,
         out_specs=(ANY, VMEM, VMEM),
         scratch_shapes=scratch(6),
         compiler_params=SMALL,
@@ -305,8 +362,6 @@
         sources2,
         global_params[:, 0],
         momentum[:, 0],
-        factor,
-        factor2,
         pick(halves, core),
         pseudo2,
     )

time: 79.2 us -> 74.6 us (0.942)
  waiting for transfers between devices: 25.3 us -> 16.1 us
  starting transfers between devices: 31.8 us -> 33.2 us
  Pallas kernels: 6.94 us -> 7.96 us
  blocking collectives: 13.7 us -> 14.5 us
    all_to_all x1 -> x0, waiting for transfers between devices: 18.7 us -> none  [shards(): lax.all_to_all(pair.reshape(chips, block, width), CHIPS, 0, 0, tiled=True)]
    ppermute x14 -> x20, waiting for transfers between devices: 6.65 us -> 16.1 us  [over(): return lax.ppermute(array, axis, [(i, i ^ jump) for i in range(size)])]
    ppermute x14 -> x20, starting transfers between devices: 24.1 us -> 33.2 us  [over(): return lax.ppermute(array, axis, [(i, i ^ jump) for i in range(size)])]
    all_to_all x1 -> x0, starting transfers between devices: 7.71 us -> none  [shards(): lax.all_to_all(pair.reshape(chips, block, width), CHIPS, 0, 0, tiled=True)]
    pallas_call x2 -> x4, Pallas kernels: 1.23 us -> 2.19 us  [the longest x3 1.91 us: reduced(): pl.pallas_call(kernel, out_shape=outs, in_specs=[SMEM] + [VMEM] * (2 + le...]
    select_n x2, other arithmetic: 0.08 us -> 0.96 us  [swapped_rows(): jnp.where(first, jnp.concatenate((kept, came), axis=0), jnp.concatenate((...]
    all_to_all x1, blocking collectives: 13.7 us -> 14.5 us  [shards(): sums = lax.all_to_all(sums, GROUPS, 0, 0, tiled=True)]
  transfers between devices with their start and end apart: 15 -> 20, of which waited for: 8 -> 11; matrix products, arithmetic and copies ran while one was open for 0% -> 2% of each run, Pallas kernels for 3% -> 6%
where the time goes in v8:
time: 74.6 us; the launch traced here: 74.4 us
  starting transfers between devices  33.2 us (45%)
  waiting for transfers between devices  16.1 us (22%)
  blocking collectives  14.5 us (19%)
  Pallas kernels  7.96 us (11%)
  other arithmetic  1.03 us (1%)
  between operations  0.79 us (1%)
    ppermute x20, starting transfers between devices, over(): return lax.ppermute(array, axis, [(i, i ^ jump) for i in range(size)])  33.2 us
    ppermute x20, waiting for transfers between devices, over(): return lax.ppermute(array, axis, [(i, i ^ jump) for i in range(size)])  16.1 us
    all_to_all x1, blocking collectives, shards(): sums = lax.all_to_all(sums, GROUPS, 0, 0, tiled=True)  14.5 us
    pallas_call x1, Pallas kernels, shards(): pl.pallas_call(mix_and_state, out_shape=(mixed_type, state, state), in_sp...  2.72 us
    pallas_call x3, Pallas kernels, reduced(): pl.pallas_call(kernel, out_shape=outs, in_specs=[SMEM] + [VMEM] * (2 + le...  1.91 us
  transfers between devices with their start and end apart: 20, of which 11 were waited for; matrix products, arithmetic and copies ran while one was open for 2% of the time, Pallas kernels for 6%

profile of v8, /device:TPU:1, one launch (start us, length us, event | category | flops | bytes accessed | tf_op | source)
XLA Modules:
  0.0 74.4 jit_solution(13791886495743351550)
XLA Ops:
  0.7 1.4 %cut.1 = bf16[128,3072]{1,0:T(8,128)(2,1)S(1)} custom-call(s32[1]{0:T(128)} %bitcast.10.which_ref, bf16[2,128,3072]{2,1,0:T(8,128)(2,1)} %bitcast.36), custom_call_target="tpu_custom_call" | custom-call | tf_op jit(solution)/shard_map/cut/pallas_call | solution.py:234
  2.1 0.0 copy-start.2
  2.1 3.3 %collective-permute-start.2 = (bf16[128,3072]{1,0:T(8,128)(2,1)S(1)}, bf16[128,3072]{1,0:T(8,128)(2,1)S(1)}, u32[]{:S(2)}, u32[]{:S(2)}) collective-permute-start(bf16[128,3072]{1,0:T(8,128)(2,1)S(1)} %cut.1), channel_id=1, source_target_pairs={{0,8},{8,0},{1,9},{9,1},{2,10},{10,2},{3,11},{11,3},{4,12},{12,4},... | collective-permute-start | bytes 2359304 | tf_op jit(solution)/shard_map/ppermute | solution.py:25
  5.4 0.1 collective-permute-start
  5.5 0.1 pad_add_fusion.where_ref
  5.6 1.7 %collective-permute-done.2 = bf16[128,3072]{1,0:T(8,128)(2,1)S(1)} collective-permute-done((bf16[128,3072]{1,0:T(8,128)(2,1)S(1)}, bf16[128,3072]{1,0:T(8,128)(2,1)S(1)}, u32[]{:S(2)}, u32[]{:S(2)}) %collective-permute-start.2) | collective-permute-done | bytes 786464 | tf_op jit(solution)/shard_map/ppermute | solution.py:25
  7.3 0.6 reduced.3
  8.0 0.1 collective-permute-start.3
  8.1 1.2 %collective-permute-start.4 = (bf16[4,2,8,1536]{3,2,1,0:T(8,128)(2,1)S(1)}, bf16[4,2,8,1536]{3,2,1,0:T(8,128)(2,1)S(1)}, u32[]{:S(2)}, u32[]{:S(2)}) collective-permute-start(bf16[4,2,8,1536]{3,2,1,0:T(8,128)(2,1)S(1)} %get-tuple-element.27), channel_id=1, source_target_pairs={{0,32},{32,0},{1,33},{33,1},{2,34},{34,2},{3,35},{35,3},{4,36},{36... | collective-permute-start | bytes 589832 | tf_op jit(solution)/shard_map/ppermute | solution.py:25
  9.2 0.6 dynamic-slice_bitcast_fusion.3
  9.9 0.9 %collective-permute-start.1 = (f32[4,3072]{1,0:T(4,128)}, f32[4,3072]{1,0:T(4,128)}, u32[]{:S(2)}, u32[]{:S(2)}) collective-permute-start(f32[4,3072]{1,0:T(4,128)} %get-tuple-element.57), channel_id=1, source_target_pairs={{0,8},{8,0},{1,9},{9,1},{2,10},{10,2},{3,11},{11,3},{4,12},{12,4},... | collective-permute-start | bytes 147464 | tf_op jit(solution)/shard_map/ppermute | solution.py:25
  10.8 3.4 %collective-permute-done.3.left_ref = bf16[4,2,8,1536]{3,2,1,0:T(8,128)(2,1)S(1)} collective-permute-done((bf16[4,2,8,1536]{3,2,1,0:T(8,128)(2,1)S(1)}, bf16[4,2,8,1536]{3,2,1,0:T(8,128)(2,1)S(1)}, u32[]{:S(2)}, u32[]{:S(2)}) %collective-permute-start.3) | collective-permute-done | bytes 196640 | tf_op jit(solution)/shard_map/ppermute | solution.py:25
  14.2 0.1 collective-permute-done.4.right_ref
  14.3 0.6 reduced.4
  14.9 0.9 %collective-permute-start.5 = (bf16[4,8,1536]{2,1,0:T(8,128)(2,1)S(1)}, bf16[4,8,1536]{2,1,0:T(8,128)(2,1)S(1)}, u32[]{:S(2)}, u32[]{:S(2)}) collective-permute-start(bf16[4,8,1536]{2,1,0:T(8,128)(2,1)S(1)} %get-tuple-element.28), channel_id=1, source_target_pairs={{0,32},{32,0},{1,33},{33,1},{2,34},{34,2},{3,35},{35,3},{4,36},{36... | collective-permute-start | bytes 294920 | tf_op jit(solution)/shard_map/ppermute | solution.py:25
  15.7 0.4 collective-permute-start.6
  16.1 0.0 collective-permute-done
  16.2 2.3 %collective-permute-done.5.left2_ref = bf16[4,8,1536]{2,1,0:T(8,128)(2,1)S(1)} collective-permute-done((bf16[4,8,1536]{2,1,0:T(8,128)(2,1)S(1)}, bf16[4,8,1536]{2,1,0:T(8,128)(2,1)S(1)}, u32[]{:S(2)}, u32[]{:S(2)}) %collective-permute-start.5) | collective-permute-done | bytes 98336 | tf_op jit(solution)/shard_map/ppermute | solution.py:25
  18.4 1.1 %collective-permute-done.6.right2_ref = bf16[4,8,1536]{2,1,0:T(8,128)(2,1)S(1)} collective-permute-done((bf16[4,8,1536]{2,1,0:T(8,128)(2,1)S(1)}, bf16[4,8,1536]{2,1,0:T(8,128)(2,1)S(1)}, u32[]{:S(2)}, u32[]{:S(2)}) %collective-permute-start.6) | collective-permute-done | bytes 98336 | tf_op jit(solution)/shard_map/ppermute | solution.py:25
  19.5 0.6 reduced.5
  20.2 5.8 %collective-permute-start.7 = (bf16[8,3072]{1,0:T(8,128)(2,1)S(1)}, bf16[8,3072]{1,0:T(8,128)(2,1)S(1)}, u32[]{:S(2)}, u32[]{:S(2)}) collective-permute-start(bf16[8,3072]{1,0:T(8,128)(2,1)S(1)} %get-tuple-element.31), channel_id=1, source_target_pairs={{0,128},{64,192},{128,0},{192,64},{1,129},{65,193},{129,1},{193,65... | collective-permute-start | bytes 147464 | tf_op jit(solution)/shard_map/ppermute | solution.py:25
  26.0 1.2 %collective-permute-start.8 = (bf16[8,3072]{1,0:T(8,128)(2,1)S(1)}, bf16[8,3072]{1,0:T(8,128)(2,1)S(1)}, u32[]{:S(2)}, u32[]{:S(2)}) collective-permute-start(bf16[8,3072]{1,0:T(8,128)(2,1)S(1)} %get-tuple-element.32), channel_id=1, source_target_pairs={{0,64},{64,0},{128,192},{192,128},{1,65},{65,1},{129,193},{193,129... | collective-permute-start | bytes 147464 | tf_op jit(solution)/shard_map/ppermute | solution.py:25
  27.2 0.9 %maximum_select_fusion.1.moment_ref = f32[8,3072]{1,0:T(8,128)S(1)} fusion(f32[4,3072]{1,0:T(4,128)} %collective-permute-done.1, f32[4,3072]{1,0:T(4,128)S(1)} %get-tuple-element.56, pred[]{:T(512)S(6)} %eq.3), kind=kLoop, calls=%fused_computation.3 | loop fusion | flops 73728 | bytes 196609 | tf_op jit(solution)/shard_map/jit(_where)/select_n | solution.py:225
  28.1 0.0 collective-permute-done.7.refs_0_
  28.1 2.0 %collective-permute-done.8.refs_1_ = bf16[8,3072]{1,0:T(8,128)(2,1)S(1)} collective-permute-done((bf16[8,3072]{1,0:T(8,128)(2,1)S(1)}, bf16[8,3072]{1,0:T(8,128)(2,1)S(1)}, u32[]{:S(2)}, u32[]{:S(2)}) %collective-permute-start.8) | collective-permute-done | bytes 49184 | tf_op jit(solution)/shard_map/ppermute | solution.py:25
  30.1 2.6 %collective-permute-done.9.refs_2_ = bf16[8,3072]{1,0:T(8,128)(2,1)S(1)} collective-permute-done((bf16[8,3072]{1,0:T(8,128)(2,1)S(1)}, bf16[8,3072]{1,0:T(8,128)(2,1)S(1)}, u32[]{:S(2)}, u32[]{:S(2)}) %collective-permute-start.9) | collective-permute-done | bytes 49184 | tf_op jit(solution)/shard_map/ppermute | solution.py:25
  32.7 0.2 total.1
  32.9 0.3 collective-permute-start.12
  33.2 1.3 %collective-permute-start.11 = (bf16[2,8,3200]{2,1,0:T(8,128)(2,1)S(1)}, bf16[2,8,3200]{2,1,0:T(8,128)(2,1)S(1)}, u32[]{:S(2)}, u32[]{:S(2)}) collective-permute-start(bf16[2,8,3200]{2,1,0:T(8,128)(2,1)S(1)} %get-tuple-element.36.refs_0_), channel_id=1, source_target_pairs={{0,64},{64,0},{128,192},{192,128},{1,65},{65,1},{129,193},{193,129... | collective-permute-start | bytes 307208 | tf_op jit(solution)/shard_map/ppermute | solution.py:25
  34.5 4.2 %collective-permute-start.10 = (bf16[2,8,3200]{2,1,0:T(8,128)(2,1)S(1)}, bf16[2,8,3200]{2,1,0:T(8,128)(2,1)S(1)}, u32[]{:S(2)}, u32[]{:S(2)}) collective-permute-start(bf16[2,8,3200]{2,1,0:T(8,128)(2,1)S(1)} %get-tuple-element.36.refs_0_), channel_id=1, source_target_pairs={{0,128},{64,192},{128,0},{192,64},{1,129},{65,193},{129,1},{193,65... | collective-permute-start | bytes 307208 | tf_op jit(solution)/shard_map/ppermute | solution.py:25
  38.8 5.1 %collective-permute-start.13 = (f32[4,3072]{1,0:T(4,128)S(1)}, f32[4,3072]{1,0:T(4,128)S(1)}, u32[]{:S(2)}, u32[]{:S(2)}) collective-permute-start(f32[4,3072]{1,0:T(4,128)S(1)} %get-tuple-element.55), channel_id=1, source_target_pairs={{0,8},{8,0},{1,9},{9,1},{2,10},{10,2},{3,11},{11,3},{4,12},{12,4},... | collective-permute-start | bytes 147464 | tf_op jit(solution)/shard_map/ppermute | solution.py:25
  43.9 0.9 %collective-permute-done.13.refs_3_ = f32[4,3072]{1,0:T(4,128)S(1)} collective-permute-done((f32[4,3072]{1,0:T(4,128)S(1)}, f32[4,3072]{1,0:T(4,128)S(1)}, u32[]{:S(2)}, u32[]{:S(2)}) %collective-permute-start.13) | collective-permute-done | bytes 49184 | tf_op jit(solution)/shard_map/ppermute | solution.py:25
  44.8 0.0 collective-permute-done.12.refs_3_
  44.8 0.0 collective-permute-done.11.refs_2_
  44.8 0.1 join.1
  44.9 0.3 collective-permute-start.15
  45.1 0.7 collective-permute-start.14
  45.8 14.5 %all_to_all.5.sums_ref = f32[32,1,128]{2,1,0:T(1,128)S(1)} all-to-all(f32[32,1,128]{2,1,0:T(1,128)S(1)} %get-tuple-element.40), channel_id=1, replica_groups=mesh['zh'=4,'zl'=2,'yl'=2,'core'=2,'x'=4,'yh'=2] {'zl','yl','x','yh'}, dimensions={0} | all-to-all | bytes 32768 | tf_op jit(solution)/shard_map/all_to_all | solution.py:310
  60.3 0.3 source.1.sources_ref
  60.6 5.6 %collective-permute-start.18 = (bf16[3,4,8,3200]{3,2,1,0:T(8,128)(2,1)S(1)}, bf16[3,4,8,3200]{3,2,1,0:T(8,128)(2,1)S(1)}, u32[]{:S(2)}, u32[]{:S(2)}) collective-permute-start(bf16[3,4,8,3200]{3,2,1,0:T(8,128)(2,1)S(1)} %source.1.sources_ref), channel_id=1, source_target_pairs={{0,8},{8,0},{1,9},{9,1},{2,10},{10,2},{3,11},{11,3},{4,12},{12,4},... | collective-permute-start | bytes 1843208 | tf_op jit(solution)/shard_map/ppermute | solution.py:25
  66.2 0.4 collective-permute-start.17
  66.6 0.3 collective-permute-start.16
  67.0 0.9 %collective-permute-done.18.sources2_ref = bf16[3,4,8,3200]{3,2,1,0:T(8,128)(2,1)S(1)} collective-permute-done((bf16[3,4,8,3200]{3,2,1,0:T(8,128)(2,1)S(1)}, bf16[3,4,8,3200]{3,2,1,0:T(8,128)(2,1)S(1)}, u32[]{:S(2)}, u32[]{:S(2)}) %collective-permute-start.18) | collective-permute-done | bytes 614432 | tf_op jit(solution)/shard_map/ppermute | solution.py:25
  67.9 2.7 %mix.1 = (bf16[2,16,8,3072]{3,2,1,0:T(8,128)(2,1)}, f32[2,4,3072]{2,1,0:T(4,128)}, f32[2,4,3072]{2,1,0:T(4,128)}) custom-call(s32[4]{0:T(128)S(1)} %pad_add_fusion.where_ref, bf16[2,16,8,3072]{3,2,1,0:T(8,128)(2,1)S(1)} %bitcast.40, bf16[3,4,8,3200]{3,2,1,0:T(8,128)(2,1)S(1)} %source.1.sources_ref, ...), custom_call_target="tpu_custom_call" | custom-call | tf_op jit(solution)/shard_map/mix/pallas_call | solution.py:350
  70.6 0.1 collective-permute-done.17
  70.8 1.2 %collective-permute-start.19 = (bf16[4,8,3072]{2,1,0:T(8,128)(2,1)S(1)}, bf16[4,8,3072]{2,1,0:T(8,128)(2,1)S(1)}, u32[]{:S(2)}, u32[]{:S(2)}) collective-permute-start(bf16[4,8,3072]{2,1,0:T(8,128)(2,1)S(1)} %constant_dynamic-update-slice_fusion.source_ref), channel_id=1, source_target_pairs={{0,8},{8,0},{1,9},{9,1},{2,10},{10,2},{3,11},{11,3},{4,12},{12,4},... | collective-permute-start | bytes 589832 | tf_op jit(solution)/shard_map/ppermute | solution.py:25
  71.9 1.1 %collective-permute-done.19.source2_ref = bf16[4,8,3072]{2,1,0:T(8,128)(2,1)S(1)} collective-permute-done((bf16[4,8,3072]{2,1,0:T(8,128)(2,1)S(1)}, bf16[4,8,3072]{2,1,0:T(8,128)(2,1)S(1)}, u32[]{:S(2)}, u32[]{:S(2)}) %collective-permute-start.19) | collective-permute-done | bytes 196640 | tf_op jit(solution)/shard_map/ppermute | solution.py:25
  73.0 1.4 %mix_last.1 = bf16[2,16,8,3072]{3,2,1,0:T(8,128)(2,1)} custom-call(s32[4]{0:T(128)S(1)} %pad_add_fusion.where_ref, bf16[2,16,8,3072]{3,2,1,0:T(8,128)(2,1)S(1)} %bitcast.41, bf16[4,8,3072]{2,1,0:T(8,128)(2,1)S(1)} %constant_dynamic-update-slice_fusion.source_ref, ...), custom_call_target="tpu_custom_call", output_to_operand_aliasing={{}: (4, {})} | custom-call | tf_op jit(solution)/shard_map/mix_last/pallas_call | solution.py:370
  (18 shorter events, 0.1 us)
Async XLA Ops:
  0.6 6.7 %copy-start = (bf16[2,1,1,128,3072]{4,3,2,1,0:T(8,128)(2,1)S(1)}, bf16[2,1,1,128,3072]{4,3,2,1,0:T(8,128)(2,1)}, u32[]{:S(2)}) copy-start(bf16[2,1,1,128,3072]{4,3,2,1,0:T(8,128)(2,1)} %param.3) | copy-start | bytes 4718596
  0.6 4.8 %copy-start.1 = (f32[2,1,4,3072]{3,2,1,0:T(4,128)S(1)}, f32[2,1,4,3072]{3,2,1,0:T(4,128)}, u32[]{:S(2)}) copy-start(f32[2,1,4,3072]{3,2,1,0:T(4,128)} %param.4) | copy-start | bytes 294916
  2.1 7.2 %copy-start.2 = (f32[2,1,4,3072]{3,2,1,0:T(4,128)S(1)}, f32[2,1,4,3072]{3,2,1,0:T(4,128)}, u32[]{:S(2)}) copy-start(f32[2,1,4,3072]{3,2,1,0:T(4,128)} %param.5) | copy-start | bytes 294916
  2.1 5.2 %collective-permute-start.2 = (bf16[128,3072]{1,0:T(8,128)(2,1)S(1)}, bf16[128,3072]{1,0:T(8,128)(2,1)S(1)}, u32[]{:S(2)}, u32[]{:S(2)}) collective-permute-start(bf16[128,3072]{1,0:T(8,128)(2,1)S(1)} %cut.1), channel_id=1, source_target_pairs={{0,8},{8,0},{1,9},{9,1},{2,10},{10,2},{3,11},{11,3},{4,12},{12,4},... | collective-permute-start | bytes 2359304 | tf_op jit(solution)/shard_map/ppermute | solution.py:25
  5.4 10.7 %collective-permute-start = (f32[4,3072]{1,0:T(4,128)S(1)}, f32[4,3072]{1,0:T(4,128)S(1)}, u32[]{:S(2)}, u32[]{:S(2)}) collective-permute-start(f32[4,3072]{1,0:T(4,128)S(1)} %get-tuple-element.59), channel_id=1, source_target_pairs={{0,8},{8,0},{1,9},{9,1},{2,10},{10,2},{3,11},{11,3},{4,12},{12,4},... | collective-permute-start | bytes 147464 | tf_op jit(solution)/shard_map/ppermute | solution.py:25
  8.0 6.2 %collective-permute-start.3 = (bf16[4,2,8,1536]{3,2,1,0:T(8,128)(2,1)S(1)}, bf16[4,2,8,1536]{3,2,1,0:T(8,128)(2,1)S(1)}, u32[]{:S(2)}, u32[]{:S(2)}) collective-permute-start(bf16[4,2,8,1536]{3,2,1,0:T(8,128)(2,1)S(1)} %get-tuple-element.26), channel_id=1, source_target_pairs={{0,16},{16,0},{1,17},{17,1},{2,18},{18,2},{3,19},{19,3},{4,20},{20... | collective-permute-start | bytes 589832 | tf_op jit(solution)/shard_map/ppermute | solution.py:25
  8.1 6.2 %collective-permute-start.4 = (bf16[4,2,8,1536]{3,2,1,0:T(8,128)(2,1)S(1)}, bf16[4,2,8,1536]{3,2,1,0:T(8,128)(2,1)S(1)}, u32[]{:S(2)}, u32[]{:S(2)}) collective-permute-start(bf16[4,2,8,1536]{3,2,1,0:T(8,128)(2,1)S(1)} %get-tuple-element.27), channel_id=1, source_target_pairs={{0,32},{32,0},{1,33},{33,1},{2,34},{34,2},{3,35},{35,3},{4,36},{36... | collective-permute-start | bytes 589832 | tf_op jit(solution)/shard_map/ppermute | solution.py:25
  9.9 17.3 %collective-permute-start.1 = (f32[4,3072]{1,0:T(4,128)}, f32[4,3072]{1,0:T(4,128)}, u32[]{:S(2)}, u32[]{:S(2)}) collective-permute-start(f32[4,3072]{1,0:T(4,128)} %get-tuple-element.57), channel_id=1, source_target_pairs={{0,8},{8,0},{1,9},{9,1},{2,10},{10,2},{3,11},{11,3},{4,12},{12,4},... | collective-permute-start | bytes 147464 | tf_op jit(solution)/shard_map/ppermute | solution.py:25
  14.9 3.6 %collective-permute-start.5 = (bf16[4,8,1536]{2,1,0:T(8,128)(2,1)S(1)}, bf16[4,8,1536]{2,1,0:T(8,128)(2,1)S(1)}, u32[]{:S(2)}, u32[]{:S(2)}) collective-permute-start(bf16[4,8,1536]{2,1,0:T(8,128)(2,1)S(1)} %get-tuple-element.28), channel_id=1, source_target_pairs={{0,32},{32,0},{1,33},{33,1},{2,34},{34,2},{3,35},{35,3},{4,36},{36... | collective-permute-start | bytes 294920 | tf_op jit(solution)/shard_map/ppermute | solution.py:25
  15.7 3.8 %collective-permute-start.6 = (bf16[4,8,1536]{2,1,0:T(8,128)(2,1)S(1)}, bf16[4,8,1536]{2,1,0:T(8,128)(2,1)S(1)}, u32[]{:S(2)}, u32[]{:S(2)}) collective-permute-start(bf16[4,8,1536]{2,1,0:T(8,128)(2,1)S(1)} %get-tuple-element.29), channel_id=1, source_target_pairs={{0,16},{16,0},{1,17},{17,1},{2,18},{18,2},{3,19},{19,3},{4,20},{20... | collective-permute-start | bytes 294920 | tf_op jit(solution)/shard_map/ppermute | solution.py:25
  20.2 7.9 %collective-permute-start.7 = (bf16[8,3072]{1,0:T(8,128)(2,1)S(1)}, bf16[8,3072]{1,0:T(8,128)(2,1)S(1)}, u32[]{:S(2)}, u32[]{:S(2)}) collective-permute-start(bf16[8,3072]{1,0:T(8,128)(2,1)S(1)} %get-tuple-element.31), channel_id=1, source_target_pairs={{0,128},{64,192},{128,0},{192,64},{1,129},{65,193},{129,1},{193,65... | collective-permute-start | bytes 147464 | tf_op jit(solution)/shard_map/ppermute | solution.py:25
  26.0 4.1 %collective-permute-start.8 = (bf16[8,3072]{1,0:T(8,128)(2,1)S(1)}, bf16[8,3072]{1,0:T(8,128)(2,1)S(1)}, u32[]{:S(2)}, u32[]{:S(2)}) collective-permute-start(bf16[8,3072]{1,0:T(8,128)(2,1)S(1)} %get-tuple-element.32), channel_id=1, source_target_pairs={{0,64},{64,0},{128,192},{192,128},{1,65},{65,1},{129,193},{193,129... | collective-permute-start | bytes 147464 | tf_op jit(solution)/shard_map/ppermute | solution.py:25
  27.2 5.6 %collective-permute-start.9 = (bf16[8,3072]{1,0:T(8,128)(2,1)S(1)}, bf16[8,3072]{1,0:T(8,128)(2,1)S(1)}, u32[]{:S(2)}, u32[]{:S(2)}) collective-permute-start(bf16[8,3072]{1,0:T(8,128)(2,1)S(1)} %get-tuple-element.33), channel_id=1, source_target_pairs={{0,192},{64,128},{128,64},{192,0},{1,193},{65,129},{129,65},{193,1... | collective-permute-start | bytes 147464 | tf_op jit(solution)/shard_map/ppermute | solution.py:25
  32.9 11.8 %collective-permute-start.12 = (bf16[2,8,3200]{2,1,0:T(8,128)(2,1)S(1)}, bf16[2,8,3200]{2,1,0:T(8,128)(2,1)S(1)}, u32[]{:S(2)}, u32[]{:S(2)}) collective-permute-start(bf16[2,8,3200]{2,1,0:T(8,128)(2,1)S(1)} %get-tuple-element.36.refs_0_), channel_id=1, source_target_pairs={{0,192},{64,128},{128,64},{192,0},{1,193},{65,129},{129,65},{193,1... | collective-permute-start | bytes 307208 | tf_op jit(solution)/shard_map/ppermute | solution.py:25
  33.2 11.5 %collective-permute-start.11 = (bf16[2,8,3200]{2,1,0:T(8,128)(2,1)S(1)}, bf16[2,8,3200]{2,1,0:T(8,128)(2,1)S(1)}, u32[]{:S(2)}, u32[]{:S(2)}) collective-permute-start(bf16[2,8,3200]{2,1,0:T(8,128)(2,1)S(1)} %get-tuple-element.36.refs_0_), channel_id=1, source_target_pairs={{0,64},{64,0},{128,192},{192,128},{1,65},{65,1},{129,193},{193,129... | collective-permute-start | bytes 307208 | tf_op jit(solution)/shard_map/ppermute | solution.py:25
  34.5 10.2 %collective-permute-start.10 = (bf16[2,8,3200]{2,1,0:T(8,128)(2,1)S(1)}, bf16[2,8,3200]{2,1,0:T(8,128)(2,1)S(1)}, u32[]{:S(2)}, u32[]{:S(2)}) collective-permute-start(bf16[2,8,3200]{2,1,0:T(8,128)(2,1)S(1)} %get-tuple-element.36.refs_0_), channel_id=1, source_target_pairs={{0,128},{64,192},{128,0},{192,64},{1,129},{65,193},{129,1},{193,65... | collective-permute-start | bytes 307208 | tf_op jit(solution)/shard_map/ppermute | solution.py:25
  38.8 6.0 %collective-permute-start.13 = (f32[4,3072]{1,0:T(4,128)S(1)}, f32[4,3072]{1,0:T(4,128)S(1)}, u32[]{:S(2)}, u32[]{:S(2)}) collective-permute-start(f32[4,3072]{1,0:T(4,128)S(1)} %get-tuple-element.55), channel_id=1, source_target_pairs={{0,8},{8,0},{1,9},{9,1},{2,10},{10,2},{3,11},{11,3},{4,12},{12,4},... | collective-permute-start | bytes 147464 | tf_op jit(solution)/shard_map/ppermute | solution.py:25
  44.9 15.4 %collective-permute-start.15 = (bf16[4,2,8,3072]{3,2,1,0:T(8,128)(2,1)S(1)}, bf16[4,2,8,3072]{3,2,1,0:T(8,128)(2,1)S(1)}, u32[]{:S(2)}, u32[]{:S(2)}) collective-permute-start(bf16[4,2,8,3072]{3,2,1,0:T(8,128)(2,1)S(1)} %get-tuple-element.41.refs_0_), channel_id=1, source_target_pairs={{0,16},{16,0},{1,17},{17,1},{2,18},{18,2},{3,19},{19,3},{4,20},{20... | collective-permute-start | bytes 1179656 | tf_op jit(solution)/shard_map/ppermute | solution.py:25
  45.1 15.2 %collective-permute-start.14 = (bf16[4,2,8,3072]{3,2,1,0:T(8,128)(2,1)S(1)}, bf16[4,2,8,3072]{3,2,1,0:T(8,128)(2,1)S(1)}, u32[]{:S(2)}, u32[]{:S(2)}) collective-permute-start(bf16[4,2,8,3072]{3,2,1,0:T(8,128)(2,1)S(1)} %get-tuple-element.41.refs_0_), channel_id=1, source_target_pairs={{0,32},{32,0},{1,33},{33,1},{2,34},{34,2},{3,35},{35,3},{4,36},{36... | collective-permute-start | bytes 1179656 | tf_op jit(solution)/shard_map/ppermute | solution.py:25
  60.6 7.3 %collective-permute-start.18 = (bf16[3,4,8,3200]{3,2,1,0:T(8,128)(2,1)S(1)}, bf16[3,4,8,3200]{3,2,1,0:T(8,128)(2,1)S(1)}, u32[]{:S(2)}, u32[]{:S(2)}) collective-permute-start(bf16[3,4,8,3200]{3,2,1,0:T(8,128)(2,1)S(1)} %source.1.sources_ref), channel_id=1, source_target_pairs={{0,8},{8,0},{1,9},{9,1},{2,10},{10,2},{3,11},{11,3},{4,12},{12,4},... | collective-permute-start | bytes 1843208 | tf_op jit(solution)/shard_map/ppermute | solution.py:25
  66.2 4.5 %collective-permute-start.17 = (bf16[4,8,1536]{2,1,0:T(8,128)(2,1)S(1)}, bf16[4,8,1536]{2,1,0:T(8,128)(2,1)S(1)}, u32[]{:S(2)}, u32[]{:S(2)}) collective-permute-start(bf16[4,8,1536]{2,1,0:T(8,128)(2,1)S(1)} %get-tuple-element.52), channel_id=1, source_target_pairs={{0,32},{32,0},{1,33},{33,1},{2,34},{34,2},{3,35},{35,3},{4,36},{36... | collective-permute-start | bytes 294920 | tf_op jit(solution)/shard_map/ppermute | solution.py:25
  66.6 4.1 %collective-permute-start.16 = (bf16[4,8,1536]{2,1,0:T(8,128)(2,1)S(1)}, bf16[4,8,1536]{2,1,0:T(8,128)(2,1)S(1)}, u32[]{:S(2)}, u32[]{:S(2)}) collective-permute-start(bf16[4,8,1536]{2,1,0:T(8,128)(2,1)S(1)} %get-tuple-element.53), channel_id=1, source_target_pairs={{0,16},{16,0},{1,17},{17,1},{2,18},{18,2},{3,19},{19,3},{4,20},{20... | collective-permute-start | bytes 294920 | tf_op jit(solution)/shard_map/ppermute | solution.py:25
  70.8 2.3 %collective-permute-start.19 = (bf16[4,8,3072]{2,1,0:T(8,128)(2,1)S(1)}, bf16[4,8,3072]{2,1,0:T(8,128)(2,1)S(1)}, u32[]{:S(2)}, u32[]{:S(2)}) collective-permute-start(bf16[4,8,3072]{2,1,0:T(8,128)(2,1)S(1)} %constant_dynamic-update-slice_fusion.source_ref), channel_id=1, source_target_pairs={{0,8},{8,0},{1,9},{9,1},{2,10},{10,2},{3,11},{11,3},{4,12},{12,4},... | collective-permute-start | bytes 589832 | tf_op jit(solution)/shard_map/ppermute | solution.py:25

commit v9 on v8

--- a/solution.py
+++ b/solution.py
@@ -31,6 +31,10 @@
 
 def over_y(array):
     return over("yl", 2, 1, array)
+
+
+def over_both(array):
+    return over(("zl", "yl"), 4, 3, array)
 
 
 def over_z(array):
@@ -52,52 +56,32 @@
         copy.wait()
 
 
-def pair_of(weights_ref, got_ref, core, at, columns):
-    own = weights_ref[(core, *at)][:, columns].astype(jnp.float32)
-    return own + got_ref[at][:, columns].astype(jnp.float32)
-
-
-def first_kernel(where_ref, weights_ref, got_ref, left_ref, right_ref):
+OTHERS = ((1, 0), (0, 1), (1, 1))
+
+
+def pair_of(weights_ref, got_ref, core, at):
+    own = weights_ref[(core, *at)].astype(jnp.float32)
+    return own + got_ref[at].astype(jnp.float32)
+
+
+def pairs_kernel(where_ref, weights_ref, got_ref, *outs):
     core, zl, yl = where_ref[0], where_ref[2], where_ref[3]
-    half = left_ref.shape[3]
-    for zh in range(4):
-        for bit in range(2):
-            pair = pair_of(weights_ref, got_ref, core, (zh, bit, 1 - yl), slice(0, half))
-            left_ref[zh, bit] = pair.astype(jnp.bfloat16)
-            pair = pair_of(
-                weights_ref, got_ref, core, (zh, 1 - zl, bit), slice(half, None)
-            )
-            right_ref[zh, bit] = pair.astype(jnp.bfloat16)
-
-
-def second_kernel(where_ref, weights_ref, got_ref, left_ref, right_ref, left2_ref, right2_ref):
-    core, zl, yl = where_ref[0], where_ref[2], where_ref[3]
-    half = left_ref.shape[3]
-    for zh in range(4):
-        pair = pair_of(weights_ref, got_ref, core, (zh, 1 - zl, yl), slice(0, half))
-        quad = pair + left_ref[zh, 1 - zl].astype(jnp.float32)
-        left2_ref[zh] = quad.astype(jnp.bfloat16)
-        pair = pair_of(weights_ref, got_ref, core, (zh, zl, 1 - yl), slice(half, None))
-        quad = pair + right_ref[zh, 1 - yl].astype(jnp.float32)
-        right2_ref[zh] = quad.astype(jnp.bfloat16)
-
-
-def third_kernel(
-    where_ref, weights_ref, got_ref, left_ref, right_ref, left2_ref, right2_ref, *outs
-):
+    for (to_z, to_y), out_ref in zip(OTHERS, outs):
+        for zh in range(4):
+            at = (zh, zl ^ to_z, yl ^ to_y)
+            pair = pair_of(weights_ref, got_ref, core, at)
+            out_ref[zh] = pair.astype(jnp.bfloat16)
+
+
+def eights_kernel(where_ref, weights_ref, got_ref, *refs):
     core, zh, zl, yl = (where_ref[i] for i in range(4))
-    half = left_ref.shape[3]
+    came, outs = refs[: len(OTHERS)], refs[len(OTHERS) :]
     for jump, out_ref in zip(JUMPS, outs):
         to = zh ^ jump
-        at = (to, zl, yl)
-        left = pair_of(weights_ref, got_ref, core, at, slice(0, half))
-        left += left_ref[to, zl].astype(jnp.float32)
-        left += left2_ref[to].astype(jnp.float32)
-        right = pair_of(weights_ref, got_ref, core, at, slice(half, None))
-        right += right_ref[to, yl].astype(jnp.float32)
-        right += right2_ref[to].astype(jnp.float32)
-        out_ref[:, :half] = left.astype(out_ref.dtype)
-        out_ref[:, half:] = right.astype(out_ref.dtype)
+        total = pair_of(weights_ref, got_ref, core, (to, zl, yl))
+        for ref in came:
+            total += ref[to].astype(jnp.float32)
+        out_ref[...] = total.astype(out_ref.dtype)
 
 
 def split_lines(value, rows):
@@ -256,22 +240,15 @@
             name="reduced",
         )(where, spread, got, *given)
 
-    left, right = reduced(
-        first_kernel, (pltpu.VMEM((sizes[0], 2, block, half), bf16),) * 2
-    )
-    left, right = over_y(left), over_z(right)
-    left2, right2 = reduced(
-        second_kernel, (pltpu.VMEM((sizes[0], block, half), bf16),) * 2, left, right
-    )
-    left2, right2 = over_z(left2), over_y(right2)
+    pairs = reduced(
+        pairs_kernel, (pltpu.VMEM((sizes[0], block, width), bf16),) * len(OTHERS)
+    )
+    pairs = [over_z(pairs[0]), over_y(pairs[1]), over_both(pairs[2])]
     own, *sums = reduced(
-        third_kernel,
+        eights_kernel,
         (pltpu.VMEM((block, width), f32),)
         + (pltpu.VMEM((block, width), bf16),) * (len(JUMPS) - 1),
-        left,
-        right,
-        left2,
-        right2,
+        *pairs,
     )
     sums = [over("zh", 4, jump, one) for jump, one in zip(JUMPS[1:], sums)]
     pseudo, pack = pl.pallas_call(

time: 74.6 us -> 73.6 us (0.987)
  waiting for transfers between devices: 16.1 us -> 15.3 us
    ppermute x20 -> x19, waiting for transfers between devices: 16.1 us -> 15.3 us  [over(): return lax.ppermute(array, axis, [(i, i ^ jump) for i in range(size)])]
    ppermute x20 -> x19, starting transfers between devices: 33.2 us -> 33.9 us  [over(): return lax.ppermute(array, axis, [(i, i ^ jump) for i in range(size)])]
    pallas_call x3 -> x2, Pallas kernels: 1.91 us -> 1.36 us  [reduced(): pl.pallas_call(kernel, out_shape=outs, in_specs=[SMEM] + [VMEM] * (2 + le...]
  transfers between devices with their start and end apart: 20 -> 19, of which waited for: 11 -> 11; matrix products, arithmetic and copies ran while one was open for 2% -> 2% of each run, Pallas kernels for 6% -> 6%
where the time goes in v9:
time: 73.6 us; the launch traced here: 73.4 us
  starting transfers between devices  33.9 us (46%)
  waiting for transfers between devices  15.3 us (21%)
  blocking collectives  14.3 us (19%)
  Pallas kernels  7.39 us (10%)
  other arithmetic  1.03 us (1%)
  between operations  0.77 us (1%)
    ppermute x19, starting transfers between devices, over(): return lax.ppermute(array, axis, [(i, i ^ jump) for i in range(size)])  33.9 us
    ppermute x19, waiting for transfers between devices, over(): return lax.ppermute(array, axis, [(i, i ^ jump) for i in range(size)])  15.3 us
    all_to_all x1, blocking collectives, shards(): sums = lax.all_to_all(sums, GROUPS, 0, 0, tiled=True)  14.3 us
    pallas_call x1, Pallas kernels, shards(): pl.pallas_call(mix_and_state, out_shape=(mixed_type, state, state), in_sp...  2.72 us
  transfers between devices with their start and end apart: 19, of which 11 were waited for; matrix products, arithmetic and copies ran while one was open for 2% of the time, Pallas kernels for 6%

profile of v9, /device:TPU:1, one launch (start us, length us, event | category | flops | bytes accessed | tf_op | source)
XLA Modules:
  0.0 73.4 jit_solution(13930142395842619271)
XLA Ops:
  0.7 1.4 %cut.1 = bf16[128,3072]{1,0:T(8,128)(2,1)S(1)} custom-call(s32[1]{0:T(128)} %bitcast.10.which_ref, bf16[2,128,3072]{2,1,0:T(8,128)(2,1)} %bitcast.36), custom_call_target="tpu_custom_call" | custom-call | tf_op jit(solution)/shard_map/cut/pallas_call | solution.py:218
  2.0 3.3 %collective-permute-start.2 = (bf16[128,3072]{1,0:T(8,128)(2,1)S(1)}, bf16[128,3072]{1,0:T(8,128)(2,1)S(1)}, u32[]{:S(2)}, u32[]{:S(2)}) collective-permute-start(bf16[128,3072]{1,0:T(8,128)(2,1)S(1)} %cut.1), channel_id=1, source_target_pairs={{0,8},{8,0},{1,9},{9,1},{2,10},{10,2},{3,11},{11,3},{4,12},{12,4},... | collective-permute-start | bytes 2359304 | tf_op jit(solution)/shard_map/ppermute | solution.py:25
  5.4 0.6 dynamic-slice_bitcast_fusion.5
  6.0 0.0 collective-permute-start
  6.0 0.6 collective-permute-start.1
  6.6 0.1 pad_add_fusion.where_ref
  6.7 0.6 collective-permute-done.2
  7.3 0.7 reduced.2
  8.0 0.1 collective-permute-start.3
  8.1 1.2 %collective-permute-start.4 = (bf16[4,8,3072]{2,1,0:T(8,128)(2,1)S(1)}, bf16[4,8,3072]{2,1,0:T(8,128)(2,1)S(1)}, u32[]{:S(2)}, u32[]{:S(2)}) collective-permute-start(bf16[4,8,3072]{2,1,0:T(8,128)(2,1)S(1)} %get-tuple-element.26), channel_id=1, source_target_pairs={{0,16},{16,0},{1,17},{17,1},{2,18},{18,2},{3,19},{19,3},{4,20},{20... | collective-permute-start | bytes 589832 | tf_op jit(solution)/shard_map/ppermute | solution.py:25
  9.3 1.5 %collective-permute-start.5 = (bf16[4,8,3072]{2,1,0:T(8,128)(2,1)S(1)}, bf16[4,8,3072]{2,1,0:T(8,128)(2,1)S(1)}, u32[]{:S(2)}, u32[]{:S(2)}) collective-permute-start(bf16[4,8,3072]{2,1,0:T(8,128)(2,1)S(1)} %get-tuple-element.27), channel_id=1, source_target_pairs={{0,48},{16,32},{32,16},{48,0},{1,49},{17,33},{33,17},{49,1},{2,50}... | collective-permute-start | bytes 589832 | tf_op jit(solution)/shard_map/ppermute | solution.py:25
  10.7 0.0 collective-permute-done
  10.7 0.9 %maximum_select_fusion.outer_ref = f32[8,3072]{1,0:T(8,128)S(1)} fusion(f32[4,3072]{1,0:T(4,128)} %collective-permute-done, f32[4,3072]{1,0:T(4,128)S(1)} %get-tuple-element.56, pred[]{:T(512)S(6)} %eq.3), kind=kLoop, calls=%fused_computation.2 | loop fusion | flops 73728 | bytes 196609 | tf_op jit(solution)/shard_map/jit(_where)/select_n | solution.py:209
  11.6 2.5 %collective-permute-done.3.refs_0_ = bf16[4,8,3072]{2,1,0:T(8,128)(2,1)S(1)} collective-permute-done((bf16[4,8,3072]{2,1,0:T(8,128)(2,1)S(1)}, bf16[4,8,3072]{2,1,0:T(8,128)(2,1)S(1)}, u32[]{:S(2)}, u32[]{:S(2)}) %collective-permute-start.3) | collective-permute-done | bytes 196640 | tf_op jit(solution)/shard_map/ppermute | solution.py:25
  14.2 0.4 collective-permute-done.4.refs_1_
  14.5 3.6 %collective-permute-done.5.refs_2_ = bf16[4,8,3072]{2,1,0:T(8,128)(2,1)S(1)} collective-permute-done((bf16[4,8,3072]{2,1,0:T(8,128)(2,1)S(1)}, bf16[4,8,3072]{2,1,0:T(8,128)(2,1)S(1)}, u32[]{:S(2)}, u32[]{:S(2)}) %collective-permute-start.5) | collective-permute-done | bytes 196640 | tf_op jit(solution)/shard_map/ppermute | solution.py:25
  18.1 0.7 reduced.3
  18.8 6.6 %collective-permute-start.6 = (bf16[8,3072]{1,0:T(8,128)(2,1)S(1)}, bf16[8,3072]{1,0:T(8,128)(2,1)S(1)}, u32[]{:S(2)}, u32[]{:S(2)}) collective-permute-start(bf16[8,3072]{1,0:T(8,128)(2,1)S(1)} %get-tuple-element.29), channel_id=1, source_target_pairs={{0,128},{64,192},{128,0},{192,64},{1,129},{65,193},{129,1},{193,65... | collective-permute-start | bytes 147464 | tf_op jit(solution)/shard_map/ppermute | solution.py:25
  25.3 1.2 %collective-permute-start.7 = (bf16[8,3072]{1,0:T(8,128)(2,1)S(1)}, bf16[8,3072]{1,0:T(8,128)(2,1)S(1)}, u32[]{:S(2)}, u32[]{:S(2)}) collective-permute-start(bf16[8,3072]{1,0:T(8,128)(2,1)S(1)} %get-tuple-element.30), channel_id=1, source_target_pairs={{0,64},{64,0},{128,192},{192,128},{1,65},{65,1},{129,193},{193,129... | collective-permute-start | bytes 147464 | tf_op jit(solution)/shard_map/ppermute | solution.py:25
  26.5 0.0 collective-permute-start.8
  26.5 0.0 collective-permute-done.1
  26.6 0.3 collective-permute-done.6.refs_0_
  26.9 3.6 %collective-permute-done.7.refs_1_ = bf16[8,3072]{1,0:T(8,128)(2,1)S(1)} collective-permute-done((bf16[8,3072]{1,0:T(8,128)(2,1)S(1)}, bf16[8,3072]{1,0:T(8,128)(2,1)S(1)}, u32[]{:S(2)}, u32[]{:S(2)}) %collective-permute-start.7) | collective-permute-done | bytes 49184 | tf_op jit(solution)/shard_map/ppermute | solution.py:25
  30.6 1.3 %collective-permute-done.8.refs_2_ = bf16[8,3072]{1,0:T(8,128)(2,1)S(1)} collective-permute-done((bf16[8,3072]{1,0:T(8,128)(2,1)S(1)}, bf16[8,3072]{1,0:T(8,128)(2,1)S(1)}, u32[]{:S(2)}, u32[]{:S(2)}) %collective-permute-start.8) | collective-permute-done | bytes 49184 | tf_op jit(solution)/shard_map/ppermute | solution.py:25
  31.8 0.2 total.1
  32.1 0.6 collective-permute-start.11
  32.7 1.8 %collective-permute-start.10 = (bf16[2,8,3200]{2,1,0:T(8,128)(2,1)S(1)}, bf16[2,8,3200]{2,1,0:T(8,128)(2,1)S(1)}, u32[]{:S(2)}, u32[]{:S(2)}) collective-permute-start(bf16[2,8,3200]{2,1,0:T(8,128)(2,1)S(1)} %get-tuple-element.34.refs_0_), channel_id=1, source_target_pairs={{0,64},{64,0},{128,192},{192,128},{1,65},{65,1},{129,193},{193,129... | collective-permute-start | bytes 307208 | tf_op jit(solution)/shard_map/ppermute | solution.py:25
  34.5 3.3 %collective-permute-start.9 = (bf16[2,8,3200]{2,1,0:T(8,128)(2,1)S(1)}, bf16[2,8,3200]{2,1,0:T(8,128)(2,1)S(1)}, u32[]{:S(2)}, u32[]{:S(2)}) collective-permute-start(bf16[2,8,3200]{2,1,0:T(8,128)(2,1)S(1)} %get-tuple-element.34.refs_0_), channel_id=1, source_target_pairs={{0,128},{64,192},{128,0},{192,64},{1,129},{65,193},{129,1},{193,65... | collective-permute-start | bytes 307208 | tf_op jit(solution)/shard_map/ppermute | solution.py:25
  37.9 3.7 %collective-permute-start.12 = (f32[4,3072]{1,0:T(4,128)S(1)}, f32[4,3072]{1,0:T(4,128)S(1)}, u32[]{:S(2)}, u32[]{:S(2)}) collective-permute-start(f32[4,3072]{1,0:T(4,128)S(1)} %get-tuple-element.53), channel_id=1, source_target_pairs={{0,8},{8,0},{1,9},{9,1},{2,10},{10,2},{3,11},{11,3},{4,12},{12,4},... | collective-permute-start | bytes 147464 | tf_op jit(solution)/shard_map/ppermute | solution.py:25
  41.5 0.9 %collective-permute-done.12.refs_3_ = f32[4,3072]{1,0:T(4,128)S(1)} collective-permute-done((f32[4,3072]{1,0:T(4,128)S(1)}, f32[4,3072]{1,0:T(4,128)S(1)}, u32[]{:S(2)}, u32[]{:S(2)}) %collective-permute-start.12) | collective-permute-done | bytes 49184 | tf_op jit(solution)/shard_map/ppermute | solution.py:25
  42.4 0.0 collective-permute-done.11.refs_3_
  42.4 0.0 collective-permute-done.10.refs_2_
  42.4 0.0 collective-permute-done.9.refs_1_
  42.4 0.1 join.1
  42.5 1.1 %collective-permute-start.14 = (bf16[4,2,8,3072]{3,2,1,0:T(8,128)(2,1)S(1)}, bf16[4,2,8,3072]{3,2,1,0:T(8,128)(2,1)S(1)}, u32[]{:S(2)}, u32[]{:S(2)}) collective-permute-start(bf16[4,2,8,3072]{3,2,1,0:T(8,128)(2,1)S(1)} %get-tuple-element.39.refs_0_), channel_id=1, source_target_pairs={{0,16},{16,0},{1,17},{17,1},{2,18},{18,2},{3,19},{19,3},{4,20},{20... | collective-permute-start | bytes 1179656 | tf_op jit(solution)/shard_map/ppermute | solution.py:25
  43.6 1.5 %collective-permute-start.13 = (bf16[4,2,8,3072]{3,2,1,0:T(8,128)(2,1)S(1)}, bf16[4,2,8,3072]{3,2,1,0:T(8,128)(2,1)S(1)}, u32[]{:S(2)}, u32[]{:S(2)}) collective-permute-start(bf16[4,2,8,3072]{3,2,1,0:T(8,128)(2,1)S(1)} %get-tuple-element.39.refs_0_), channel_id=1, source_target_pairs={{0,32},{32,0},{1,33},{33,1},{2,34},{34,2},{3,35},{35,3},{4,36},{36... | collective-permute-start | bytes 1179656 | tf_op jit(solution)/shard_map/ppermute | solution.py:25
  45.1 14.3 %all_to_all.5.sums_ref = f32[32,1,128]{2,1,0:T(1,128)S(1)} all-to-all(f32[32,1,128]{2,1,0:T(1,128)S(1)} %get-tuple-element.38), channel_id=1, replica_groups=mesh['zh'=4,'zl'=2,'yl'=2,'core'=2,'x'=4,'yh'=2] {'zl','yl','x','yh'}, dimensions={0} | all-to-all | bytes 32768 | tf_op jit(solution)/shard_map/all_to_all | solution.py:287
  59.4 0.3 source.1.sources_ref
  59.7 5.5 %collective-permute-start.17 = (bf16[3,4,8,3200]{3,2,1,0:T(8,128)(2,1)S(1)}, bf16[3,4,8,3200]{3,2,1,0:T(8,128)(2,1)S(1)}, u32[]{:S(2)}, u32[]{:S(2)}) collective-permute-start(bf16[3,4,8,3200]{3,2,1,0:T(8,128)(2,1)S(1)} %source.1.sources_ref), channel_id=1, source_target_pairs={{0,8},{8,0},{1,9},{9,1},{2,10},{10,2},{3,11},{11,3},{4,12},{12,4},... | collective-permute-start | bytes 1843208 | tf_op jit(solution)/shard_map/ppermute | solution.py:25
  65.2 0.4 collective-permute-start.16
  65.6 0.3 collective-permute-start.15
  65.9 0.9 %collective-permute-done.17.sources2_ref = bf16[3,4,8,3200]{3,2,1,0:T(8,128)(2,1)S(1)} collective-permute-done((bf16[3,4,8,3200]{3,2,1,0:T(8,128)(2,1)S(1)}, bf16[3,4,8,3200]{3,2,1,0:T(8,128)(2,1)S(1)}, u32[]{:S(2)}, u32[]{:S(2)}) %collective-permute-start.17) | collective-permute-done | bytes 614432 | tf_op jit(solution)/shard_map/ppermute | solution.py:25
  66.8 2.7 %mix.1 = (bf16[2,16,8,3072]{3,2,1,0:T(8,128)(2,1)}, f32[2,4,3072]{2,1,0:T(4,128)}, f32[2,4,3072]{2,1,0:T(4,128)}) custom-call(s32[4]{0:T(128)S(1)} %pad_add_fusion.where_ref, bf16[2,16,8,3072]{3,2,1,0:T(8,128)(2,1)S(1)} %bitcast.39, bf16[3,4,8,3200]{3,2,1,0:T(8,128)(2,1)S(1)} %source.1.sources_ref, ...), custom_call_target="tpu_custom_call" | custom-call | tf_op jit(solution)/shard_map/mix/pallas_call | solution.py:327
  69.6 0.1 collective-permute-done.16
  69.7 0.0 collective-permute-done.15
  69.7 1.2 %collective-permute-start.18 = (bf16[4,8,3072]{2,1,0:T(8,128)(2,1)S(1)}, bf16[4,8,3072]{2,1,0:T(8,128)(2,1)S(1)}, u32[]{:S(2)}, u32[]{:S(2)}) collective-permute-start(bf16[4,8,3072]{2,1,0:T(8,128)(2,1)S(1)} %constant_dynamic-update-slice_fusion.source_ref), channel_id=1, source_target_pairs={{0,8},{8,0},{1,9},{9,1},{2,10},{10,2},{3,11},{11,3},{4,12},{12,4},... | collective-permute-start | bytes 589832 | tf_op jit(solution)/shard_map/ppermute | solution.py:25
  70.9 1.1 %collective-permute-done.18.source2_ref = bf16[4,8,3072]{2,1,0:T(8,128)(2,1)S(1)} collective-permute-done((bf16[4,8,3072]{2,1,0:T(8,128)(2,1)S(1)}, bf16[4,8,3072]{2,1,0:T(8,128)(2,1)S(1)}, u32[]{:S(2)}, u32[]{:S(2)}) %collective-permute-start.18) | collective-permute-done | bytes 196640 | tf_op jit(solution)/shard_map/ppermute | solution.py:25
  72.0 1.4 %mix_last.1 = bf16[2,16,8,3072]{3,2,1,0:T(8,128)(2,1)} custom-call(s32[4]{0:T(128)S(1)} %pad_add_fusion.where_ref, bf16[2,16,8,3072]{3,2,1,0:T(8,128)(2,1)S(1)} %bitcast.40, bf16[4,8,3072]{2,1,0:T(8,128)(2,1)S(1)} %constant_dynamic-update-slice_fusion.source_ref, ...), custom_call_target="tpu_custom_call", output_to_operand_aliasing={{}: (4, {})} | custom-call | tf_op jit(solution)/shard_map/mix_last/pallas_call | solution.py:347
  (15 shorter events, 0.1 us)
Async XLA Ops:
  0.6 6.7 %copy-start = (bf16[2,1,1,128,3072]{4,3,2,1,0:T(8,128)(2,1)S(1)}, bf16[2,1,1,128,3072]{4,3,2,1,0:T(8,128)(2,1)}, u32[]{:S(2)}) copy-start(bf16[2,1,1,128,3072]{4,3,2,1,0:T(8,128)(2,1)} %param.3) | copy-start | bytes 4718596
  0.6 4.7 %copy-start.1 = (f32[2,1,4,3072]{3,2,1,0:T(4,128)S(1)}, f32[2,1,4,3072]{3,2,1,0:T(4,128)}, u32[]{:S(2)}) copy-start(f32[2,1,4,3072]{3,2,1,0:T(4,128)} %param.4) | copy-start | bytes 294916
  0.7 5.4 %copy-start.2 = (f32[2,1,4,3072]{3,2,1,0:T(4,128)S(1)}, f32[2,1,4,3072]{3,2,1,0:T(4,128)}, u32[]{:S(2)}) copy-start(f32[2,1,4,3072]{3,2,1,0:T(4,128)} %param.5) | copy-start | bytes 294916
  2.0 5.2 %collective-permute-start.2 = (bf16[128,3072]{1,0:T(8,128)(2,1)S(1)}, bf16[128,3072]{1,0:T(8,128)(2,1)S(1)}, u32[]{:S(2)}, u32[]{:S(2)}) collective-permute-start(bf16[128,3072]{1,0:T(8,128)(2,1)S(1)} %cut.1), channel_id=1, source_target_pairs={{0,8},{8,0},{1,9},{9,1},{2,10},{10,2},{3,11},{11,3},{4,12},{12,4},... | collective-permute-start | bytes 2359304 | tf_op jit(solution)/shard_map/ppermute | solution.py:25
  6.0 4.7 %collective-permute-start = (f32[4,3072]{1,0:T(4,128)}, f32[4,3072]{1,0:T(4,128)}, u32[]{:S(2)}, u32[]{:S(2)}) collective-permute-start(f32[4,3072]{1,0:T(4,128)} %get-tuple-element.57), channel_id=1, source_target_pairs={{0,8},{8,0},{1,9},{9,1},{2,10},{10,2},{3,11},{11,3},{4,12},{12,4},... | collective-permute-start | bytes 147464 | tf_op jit(solution)/shard_map/ppermute | solution.py:25
  6.0 20.5 %collective-permute-start.1 = (f32[4,3072]{1,0:T(4,128)S(1)}, f32[4,3072]{1,0:T(4,128)S(1)}, u32[]{:S(2)}, u32[]{:S(2)}) collective-permute-start(f32[4,3072]{1,0:T(4,128)S(1)} %get-tuple-element.55), channel_id=1, source_target_pairs={{0,8},{8,0},{1,9},{9,1},{2,10},{10,2},{3,11},{11,3},{4,12},{12,4},... | collective-permute-start | bytes 147464 | tf_op jit(solution)/shard_map/ppermute | solution.py:25
  8.0 6.2 %collective-permute-start.3 = (bf16[4,8,3072]{2,1,0:T(8,128)(2,1)S(1)}, bf16[4,8,3072]{2,1,0:T(8,128)(2,1)S(1)}, u32[]{:S(2)}, u32[]{:S(2)}) collective-permute-start(bf16[4,8,3072]{2,1,0:T(8,128)(2,1)S(1)} %get-tuple-element.25), channel_id=1, source_target_pairs={{0,32},{32,0},{1,33},{33,1},{2,34},{34,2},{3,35},{35,3},{4,36},{36... | collective-permute-start | bytes 589832 | tf_op jit(solution)/shard_map/ppermute | solution.py:25
  8.1 6.5 %collective-permute-start.4 = (bf16[4,8,3072]{2,1,0:T(8,128)(2,1)S(1)}, bf16[4,8,3072]{2,1,0:T(8,128)(2,1)S(1)}, u32[]{:S(2)}, u32[]{:S(2)}) collective-permute-start(bf16[4,8,3072]{2,1,0:T(8,128)(2,1)S(1)} %get-tuple-element.26), channel_id=1, source_target_pairs={{0,16},{16,0},{1,17},{17,1},{2,18},{18,2},{3,19},{19,3},{4,20},{20... | collective-permute-start | bytes 589832 | tf_op jit(solution)/shard_map/ppermute | solution.py:25
  9.3 8.8 %collective-permute-start.5 = (bf16[4,8,3072]{2,1,0:T(8,128)(2,1)S(1)}, bf16[4,8,3072]{2,1,0:T(8,128)(2,1)S(1)}, u32[]{:S(2)}, u32[]{:S(2)}) collective-permute-start(bf16[4,8,3072]{2,1,0:T(8,128)(2,1)S(1)} %get-tuple-element.27), channel_id=1, source_target_pairs={{0,48},{16,32},{32,16},{48,0},{1,49},{17,33},{33,17},{49,1},{2,50}... | collective-permute-start | bytes 589832 | tf_op jit(solution)/shard_map/ppermute | solution.py:25
  18.8 8.2 %collective-permute-start.6 = (bf16[8,3072]{1,0:T(8,128)(2,1)S(1)}, bf16[8,3072]{1,0:T(8,128)(2,1)S(1)}, u32[]{:S(2)}, u32[]{:S(2)}) collective-permute-start(bf16[8,3072]{1,0:T(8,128)(2,1)S(1)} %get-tuple-element.29), channel_id=1, source_target_pairs={{0,128},{64,192},{128,0},{192,64},{1,129},{65,193},{129,1},{193,65... | collective-permute-start | bytes 147464 | tf_op jit(solution)/shard_map/ppermute | solution.py:25
  25.3 5.2 %collective-permute-start.7 = (bf16[8,3072]{1,0:T(8,128)(2,1)S(1)}, bf16[8,3072]{1,0:T(8,128)(2,1)S(1)}, u32[]{:S(2)}, u32[]{:S(2)}) collective-permute-start(bf16[8,3072]{1,0:T(8,128)(2,1)S(1)} %get-tuple-element.30), channel_id=1, source_target_pairs={{0,64},{64,0},{128,192},{192,128},{1,65},{65,1},{129,193},{193,129... | collective-permute-start | bytes 147464 | tf_op jit(solution)/shard_map/ppermute | solution.py:25
  26.5 5.3 %collective-permute-start.8 = (bf16[8,3072]{1,0:T(8,128)(2,1)S(1)}, bf16[8,3072]{1,0:T(8,128)(2,1)S(1)}, u32[]{:S(2)}, u32[]{:S(2)}) collective-permute-start(bf16[8,3072]{1,0:T(8,128)(2,1)S(1)} %get-tuple-element.31), channel_id=1, source_target_pairs={{0,192},{64,128},{128,64},{192,0},{1,193},{65,129},{129,65},{193,1... | collective-permute-start | bytes 147464 | tf_op jit(solution)/shard_map/ppermute | solution.py:25
  32.1 10.4 %collective-permute-start.11 = (bf16[2,8,3200]{2,1,0:T(8,128)(2,1)S(1)}, bf16[2,8,3200]{2,1,0:T(8,128)(2,1)S(1)}, u32[]{:S(2)}, u32[]{:S(2)}) collective-permute-start(bf16[2,8,3200]{2,1,0:T(8,128)(2,1)S(1)} %get-tuple-element.34.refs_0_), channel_id=1, source_target_pairs={{0,192},{64,128},{128,64},{192,0},{1,193},{65,129},{129,65},{193,1... | collective-permute-start | bytes 307208 | tf_op jit(solution)/shard_map/ppermute | solution.py:25
  32.7 9.7 %collective-permute-start.10 = (bf16[2,8,3200]{2,1,0:T(8,128)(2,1)S(1)}, bf16[2,8,3200]{2,1,0:T(8,128)(2,1)S(1)}, u32[]{:S(2)}, u32[]{:S(2)}) collective-permute-start(bf16[2,8,3200]{2,1,0:T(8,128)(2,1)S(1)} %get-tuple-element.34.refs_0_), channel_id=1, source_target_pairs={{0,64},{64,0},{128,192},{192,128},{1,65},{65,1},{129,193},{193,129... | collective-permute-start | bytes 307208 | tf_op jit(solution)/shard_map/ppermute | solution.py:25
  34.5 7.9 %collective-permute-start.9 = (bf16[2,8,3200]{2,1,0:T(8,128)(2,1)S(1)}, bf16[2,8,3200]{2,1,0:T(8,128)(2,1)S(1)}, u32[]{:S(2)}, u32[]{:S(2)}) collective-permute-start(bf16[2,8,3200]{2,1,0:T(8,128)(2,1)S(1)} %get-tuple-element.34.refs_0_), channel_id=1, source_target_pairs={{0,128},{64,192},{128,0},{192,64},{1,129},{65,193},{129,1},{193,65... | collective-permute-start | bytes 307208 | tf_op jit(solution)/shard_map/ppermute | solution.py:25
  37.9 4.5 %collective-permute-start.12 = (f32[4,3072]{1,0:T(4,128)S(1)}, f32[4,3072]{1,0:T(4,128)S(1)}, u32[]{:S(2)}, u32[]{:S(2)}) collective-permute-start(f32[4,3072]{1,0:T(4,128)S(1)} %get-tuple-element.53), channel_id=1, source_target_pairs={{0,8},{8,0},{1,9},{9,1},{2,10},{10,2},{3,11},{11,3},{4,12},{12,4},... | collective-permute-start | bytes 147464 | tf_op jit(solution)/shard_map/ppermute | solution.py:25
  42.5 16.9 %collective-permute-start.14 = (bf16[4,2,8,3072]{3,2,1,0:T(8,128)(2,1)S(1)}, bf16[4,2,8,3072]{3,2,1,0:T(8,128)(2,1)S(1)}, u32[]{:S(2)}, u32[]{:S(2)}) collective-permute-start(bf16[4,2,8,3072]{3,2,1,0:T(8,128)(2,1)S(1)} %get-tuple-element.39.refs_0_), channel_id=1, source_target_pairs={{0,16},{16,0},{1,17},{17,1},{2,18},{18,2},{3,19},{19,3},{4,20},{20... | collective-permute-start | bytes 1179656 | tf_op jit(solution)/shard_map/ppermute | solution.py:25
  43.6 15.8 %collective-permute-start.13 = (bf16[4,2,8,3072]{3,2,1,0:T(8,128)(2,1)S(1)}, bf16[4,2,8,3072]{3,2,1,0:T(8,128)(2,1)S(1)}, u32[]{:S(2)}, u32[]{:S(2)}) collective-permute-start(bf16[4,2,8,3072]{3,2,1,0:T(8,128)(2,1)S(1)} %get-tuple-element.39.refs_0_), channel_id=1, source_target_pairs={{0,32},{32,0},{1,33},{33,1},{2,34},{34,2},{3,35},{35,3},{4,36},{36... | collective-permute-start | bytes 1179656 | tf_op jit(solution)/shard_map/ppermute | solution.py:25
  59.7 7.2 %collective-permute-start.17 = (bf16[3,4,8,3200]{3,2,1,0:T(8,128)(2,1)S(1)}, bf16[3,4,8,3200]{3,2,1,0:T(8,128)(2,1)S(1)}, u32[]{:S(2)}, u32[]{:S(2)}) collective-permute-start(bf16[3,4,8,3200]{3,2,1,0:T(8,128)(2,1)S(1)} %source.1.sources_ref), channel_id=1, source_target_pairs={{0,8},{8,0},{1,9},{9,1},{2,10},{10,2},{3,11},{11,3},{4,12},{12,4},... | collective-permute-start | bytes 1843208 | tf_op jit(solution)/shard_map/ppermute | solution.py:25
  65.2 4.5 %collective-permute-start.16 = (bf16[4,8,1536]{2,1,0:T(8,128)(2,1)S(1)}, bf16[4,8,1536]{2,1,0:T(8,128)(2,1)S(1)}, u32[]{:S(2)}, u32[]{:S(2)}) collective-permute-start(bf16[4,8,1536]{2,1,0:T(8,128)(2,1)S(1)} %get-tuple-element.50), channel_id=1, source_target_pairs={{0,32},{32,0},{1,33},{33,1},{2,34},{34,2},{3,35},{35,3},{4,36},{36... | collective-permute-start | bytes 294920 | tf_op jit(solution)/shard_map/ppermute | solution.py:25
  65.6 4.1 %collective-permute-start.15 = (bf16[4,8,1536]{2,1,0:T(8,128)(2,1)S(1)}, bf16[4,8,1536]{2,1,0:T(8,128)(2,1)S(1)}, u32[]{:S(2)}, u32[]{:S(2)}) collective-permute-start(bf16[4,8,1536]{2,1,0:T(8,128)(2,1)S(1)} %get-tuple-element.51), channel_id=1, source_target_pairs={{0,16},{16,0},{1,17},{17,1},{2,18},{18,2},{3,19},{19,3},{4,20},{20... | collective-permute-start | bytes 294920 | tf_op jit(solution)/shard_map/ppermute | solution.py:25
  69.7 2.3 %collective-permute-start.18 = (bf16[4,8,3072]{2,1,0:T(8,128)(2,1)S(1)}, bf16[4,8,3072]{2,1,0:T(8,128)(2,1)S(1)}, u32[]{:S(2)}, u32[]{:S(2)}) collective-permute-start(bf16[4,8,3072]{2,1,0:T(8,128)(2,1)S(1)} %constant_dynamic-update-slice_fusion.source_ref), channel_id=1, source_target_pairs={{0,8},{8,0},{1,9},{9,1},{2,10},{10,2},{3,11},{11,3},{4,12},{12,4},... | collective-permute-start | bytes 589832 | tf_op jit(solution)/shard_map/ppermute | solution.py:25

commit v10 on v9

--- a/solution.py
+++ b/solution.py
@@ -69,8 +69,7 @@
     for (to_z, to_y), out_ref in zip(OTHERS, outs):
         for zh in range(4):
             at = (zh, zl ^ to_z, yl ^ to_y)
-            pair = pair_of(weights_ref, got_ref, core, at)
-            out_ref[zh] = pair.astype(jnp.bfloat16)
+            out_ref[zh] = weights_ref[(core, *at)] + got_ref[at]
 
 
 def eights_kernel(where_ref, weights_ref, got_ref, *refs):
@@ -174,9 +173,9 @@
         low = (1 - zl if other_z else zl) * 2 + (1 - yl if other_y else yl)
         for k, jump in enumerate(JUMPS):
             chip = 4 * (zh ^ jump) + low
-            own = weights_ref[frag, chip].astype(jnp.float32)
-            source = source_ref[k, :, : own.shape[1]].astype(jnp.float32)
-            mixed_ref[number, k] = (0.5 * own + 0.5 * source).astype(jnp.bfloat16)
+            own = weights_ref[frag, chip]
+            source = source_ref[k, :, : own.shape[1]]
+            mixed_ref[number, k] = jnp.bfloat16(0.5) * (own + source)
             stores.append(
                 pltpu.make_async_copy(
                     mixed_ref.at[number, k], mixed_hbm.at[frag, chip], sems.at[number, k]
@@ -265,8 +264,9 @@
     halves = pseudo.reshape(2, share_rows, width)
     pseudo2 = over_core(pick(halves, other))
 
-    packs = [pack] + [over("zh", 4, jump, pack) for jump in JUMPS[1:]]
+    packs = [over("zh", 4, jump, pack) for jump in JUMPS[:0:-1]]
     packs, pseudo2 = lax.optimization_barrier((packs, pseudo2))
+    packs = [pack] + packs[::-1]
     groups = lax.axis_size(GROUPS)
     joined, sums = pl.pallas_call(
         join_kernel,

time: 73.6 us -> 73.7 us (level)
  waiting for transfers between devices: 15.3 us -> 18.7 us
  starting transfers between devices: 33.9 us -> 31.5 us
    ppermute x19, waiting for transfers between devices: 15.3 us -> 18.7 us  [over(): return lax.ppermute(array, axis, [(i, i ^ jump) for i in range(size)])]
    ppermute x19, starting transfers between devices: 33.9 us -> 31.5 us  [over(): return lax.ppermute(array, axis, [(i, i ^ jump) for i in range(size)])]
  transfers between devices with their start and end apart: 19 -> 19, of which waited for: 11 -> 12; matrix products, arithmetic and copies ran while one was open for 2% -> 2% of each run, Pallas kernels for 6% -> 5%
where the time goes in v10:
time: 73.7 us; the launch traced here: 73.5 us
  starting transfers between devices  31.5 us (43%)
  waiting for transfers between devices  18.7 us (25%)
  blocking collectives  13.6 us (18%)
  Pallas kernels  7.12 us (10%)
  other arithmetic  1.03 us (1%)
  between operations  0.78 us (1%)
    ppermute x19, starting transfers between devices, over(): return lax.ppermute(array, axis, [(i, i ^ jump) for i in range(size)])  31.5 us
    ppermute x19, waiting for transfers between devices, over(): return lax.ppermute(array, axis, [(i, i ^ jump) for i in range(size)])  18.7 us
    all_to_all x1, blocking collectives, shards(): sums = lax.all_to_all(sums, GROUPS, 0, 0, tiled=True)  13.6 us
    pallas_call x1, Pallas kernels, shards(): pl.pallas_call(mix_and_state, out_shape=(mixed_type, state, state), in_sp...  2.55 us
  transfers between devices with their start and end apart: 19, of which 12 were waited for; matrix products, arithmetic and copies ran while one was open for 2% of the time, Pallas kernels for 5%

profile of v10, /device:TPU:1, one launch (start us, length us, event | category | flops | bytes accessed | tf_op | source)
XLA Modules:
  0.0 73.5 jit_solution(17843903916657769717)
XLA Ops:
  0.7 1.4 %cut.1 = bf16[128,3072]{1,0:T(8,128)(2,1)S(1)} custom-call(s32[1]{0:T(128)} %bitcast.10.which_ref, bf16[2,128,3072]{2,1,0:T(8,128)(2,1)} %bitcast.36), custom_call_target="tpu_custom_call" | custom-call | tf_op jit(solution)/shard_map/cut/pallas_call | solution.py:217
  2.0 3.3 %collective-permute-start.2 = (bf16[128,3072]{1,0:T(8,128)(2,1)S(1)}, bf16[128,3072]{1,0:T(8,128)(2,1)S(1)}, u32[]{:S(2)}, u32[]{:S(2)}) collective-permute-start(bf16[128,3072]{1,0:T(8,128)(2,1)S(1)} %cut.1), channel_id=1, source_target_pairs={{0,8},{8,0},{1,9},{9,1},{2,10},{10,2},{3,11},{11,3},{4,12},{12,4},... | collective-permute-start | bytes 2359304 | tf_op jit(solution)/shard_map/ppermute | solution.py:25
  5.4 0.6 dynamic-slice_bitcast_fusion.5
  6.0 0.0 collective-permute-start
  6.0 0.6 collective-permute-start.1
  6.6 0.1 pad_add_fusion.where_ref
  6.7 0.6 collective-permute-done.2
  7.3 0.6 reduced.2
  7.9 0.1 collective-permute-start.3
  8.0 1.2 %collective-permute-start.4 = (bf16[4,8,3072]{2,1,0:T(8,128)(2,1)S(1)}, bf16[4,8,3072]{2,1,0:T(8,128)(2,1)S(1)}, u32[]{:S(2)}, u32[]{:S(2)}) collective-permute-start(bf16[4,8,3072]{2,1,0:T(8,128)(2,1)S(1)} %get-tuple-element.25), channel_id=1, source_target_pairs={{0,16},{16,0},{1,17},{17,1},{2,18},{18,2},{3,19},{19,3},{4,20},{20... | collective-permute-start | bytes 589832 | tf_op jit(solution)/shard_map/ppermute | solution.py:25
  9.2 1.5 %collective-permute-start.5 = (bf16[4,8,3072]{2,1,0:T(8,128)(2,1)S(1)}, bf16[4,8,3072]{2,1,0:T(8,128)(2,1)S(1)}, u32[]{:S(2)}, u32[]{:S(2)}) collective-permute-start(bf16[4,8,3072]{2,1,0:T(8,128)(2,1)S(1)} %get-tuple-element.26), channel_id=1, source_target_pairs={{0,48},{16,32},{32,16},{48,0},{1,49},{17,33},{33,17},{49,1},{2,50}... | collective-permute-start | bytes 589832 | tf_op jit(solution)/shard_map/ppermute | solution.py:25
  10.6 0.0 collective-permute-done
  10.6 0.9 %maximum_select_fusion.outer_ref = f32[8,3072]{1,0:T(8,128)S(1)} fusion(f32[4,3072]{1,0:T(4,128)} %collective-permute-done, f32[4,3072]{1,0:T(4,128)S(1)} %get-tuple-element.54, pred[]{:T(512)S(6)} %eq.3), kind=kLoop, calls=%fused_computation.2 | loop fusion | flops 73728 | bytes 196609 | tf_op jit(solution)/shard_map/jit(_where)/select_n | solution.py:208
  11.6 2.5 %collective-permute-done.3.refs_0_ = bf16[4,8,3072]{2,1,0:T(8,128)(2,1)S(1)} collective-permute-done((bf16[4,8,3072]{2,1,0:T(8,128)(2,1)S(1)}, bf16[4,8,3072]{2,1,0:T(8,128)(2,1)S(1)}, u32[]{:S(2)}, u32[]{:S(2)}) %collective-permute-start.3) | collective-permute-done | bytes 196640 | tf_op jit(solution)/shard_map/ppermute | solution.py:25
  14.1 0.4 collective-permute-done.4.refs_1_
  14.5 3.6 %collective-permute-done.5.refs_2_ = bf16[4,8,3072]{2,1,0:T(8,128)(2,1)S(1)} collective-permute-done((bf16[4,8,3072]{2,1,0:T(8,128)(2,1)S(1)}, bf16[4,8,3072]{2,1,0:T(8,128)(2,1)S(1)}, u32[]{:S(2)}, u32[]{:S(2)}) %collective-permute-start.5) | collective-permute-done | bytes 196640 | tf_op jit(solution)/shard_map/ppermute | solution.py:25
  18.0 0.7 reduced.3
  18.7 6.6 %collective-permute-start.6 = (bf16[8,3072]{1,0:T(8,128)(2,1)S(1)}, bf16[8,3072]{1,0:T(8,128)(2,1)S(1)}, u32[]{:S(2)}, u32[]{:S(2)}) collective-permute-start(bf16[8,3072]{1,0:T(8,128)(2,1)S(1)} %get-tuple-element.28), channel_id=1, source_target_pairs={{0,128},{64,192},{128,0},{192,64},{1,129},{65,193},{129,1},{193,65... | collective-permute-start | bytes 147464 | tf_op jit(solution)/shard_map/ppermute | solution.py:25
  25.3 1.2 %collective-permute-start.7 = (bf16[8,3072]{1,0:T(8,128)(2,1)S(1)}, bf16[8,3072]{1,0:T(8,128)(2,1)S(1)}, u32[]{:S(2)}, u32[]{:S(2)}) collective-permute-start(bf16[8,3072]{1,0:T(8,128)(2,1)S(1)} %get-tuple-element.29), channel_id=1, source_target_pairs={{0,64},{64,0},{128,192},{192,128},{1,65},{65,1},{129,193},{193,129... | collective-permute-start | bytes 147464 | tf_op jit(solution)/shard_map/ppermute | solution.py:25
  26.5 0.0 collective-permute-start.8
  26.5 0.3 collective-permute-done.6.refs_0_
  26.9 3.6 %collective-permute-done.7.refs_1_ = bf16[8,3072]{1,0:T(8,128)(2,1)S(1)} collective-permute-done((bf16[8,3072]{1,0:T(8,128)(2,1)S(1)}, bf16[8,3072]{1,0:T(8,128)(2,1)S(1)}, u32[]{:S(2)}, u32[]{:S(2)}) %collective-permute-start.7) | collective-permute-done | bytes 49184 | tf_op jit(solution)/shard_map/ppermute | solution.py:25
  30.5 1.3 %collective-permute-done.8.refs_2_ = bf16[8,3072]{1,0:T(8,128)(2,1)S(1)} collective-permute-done((bf16[8,3072]{1,0:T(8,128)(2,1)S(1)}, bf16[8,3072]{1,0:T(8,128)(2,1)S(1)}, u32[]{:S(2)}, u32[]{:S(2)}) %collective-permute-start.8) | collective-permute-done | bytes 49184 | tf_op jit(solution)/shard_map/ppermute | solution.py:25
  31.8 0.2 total.1
  32.0 2.2 %collective-permute-start.11 = (bf16[2,8,3200]{2,1,0:T(8,128)(2,1)S(1)}, bf16[2,8,3200]{2,1,0:T(8,128)(2,1)S(1)}, u32[]{:S(2)}, u32[]{:S(2)}) collective-permute-start(bf16[2,8,3200]{2,1,0:T(8,128)(2,1)S(1)} %get-tuple-element.31.refs_0_), channel_id=1, source_target_pairs={{0,128},{64,192},{128,0},{192,64},{1,129},{65,193},{129,1},{193,65... | collective-permute-start | bytes 307208 | tf_op jit(solution)/shard_map/ppermute | solution.py:25
  34.1 0.5 collective-permute-start.10
  34.7 3.1 %collective-permute-start.9 = (bf16[2,8,3200]{2,1,0:T(8,128)(2,1)S(1)}, bf16[2,8,3200]{2,1,0:T(8,128)(2,1)S(1)}, u32[]{:S(2)}, u32[]{:S(2)}) collective-permute-start(bf16[2,8,3200]{2,1,0:T(8,128)(2,1)S(1)} %get-tuple-element.31.refs_0_), channel_id=1, source_target_pairs={{0,192},{64,128},{128,64},{192,0},{1,193},{65,129},{129,65},{193,1... | collective-permute-start | bytes 307208 | tf_op jit(solution)/shard_map/ppermute | solution.py:25
  37.8 3.7 %collective-permute-start.12 = (f32[4,3072]{1,0:T(4,128)S(1)}, f32[4,3072]{1,0:T(4,128)S(1)}, u32[]{:S(2)}, u32[]{:S(2)}) collective-permute-start(f32[4,3072]{1,0:T(4,128)S(1)} %get-tuple-element.51), channel_id=1, source_target_pairs={{0,8},{8,0},{1,9},{9,1},{2,10},{10,2},{3,11},{11,3},{4,12},{12,4},... | collective-permute-start | bytes 147464 | tf_op jit(solution)/shard_map/ppermute | solution.py:25
  41.4 0.9 %collective-permute-done.12.refs_3_ = f32[4,3072]{1,0:T(4,128)S(1)} collective-permute-done((f32[4,3072]{1,0:T(4,128)S(1)}, f32[4,3072]{1,0:T(4,128)S(1)}, u32[]{:S(2)}, u32[]{:S(2)}) %collective-permute-start.12) | collective-permute-done | bytes 49184 | tf_op jit(solution)/shard_map/ppermute | solution.py:25
  42.3 0.0 collective-permute-done.11.refs_1_
  42.3 3.2 %collective-permute-done.10.refs_2_ = bf16[2,8,3200]{2,1,0:T(8,128)(2,1)S(1)} collective-permute-done((bf16[2,8,3200]{2,1,0:T(8,128)(2,1)S(1)}, bf16[2,8,3200]{2,1,0:T(8,128)(2,1)S(1)}, u32[]{:S(2)}, u32[]{:S(2)}) %collective-permute-start.10) | collective-permute-done | bytes 102432 | tf_op jit(solution)/shard_map/ppermute | solution.py:25
  45.5 0.0 collective-permute-done.9.refs_3_
  45.5 0.1 join.1
  45.6 0.1 collective-permute-start.14
  45.7 2.2 %collective-permute-start.13 = (bf16[4,2,8,3072]{3,2,1,0:T(8,128)(2,1)S(1)}, bf16[4,2,8,3072]{3,2,1,0:T(8,128)(2,1)S(1)}, u32[]{:S(2)}, u32[]{:S(2)}) collective-permute-start(bf16[4,2,8,3072]{3,2,1,0:T(8,128)(2,1)S(1)} %get-tuple-element.37.refs_0_), channel_id=1, source_target_pairs={{0,32},{32,0},{1,33},{33,1},{2,34},{34,2},{3,35},{35,3},{4,36},{36... | collective-permute-start | bytes 1179656 | tf_op jit(solution)/shard_map/ppermute | solution.py:25
  48.0 13.6 %all_to_all.5.sums_ref = f32[32,1,128]{2,1,0:T(1,128)S(1)} all-to-all(f32[32,1,128]{2,1,0:T(1,128)S(1)} %get-tuple-element.36), channel_id=1, replica_groups=mesh['zh'=4,'zl'=2,'yl'=2,'core'=2,'x'=4,'yh'=2] {'zl','yl','x','yh'}, dimensions={0} | all-to-all | bytes 32768 | tf_op jit(solution)/shard_map/all_to_all | solution.py:287
  61.6 0.0 collective-permute-done.14.refs_2_
  61.6 0.0 collective-permute-done.13.refs_1_
  61.6 0.3 source.1.sources_ref
  61.9 3.5 %collective-permute-start.17 = (bf16[3,4,8,3200]{3,2,1,0:T(8,128)(2,1)S(1)}, bf16[3,4,8,3200]{3,2,1,0:T(8,128)(2,1)S(1)}, u32[]{:S(2)}, u32[]{:S(2)}) collective-permute-start(bf16[3,4,8,3200]{3,2,1,0:T(8,128)(2,1)S(1)} %source.1.sources_ref), channel_id=1, source_target_pairs={{0,8},{8,0},{1,9},{9,1},{2,10},{10,2},{3,11},{11,3},{4,12},{12,4},... | collective-permute-start | bytes 1843208 | tf_op jit(solution)/shard_map/ppermute | solution.py:25
  65.4 0.4 collective-permute-start.16
  65.8 0.3 collective-permute-start.15
  66.1 0.9 %collective-permute-done.17.sources2_ref = bf16[3,4,8,3200]{3,2,1,0:T(8,128)(2,1)S(1)} collective-permute-done((bf16[3,4,8,3200]{3,2,1,0:T(8,128)(2,1)S(1)}, bf16[3,4,8,3200]{3,2,1,0:T(8,128)(2,1)S(1)}, u32[]{:S(2)}, u32[]{:S(2)}) %collective-permute-start.17) | collective-permute-done | bytes 614432 | tf_op jit(solution)/shard_map/ppermute | solution.py:25
  67.0 2.6 %mix.1 = (bf16[2,16,8,3072]{3,2,1,0:T(8,128)(2,1)}, f32[2,4,3072]{2,1,0:T(4,128)}, f32[2,4,3072]{2,1,0:T(4,128)}) custom-call(s32[4]{0:T(128)S(1)} %pad_add_fusion.where_ref, bf16[2,16,8,3072]{3,2,1,0:T(8,128)(2,1)S(1)} %bitcast.39, bf16[3,4,8,3200]{3,2,1,0:T(8,128)(2,1)S(1)} %source.1.sources_ref, ...), custom_call_target="tpu_custom_call" | custom-call | tf_op jit(solution)/shard_map/mix/pallas_call | solution.py:327
  69.6 0.3 collective-permute-done.16
  69.9 1.2 %collective-permute-start.18 = (bf16[4,8,3072]{2,1,0:T(8,128)(2,1)S(1)}, bf16[4,8,3072]{2,1,0:T(8,128)(2,1)S(1)}, u32[]{:S(2)}, u32[]{:S(2)}) collective-permute-start(bf16[4,8,3072]{2,1,0:T(8,128)(2,1)S(1)} %constant_dynamic-update-slice_fusion.source_ref), channel_id=1, source_target_pairs={{0,8},{8,0},{1,9},{9,1},{2,10},{10,2},{3,11},{11,3},{4,12},{12,4},... | collective-permute-start | bytes 589832 | tf_op jit(solution)/shard_map/ppermute | solution.py:25
  71.1 1.1 %collective-permute-done.18.source2_ref = bf16[4,8,3072]{2,1,0:T(8,128)(2,1)S(1)} collective-permute-done((bf16[4,8,3072]{2,1,0:T(8,128)(2,1)S(1)}, bf16[4,8,3072]{2,1,0:T(8,128)(2,1)S(1)}, u32[]{:S(2)}, u32[]{:S(2)}) %collective-permute-start.18) | collective-permute-done | bytes 196640 | tf_op jit(solution)/shard_map/ppermute | solution.py:25
  72.2 1.4 %mix_last.1 = bf16[2,16,8,3072]{3,2,1,0:T(8,128)(2,1)} custom-call(s32[4]{0:T(128)S(1)} %pad_add_fusion.where_ref, bf16[2,16,8,3072]{3,2,1,0:T(8,128)(2,1)S(1)} %bitcast.40, bf16[4,8,3072]{2,1,0:T(8,128)(2,1)S(1)} %constant_dynamic-update-slice_fusion.source_ref, ...), custom_call_target="tpu_custom_call", output_to_operand_aliasing={{}: (4, {})} | custom-call | tf_op jit(solution)/shard_map/mix_last/pallas_call | solution.py:347
  (15 shorter events, 0.1 us)
Async XLA Ops:
  0.6 6.7 %copy-start = (bf16[2,1,1,128,3072]{4,3,2,1,0:T(8,128)(2,1)S(1)}, bf16[2,1,1,128,3072]{4,3,2,1,0:T(8,128)(2,1)}, u32[]{:S(2)}) copy-start(bf16[2,1,1,128,3072]{4,3,2,1,0:T(8,128)(2,1)} %param.3) | copy-start | bytes 4718596
  0.6 4.7 %copy-start.1 = (f32[2,1,4,3072]{3,2,1,0:T(4,128)S(1)}, f32[2,1,4,3072]{3,2,1,0:T(4,128)}, u32[]{:S(2)}) copy-start(f32[2,1,4,3072]{3,2,1,0:T(4,128)} %param.4) | copy-start | bytes 294916
  0.7 5.4 %copy-start.2 = (f32[2,1,4,3072]{3,2,1,0:T(4,128)S(1)}, f32[2,1,4,3072]{3,2,1,0:T(4,128)}, u32[]{:S(2)}) copy-start(f32[2,1,4,3072]{3,2,1,0:T(4,128)} %param.5) | copy-start | bytes 294916
  2.0 5.2 %collective-permute-start.2 = (bf16[128,3072]{1,0:T(8,128)(2,1)S(1)}, bf16[128,3072]{1,0:T(8,128)(2,1)S(1)}, u32[]{:S(2)}, u32[]{:S(2)}) collective-permute-start(bf16[128,3072]{1,0:T(8,128)(2,1)S(1)} %cut.1), channel_id=1, source_target_pairs={{0,8},{8,0},{1,9},{9,1},{2,10},{10,2},{3,11},{11,3},{4,12},{12,4},... | collective-permute-start | bytes 2359304 | tf_op jit(solution)/shard_map/ppermute | solution.py:25
  6.0 4.6 %collective-permute-start = (f32[4,3072]{1,0:T(4,128)}, f32[4,3072]{1,0:T(4,128)}, u32[]{:S(2)}, u32[]{:S(2)}) collective-permute-start(f32[4,3072]{1,0:T(4,128)} %get-tuple-element.55), channel_id=1, source_target_pairs={{0,8},{8,0},{1,9},{9,1},{2,10},{10,2},{3,11},{11,3},{4,12},{12,4},... | collective-permute-start | bytes 147464 | tf_op jit(solution)/shard_map/ppermute | solution.py:25
  6.0 20.4 %collective-permute-start.1 = (f32[4,3072]{1,0:T(4,128)S(1)}, f32[4,3072]{1,0:T(4,128)S(1)}, u32[]{:S(2)}, u32[]{:S(2)}) collective-permute-start(f32[4,3072]{1,0:T(4,128)S(1)} %get-tuple-element.53), channel_id=1, source_target_pairs={{0,8},{8,0},{1,9},{9,1},{2,10},{10,2},{3,11},{11,3},{4,12},{12,4},... | collective-permute-start | bytes 147464 | tf_op jit(solution)/shard_map/ppermute | solution.py:25
  7.9 6.2 %collective-permute-start.3 = (bf16[4,8,3072]{2,1,0:T(8,128)(2,1)S(1)}, bf16[4,8,3072]{2,1,0:T(8,128)(2,1)S(1)}, u32[]{:S(2)}, u32[]{:S(2)}) collective-permute-start(bf16[4,8,3072]{2,1,0:T(8,128)(2,1)S(1)} %get-tuple-element.24), channel_id=1, source_target_pairs={{0,32},{32,0},{1,33},{33,1},{2,34},{34,2},{3,35},{35,3},{4,36},{36... | collective-permute-start | bytes 589832 | tf_op jit(solution)/shard_map/ppermute | solution.py:25
  8.0 6.5 %collective-permute-start.4 = (bf16[4,8,3072]{2,1,0:T(8,128)(2,1)S(1)}, bf16[4,8,3072]{2,1,0:T(8,128)(2,1)S(1)}, u32[]{:S(2)}, u32[]{:S(2)}) collective-permute-start(bf16[4,8,3072]{2,1,0:T(8,128)(2,1)S(1)} %get-tuple-element.25), channel_id=1, source_target_pairs={{0,16},{16,0},{1,17},{17,1},{2,18},{18,2},{3,19},{19,3},{4,20},{20... | collective-permute-start | bytes 589832 | tf_op jit(solution)/shard_map/ppermute | solution.py:25
  9.2 8.8 %collective-permute-start.5 = (bf16[4,8,3072]{2,1,0:T(8,128)(2,1)S(1)}, bf16[4,8,3072]{2,1,0:T(8,128)(2,1)S(1)}, u32[]{:S(2)}, u32[]{:S(2)}) collective-permute-start(bf16[4,8,3072]{2,1,0:T(8,128)(2,1)S(1)} %get-tuple-element.26), channel_id=1, source_target_pairs={{0,48},{16,32},{32,16},{48,0},{1,49},{17,33},{33,17},{49,1},{2,50}... | collective-permute-start | bytes 589832 | tf_op jit(solution)/shard_map/ppermute | solution.py:25
  18.7 8.2 %collective-permute-start.6 = (bf16[8,3072]{1,0:T(8,128)(2,1)S(1)}, bf16[8,3072]{1,0:T(8,128)(2,1)S(1)}, u32[]{:S(2)}, u32[]{:S(2)}) collective-permute-start(bf16[8,3072]{1,0:T(8,128)(2,1)S(1)} %get-tuple-element.28), channel_id=1, source_target_pairs={{0,128},{64,192},{128,0},{192,64},{1,129},{65,193},{129,1},{193,65... | collective-permute-start | bytes 147464 | tf_op jit(solution)/shard_map/ppermute | solution.py:25
  25.3 5.2 %collective-permute-start.7 = (bf16[8,3072]{1,0:T(8,128)(2,1)S(1)}, bf16[8,3072]{1,0:T(8,128)(2,1)S(1)}, u32[]{:S(2)}, u32[]{:S(2)}) collective-permute-start(bf16[8,3072]{1,0:T(8,128)(2,1)S(1)} %get-tuple-element.29), channel_id=1, source_target_pairs={{0,64},{64,0},{128,192},{192,128},{1,65},{65,1},{129,193},{193,129... | collective-permute-start | bytes 147464 | tf_op jit(solution)/shard_map/ppermute | solution.py:25
  26.5 5.3 %collective-permute-start.8 = (bf16[8,3072]{1,0:T(8,128)(2,1)S(1)}, bf16[8,3072]{1,0:T(8,128)(2,1)S(1)}, u32[]{:S(2)}, u32[]{:S(2)}) collective-permute-start(bf16[8,3072]{1,0:T(8,128)(2,1)S(1)} %get-tuple-element.30), channel_id=1, source_target_pairs={{0,192},{64,128},{128,64},{192,0},{1,193},{65,129},{129,65},{193,1... | collective-permute-start | bytes 147464 | tf_op jit(solution)/shard_map/ppermute | solution.py:25
  32.0 10.4 %collective-permute-start.11 = (bf16[2,8,3200]{2,1,0:T(8,128)(2,1)S(1)}, bf16[2,8,3200]{2,1,0:T(8,128)(2,1)S(1)}, u32[]{:S(2)}, u32[]{:S(2)}) collective-permute-start(bf16[2,8,3200]{2,1,0:T(8,128)(2,1)S(1)} %get-tuple-element.31.refs_0_), channel_id=1, source_target_pairs={{0,128},{64,192},{128,0},{192,64},{1,129},{65,193},{129,1},{193,65... | collective-permute-start | bytes 307208 | tf_op jit(solution)/shard_map/ppermute | solution.py:25
  34.1 11.4 %collective-permute-start.10 = (bf16[2,8,3200]{2,1,0:T(8,128)(2,1)S(1)}, bf16[2,8,3200]{2,1,0:T(8,128)(2,1)S(1)}, u32[]{:S(2)}, u32[]{:S(2)}) collective-permute-start(bf16[2,8,3200]{2,1,0:T(8,128)(2,1)S(1)} %get-tuple-element.31.refs_0_), channel_id=1, source_target_pairs={{0,64},{64,0},{128,192},{192,128},{1,65},{65,1},{129,193},{193,129... | collective-permute-start | bytes 307208 | tf_op jit(solution)/shard_map/ppermute | solution.py:25
  34.7 10.9 %collective-permute-start.9 = (bf16[2,8,3200]{2,1,0:T(8,128)(2,1)S(1)}, bf16[2,8,3200]{2,1,0:T(8,128)(2,1)S(1)}, u32[]{:S(2)}, u32[]{:S(2)}) collective-permute-start(bf16[2,8,3200]{2,1,0:T(8,128)(2,1)S(1)} %get-tuple-element.31.refs_0_), channel_id=1, source_target_pairs={{0,192},{64,128},{128,64},{192,0},{1,193},{65,129},{129,65},{193,1... | collective-permute-start | bytes 307208 | tf_op jit(solution)/shard_map/ppermute | solution.py:25
  37.8 4.5 %collective-permute-start.12 = (f32[4,3072]{1,0:T(4,128)S(1)}, f32[4,3072]{1,0:T(4,128)S(1)}, u32[]{:S(2)}, u32[]{:S(2)}) collective-permute-start(f32[4,3072]{1,0:T(4,128)S(1)} %get-tuple-element.51), channel_id=1, source_target_pairs={{0,8},{8,0},{1,9},{9,1},{2,10},{10,2},{3,11},{11,3},{4,12},{12,4},... | collective-permute-start | bytes 147464 | tf_op jit(solution)/shard_map/ppermute | solution.py:25
  45.6 16.0 %collective-permute-start.14 = (bf16[4,2,8,3072]{3,2,1,0:T(8,128)(2,1)S(1)}, bf16[4,2,8,3072]{3,2,1,0:T(8,128)(2,1)S(1)}, u32[]{:S(2)}, u32[]{:S(2)}) collective-permute-start(bf16[4,2,8,3072]{3,2,1,0:T(8,128)(2,1)S(1)} %get-tuple-element.37.refs_0_), channel_id=1, source_target_pairs={{0,16},{16,0},{1,17},{17,1},{2,18},{18,2},{3,19},{19,3},{4,20},{20... | collective-permute-start | bytes 1179656 | tf_op jit(solution)/shard_map/ppermute | solution.py:25
  45.7 15.9 %collective-permute-start.13 = (bf16[4,2,8,3072]{3,2,1,0:T(8,128)(2,1)S(1)}, bf16[4,2,8,3072]{3,2,1,0:T(8,128)(2,1)S(1)}, u32[]{:S(2)}, u32[]{:S(2)}) collective-permute-start(bf16[4,2,8,3072]{3,2,1,0:T(8,128)(2,1)S(1)} %get-tuple-element.37.refs_0_), channel_id=1, source_target_pairs={{0,32},{32,0},{1,33},{33,1},{2,34},{34,2},{3,35},{35,3},{4,36},{36... | collective-permute-start | bytes 1179656 | tf_op jit(solution)/shard_map/ppermute | solution.py:25
  61.9 5.1 %collective-permute-start.17 = (bf16[3,4,8,3200]{3,2,1,0:T(8,128)(2,1)S(1)}, bf16[3,4,8,3200]{3,2,1,0:T(8,128)(2,1)S(1)}, u32[]{:S(2)}, u32[]{:S(2)}) collective-permute-start(bf16[3,4,8,3200]{3,2,1,0:T(8,128)(2,1)S(1)} %source.1.sources_ref), channel_id=1, source_target_pairs={{0,8},{8,0},{1,9},{9,1},{2,10},{10,2},{3,11},{11,3},{4,12},{12,4},... | collective-permute-start | bytes 1843208 | tf_op jit(solution)/shard_map/ppermute | solution.py:25
  65.4 4.5 %collective-permute-start.16 = (bf16[4,8,1536]{2,1,0:T(8,128)(2,1)S(1)}, bf16[4,8,1536]{2,1,0:T(8,128)(2,1)S(1)}, u32[]{:S(2)}, u32[]{:S(2)}) collective-permute-start(bf16[4,8,1536]{2,1,0:T(8,128)(2,1)S(1)} %get-tuple-element.48), channel_id=1, source_target_pairs={{0,32},{32,0},{1,33},{33,1},{2,34},{34,2},{3,35},{35,3},{4,36},{36... | collective-permute-start | bytes 294920 | tf_op jit(solution)/shard_map/ppermute | solution.py:25
  65.8 4.1 %collective-permute-start.15 = (bf16[4,8,1536]{2,1,0:T(8,128)(2,1)S(1)}, bf16[4,8,1536]{2,1,0:T(8,128)(2,1)S(1)}, u32[]{:S(2)}, u32[]{:S(2)}) collective-permute-start(bf16[4,8,1536]{2,1,0:T(8,128)(2,1)S(1)} %get-tuple-element.49), channel_id=1, source_target_pairs={{0,16},{16,0},{1,17},{17,1},{2,18},{18,2},{3,19},{19,3},{4,20},{20... | collective-permute-start | bytes 294920 | tf_op jit(solution)/shard_map/ppermute | solution.py:25
  69.9 2.3 %collective-permute-start.18 = (bf16[4,8,3072]{2,1,0:T(8,128)(2,1)S(1)}, bf16[4,8,3072]{2,1,0:T(8,128)(2,1)S(1)}, u32[]{:S(2)}, u32[]{:S(2)}) collective-permute-start(bf16[4,8,3072]{2,1,0:T(8,128)(2,1)S(1)} %constant_dynamic-update-slice_fusion.source_ref), channel_id=1, source_target_pairs={{0,8},{8,0},{1,9},{9,1},{2,10},{10,2},{3,11},{11,3},{4,12},{12,4},... | collective-permute-start | bytes 589832 | tf_op jit(solution)/shard_map/ppermute | solution.py:25

commit v11 on v9

--- a/solution.py
+++ b/solution.py
@@ -128,7 +128,7 @@
 
 
 def source_kernel(max_norm, sums_ref, *refs):
-    joined_refs, source_ref = refs[:-1], refs[-1]
+    joined_refs, source_ref = (refs[0], refs[2], refs[1]), refs[-1]
     rows, width = joined_refs[0].shape[2:]
     square_sum = jnp.sum(sums_ref[:, 0, :1], axis=0, keepdims=True)
     factor = jnp.minimum(1.0, max_norm / (jnp.sqrt(square_sum) + 1e-06))
@@ -285,8 +285,8 @@
     )(*packs)
 
     sums = lax.all_to_all(sums, GROUPS, 0, 0, tiled=True)
+    far = over_y(joined)
     after = over_z(joined)
-    far = over_y(joined)
     sources = pl.pallas_call(
         functools.partial(source_kernel, max_norm),
         out_shape=pltpu.VMEM((3, len(JUMPS), block, width + EXTRA), bf16),
@@ -294,10 +294,10 @@
         out_specs=VMEM,
         compiler_params=SMALL,
         name="source",
-    )(sums, joined, after, far)
-
+    )(sums, joined, far, after)
+
+    right = over_z(sources[2, :, :, width // 2 : width])
     left = over_y(sources[1, :, :, : width // 2])
-    right = over_z(sources[2, :, :, width // 2 : width])
     sources2 = over_core(sources)
 
     blocks = weights.reshape(2, chips, block, width)

time: 73.6 us -> 73.6 us (level)
  no operation moved by 1% of the time
where the time goes in v11:
time: 73.6 us; the launch traced here: 73.4 us
  starting transfers between devices  33.8 us (46%)
  waiting for transfers between devices  15.3 us (21%)
  blocking collectives  14.3 us (19%)
  Pallas kernels  7.39 us (10%)
  other arithmetic  1.03 us (1%)
  between operations  0.77 us (1%)
    ppermute x19, starting transfers between devices, over(): return lax.ppermute(array, axis, [(i, i ^ jump) for i in range(size)])  33.8 us
    ppermute x19, waiting for transfers between devices, over(): return lax.ppermute(array, axis, [(i, i ^ jump) for i in range(size)])  15.3 us
    all_to_all x1, blocking collectives, shards(): sums = lax.all_to_all(sums, GROUPS, 0, 0, tiled=True)  14.3 us
    pallas_call x1, Pallas kernels, shards(): pl.pallas_call(mix_and_state, out_shape=(mixed_type, state, state), in_sp...  2.72 us
  transfers between devices with their start and end apart: 19, of which 11 were waited for; matrix products, arithmetic and copies ran while one was open for 2% of the time, Pallas kernels for 6%

profile of v11, /device:TPU:1, one launch (start us, length us, event | category | flops | bytes accessed | tf_op | source)
XLA Modules:
  0.0 73.4 jit_solution(14612057736390002111)
XLA Ops:
  0.7 1.4 %cut.1 = bf16[128,3072]{1,0:T(8,128)(2,1)S(1)} custom-call(s32[1]{0:T(128)} %bitcast.10.which_ref, bf16[2,128,3072]{2,1,0:T(8,128)(2,1)} %bitcast.36), custom_call_target="tpu_custom_call" | custom-call | tf_op jit(solution)/shard_map/cut/pallas_call | solution.py:218
  2.0 3.3 %collective-permute-start.2 = (bf16[128,3072]{1,0:T(8,128)(2,1)S(1)}, bf16[128,3072]{1,0:T(8,128)(2,1)S(1)}, u32[]{:S(2)}, u32[]{:S(2)}) collective-permute-start(bf16[128,3072]{1,0:T(8,128)(2,1)S(1)} %cut.1), channel_id=1, source_target_pairs={{0,8},{8,0},{1,9},{9,1},{2,10},{10,2},{3,11},{11,3},{4,12},{12,4},... | collective-permute-start | bytes 2359304 | tf_op jit(solution)/shard_map/ppermute | solution.py:25
  5.4 0.6 dynamic-slice_bitcast_fusion.5
  6.0 0.0 collective-permute-start
  6.0 0.6 collective-permute-start.1
  6.6 0.1 pad_add_fusion.where_ref
  6.7 0.6 collective-permute-done.2
  7.3 0.7 reduced.2
  8.0 0.1 collective-permute-start.3
  8.1 1.2 %collective-permute-start.4 = (bf16[4,8,3072]{2,1,0:T(8,128)(2,1)S(1)}, bf16[4,8,3072]{2,1,0:T(8,128)(2,1)S(1)}, u32[]{:S(2)}, u32[]{:S(2)}) collective-permute-start(bf16[4,8,3072]{2,1,0:T(8,128)(2,1)S(1)} %get-tuple-element.26), channel_id=1, source_target_pairs={{0,16},{16,0},{1,17},{17,1},{2,18},{18,2},{3,19},{19,3},{4,20},{20... | collective-permute-start | bytes 589832 | tf_op jit(solution)/shard_map/ppermute | solution.py:25
  9.3 1.5 %collective-permute-start.5 = (bf16[4,8,3072]{2,1,0:T(8,128)(2,1)S(1)}, bf16[4,8,3072]{2,1,0:T(8,128)(2,1)S(1)}, u32[]{:S(2)}, u32[]{:S(2)}) collective-permute-start(bf16[4,8,3072]{2,1,0:T(8,128)(2,1)S(1)} %get-tuple-element.27), channel_id=1, source_target_pairs={{0,48},{16,32},{32,16},{48,0},{1,49},{17,33},{33,17},{49,1},{2,50}... | collective-permute-start | bytes 589832 | tf_op jit(solution)/shard_map/ppermute | solution.py:25
  10.7 0.0 collective-permute-done
  10.7 0.9 %maximum_select_fusion.outer_ref = f32[8,3072]{1,0:T(8,128)S(1)} fusion(f32[4,3072]{1,0:T(4,128)} %collective-permute-done, f32[4,3072]{1,0:T(4,128)S(1)} %get-tuple-element.56, pred[]{:T(512)S(6)} %eq.3), kind=kLoop, calls=%fused_computation.2 | loop fusion | flops 73728 | bytes 196609 | tf_op jit(solution)/shard_map/jit(_where)/select_n | solution.py:209
  11.6 2.5 %collective-permute-done.3.refs_0_ = bf16[4,8,3072]{2,1,0:T(8,128)(2,1)S(1)} collective-permute-done((bf16[4,8,3072]{2,1,0:T(8,128)(2,1)S(1)}, bf16[4,8,3072]{2,1,0:T(8,128)(2,1)S(1)}, u32[]{:S(2)}, u32[]{:S(2)}) %collective-permute-start.3) | collective-permute-done | bytes 196640 | tf_op jit(solution)/shard_map/ppermute | solution.py:25
  14.2 0.4 collective-permute-done.4.refs_1_
  14.5 3.6 %collective-permute-done.5.refs_2_ = bf16[4,8,3072]{2,1,0:T(8,128)(2,1)S(1)} collective-permute-done((bf16[4,8,3072]{2,1,0:T(8,128)(2,1)S(1)}, bf16[4,8,3072]{2,1,0:T(8,128)(2,1)S(1)}, u32[]{:S(2)}, u32[]{:S(2)}) %collective-permute-start.5) | collective-permute-done | bytes 196640 | tf_op jit(solution)/shard_map/ppermute | solution.py:25
  18.1 0.7 reduced.3
  18.8 6.6 %collective-permute-start.6 = (bf16[8,3072]{1,0:T(8,128)(2,1)S(1)}, bf16[8,3072]{1,0:T(8,128)(2,1)S(1)}, u32[]{:S(2)}, u32[]{:S(2)}) collective-permute-start(bf16[8,3072]{1,0:T(8,128)(2,1)S(1)} %get-tuple-element.29), channel_id=1, source_target_pairs={{0,128},{64,192},{128,0},{192,64},{1,129},{65,193},{129,1},{193,65... | collective-permute-start | bytes 147464 | tf_op jit(solution)/shard_map/ppermute | solution.py:25
  25.3 1.2 %collective-permute-start.7 = (bf16[8,3072]{1,0:T(8,128)(2,1)S(1)}, bf16[8,3072]{1,0:T(8,128)(2,1)S(1)}, u32[]{:S(2)}, u32[]{:S(2)}) collective-permute-start(bf16[8,3072]{1,0:T(8,128)(2,1)S(1)} %get-tuple-element.30), channel_id=1, source_target_pairs={{0,64},{64,0},{128,192},{192,128},{1,65},{65,1},{129,193},{193,129... | collective-permute-start | bytes 147464 | tf_op jit(solution)/shard_map/ppermute | solution.py:25
  26.5 0.0 collective-permute-start.8
  26.5 0.0 collective-permute-done.1
  26.6 0.3 collective-permute-done.6.refs_0_
  26.9 3.6 %collective-permute-done.7.refs_1_ = bf16[8,3072]{1,0:T(8,128)(2,1)S(1)} collective-permute-done((bf16[8,3072]{1,0:T(8,128)(2,1)S(1)}, bf16[8,3072]{1,0:T(8,128)(2,1)S(1)}, u32[]{:S(2)}, u32[]{:S(2)}) %collective-permute-start.7) | collective-permute-done | bytes 49184 | tf_op jit(solution)/shard_map/ppermute | solution.py:25
  30.6 1.3 %collective-permute-done.8.refs_2_ = bf16[8,3072]{1,0:T(8,128)(2,1)S(1)} collective-permute-done((bf16[8,3072]{1,0:T(8,128)(2,1)S(1)}, bf16[8,3072]{1,0:T(8,128)(2,1)S(1)}, u32[]{:S(2)}, u32[]{:S(2)}) %collective-permute-start.8) | collective-permute-done | bytes 49184 | tf_op jit(solution)/shard_map/ppermute | solution.py:25
  31.8 0.2 total.1
  32.1 0.6 collective-permute-start.11
  32.7 1.8 %collective-permute-start.10 = (bf16[2,8,3200]{2,1,0:T(8,128)(2,1)S(1)}, bf16[2,8,3200]{2,1,0:T(8,128)(2,1)S(1)}, u32[]{:S(2)}, u32[]{:S(2)}) collective-permute-start(bf16[2,8,3200]{2,1,0:T(8,128)(2,1)S(1)} %get-tuple-element.34.refs_0_), channel_id=1, source_target_pairs={{0,64},{64,0},{128,192},{192,128},{1,65},{65,1},{129,193},{193,129... | collective-permute-start | bytes 307208 | tf_op jit(solution)/shard_map/ppermute | solution.py:25
  34.5 3.3 %collective-permute-start.9 = (bf16[2,8,3200]{2,1,0:T(8,128)(2,1)S(1)}, bf16[2,8,3200]{2,1,0:T(8,128)(2,1)S(1)}, u32[]{:S(2)}, u32[]{:S(2)}) collective-permute-start(bf16[2,8,3200]{2,1,0:T(8,128)(2,1)S(1)} %get-tuple-element.34.refs_0_), channel_id=1, source_target_pairs={{0,128},{64,192},{128,0},{192,64},{1,129},{65,193},{129,1},{193,65... | collective-permute-start | bytes 307208 | tf_op jit(solution)/shard_map/ppermute | solution.py:25
  37.9 3.7 %collective-permute-start.12 = (f32[4,3072]{1,0:T(4,128)S(1)}, f32[4,3072]{1,0:T(4,128)S(1)}, u32[]{:S(2)}, u32[]{:S(2)}) collective-permute-start(f32[4,3072]{1,0:T(4,128)S(1)} %get-tuple-element.53), channel_id=1, source_target_pairs={{0,8},{8,0},{1,9},{9,1},{2,10},{10,2},{3,11},{11,3},{4,12},{12,4},... | collective-permute-start | bytes 147464 | tf_op jit(solution)/shard_map/ppermute | solution.py:25
  41.5 0.9 %collective-permute-done.12.refs_3_ = f32[4,3072]{1,0:T(4,128)S(1)} collective-permute-done((f32[4,3072]{1,0:T(4,128)S(1)}, f32[4,3072]{1,0:T(4,128)S(1)}, u32[]{:S(2)}, u32[]{:S(2)}) %collective-permute-start.12) | collective-permute-done | bytes 49184 | tf_op jit(solution)/shard_map/ppermute | solution.py:25
  42.4 0.0 collective-permute-done.11.refs_3_
  42.4 0.0 collective-permute-done.10.refs_2_
  42.4 0.0 collective-permute-done.9.refs_1_
  42.4 0.1 join.1
  42.5 2.5 %collective-permute-start.14 = (bf16[4,2,8,3072]{3,2,1,0:T(8,128)(2,1)S(1)}, bf16[4,2,8,3072]{3,2,1,0:T(8,128)(2,1)S(1)}, u32[]{:S(2)}, u32[]{:S(2)}) collective-permute-start(bf16[4,2,8,3072]{3,2,1,0:T(8,128)(2,1)S(1)} %get-tuple-element.39.refs_0_), channel_id=1, source_target_pairs={{0,32},{32,0},{1,33},{33,1},{2,34},{34,2},{3,35},{35,3},{4,36},{36... | collective-permute-start | bytes 1179656 | tf_op jit(solution)/shard_map/ppermute | solution.py:25
  45.0 0.0 collective-permute-start.13
  45.0 14.3 %all_to_all.5.sums_ref = f32[32,1,128]{2,1,0:T(1,128)S(1)} all-to-all(f32[32,1,128]{2,1,0:T(1,128)S(1)} %get-tuple-element.38), channel_id=1, replica_groups=mesh['zh'=4,'zl'=2,'yl'=2,'core'=2,'x'=4,'yh'=2] {'zl','yl','x','yh'}, dimensions={0} | all-to-all | bytes 32768 | tf_op jit(solution)/shard_map/all_to_all | solution.py:287
  59.3 0.0 collective-permute-done.14.refs_2_
  59.3 0.3 source.1.sources_ref
  59.6 5.6 %collective-permute-start.17 = (bf16[3,4,8,3200]{3,2,1,0:T(8,128)(2,1)S(1)}, bf16[3,4,8,3200]{3,2,1,0:T(8,128)(2,1)S(1)}, u32[]{:S(2)}, u32[]{:S(2)}) collective-permute-start(bf16[3,4,8,3200]{3,2,1,0:T(8,128)(2,1)S(1)} %source.1.sources_ref), channel_id=1, source_target_pairs={{0,8},{8,0},{1,9},{9,1},{2,10},{10,2},{3,11},{11,3},{4,12},{12,4},... | collective-permute-start | bytes 1843208 | tf_op jit(solution)/shard_map/ppermute | solution.py:25
  65.2 0.4 collective-permute-start.16
  65.6 0.3 collective-permute-start.15
  65.9 0.9 %collective-permute-done.17.sources2_ref = bf16[3,4,8,3200]{3,2,1,0:T(8,128)(2,1)S(1)} collective-permute-done((bf16[3,4,8,3200]{3,2,1,0:T(8,128)(2,1)S(1)}, bf16[3,4,8,3200]{3,2,1,0:T(8,128)(2,1)S(1)}, u32[]{:S(2)}, u32[]{:S(2)}) %collective-permute-start.17) | collective-permute-done | bytes 614432 | tf_op jit(solution)/shard_map/ppermute | solution.py:25
  66.8 2.7 %mix.1 = (bf16[2,16,8,3072]{3,2,1,0:T(8,128)(2,1)}, f32[2,4,3072]{2,1,0:T(4,128)}, f32[2,4,3072]{2,1,0:T(4,128)}) custom-call(s32[4]{0:T(128)S(1)} %pad_add_fusion.where_ref, bf16[2,16,8,3072]{3,2,1,0:T(8,128)(2,1)S(1)} %bitcast.39, bf16[3,4,8,3200]{3,2,1,0:T(8,128)(2,1)S(1)} %source.1.sources_ref, ...), custom_call_target="tpu_custom_call" | custom-call | tf_op jit(solution)/shard_map/mix/pallas_call | solution.py:327
  69.6 0.1 collective-permute-done.16
  69.7 1.2 %collective-permute-start.18 = (bf16[4,8,3072]{2,1,0:T(8,128)(2,1)S(1)}, bf16[4,8,3072]{2,1,0:T(8,128)(2,1)S(1)}, u32[]{:S(2)}, u32[]{:S(2)}) collective-permute-start(bf16[4,8,3072]{2,1,0:T(8,128)(2,1)S(1)} %constant_dynamic-update-slice_fusion.source_ref), channel_id=1, source_target_pairs={{0,8},{8,0},{1,9},{9,1},{2,10},{10,2},{3,11},{11,3},{4,12},{12,4},... | collective-permute-start | bytes 589832 | tf_op jit(solution)/shard_map/ppermute | solution.py:25
  70.9 1.1 %collective-permute-done.18.source2_ref = bf16[4,8,3072]{2,1,0:T(8,128)(2,1)S(1)} collective-permute-done((bf16[4,8,3072]{2,1,0:T(8,128)(2,1)S(1)}, bf16[4,8,3072]{2,1,0:T(8,128)(2,1)S(1)}, u32[]{:S(2)}, u32[]{:S(2)}) %collective-permute-start.18) | collective-permute-done | bytes 196640 | tf_op jit(solution)/shard_map/ppermute | solution.py:25
  72.0 1.4 %mix_last.1 = bf16[2,16,8,3072]{3,2,1,0:T(8,128)(2,1)} custom-call(s32[4]{0:T(128)S(1)} %pad_add_fusion.where_ref, bf16[2,16,8,3072]{3,2,1,0:T(8,128)(2,1)S(1)} %bitcast.40, bf16[4,8,3072]{2,1,0:T(8,128)(2,1)S(1)} %constant_dynamic-update-slice_fusion.source_ref, ...), custom_call_target="tpu_custom_call", output_to_operand_aliasing={{}: (4, {})} | custom-call | tf_op jit(solution)/shard_map/mix_last/pallas_call | solution.py:347
  (15 shorter events, 0.1 us)
Async XLA Ops:
  0.6 6.7 %copy-start = (bf16[2,1,1,128,3072]{4,3,2,1,0:T(8,128)(2,1)S(1)}, bf16[2,1,1,128,3072]{4,3,2,1,0:T(8,128)(2,1)}, u32[]{:S(2)}) copy-start(bf16[2,1,1,128,3072]{4,3,2,1,0:T(8,128)(2,1)} %param.3) | copy-start | bytes 4718596
  0.6 4.7 %copy-start.1 = (f32[2,1,4,3072]{3,2,1,0:T(4,128)S(1)}, f32[2,1,4,3072]{3,2,1,0:T(4,128)}, u32[]{:S(2)}) copy-start(f32[2,1,4,3072]{3,2,1,0:T(4,128)} %param.4) | copy-start | bytes 294916
  0.7 5.4 %copy-start.2 = (f32[2,1,4,3072]{3,2,1,0:T(4,128)S(1)}, f32[2,1,4,3072]{3,2,1,0:T(4,128)}, u32[]{:S(2)}) copy-start(f32[2,1,4,3072]{3,2,1,0:T(4,128)} %param.5) | copy-start | bytes 294916
  2.0 5.2 %collective-permute-start.2 = (bf16[128,3072]{1,0:T(8,128)(2,1)S(1)}, bf16[128,3072]{1,0:T(8,128)(2,1)S(1)}, u32[]{:S(2)}, u32[]{:S(2)}) collective-permute-start(bf16[128,3072]{1,0:T(8,128)(2,1)S(1)} %cut.1), channel_id=1, source_target_pairs={{0,8},{8,0},{1,9},{9,1},{2,10},{10,2},{3,11},{11,3},{4,12},{12,4},... | collective-permute-start | bytes 2359304 | tf_op jit(solution)/shard_map/ppermute | solution.py:25
  6.0 4.7 %collective-permute-start = (f32[4,3072]{1,0:T(4,128)}, f32[4,3072]{1,0:T(4,128)}, u32[]{:S(2)}, u32[]{:S(2)}) collective-permute-start(f32[4,3072]{1,0:T(4,128)} %get-tuple-element.57), channel_id=1, source_target_pairs={{0,8},{8,0},{1,9},{9,1},{2,10},{10,2},{3,11},{11,3},{4,12},{12,4},... | collective-permute-start | bytes 147464 | tf_op jit(solution)/shard_map/ppermute | solution.py:25
  6.0 20.5 %collective-permute-start.1 = (f32[4,3072]{1,0:T(4,128)S(1)}, f32[4,3072]{1,0:T(4,128)S(1)}, u32[]{:S(2)}, u32[]{:S(2)}) collective-permute-start(f32[4,3072]{1,0:T(4,128)S(1)} %get-tuple-element.55), channel_id=1, source_target_pairs={{0,8},{8,0},{1,9},{9,1},{2,10},{10,2},{3,11},{11,3},{4,12},{12,4},... | collective-permute-start | bytes 147464 | tf_op jit(solution)/shard_map/ppermute | solution.py:25
  8.0 6.2 %collective-permute-start.3 = (bf16[4,8,3072]{2,1,0:T(8,128)(2,1)S(1)}, bf16[4,8,3072]{2,1,0:T(8,128)(2,1)S(1)}, u32[]{:S(2)}, u32[]{:S(2)}) collective-permute-start(bf16[4,8,3072]{2,1,0:T(8,128)(2,1)S(1)} %get-tuple-element.25), channel_id=1, source_target_pairs={{0,32},{32,0},{1,33},{33,1},{2,34},{34,2},{3,35},{35,3},{4,36},{36... | collective-permute-start | bytes 589832 | tf_op jit(solution)/shard_map/ppermute | solution.py:25
  8.1 6.5 %collective-permute-start.4 = (bf16[4,8,3072]{2,1,0:T(8,128)(2,1)S(1)}, bf16[4,8,3072]{2,1,0:T(8,128)(2,1)S(1)}, u32[]{:S(2)}, u32[]{:S(2)}) collective-permute-start(bf16[4,8,3072]{2,1,0:T(8,128)(2,1)S(1)} %get-tuple-element.26), channel_id=1, source_target_pairs={{0,16},{16,0},{1,17},{17,1},{2,18},{18,2},{3,19},{19,3},{4,20},{20... | collective-permute-start | bytes 589832 | tf_op jit(solution)/shard_map/ppermute | solution.py:25
  9.3 8.8 %collective-permute-start.5 = (bf16[4,8,3072]{2,1,0:T(8,128)(2,1)S(1)}, bf16[4,8,3072]{2,1,0:T(8,128)(2,1)S(1)}, u32[]{:S(2)}, u32[]{:S(2)}) collective-permute-start(bf16[4,8,3072]{2,1,0:T(8,128)(2,1)S(1)} %get-tuple-element.27), channel_id=1, source_target_pairs={{0,48},{16,32},{32,16},{48,0},{1,49},{17,33},{33,17},{49,1},{2,50}... | collective-permute-start | bytes 589832 | tf_op jit(solution)/shard_map/ppermute | solution.py:25
  18.8 8.2 %collective-permute-start.6 = (bf16[8,3072]{1,0:T(8,128)(2,1)S(1)}, bf16[8,3072]{1,0:T(8,128)(2,1)S(1)}, u32[]{:S(2)}, u32[]{:S(2)}) collective-permute-start(bf16[8,3072]{1,0:T(8,128)(2,1)S(1)} %get-tuple-element.29), channel_id=1, source_target_pairs={{0,128},{64,192},{128,0},{192,64},{1,129},{65,193},{129,1},{193,65... | collective-permute-start | bytes 147464 | tf_op jit(solution)/shard_map/ppermute | solution.py:25
  25.3 5.2 %collective-permute-start.7 = (bf16[8,3072]{1,0:T(8,128)(2,1)S(1)}, bf16[8,3072]{1,0:T(8,128)(2,1)S(1)}, u32[]{:S(2)}, u32[]{:S(2)}) collective-permute-start(bf16[8,3072]{1,0:T(8,128)(2,1)S(1)} %get-tuple-element.30), channel_id=1, source_target_pairs={{0,64},{64,0},{128,192},{192,128},{1,65},{65,1},{129,193},{193,129... | collective-permute-start | bytes 147464 | tf_op jit(solution)/shard_map/ppermute | solution.py:25
  26.5 5.3 %collective-permute-start.8 = (bf16[8,3072]{1,0:T(8,128)(2,1)S(1)}, bf16[8,3072]{1,0:T(8,128)(2,1)S(1)}, u32[]{:S(2)}, u32[]{:S(2)}) collective-permute-start(bf16[8,3072]{1,0:T(8,128)(2,1)S(1)} %get-tuple-element.31), channel_id=1, source_target_pairs={{0,192},{64,128},{128,64},{192,0},{1,193},{65,129},{129,65},{193,1... | collective-permute-start | bytes 147464 | tf_op jit(solution)/shard_map/ppermute | solution.py:25
  32.1 10.4 %collective-permute-start.11 = (bf16[2,8,3200]{2,1,0:T(8,128)(2,1)S(1)}, bf16[2,8,3200]{2,1,0:T(8,128)(2,1)S(1)}, u32[]{:S(2)}, u32[]{:S(2)}) collective-permute-start(bf16[2,8,3200]{2,1,0:T(8,128)(2,1)S(1)} %get-tuple-element.34.refs_0_), channel_id=1, source_target_pairs={{0,192},{64,128},{128,64},{192,0},{1,193},{65,129},{129,65},{193,1... | collective-permute-start | bytes 307208 | tf_op jit(solution)/shard_map/ppermute | solution.py:25
  32.7 9.7 %collective-permute-start.10 = (bf16[2,8,3200]{2,1,0:T(8,128)(2,1)S(1)}, bf16[2,8,3200]{2,1,0:T(8,128)(2,1)S(1)}, u32[]{:S(2)}, u32[]{:S(2)}) collective-permute-start(bf16[2,8,3200]{2,1,0:T(8,128)(2,1)S(1)} %get-tuple-element.34.refs_0_), channel_id=1, source_target_pairs={{0,64},{64,0},{128,192},{192,128},{1,65},{65,1},{129,193},{193,129... | collective-permute-start | bytes 307208 | tf_op jit(solution)/shard_map/ppermute | solution.py:25
  34.5 7.9 %collective-permute-start.9 = (bf16[2,8,3200]{2,1,0:T(8,128)(2,1)S(1)}, bf16[2,8,3200]{2,1,0:T(8,128)(2,1)S(1)}, u32[]{:S(2)}, u32[]{:S(2)}) collective-permute-start(bf16[2,8,3200]{2,1,0:T(8,128)(2,1)S(1)} %get-tuple-element.34.refs_0_), channel_id=1, source_target_pairs={{0,128},{64,192},{128,0},{192,64},{1,129},{65,193},{129,1},{193,65... | collective-permute-start | bytes 307208 | tf_op jit(solution)/shard_map/ppermute | solution.py:25
  37.9 4.5 %collective-permute-start.12 = (f32[4,3072]{1,0:T(4,128)S(1)}, f32[4,3072]{1,0:T(4,128)S(1)}, u32[]{:S(2)}, u32[]{:S(2)}) collective-permute-start(f32[4,3072]{1,0:T(4,128)S(1)} %get-tuple-element.53), channel_id=1, source_target_pairs={{0,8},{8,0},{1,9},{9,1},{2,10},{10,2},{3,11},{11,3},{4,12},{12,4},... | collective-permute-start | bytes 147464 | tf_op jit(solution)/shard_map/ppermute | solution.py:25
  42.5 16.8 %collective-permute-start.14 = (bf16[4,2,8,3072]{3,2,1,0:T(8,128)(2,1)S(1)}, bf16[4,2,8,3072]{3,2,1,0:T(8,128)(2,1)S(1)}, u32[]{:S(2)}, u32[]{:S(2)}) collective-permute-start(bf16[4,2,8,3072]{3,2,1,0:T(8,128)(2,1)S(1)} %get-tuple-element.39.refs_0_), channel_id=1, source_target_pairs={{0,32},{32,0},{1,33},{33,1},{2,34},{34,2},{3,35},{35,3},{4,36},{36... | collective-permute-start | bytes 1179656 | tf_op jit(solution)/shard_map/ppermute | solution.py:25
  45.0 14.3 %collective-permute-start.13 = (bf16[4,2,8,3072]{3,2,1,0:T(8,128)(2,1)S(1)}, bf16[4,2,8,3072]{3,2,1,0:T(8,128)(2,1)S(1)}, u32[]{:S(2)}, u32[]{:S(2)}) collective-permute-start(bf16[4,2,8,3072]{3,2,1,0:T(8,128)(2,1)S(1)} %get-tuple-element.39.refs_0_), channel_id=1, source_target_pairs={{0,16},{16,0},{1,17},{17,1},{2,18},{18,2},{3,19},{19,3},{4,20},{20... | collective-permute-start | bytes 1179656 | tf_op jit(solution)/shard_map/ppermute | solution.py:25
  59.6 7.2 %collective-permute-start.17 = (bf16[3,4,8,3200]{3,2,1,0:T(8,128)(2,1)S(1)}, bf16[3,4,8,3200]{3,2,1,0:T(8,128)(2,1)S(1)}, u32[]{:S(2)}, u32[]{:S(2)}) collective-permute-start(bf16[3,4,8,3200]{3,2,1,0:T(8,128)(2,1)S(1)} %source.1.sources_ref), channel_id=1, source_target_pairs={{0,8},{8,0},{1,9},{9,1},{2,10},{10,2},{3,11},{11,3},{4,12},{12,4},... | collective-permute-start | bytes 1843208 | tf_op jit(solution)/shard_map/ppermute | solution.py:25
  65.2 4.5 %collective-permute-start.16 = (bf16[4,8,1536]{2,1,0:T(8,128)(2,1)S(1)}, bf16[4,8,1536]{2,1,0:T(8,128)(2,1)S(1)}, u32[]{:S(2)}, u32[]{:S(2)}) collective-permute-start(bf16[4,8,1536]{2,1,0:T(8,128)(2,1)S(1)} %get-tuple-element.50), channel_id=1, source_target_pairs={{0,32},{32,0},{1,33},{33,1},{2,34},{34,2},{3,35},{35,3},{4,36},{36... | collective-permute-start | bytes 294920 | tf_op jit(solution)/shard_map/ppermute | solution.py:25
  65.6 4.1 %collective-permute-start.15 = (bf16[4,8,1536]{2,1,0:T(8,128)(2,1)S(1)}, bf16[4,8,1536]{2,1,0:T(8,128)(2,1)S(1)}, u32[]{:S(2)}, u32[]{:S(2)}) collective-permute-start(bf16[4,8,1536]{2,1,0:T(8,128)(2,1)S(1)} %get-tuple-element.51), channel_id=1, source_target_pairs={{0,16},{16,0},{1,17},{17,1},{2,18},{18,2},{3,19},{19,3},{4,20},{20... | collective-permute-start | bytes 294920 | tf_op jit(solution)/shard_map/ppermute | solution.py:25
  69.7 2.3 %collective-permute-start.18 = (bf16[4,8,3072]{2,1,0:T(8,128)(2,1)S(1)}, bf16[4,8,3072]{2,1,0:T(8,128)(2,1)S(1)}, u32[]{:S(2)}, u32[]{:S(2)}) collective-permute-start(bf16[4,8,3072]{2,1,0:T(8,128)(2,1)S(1)} %constant_dynamic-update-slice_fusion.source_ref), channel_id=1, source_target_pairs={{0,8},{8,0},{1,9},{9,1},{2,10},{10,2},{3,11},{11,3},{4,12},{12,4},... | collective-permute-start | bytes 589832 | tf_op jit(solution)/shard_map/ppermute | solution.py:25
